TPU v7x, 32 devices: a whole 2x2x4 slice. The times are simulated.
32 devices in a mesh: dp: 4 (over y, core), frame: 2 (over x), lon: 4 (over z).
Axes of the slice: x: 2, y: 2, z: 4, core: 2. Of those that a mesh axis runs over, the one named last changes fastest.
Arguments:
- fields: bfloat16 [4, 2, 4, 1440, 1024], P('dp', 'frame', None, 'lon'), may hold values from -6 to 6
- band_rows: int32 [4, 4], P('dp'), may hold values from 0 to 719
- earliest_past_snapshot: int32 [4], P('dp'), may hold values from 0 to 1
- lat_table: bfloat16 [720, 1024], replicated, may hold values from -3 to 3
- norm_gain: float32 [1024], replicated, may hold values from 0.5 to 1.5
- w_in1: bfloat16 [2, 16, 64, 64], P(None, 'lon'), may hold values from -0.5 to 0.5
- b_in1: float32 [2, 1024], P(None, 'lon'), may hold values from -1.5 to 1.5
- w_out2: bfloat16 [2, 16, 64, 64], P(None, 'lon'), may hold values from -0.5 to 0.5
- b_out2: float32 [2, 1024], P(None, 'lon'), may hold values from -0.25 to 0.25
- w_query: bfloat16 [1024, 1024], replicated, may hold values from -0.1875 to 0.1875
- w_keyval: bfloat16 [1024, 512], replicated, may hold values from -0.1875 to 0.1875
- w_output: bfloat16 [1024, 1024], replicated, may hold values from -0.1875 to 0.1875
- score_scale: float32 [16], replicated, may hold values from 0.5 to 100
- spec_cot: bfloat16 [4, 2, 4, 2, 368, 1024], P('dp', 'frame', None, None, None, 'lon'), may hold values from -0.05517578 to 0.05517578
Outputs:
- predicted_output_fields: bfloat16 [4, 2, 4, 1440, 1024], P('dp', 'frame', None, 'lon')
- mask_coefficient2_derivative: float32 [2, 16, 64, 64], P(None, 'lon')
- mask_offset2_derivative: float32 [2, 1024], P(None, 'lon')
All inputs are finite; a program needn't handle non-finite values.
Results may differ from a plain program's by a relative error of at most 0.03.
Values may be sent and summed in bfloat16 or wider, within the bound.
No kernel may reach another device: no remote copies, remote signals or barrier semaphores. Data moves between devices by JAX's collectives and lax.ppermute only.
A program may use at most 64 MiB of HBM per device.

v0:
```python
import math

import jax
import jax.numpy as jnp
from jax import lax
from jax.sharding import PartitionSpec as P


def transform_table(length, modes):
    longitude = jnp.arange(length, dtype=jnp.int32)
    zonal_wavenumber = jnp.arange(modes, dtype=jnp.int32)
    turns_mod = longitude[:, None] * zonal_wavenumber[None, :] % length
    angles = turns_mod.astype(jnp.float32) * (2.0 * math.pi / length)
    return jnp.concatenate([jnp.cos(angles), -jnp.sin(angles)], axis=1).astype(jnp.bfloat16)


def inverse_table(forward, modes):
    zonal_wavenumber = jnp.arange(modes, dtype=jnp.int32)
    factor = jnp.where(zonal_wavenumber == 0, 1.0, 2.0).astype(jnp.float32)
    factor = jnp.concatenate([factor, factor])
    return (forward.astype(jnp.float32) * factor[None, :]).astype(jnp.bfloat16)


def block_mix(left, weight):
    return jnp.einsum("rmgc,gce->rmge", left, weight, preferred_element_type=jnp.float32)


def filter_modes(spectrum, w_in1, b_in1, w_out2, b_out2):
    spectral_real = spectrum[:, 0]
    spec_im = spectrum[:, 1]
    first_re = jax.nn.relu(
        block_mix(spectral_real, w_in1[0]) - block_mix(spec_im, w_in1[1]) + b_in1[0]
    ).astype(jnp.bfloat16)
    first_im = jax.nn.relu(
        block_mix(spectral_real, w_in1[1]) + block_mix(spec_im, w_in1[0]) + b_in1[1]
    ).astype(jnp.bfloat16)
    second_re = (
        block_mix(first_re, w_out2[0]) - block_mix(first_im, w_out2[1]) + b_out2[0]
    ).astype(jnp.bfloat16)
    second_im = (
        block_mix(first_re, w_out2[1]) + block_mix(first_im, w_out2[0]) + b_out2[1]
    ).astype(jnp.bfloat16)
    return (first_re, first_im, jnp.concatenate([second_re, second_im], axis=1))


def head_norm(values_in):
    return values_in * lax.rsqrt(jnp.mean(values_in * values_in, axis=-1, keepdims=True) + 1e-06)


def attend(
    queries, keys_all, value_rows_full, query_frame, first_seen, score_scale, kv_heads, head_size
):
    site_count, query_frames, width = queries.shape
    key_frames = keys_all.shape[1]
    groups = width // head_size // kv_heads
    q_five = queries.reshape(site_count, query_frames, kv_heads, groups, head_size)
    k_four = keys_all.reshape(site_count, key_frames, kv_heads, head_size)
    v_four = value_rows_full.reshape(site_count, key_frames, kv_heads, head_size)
    scores = jnp.einsum("sqkgd,stkd->kgqts", q_five, k_four, preferred_element_type=jnp.float32)
    scores = scores * (score_scale.reshape(kv_heads, groups, 1, 1, 1) / math.sqrt(head_size))
    key_ids = jnp.arange(key_frames, dtype=jnp.int32)[None, :, None]
    query_ids = query_frame[:, None, None]
    seen = (key_ids <= query_ids) & (
        (key_ids >= first_seen[None, None, :]) | (key_ids == query_ids)
    )
    scores = jnp.where(seen[None, None], scores, -1e30)
    top_score = jnp.max(scores, axis=-2, keepdims=True)
    weights = jnp.exp(scores - top_score)
    probs = (weights / jnp.sum(weights, axis=-2, keepdims=True)).astype(jnp.bfloat16)
    attended = jnp.einsum("kgqts,stkd->sqkgd", probs, v_four, preferred_element_type=jnp.float32)
    return attended.astype(jnp.bfloat16).reshape(site_count, query_frames, width)


def body(
    fields,
    band_rows,
    earliest_past_snapshot,
    lat_table,
    norm_gain,
    w_in1,
    b_in1,
    w_out2,
    b_out2,
    w_query,
    w_keyval,
    w_output,
    score_scale,
    spec_cot,
):
    samples, _, lat_rows, lon_local, width = fields.shape
    grid_rows = samples * lat_rows
    length = lon_local * lax.axis_size("lon")
    modes = spec_cot.shape[4]
    local_width = spec_cot.shape[5]
    blocks = w_in1.shape[1]
    block_size = w_in1.shape[2]
    forward = transform_table(length, modes)
    backward = inverse_table(forward, modes)
    scale_t = 1.0 / math.sqrt(length)
    lat_count = lat_table.shape[0]
    onehot = (
        band_rows[:, :, None] == jnp.arange(lat_count, dtype=jnp.int32)[None, None, :]
    ).astype(jnp.bfloat16)
    embedding = jnp.dot(
        onehot.reshape(grid_rows, lat_count), lat_table, preferred_element_type=jnp.float32
    )
    inputs = fields[:, 0].astype(jnp.float32) + embedding.reshape(samples, lat_rows, 1, width)
    center = jnp.mean(inputs, axis=-1, keepdims=True)
    spread = jnp.mean(jnp.square(inputs - center), axis=-1, keepdims=True)
    normed = ((inputs - center) * lax.rsqrt(spread + 1e-05) * norm_gain).astype(jnp.bfloat16)
    gathered = lax.all_to_all(
        normed.reshape(grid_rows, lon_local, width), "lon", split_axis=2, concat_axis=1, tiled=True
    )
    spectrum = (
        jnp.einsum("rnc,nk->rkc", gathered, forward, preferred_element_type=jnp.float32) * scale_t
    ).astype(jnp.bfloat16)
    spectrum = spectrum.reshape(grid_rows, 2, modes, blocks, block_size)
    first_re, first_im, mixed = filter_modes(
        spectrum,
        w_in1,
        b_in1.reshape(2, blocks, block_size),
        w_out2,
        b_out2.reshape(2, blocks, block_size),
    )
    mixed = mixed.reshape(grid_rows, 2 * modes, local_width)
    grid_part = (
        jnp.einsum("rkc,nk->rnc", mixed, backward, preferred_element_type=jnp.float32) * scale_t
    ).astype(jnp.bfloat16)
    returned = lax.all_to_all(grid_part, "lon", split_axis=1, concat_axis=2, tiled=True)
    hidden = (
        inputs + returned.reshape(samples, lat_rows, lon_local, width).astype(jnp.float32)
    ).astype(jnp.bfloat16)
    cotangent = spec_cot.reshape(grid_rows, 2, modes, blocks, block_size)
    grad_re = jnp.einsum(
        "rmgc,rmge->gce", first_re, cotangent[:, 0], preferred_element_type=jnp.float32
    )
    grad_re = grad_re + jnp.einsum(
        "rmgc,rmge->gce", first_im, cotangent[:, 1], preferred_element_type=jnp.float32
    )
    grad_im = jnp.einsum(
        "rmgc,rmge->gce", first_re, cotangent[:, 1], preferred_element_type=jnp.float32
    )
    grad_im = grad_im - jnp.einsum(
        "rmgc,rmge->gce", first_im, cotangent[:, 0], preferred_element_type=jnp.float32
    )
    bias_terms = jnp.sum(cotangent.astype(jnp.float32), axis=(0, 2)).reshape(2, local_width)
    mask_coefficient2_derivative, mask_offset2_derivative = lax.psum(
        (jnp.stack([grad_re, grad_im]), bias_terms), ("dp", "frame")
    )
    site_count = grid_rows * lon_local
    tokens = hidden.reshape(site_count, width)
    head_count = score_scale.shape[0]
    head_size = width // head_count
    kv_width = w_keyval.shape[1] // 2
    kv_heads = kv_width // head_size
    query = jnp.dot(tokens, w_query, preferred_element_type=jnp.float32).reshape(
        site_count, head_count, head_size
    )
    qnorm = head_norm(query).astype(jnp.bfloat16).reshape(site_count, 1, width)
    keyval = jnp.dot(tokens, w_keyval, preferred_element_type=jnp.float32)
    knorm = (
        head_norm(keyval[:, :kv_width].reshape(site_count, kv_heads, head_size))
        .astype(jnp.bfloat16)
        .reshape(site_count, 1, kv_width)
    )
    values = keyval[:, kv_width:].astype(jnp.bfloat16).reshape(site_count, 1, kv_width)
    first_seen = jnp.broadcast_to(
        earliest_past_snapshot[:, None], (samples, lat_rows * lon_local)
    ).reshape(site_count)
    own_frame = lax.axis_index("frame")
    keys_all, value_rows_full = (
        lax.all_gather(knorm, "frame", axis=1, tiled=True),
        lax.all_gather(values, "frame", axis=1, tiled=True),
    )
    query_frame = jnp.reshape(own_frame, (1,))
    attended = attend(
        qnorm, keys_all, value_rows_full, query_frame, first_seen, score_scale, kv_heads, head_size
    )
    output = jnp.dot(
        attended.reshape(site_count, width), w_output, preferred_element_type=jnp.float32
    )
    predicted_output_fields = (
        (tokens.astype(jnp.float32) + output)
        .astype(jnp.bfloat16)
        .reshape(samples, 1, lat_rows, lon_local, width)
    )
    return (predicted_output_fields, mask_coefficient2_derivative, mask_offset2_derivative)


def solution(mesh):
    placed = (
        P("dp", "frame", None, "lon", None),
        P("dp", None),
        P("dp"),
        P(),
        P(),
        P(None, "lon", None, None),
        P(None, "lon"),
        P(None, "lon", None, None),
        P(None, "lon"),
        P(),
        P(),
        P(),
        P(),
        P("dp", "frame", None, None, None, "lon"),
    )
    return jax.shard_map(
        body,
        mesh=mesh,
        in_specs=placed,
        out_specs=(P("dp", "frame", None, "lon", None), P(None, "lon", None, None), P(None, "lon")),
        check_vma=False,
    )
```

profile of v0, /device:TPU:0, one launch (start us, length us, event | category | flops | bytes accessed | tf_op | source)
XLA Modules:
  0.0 437.1 jit_solution(6309243062081388970)
XLA Ops:
  8.0 1.9 fusion.54
  9.9 2.6 fusion.2
  12.5 1.1 multiply_reduce_fusion.1
  13.6 2.3 multiply_convert_fusion.2
  15.9 5.8 %copy.114 = bf16[4,360,1024]{1,0,2:T(4,128)(2,1)} copy(bf16[4,360,1024]{2,1,0:T(8,128)(2,1)} %multiply_convert_fusion.2) | data formatting | bytes 5898240 | tf_op jit(solution)/shard_map/convert_element_type | solution.py:110
  21.8 7.0 %all-to-all-start = ((bf16[4,360,1024]{1,0,2:T(4,128)(2,1)}), bf16[4,360,1024]{1,0,2:T(4,128)(2,1)}, u32[]{:S(2)}, u32[]{:S(2)}) async-start(bf16[4,360,1024]{1,0,2:T(4,128)(2,1)} %copy.114), calls=%async_computation | async-start | bytes 6291456 | tf_op jit(solution)/shard_map/all_to_all | solution.py:111
  29.2 10.3 %negate_convert_fusion = (bf16[1440,368]{1,0:T(8,128)(2,1)S(1)}, bf16[1440,368]{1,0:T(8,128)(2,1)}) fusion(), kind=kLoop, calls=%fused_computation.33 | loop fusion | flops 6359040 | bytes 2119680 | tf_op jit(solution)/shard_map/convert.11
  39.5 60.0 %all-to-all-done = bf16[4,360,1024]{1,0,2:T(4,128)(2,1)} async-done(((bf16[4,360,1024]{1,0,2:T(4,128)(2,1)}), bf16[4,360,1024]{1,0,2:T(4,128)(2,1)}, u32[]{:S(2)}, u32[]{:S(2)}) %all-to-all-start) | async-done | bytes 2949152 | tf_op jit(solution)/shard_map/all_to_all | solution.py:111
  99.5 5.8 %copy.115 = bf16[4,360,4,256]{3,1,2,0:T(8,128)(2,1)} copy(bf16[4,360,4,256]{1,0,3,2:T(4,128)(2,1)} %bitcast.7) | data formatting | bytes 5898240 | tf_op jit(solution)/shard_map/all_to_all | solution.py:111
  105.3 6.0 %fusion.19 = bf16[4,736,256]{2,1,0:T(8,128)(2,1)} fusion(bf16[4,1440,256]{2,1,0:T(8,128)(2,1)} %bitcast.203, bf16[1440,368]{1,0:T(8,128)(2,1)S(1)} %get-tuple-element.15, bf16[1440,368]{1,0:T(8,128)(2,1)} %get-tuple-element.16), kind=kOutput, calls=%fused_computation.45 | convolution fusion | flops 2176299008 | bytes 6576128 | tf_op jit(solution)/shard_map/rnc,nk->rkc/dot_general | solution.py:115
  111.3 5.5 %reshape.332 = bf16[4,2,368,4,64]{4,3,2,1,0:T(4,128)(2,1)} reshape(bf16[4,736,256]{2,1,0:T(8,128)(2,1)} %fusion.19) | data formatting | bytes 3014656 | tf_op jit(solution)/shard_map/reshape | solution.py:117
  116.8 4.5 %fusion.59 = (bf16[4,1,368,4,64]{4,3,2,1,0:T(4,128)(2,1)}, bf16[4,1,368,4,64]{4,3,2,1,0:T(4,128)(2,1)}) fusion(bf16[4,2,368,4,64]{4,3,2,1,0:T(4,128)(2,1)} %reshape.332), kind=kLoop, calls=%fused_computation.109 | loop fusion | bytes 3014656 | tf_op jit(solution)/shard_map/slice | solution.py:30
  121.3 2.7 copy.154
  124.0 1.6 fusion.32
  125.6 1.6 fusion.34
  127.1 3.4 copy.156
  130.6 2.1 fusion.22
  132.7 0.4 fusion.40
  133.1 0.4 fusion.36
  133.8 0.5 copy-done.6
  134.3 0.4 fusion.23
  134.8 0.4 fusion.24
  135.2 0.4 copy-done.3
  135.6 0.4 fusion.25
  136.1 0.6 pad_maximum_fusion.1
  136.8 0.5 copy-done.13
  137.6 2.5 fusion.3
  140.2 12.5 %copy.125 = bf16[4,1440,256]{2,0,1:T(4,128)(2,1)} copy(bf16[4,1440,256]{2,1,0:T(8,128)(2,1)S(1)} %fusion.3) | data formatting | bytes 5898240 | tf_op jit(solution)/shard_map/convert_element_type | solution.py:128
  152.7 4.6 %all-to-all-start.1 = ((bf16[4,1440,256]{2,0,1:T(4,128)(2,1)}), bf16[4,1440,256]{2,0,1:T(4,128)(2,1)}, u32[]{:S(2)}, u32[]{:S(2)}) async-start(bf16[4,1440,256]{2,0,1:T(4,128)(2,1)} %copy.125), calls=%async_computation.1 | async-start | bytes 5898240 | tf_op jit(solution)/shard_map/all_to_all | solution.py:129
  158.1 65.1 %all-to-all-done.1 = bf16[4,1440,256]{2,0,1:T(4,128)(2,1)} async-done(((bf16[4,1440,256]{2,0,1:T(4,128)(2,1)}), bf16[4,1440,256]{2,0,1:T(4,128)(2,1)}, u32[]{:S(2)}, u32[]{:S(2)}) %all-to-all-start.1) | async-done | bytes 2949152 | tf_op jit(solution)/shard_map/all_to_all | solution.py:129
  223.2 4.1 copy.126
  227.3 1.5 copy.160
  229.1 1.1 fusion.1
  230.4 1.7 fusion.62
  232.1 1.6 copy-done.7
  233.7 1.0 slice.112
  234.9 2.6 slice_multiply_fusion
  237.5 3.0 copy.129
  240.5 1.7 bitcast_reduce_fusion
  242.2 1.3 mul.128
  243.5 3.0 copy.130
  246.5 2.9 multiply_convert_fusion.5
  250.0 2.6 copy.138
  252.6 3.9 copy.132
  256.5 1.6 convert_reduce_fusion
  258.1 14.0 %psum.15 = f32[2,256]{1,0:T(2,128)} all-reduce(f32[2,256]{1,0:T(2,128)S(1)} %convert_reduce_fusion), channel_id=1, replica_groups=mesh['dp'=4,'frame'=2,'lon'=4] {'dp','frame'}, use_global_device_ids=true, to_apply=%region_8.9 | all-reduce | flops 512 | bytes 4096 | tf_op jit(solution)/shard_map/psum | solution.py:147
  272.2 1.6 fusion.60
  275.3 0.7 pad_maximum_fusion.4
  276.1 6.6 %copy.172 = f32[4,4,360,256]{3,1,2,0:T(4,128)} copy(bf16[4,4,360,256]{3,0,2,1:T(4,128)(2,1)} %bitcast.68) | data formatting | bytes 8847360 | tf_op jit(solution)/shard_map/convert_element_type | solution.py:131
  282.7 7.9 %reshape.314 = f32[4,360,1024]{2,1,0:T(8,128)} reshape(f32[4,360,4,256]{3,2,1,0:T(4,128)} %bitcast.194) | data formatting | bytes 11796480 | tf_op jit(solution)/shard_map/convert_element_type | solution.py:131
  290.6 4.8 %add_convert_fusion.1 = bf16[4,360,1024]{2,1,0:T(8,128)(2,1)S(1)} fusion(f32[4,360,1024]{2,1,0:T(8,128)} %reshape.314, bf16[1,1,4,360,1024]{4,3,2,1,0:T(8,128)(2,1)} %param.14, f32[4,1024]{1,0:T(4,128)S(1)} %fusion.54), kind=kLoop, calls=%fused_computation.12 | loop fusion | flops 5898240 | bytes 11812864 | tf_op jit(solution)/shard_map/convert_element_type | solution.py:132
  295.4 3.5 multiply_reduce_fusion
  298.9 2.6 multiply_convert_fusion
  301.6 9.8 %copy.134 = bf16[1440,4,4,64]{3,2,0,1:T(4,128)(2,1)} copy(bf16[1440,4,4,64]{0,3,2,1:T(8,128)(2,1)} %bitcast.196) | data formatting | bytes 5898240 | tf_op jit(solution)/shard_map/reshape.45
  311.3 2.6 copy.127
  313.9 8.3 %copy.135 = bf16[1440,2,4,64]{3,1,2,0:T(2,128)(2,1)} copy(bf16[1440,2,4,64]{0,3,2,1:T(8,128)(2,1)} %bitcast.199) | data formatting | bytes 2949120 | tf_op jit(solution)/shard_map/reshape | solution.py:58
  322.2 2.6 copy.131
  324.8 8.3 %copy.133 = bf16[1440,2,4,64]{3,1,0,2:T(2,128)(2,1)} copy(bf16[1440,2,4,64]{0,3,2,1:T(8,128)(2,1)} %bitcast.200) | data formatting | bytes 2949120 | tf_op jit(solution)/shard_map/reshape | solution.py:57
  333.1 32.2 %fusion.61 = (f32[4,4,1440]{1,2,0:T(8,128)}, f32[4,4,1,2,1440]{1,3,4,0,2:T(2,128)S(1)}) fusion(f32[4,4]{1,0:T(4,128)S(1)} %div.38, bf16[1440,2,4,64]{3,1,0,2:T(2,128)(2,1)} %copy.133, bf16[1440,4,4,64]{3,2,0,1:T(4,128)(2,1)} %copy.134, pred[2,1440]{0,1:T(8,128)(4,1)S(1)} %copy.128), kind=kOutput, calls=%fused_computation.111 | convolution fusion | flops 6013440 | bytes 4703104 | tf_op jit(solution)/shard_map/sqkgd,stkd->kgqts/dot_general | solution.py:59
  365.3 33.9 %fusion.4 = f32[4,4,1440]{1,2,0:T(8,128)} fusion(f32[4,4,1,2,1440]{1,3,4,0,2:T(2,128)S(1)} %get-tuple-element.14, f32[4,4,1440]{1,2,0:T(8,128)} %get-tuple-element.13), kind=kLoop, calls=%fused_computation.21 | loop fusion | flops 69120 | bytes 368640 | tf_op jit(solution)/shard_map/reduce_sum | solution.py:69
  399.2 11.9 %convert_bitcast_fusion = bf16[1440,1,4,4,64]{4,3,2,0,1:T(4,128)(2,1)} fusion(bf16[1440,2,4,64]{3,1,2,0:T(2,128)(2,1)S(1)} %copy-done.9, f32[4,4,1440]{1,2,0:T(8,128)} %fusion.4, f32[4,4,1,2,1440]{1,3,4,0,2:T(2,128)S(1)} %get-tuple-element.14, f32[4,4,1440]{1,2,0:T(8,128)S(1)} %copy-done.10), kind=kOutput, calls=%fused_computation.10 | convolution fusion | flops 7511040 | bytes 4792320 | tf_op jit(solution)/shard_map/kgqts,stkd->sqkgd/dot_general | solution.py:70
  411.1 9.8 %copy.137 = bf16[1440,1,4,4,64]{0,4,3,2,1:T(8,128)(2,1)} copy(bf16[1440,1,4,4,64]{4,3,2,0,1:T(4,128)(2,1)} %convert_bitcast_fusion) | data formatting | bytes 5898240 | tf_op jit(solution)/shard_map/convert_element_type | solution.py:71
  420.9 6.9 %add_convert_fusion = bf16[1440,1024]{1,0:T(8,128)(2,1)} fusion(bf16[1440,1024]{1,0:T(8,128)(2,1)} %copy-done.8, bf16[1440,1024]{0,1:T(8,128)(2,1)} %bitcast.201, bf16[1024,1024]{1,0:T(8,128)(2,1)S(1)} %copy-done), kind=kOutput, calls=%fused_computation.9 | convolution fusion | flops 3024322560 | bytes 10944512 | tf_op jit(solution)/shard_map/dot_general | solution.py:179
  427.8 1.7 copy.175
  (70 shorter events, 4.1 us)
Async XLA Ops:
  8.0 412.9 %copy-start = (bf16[1024,1024]{1,0:T(8,128)(2,1)S(1)}, bf16[1024,1024]{1,0:T(8,128)(2,1)}, u32[]{:S(2)}) copy-start(bf16[1024,1024]{1,0:T(8,128)(2,1)} %param.25) | copy-start | bytes 6291460
  8.0 4.5 %copy-start.1 = (bf16[1,1,4,360,1024]{4,3,2,1,0:T(8,128)(2,1)S(1)}, bf16[1,1,4,360,1024]{4,3,2,1,0:T(8,128)(2,1)}, u32[]{:S(2)}) copy-start(bf16[1,1,4,360,1024]{4,3,2,1,0:T(8,128)(2,1)} %param.14) | copy-start | bytes 8847364
  9.9 3.7 copy-start.17
  21.8 7.0 %copy-start.18 = (f32[2,256]{1,0:T(2,128)S(1)}, f32[2,256]{1,0:T(2,128)}, u32[]{:S(2)}) copy-start(f32[2,256]{1,0:T(2,128)} %param.22) | copy-start | bytes 6148
  21.8 7.0 %copy-start.19 = (f32[2,256]{1,0:T(2,128)S(1)}, f32[2,256]{1,0:T(2,128)}, u32[]{:S(2)}) copy-start(f32[2,256]{1,0:T(2,128)} %param.20) | copy-start | bytes 6148
  21.8 77.7 %all-to-all-start = ((bf16[4,360,1024]{1,0,2:T(4,128)(2,1)}), bf16[4,360,1024]{1,0,2:T(4,128)(2,1)}, u32[]{:S(2)}, u32[]{:S(2)}) async-start(bf16[4,360,1024]{1,0,2:T(4,128)(2,1)} %copy.114), calls=%async_computation | async-start | bytes 6291456 | tf_op jit(solution)/shard_map/all_to_all | solution.py:111
  39.5 65.8 %copy-start.12 = (bf16[1440,368]{1,0:T(8,128)(2,1)}, bf16[1440,368]{1,0:T(8,128)(2,1)S(1)}, u32[]{:S(2)}) copy-start(bf16[1440,368]{1,0:T(8,128)(2,1)S(1)} %get-tuple-element.15) | copy-start | bytes 3179524
  116.8 7.2 %copy-start.15 = (bf16[2,4,64,64]{3,2,1,0:T(8,128)(2,1)S(1)}, bf16[2,4,64,64]{3,2,1,0:T(8,128)(2,1)}, u32[]{:S(2)}) copy-start(bf16[2,4,64,64]{3,2,1,0:T(8,128)(2,1)} %param.19) | copy-start | bytes 196612
  127.1 5.5 %copy-start.16 = (bf16[2,4,64,64]{3,2,1,0:T(8,128)(2,1)S(1)}, bf16[2,4,64,64]{3,2,1,0:T(8,128)(2,1)}, u32[]{:S(2)}) copy-start(bf16[2,4,64,64]{3,2,1,0:T(8,128)(2,1)} %param.21) | copy-start | bytes 196612
  132.7 1.1 copy-start.5
  132.7 1.6 copy-start.6
  134.8 0.9 copy-start.3
  136.1 1.2 copy-start.13
  136.1 1.6 copy-start.14
  152.7 70.5 %all-to-all-start.1 = ((bf16[4,1440,256]{2,0,1:T(4,128)(2,1)}), bf16[4,1440,256]{2,0,1:T(4,128)(2,1)}, u32[]{:S(2)}, u32[]{:S(2)}) async-start(bf16[4,1440,256]{2,0,1:T(4,128)(2,1)} %copy.125), calls=%async_computation.1 | async-start | bytes 5898240 | tf_op jit(solution)/shard_map/all_to_all | solution.py:129
  157.3 154.1 %all-gather.5.cloned.1.call-start = ((), (), s32[]{:S(2)}) async-start(), calls=%async_computation.3 | async-start | bytes 2211840 | tf_op jit(solution)/shard_map/all_gather | solution.py:173
  227.3 1.8 copy-start.2
  229.1 1.2 copy-start.20
  230.4 1.7 copy-start.8
  232.1 1.6 copy-start.7
  234.7 87.5 %all-gather.7.cloned.1.call-start = ((), (), s32[]{:S(2)}) async-start(), calls=%async_computation.4 | async-start | bytes 2211840 | tf_op jit(solution)/shard_map/all_gather | solution.py:172
  246.5 2.9 copy-start.21
  249.4 178.4 %all-reduce.2.cloned.1.call-start = ((), (), s32[]{:S(2)}) async-start(), calls=%async_computation.2 | async-start | bytes 524288 | tf_op jit(solution)/shard_map/psum | solution.py:147
  272.2 1.7 copy-start.4
  290.6 4.8 %copy-start.11 = (bf16[1024,1024]{0,1:T(8,128)(2,1)S(1)}, bf16[1024,1024]{0,1:T(8,128)(2,1)}, u32[]{:S(2)}) copy-start(bf16[1024,1024]{0,1:T(8,128)(2,1)} %copy.132) | copy-start | bytes 6291460
  365.3 33.9 %copy-start.9 = (bf16[1440,2,4,64]{3,1,2,0:T(2,128)(2,1)S(1)}, bf16[1440,2,4,64]{3,1,2,0:T(2,128)(2,1)}, u32[]{:S(2)}) copy-start(bf16[1440,2,4,64]{3,1,2,0:T(2,128)(2,1)} %copy.135) | copy-start | bytes 4423684
  365.3 33.9 %copy-start.10 = (f32[4,4,1440]{1,2,0:T(8,128)S(1)}, f32[4,4,1440]{1,2,0:T(8,128)}, u32[]{:S(2)}) copy-start(f32[4,4,1440]{1,2,0:T(8,128)} %get-tuple-element.13) | copy-start | bytes 276484
Sparse Core Ops, SparseCore 0:
  234.8 25.2 all-gather.4
  261.6 26.2 all-gather.6
Sparse Core Ops, SparseCore 1:
  276.2 56.7 all-reduce.1
where the time goes:
time: 442 us; the launch traced here: 437 us
  local copies, waits for them, and re-layouts  125 us (28%)
  waiting for transfers between devices  125 us (28%)
  matrix products  75.3 us (17%)
  other arithmetic  69 us (16%)
  between operations  16.7 us (4%)
  blocking collectives  14 us (3%)
  starting transfers between devices  11.9 us (3%)
    all_to_all x1, waiting for transfers between devices, body(): lax.all_to_all(grid_part, 'lon', split_axis=1, concat_axis=2, tiled=True)  65.1 us
    all_to_all x1, waiting for transfers between devices, body(): lax.all_to_all(normed.reshape(grid_rows, lon_local, width), 'lon', split_...  60 us
    reduce_sum x1, other arithmetic, attend(): jnp.sum(weights, axis=-2, keepdims=True)  33.9 us
    dot_general x1, matrix products, attend(): jnp.einsum('sqkgd,stkd->kgqts', q_five, k_four, preferred_element_type=jn...  32.2 us
    unnamed x50, local copies, waits for them, and re-layouts  20 us
    convert_element_type x3, local copies, waits for them, and re-layouts, body(): returned.reshape(samples, lat_rows, lon_local, width).astype(jnp.float32)  18.6 us
    psum x1, blocking collectives, body(): lax.psum((jnp.stack([grad_re, grad_im]), bias_terms), ('dp', 'frame'))  14 us
    convert_element_type x1, local copies, waits for them, and re-layouts, body(): grid_part = (jnp.einsum('rkc,nk->rnc', mixed, backward, preferred_element...  12.5 us
  transfers between devices with their start and end apart: 5, of which 2 were waited for; matrix products, arithmetic and copies ran while one was open for 43% of the time, Pallas kernels for 0%

commit v1 on v0

--- a/solution.py
+++ b/solution.py
@@ -1,9 +1,402 @@
+import functools
 import math
 
 import jax
 import jax.numpy as jnp
+import ml_dtypes
+import numpy as np
 from jax import lax
+from jax.experimental import pallas as pl
+from jax.experimental.pallas import tpu as pltpu
 from jax.sharding import PartitionSpec as P
+
+
+def window_basis(window, length, modes, rank):
+    band = 2 * modes - 1
+    site = np.arange(window)
+    step = np.arange(1, window)
+    diagonal = -np.cos(np.pi * (window - 1 - 2 * site) / length) * np.cos(np.pi * band / length)
+    beside = np.sin(np.pi * step / length) * np.sin(np.pi * (window - step) / length)
+    _, vectors = np.linalg.eigh(np.diag(diagonal) + np.diag(beside, 1) + np.diag(beside, -1))
+    basis = vectors[:, ::-1][:, :rank]
+    lead = np.argmax(np.abs(basis) > 1e-3, axis=0)
+    return basis * np.sign(basis[lead, np.arange(rank)])[None, :]
+
+
+def window_tables(window, length, modes, rank):
+    basis = window_basis(window, length, modes, rank)
+    turns = np.arange(length)[:, None] * np.arange(modes)[None, :] % length
+    angles = 2.0 * np.pi * turns / length
+    table = np.concatenate([np.cos(angles), -np.sin(angles)], axis=1)
+    factor = np.where(np.arange(2 * modes) % modes == 0, 1.0, 2.0)
+    parts = table.reshape(length // window, window, 2 * modes)
+    spread = np.einsum("pnj,nr->prj", parts, basis) / math.sqrt(length)
+    fold = np.transpose(spread, (2, 0, 1)).reshape(2 * modes, -1)
+    unfold = spread * factor
+
+    def small(array):
+        return (np.round(array * 2.0**16) / 2.0**16).astype(ml_dtypes.bfloat16)
+
+    return small(basis), small(fold), small(unfold)
+
+
+LANES = 256
+F32 = jnp.float32
+BF16 = jnp.bfloat16
+
+
+def dot(left, right):
+    return jnp.dot(left, right, preferred_element_type=F32)
+
+
+def row_tiles(rows, size):
+    return [(low, min(low + size, rows)) for low in range(0, rows, size)]
+
+
+def latitude_row(band, block):
+    rows = block.astype(F32)
+    place = lax.broadcasted_iota(jnp.int32, rows.shape, 0)
+    return jnp.sum(jnp.where(place == band % rows.shape[0], rows, 0.0), axis=0, keepdims=True)
+
+
+def compress_kernel(row, me_ref, band_ref, x_ref, lat_ref, gain_ref, basis_ref, *rest):
+    outs, (normed_ref,) = rest[:-1], rest[-1:]
+    count = len(outs)
+    rows, width = x_ref.shape
+    embed = latitude_row(band_ref[0, row], lat_ref[...])
+    gain = gain_ref[...]
+    for low, high in row_tiles(rows, 16):
+        inputs = x_ref[low:high].astype(F32) + embed
+        center = jnp.sum(inputs, axis=-1, keepdims=True) * (1.0 / width)
+        inputs = inputs - center
+        spread = jnp.sum(inputs * inputs, axis=-1, keepdims=True) * (1.0 / width)
+        normed_ref[low:high] = (inputs * lax.rsqrt(spread + 1e-05) * gain).astype(BF16)
+    for shift, out in enumerate(outs):
+        block = lax.rem(me_ref[0] + shift, count)
+        columns = pl.ds(pl.multiple_of(block * out.shape[1], out.shape[1]), out.shape[1])
+        out[...] = dot(basis_ref[...], normed_ref[:, columns]).astype(BF16)
+
+
+def filter_kernel(count, me_ref, *refs):
+    parts, refs = refs[:count], refs[count:]
+    fold_ref, w1_ref, b1_ref, w2_ref, b2_ref, unfold_ref = refs[:6]
+    outs, first_ref, whole_ref, mixed_ref = refs[6 : 6 + count], *refs[6 + count :]
+    rank, width = parts[0].shape
+    modes = first_ref.shape[0] // 2
+    me = me_ref[0]
+    for shift, part in enumerate(parts):
+        owner = lax.rem(me + count - shift, count)
+        whole_ref[pl.ds(pl.multiple_of(owner * rank, 16), rank)] = part[...]
+    spectrum = dot(fold_ref[...], whole_ref[...]).astype(BF16)
+    first = (
+        dot(spectrum[:modes], w1_ref[:width])
+        + dot(spectrum[modes:], w1_ref[width:])
+        + b1_ref[...]
+    )
+    first = jnp.maximum(first, 0.0).astype(BF16)
+    first_ref[:modes] = first[:, :width]
+    first_ref[modes:] = first[:, width:]
+    mixed = (dot(first, w2_ref[...]) + b2_ref[...]).astype(BF16)
+    mixed_ref[:modes] = mixed[:, :width]
+    mixed_ref[modes:] = mixed[:, width:]
+    for shift, out in enumerate(outs):
+        out[...] = dot(unfold_ref[lax.rem(me + shift, count)], mixed_ref[...]).astype(BF16)
+
+
+def gradient_kernel(*refs):
+    *firsts, cot_ref, weight_ref, bias_ref = refs
+    modes, width = cot_ref.shape[2:]
+    blocks, size = weight_ref.shape[1:3]
+    contract = (((0,), (0,)), ((), ()))
+    total, bias = 0.0, 0.0
+    for row, first_ref in enumerate(firsts):
+        real, imag = cot_ref[row, 0], cot_ref[row, 1]
+        both = jnp.concatenate([real, imag], axis=1)
+        turned = jnp.concatenate([imag, -real], axis=1)
+        total += lax.dot_general(first_ref[:modes], both, contract, preferred_element_type=F32)
+        total += lax.dot_general(first_ref[modes:], turned, contract, preferred_element_type=F32)
+        bias += jnp.sum(both.astype(F32), axis=0, keepdims=True)
+    bias_ref[...] = bias
+    for part in range(2):
+        for block in range(blocks):
+            low = block * size
+            weight_ref[part, block] = total[low : low + size, part * width + low : part * width + low + size]
+
+
+def head_scale(values, ones):
+    squares = (values * values).astype(BF16)
+    return values * lax.rsqrt(dot(squares, ones) + 1e-06)
+
+
+def head_ones(head_size, value):
+    row = lax.broadcasted_iota(jnp.int32, (LANES, LANES), 0) // head_size
+    column = lax.broadcasted_iota(jnp.int32, (LANES, LANES), 1) // head_size
+    return jnp.where(row == column, value, 0.0).astype(BF16)
+
+
+def expand_kernel(row, count, head_size, me_ref, band_ref, x_ref, lat_ref, *refs):
+    parts, refs = refs[:count], refs[count:]
+    basis_ref, w_keyval_ref, hidden_ref, keyval_ref, whole_ref = refs
+    width = parts[0].shape[1]
+    me = me_ref[0]
+    for shift, part in enumerate(parts):
+        whole_ref[lax.rem(me + count - shift, count)] = part[...]
+    embed = latitude_row(band_ref[0, row], lat_ref[...])
+    for block in range(count):
+        columns = slice(block * width, block * width + width)
+        grid = dot(basis_ref[...], whole_ref[block]).astype(BF16).astype(F32)
+        inputs = x_ref[:, columns].astype(F32) + embed[:, columns]
+        hidden_ref[:, columns] = (inputs + grid).astype(BF16)
+    keyval = dot(hidden_ref[...], w_keyval_ref[...])
+    ones = head_ones(head_size, 1.0 / head_size)
+    half = keyval.shape[1] // 2
+    for low in range(0, half, LANES):
+        keyval_ref[:, low : low + LANES] = head_scale(keyval[:, low : low + LANES], ones).astype(BF16)
+    keyval_ref[:, half:] = keyval[:, half:].astype(BF16)
+
+
+def query_kernel(head_size, hidden_ref, w_query_ref, query_ref):
+    ones = head_ones(head_size, 1.0 / head_size)
+    for low in range(0, query_ref.shape[1], LANES):
+        columns = slice(low, low + LANES)
+        query = dot(hidden_ref[...], w_query_ref[:, columns])
+        query_ref[:, columns] = head_scale(query, ones).astype(BF16)
+
+
+def repeat_head(pair, upper, head_size):
+    lane = lax.broadcasted_iota(jnp.int32, pair.shape, 1)
+    rolled = pltpu.roll(pair, head_size, 1)
+    first_half = (lane < head_size) != upper
+    return jnp.where(first_half, pair, rolled)
+
+
+def attend_kernel(head_size, seen_ref, query_ref, own_ref, other_ref, hidden_ref, scale_ref, w_ref, *rest):
+    out_ref, attended_ref = rest[-2:]
+    half = own_ref.shape[1] // 2
+    pair_width = 2 * head_size
+    ones = head_ones(head_size, 1.0)
+    seen = seen_ref[0] > 0
+    for head in range(half // head_size):
+        pair = slice(head // 2 * pair_width, (head // 2 + 1) * pair_width)
+        value_pair = slice(half + pair.start, half + pair.stop)
+        upper = head % 2 == 1
+        own_key, other_key = own_ref[:, pair].astype(F32), other_ref[:, pair].astype(F32)
+        own_value, other_value = own_ref[:, value_pair].astype(F32), other_ref[:, value_pair].astype(F32)
+        key_step = repeat_head(other_key - own_key, upper, head_size)
+        value = repeat_head(own_value, upper, head_size)
+        value_step = repeat_head(other_value - own_value, upper, head_size)
+        columns = slice(head * LANES, head * LANES + LANES)
+        twice = lambda part: jnp.concatenate([part, part], axis=1)
+        product = query_ref[:, columns].astype(F32) * twice(key_step) * scale_ref[:, columns]
+        high = product.astype(BF16)
+        low = (product - high.astype(F32)).astype(BF16)
+        lead = dot(high, ones) + dot(low, ones)
+        prob = 1.0 / (1.0 + jnp.exp(-lead))
+        prob = jnp.where(seen, prob, 0.0)
+        attended_ref[:, columns] = (twice(value) + prob * twice(value_step)).astype(BF16)
+    for low in range(0, out_ref.shape[1], LANES):
+        columns = slice(low, low + LANES)
+        output = dot(attended_ref[...], w_ref[:, columns])
+        out_ref[:, columns] = (hidden_ref[:, columns].astype(F32) + output).astype(BF16)
+
+
+def whole(array):
+    return pl.BlockSpec(array.shape, lambda *_, rank=array.ndim: (0,) * rank)
+
+
+def call(kernel, prefetch, args, specs, outs, scratch, flops, grid=(1,), alias=None, out_specs=None):
+    moved = sum(math.prod(a.shape) * a.dtype.itemsize for a in outs) * 2
+    return pl.pallas_call(
+        kernel,
+        grid_spec=pltpu.PrefetchScalarGridSpec(
+            num_scalar_prefetch=len(prefetch),
+            grid=grid,
+            in_specs=specs,
+            out_specs=out_specs or [whole(out) for out in outs],
+            scratch_shapes=scratch,
+        ),
+        out_shape=outs,
+        input_output_aliases=alias or {},
+        compiler_params=pltpu.CompilerParams(vmem_limit_bytes=40 * 1024 * 1024),
+        cost_estimate=pl.CostEstimate(flops=flops, bytes_accessed=moved, transcendentals=0),
+    )(*prefetch, *args)
+
+
+def block_diagonal(weight):
+    _, blocks, size, _ = weight.shape
+    width = blocks * size
+    tiled = jnp.tile(weight.reshape(2, width, size), (1, 1, blocks))
+    row = lax.broadcasted_iota(jnp.int32, (width, width), 0) // size
+    column = lax.broadcasted_iota(jnp.int32, (width, width), 1) // size
+    real, imag = jnp.where((row == column)[None], tiled, 0)
+    return jnp.concatenate(
+        [jnp.concatenate([real, imag], axis=1), jnp.concatenate([-imag, real], axis=1)], axis=0
+    )
+
+
+def swap_blocks(parts, count):
+    moved = [
+        lax.ppermute(part, "lon", [(i, (i + shift) % count) for i in range(count)])
+        for shift, part in enumerate(parts)
+        if shift
+    ]
+    return [parts[0], *moved]
+
+
+def sum_over(array, axis):
+    size = lax.axis_size(axis)
+    if size & (size - 1):
+        return lax.psum(array, axis)
+    step = 1
+    while step < size:
+        array = array + lax.ppermute(array, axis, [(i, i ^ step) for i in range(size)])
+        step *= 2
+    return array
+
+
+def fused_body(
+    fields,
+    band_rows,
+    earliest_past_snapshot,
+    lat_table,
+    norm_gain,
+    w_in1,
+    b_in1,
+    w_out2,
+    b_out2,
+    w_query,
+    w_keyval,
+    w_output,
+    score_scale,
+    spec_cot,
+):
+    _, _, lat_rows, window, width = fields.shape
+    count = lax.axis_size("lon")
+    length = window * count
+    modes, local_width = spec_cot.shape[4:]
+    _, blocks, block_size, _ = w_in1.shape
+    head_size = width // score_scale.shape[0]
+    keyval_width = w_keyval.shape[1]
+    rank = basis_rank(window, length, modes)
+    basis, fold, unfold = (jnp.asarray(a) for a in window_tables(window, length, modes, rank))
+    me = jnp.reshape(lax.axis_index("lon"), (1,)).astype(jnp.int32)
+    frame = lax.axis_index("frame")
+    seen = ((frame == 1) & (earliest_past_snapshot <= 0)).astype(jnp.int32)
+    scale_lanes = jnp.repeat(score_scale / math.sqrt(head_size), head_size).reshape(1, width)
+    gain = norm_gain.reshape(1, width)
+    mix1, mix2 = block_diagonal(w_in1), block_diagonal(w_out2)
+    bias1, bias2 = b_in1.reshape(1, -1), b_out2.reshape(1, -1)
+
+    part_shape = jax.ShapeDtypeStruct((rank, local_width), BF16)
+    lat_block = 16
+
+    def row_specs(row):
+        return [
+            pl.BlockSpec((None, None, None, window, width), lambda *_: (0, 0, row, 0, 0)),
+            pl.BlockSpec((lat_block, width), lambda _, me, band: (band[0, row] // lat_block, 0)),
+        ]
+
+    def compress(row):
+        return call(
+            functools.partial(compress_kernel, row),
+            (me, band_rows),
+            (fields, lat_table, gain, basis.T),
+            [*row_specs(row), whole(gain), whole(basis.T)],
+            [part_shape] * count,
+            [pltpu.VMEM((window, width), BF16)],
+            2 * rank * window * width,
+        )
+
+    def mix(parts):
+        args = (*parts, fold, mix1, bias1, mix2, bias2, unfold)
+        return call(
+            functools.partial(filter_kernel, count),
+            (me,),
+            args,
+            [whole(a) for a in args],
+            [*[part_shape] * count, jax.ShapeDtypeStruct((2 * modes, local_width), BF16)],
+            [pltpu.VMEM((count * rank, local_width), BF16), pltpu.VMEM((2 * modes, local_width), BF16)],
+            16 * modes * local_width * local_width + 8 * modes * local_width * rank * count,
+        )
+
+    def expand(row, parts):
+        args = (*parts, basis, w_keyval)
+        return call(
+            functools.partial(expand_kernel, row, count, head_size),
+            (me, band_rows),
+            (fields, lat_table, *args),
+            [*row_specs(row), *[whole(a) for a in args]],
+            [
+                jax.ShapeDtypeStruct((window, width), BF16),
+                jax.ShapeDtypeStruct((window, keyval_width), BF16),
+            ],
+            [pltpu.VMEM((count, rank, local_width), BF16)],
+            2 * window * width * (rank + keyval_width),
+        )
+
+    def project(hidden):
+        return call(
+            functools.partial(query_kernel, head_size),
+            (),
+            (hidden, w_query),
+            [whole(hidden), whole(w_query)],
+            [jax.ShapeDtypeStruct(hidden.shape, BF16)],
+            [],
+            2 * window * width * width,
+        )[0]
+
+    def attention(row, query, own, other, hidden, filled):
+        args = (query, own, other, hidden, scale_lanes, w_output)
+        specs = [whole(a) for a in args]
+        alias = None
+        if filled is not None:
+            alias = {1 + len(args): 0}
+            args, specs = (*args, filled), [*specs, pl.BlockSpec(memory_space=pl.ANY)]
+        return call(
+            functools.partial(attend_kernel, head_size),
+            (seen,),
+            args,
+            specs,
+            [jax.ShapeDtypeStruct(fields.shape, BF16)],
+            [pltpu.VMEM((window, width), BF16)],
+            4 * window * width * width,
+            alias=alias,
+            out_specs=[pl.BlockSpec((None, None, None, window, width), lambda *_: (0, 0, row, 0, 0))],
+        )[0]
+
+    outward = [swap_blocks(compress(row), count) for row in range(lat_rows)]
+    homeward, firsts = [], []
+    for row in range(lat_rows):
+        *parts, first = mix(outward[row])
+        homeward.append(swap_blocks(parts, count))
+        firsts.append(first)
+    cells = []
+    for row in range(lat_rows):
+        hidden, keyval = expand(row, homeward[row])
+        earlier = lax.ppermute(keyval, "frame", [(0, 1)])
+        cells.append((project(hidden), keyval, earlier, hidden))
+
+    cotangent = spec_cot.reshape(spec_cot.shape[2:])
+    args = (*firsts, cotangent)
+    weight, bias = call(
+        gradient_kernel,
+        (),
+        args,
+        [whole(a) for a in args],
+        [
+            jax.ShapeDtypeStruct((2, blocks, block_size, block_size), F32),
+            jax.ShapeDtypeStruct((1, 2 * local_width), F32),
+        ],
+        [],
+        8 * lat_rows * modes * local_width * local_width,
+    )
+    packed = jnp.concatenate([weight.reshape(-1), bias.reshape(-1)]).reshape(-1, 128)
+    packed = sum_over(sum_over(packed, "frame"), "dp").reshape(-1)
+    cut = weight.size
+    filled = None
+    for row in range(lat_rows):
+        filled = attention(row, *cells[row], filled)
+    return (filled, packed[:cut].reshape(weight.shape), packed[cut:].reshape(2, local_width))
 
 
 def transform_table(length, modes):
@@ -71,7 +464,7 @@
     return attended.astype(jnp.bfloat16).reshape(site_count, query_frames, width)
 
 
-def body(
+def plain_body(
     fields,
     band_rows,
     earliest_past_snapshot,
@@ -187,6 +580,23 @@
     return (predicted_output_fields, mask_coefficient2_derivative, mask_offset2_derivative)
 
 
+def basis_rank(window, length, modes):
+    return -(-(window * (2 * modes - 1) // length + 24) // 16) * 16
+
+
+def body(fields, *rest):
+    width, local_width = fields.shape[-1], rest[-1].shape[-1]
+    head_size = width // rest[-2].shape[0]
+    fits = (
+        fields.shape[0] == 1
+        and lax.axis_size("frame") == 2
+        and local_width % LANES == 0
+        and 2 * head_size == 128
+        and rest[-4].shape[1] * 2 == width
+    )
+    return (fused_body if fits else plain_body)(fields, *rest)
+
+
 def solution(mesh):
     placed = (
         P("dp", "frame", None, "lon", None),

time: 442 us -> 150 us (0.34)
  the two profiles are of different devices: /device:TPU:0 before, /device:TPU:8 now
where the time goes in v1:
time: 150 us; the launch traced here: 148 us
  Pallas kernels  53.8 us (36%)
  starting transfers between devices  48.2 us (32%)
  local copies, waits for them, and re-layouts  33.2 us (22%)
  other arithmetic  6.58 us (4%)
  waiting for transfers between devices  4.28 us (3%)
  between operations  2.04 us (1%)
    pallas_call x21, Pallas kernels, call(): pl.pallas_call(kernel, grid_spec=pltpu.PrefetchScalarGridSpec(num_scalar_...  53.8 us
    ppermute x24, starting transfers between devices, swap_blocks(): lax.ppermute(part, 'lon', [(i, (i + shift) % count) for i in range(count)])  35.6 us
    unnamed x146, local copies, waits for them, and re-layouts  20.4 us
    ppermute x4, starting transfers between devices, fused_body(): earlier = lax.ppermute(keyval, 'frame', [(0, 1)])  9.61 us
    another operation x6, local copies, waits for them, and re-layouts, block_diagonal(): tiled = jnp.tile(weight.reshape(2, width, size), (1, 1, blocks))  7.73 us
    ppermute x24, waiting for transfers between devices, swap_blocks(): lax.ppermute(part, 'lon', [(i, (i + shift) % count) for i in range(count)])  4.26 us
  transfers between devices with their start and end apart: 31, of which 1 were waited for; matrix products, arithmetic and copies ran while one was open for 13% of the time, Pallas kernels for 32%

profile of v1, /device:TPU:8, one launch (start us, length us, event | category | flops | bytes accessed | tf_op | source)
XLA Modules:
  0.0 148.1 jit_solution(17797136343181831494)
XLA Ops:
  0.6 1.8 %copy-done = bf16[1,1,4,360,1024]{4,3,2,1,0:T(8,128)(2,1)S(1)} copy-done((bf16[1,1,4,360,1024]{4,3,2,1,0:T(8,128)(2,1)S(1)}, bf16[1,1,4,360,1024]{4,3,2,1,0:T(8,128)(2,1)}, u32[]{:S(2)}) %copy-start) | copy-done | bytes 2949144
  2.5 1.4 copy-done.2
  3.8 0.9 copy-done.30
  6.1 2.1 %shard_map.196 = (bf16[208,256]{1,0:T(8,128)(2,1)S(1)}, bf16[208,256]{1,0:T(8,128)(2,1)}, bf16[208,256]{1,0:T(8,128)(2,1)}, bf16[208,256]{1,0:T(8,128)(2,1)}) custom-call(s32[1]{0:T(128)} %bitcast.1.me_ref, s32[1,4]{1,0:T(1,128)S(1)} %copy-done.49, bf16[1,1,4,360,1024]{4,3,2,1,0:T(8,128)(2,1)S(1)} %copy-done, bf16[720,1024]{1,0:T(8,128)(2,1)S(1)} %copy-done.2, ...), custom_call_target="tpu_custom_call" | custom-call | flops 153354240 | bytes 851968 | tf_op jit(solution)/shard_map/pallas_call | solution.py:209
  8.2 1.6 %collective-permute-start.21 = (bf16[208,256]{1,0:T(8,128)(2,1)}, bf16[208,256]{1,0:T(8,128)(2,1)S(1)}, u32[]{:S(2)}, u32[]{:S(2)}) collective-permute-start(bf16[208,256]{1,0:T(8,128)(2,1)} %get-tuple-element.80), channel_id=1, source_target_pairs={{0,1},{1,2},{2,3},{3,0},{4,5},{5,6},{6,7},{7,4},{8,9},{9,10},{10,1... | collective-permute-start | bytes 319496 | tf_op jit(solution)/shard_map/ppermute | solution.py:239
  9.8 1.0 collective-permute-start.22
  10.8 2.0 %collective-permute-start.23 = (bf16[208,256]{1,0:T(8,128)(2,1)}, bf16[208,256]{1,0:T(8,128)(2,1)}, u32[]{:S(2)}, u32[]{:S(2)}) collective-permute-start(bf16[208,256]{1,0:T(8,128)(2,1)} %get-tuple-element.82), channel_id=1, source_target_pairs={{0,3},{1,0},{2,1},{3,2},{4,7},{5,4},{6,5},{7,6},{8,11},{9,8},{10,9... | collective-permute-start | bytes 319496 | tf_op jit(solution)/shard_map/ppermute | solution.py:239
  12.9 2.1 %shard_map.192 = (bf16[208,256]{1,0:T(8,128)(2,1)S(1)}, bf16[208,256]{1,0:T(8,128)(2,1)}, bf16[208,256]{1,0:T(8,128)(2,1)}, bf16[208,256]{1,0:T(8,128)(2,1)S(1)}) custom-call(s32[1]{0:T(128)} %bitcast.1.me_ref, s32[1,4]{1,0:T(1,128)S(1)} %copy-done.49, bf16[1,1,4,360,1024]{4,3,2,1,0:T(8,128)(2,1)S(1)} %copy-done, bf16[720,1024]{1,0:T(8,128)(2,1)S(1)} %copy-done.2, ...), custom_call_target="tpu_custom_call" | custom-call | flops 153354240 | bytes 851968 | tf_op jit(solution)/shard_map/pallas_call | solution.py:209
  15.6 3.7 %collective-permute-start.15 = (bf16[208,256]{1,0:T(8,128)(2,1)}, bf16[208,256]{1,0:T(8,128)(2,1)}, u32[]{:S(2)}, u32[]{:S(2)}) collective-permute-start(bf16[208,256]{1,0:T(8,128)(2,1)} %get-tuple-element.71), channel_id=1, source_target_pairs={{0,2},{1,3},{2,0},{3,1},{4,6},{5,7},{6,4},{7,5},{8,10},{9,11},{10,... | collective-permute-start | bytes 319496 | tf_op jit(solution)/shard_map/ppermute | solution.py:239
  20.2 1.9 %copy.24 = bf16[2,256,256]{2,1,0:T(8,128)(2,1)} copy(bf16[2,256,256]{1,2,0:T(8,128)(2,1)} %bitcast.51) | data formatting | bytes 524288 | tf_op jit(solution)/shard_map/tile | solution.py:228
  22.1 1.6 %copy.25 = bf16[2,256,64]{1,2,0:T(8,128)(2,1)} copy(bf16[2,256,64]{2,1,0:T(8,128)(2,1)} %bitcast.54) | data formatting | bytes 131072 | tf_op jit(solution)/shard_map/tile | solution.py:228
  23.7 1.6 %tile.24 = bf16[2,256,4,64]{1,3,2,0:T(8,128)(2,1)} broadcast(bf16[2,256,64]{1,2,0:T(8,128)(2,1)} %copy.25), dimensions={0,1,3} | broadcast | bytes 327680 | tf_op jit(solution)/shard_map/tile | solution.py:228
  25.3 1.8 %copy.26 = bf16[2,256,256]{2,1,0:T(8,128)(2,1)} copy(bf16[2,256,256]{1,2,0:T(8,128)(2,1)} %bitcast.52) | data formatting | bytes 524288 | tf_op jit(solution)/shard_map/tile | solution.py:228
  27.2 1.1 broadcast_select_fusion
  31.1 1.4 copy-done.3
  32.5 1.4 shard_map.188
  38.5 0.8 reshape_reshape.3.scale_ref
  39.3 1.2 maximum_maximum_fusion.1.refs_7_
  40.5 1.1 maximum_maximum_fusion.refs_5_
  41.8 2.0 %collective-permute-start.7 = (bf16[208,256]{1,0:T(8,128)(2,1)}, bf16[208,256]{1,0:T(8,128)(2,1)S(1)}, u32[]{:S(2)}, u32[]{:S(2)}) collective-permute-start(bf16[208,256]{1,0:T(8,128)(2,1)} %copy-done.67), channel_id=1, source_target_pairs={{0,1},{1,2},{2,3},{3,0},{4,5},{5,6},{6,7},{7,4},{8,9},{9,10},{10,1... | collective-permute-start | bytes 319496 | tf_op jit(solution)/shard_map/ppermute | solution.py:239
  43.9 1.4 shard_map.184
  45.4 1.9 %collective-permute-start.8 = (bf16[208,256]{1,0:T(8,128)(2,1)S(1)}, bf16[208,256]{1,0:T(8,128)(2,1)S(1)}, u32[]{:S(2)}, u32[]{:S(2)}) collective-permute-start(bf16[208,256]{1,0:T(8,128)(2,1)S(1)} %copy-done.64), channel_id=1, source_target_pairs={{0,2},{1,3},{2,0},{3,1},{4,6},{5,7},{6,4},{7,5},{8,10},{9,11},{10,... | collective-permute-start | bytes 319496 | tf_op jit(solution)/shard_map/ppermute | solution.py:239
  47.3 0.9 copy-done.40
  48.2 0.9 copy-done.46
  49.1 3.7 %shard_map.197 = (bf16[208,256]{1,0:T(8,128)(2,1)S(1)}, bf16[208,256]{1,0:T(8,128)(2,1)}, bf16[208,256]{1,0:T(8,128)(2,1)}, bf16[208,256]{1,0:T(8,128)(2,1)}, bf16[736,256]{1,0:T(8,128)(2,1)S(1)}) custom-call(s32[1]{0:T(128)} %bitcast.1.me_ref, bf16[208,256]{1,0:T(8,128)(2,1)S(1)} %copy-done.36, bf16[208,256]{1,0:T(8,128)(2,1)S(1)} %copy-done.40, ...), custom_call_target="tpu_custom_call" | custom-call | flops 1012924416 | bytes 1605632 | tf_op jit(solution)/shard_map/pallas_call | solution.py:209
  52.8 2.0 %collective-permute-start = (bf16[208,256]{1,0:T(8,128)(2,1)S(1)}, bf16[208,256]{1,0:T(8,128)(2,1)S(1)}, u32[]{:S(2)}, u32[]{:S(2)}) collective-permute-start(bf16[208,256]{1,0:T(8,128)(2,1)S(1)} %get-tuple-element.50), channel_id=1, source_target_pairs={{0,1},{1,2},{2,3},{3,0},{4,5},{5,6},{6,7},{7,4},{8,9},{9,10},{10,1... | collective-permute-start | bytes 319496 | tf_op jit(solution)/shard_map/ppermute | solution.py:239
  54.8 2.9 %collective-permute-start.1 = (bf16[208,256]{1,0:T(8,128)(2,1)S(1)}, bf16[208,256]{1,0:T(8,128)(2,1)S(1)}, u32[]{:S(2)}, u32[]{:S(2)}) collective-permute-start(bf16[208,256]{1,0:T(8,128)(2,1)S(1)} %get-tuple-element.51), channel_id=1, source_target_pairs={{0,2},{1,3},{2,0},{3,1},{4,6},{5,7},{6,4},{7,5},{8,10},{9,11},{10,... | collective-permute-start | bytes 319496 | tf_op jit(solution)/shard_map/ppermute | solution.py:239
  57.7 3.5 %shard_map.193 = (bf16[208,256]{1,0:T(8,128)(2,1)S(1)}, bf16[208,256]{1,0:T(8,128)(2,1)}, bf16[208,256]{1,0:T(8,128)(2,1)S(1)}, bf16[208,256]{1,0:T(8,128)(2,1)S(1)}, bf16[736,256]{1,0:T(8,128)(2,1)S(1)}) custom-call(s32[1]{0:T(128)} %bitcast.1.me_ref, bf16[208,256]{1,0:T(8,128)(2,1)S(1)} %get-tuple-element.69.refs_0_, ...), custom_call_target="tpu_custom_call" | custom-call | flops 1012924416 | bytes 1605632 | tf_op jit(solution)/shard_map/pallas_call | solution.py:209
  63.1 2.0 %collective-permute-start.24 = (bf16[208,256]{1,0:T(8,128)(2,1)}, bf16[208,256]{1,0:T(8,128)(2,1)}, u32[]{:S(2)}, u32[]{:S(2)}) collective-permute-start(bf16[208,256]{1,0:T(8,128)(2,1)} %get-tuple-element.84), channel_id=1, source_target_pairs={{0,1},{1,2},{2,3},{3,0},{4,5},{5,6},{6,7},{7,4},{8,9},{9,10},{10,1... | collective-permute-start | bytes 319496 | tf_op jit(solution)/shard_map/ppermute | solution.py:239
  65.2 1.9 %collective-permute-start.25 = (bf16[208,256]{1,0:T(8,128)(2,1)}, bf16[208,256]{1,0:T(8,128)(2,1)}, u32[]{:S(2)}, u32[]{:S(2)}) collective-permute-start(bf16[208,256]{1,0:T(8,128)(2,1)} %get-tuple-element.85), channel_id=1, source_target_pairs={{0,2},{1,3},{2,0},{3,1},{4,6},{5,7},{6,4},{7,5},{8,10},{9,11},{10,... | collective-permute-start | bytes 319496 | tf_op jit(solution)/shard_map/ppermute | solution.py:239
  67.0 2.1 %shard_map.189 = (bf16[208,256]{1,0:T(8,128)(2,1)S(1)}, bf16[208,256]{1,0:T(8,128)(2,1)S(1)}, bf16[208,256]{1,0:T(8,128)(2,1)S(1)}, bf16[208,256]{1,0:T(8,128)(2,1)S(1)}, bf16[736,256]{1,0:T(8,128)(2,1)S(1)}) custom-call(s32[1]{0:T(128)} %bitcast.1.me_ref, bf16[208,256]{1,0:T(8,128)(2,1)S(1)} %copy-done.42, ...), custom_call_target="tpu_custom_call" | custom-call | flops 1012924416 | bytes 1605632 | tf_op jit(solution)/shard_map/pallas_call | solution.py:209
  71.1 2.0 %collective-permute-start.17 = (bf16[208,256]{1,0:T(8,128)(2,1)}, bf16[208,256]{1,0:T(8,128)(2,1)}, u32[]{:S(2)}, u32[]{:S(2)}) collective-permute-start(bf16[208,256]{1,0:T(8,128)(2,1)} %get-tuple-element.74), channel_id=1, source_target_pairs={{0,1},{1,2},{2,3},{3,0},{4,5},{5,6},{6,7},{7,4},{8,9},{9,10},{10,1... | collective-permute-start | bytes 319496 | tf_op jit(solution)/shard_map/ppermute | solution.py:239
  73.1 2.1 %shard_map.185 = (bf16[208,256]{1,0:T(8,128)(2,1)S(1)}, bf16[208,256]{1,0:T(8,128)(2,1)S(1)}, bf16[208,256]{1,0:T(8,128)(2,1)S(1)}, bf16[208,256]{1,0:T(8,128)(2,1)S(1)}, bf16[736,256]{1,0:T(8,128)(2,1)S(1)}) custom-call(s32[1]{0:T(128)} %bitcast.1.me_ref, bf16[208,256]{1,0:T(8,128)(2,1)S(1)} %get-tuple-element.49.refs_0_, ...), custom_call_target="tpu_custom_call" | custom-call | flops 1012924416 | bytes 1605632 | tf_op jit(solution)/shard_map/pallas_call | solution.py:209
  75.3 1.4 shard_map.204
  77.5 2.9 %collective-permute-start.18 = (bf16[208,256]{1,0:T(8,128)(2,1)}, bf16[208,256]{1,0:T(8,128)(2,1)S(1)}, u32[]{:S(2)}, u32[]{:S(2)}) collective-permute-start(bf16[208,256]{1,0:T(8,128)(2,1)} %copy-done.66), channel_id=1, source_target_pairs={{0,2},{1,3},{2,0},{3,1},{4,6},{5,7},{6,4},{7,5},{8,10},{9,11},{10,... | collective-permute-start | bytes 319496 | tf_op jit(solution)/shard_map/ppermute | solution.py:239
  80.3 2.0 %collective-permute-start.10 = (bf16[208,256]{1,0:T(8,128)(2,1)}, bf16[208,256]{1,0:T(8,128)(2,1)S(1)}, u32[]{:S(2)}, u32[]{:S(2)}) collective-permute-start(bf16[208,256]{1,0:T(8,128)(2,1)} %copy-done.65), channel_id=1, source_target_pairs={{0,1},{1,2},{2,3},{3,0},{4,5},{5,6},{6,7},{7,4},{8,9},{9,10},{10,1... | collective-permute-start | bytes 319496 | tf_op jit(solution)/shard_map/ppermute | solution.py:239
  82.4 1.8 %collective-permute-start.11 = (bf16[208,256]{1,0:T(8,128)(2,1)}, bf16[208,256]{1,0:T(8,128)(2,1)S(1)}, u32[]{:S(2)}, u32[]{:S(2)}) collective-permute-start(bf16[208,256]{1,0:T(8,128)(2,1)} %copy-done.62), channel_id=1, source_target_pairs={{0,2},{1,3},{2,0},{3,1},{4,6},{5,7},{6,4},{7,5},{8,10},{9,11},{10,... | collective-permute-start | bytes 319496 | tf_op jit(solution)/shard_map/ppermute | solution.py:239
  84.2 0.9 maximum_bitcast_fusion
  85.1 4.2 %collective-permute-done.18.refs_2_ = bf16[208,256]{1,0:T(8,128)(2,1)S(1)} collective-permute-done((bf16[208,256]{1,0:T(8,128)(2,1)}, bf16[208,256]{1,0:T(8,128)(2,1)S(1)}, u32[]{:S(2)}, u32[]{:S(2)}) %collective-permute-start.18) | collective-permute-done | bytes 106528 | tf_op jit(solution)/shard_map/ppermute | solution.py:239
  89.3 1.3 collective-permute-start.28
  90.7 1.4 copy-done.5
  92.0 1.2 copy-done.11
  93.3 3.2 %shard_map.198 = (bf16[360,1024]{1,0:T(8,128)(2,1)S(1)}, bf16[360,512]{1,0:T(8,128)(2,1)}) custom-call(s32[1]{0:T(128)} %bitcast.1.me_ref, s32[1,4]{1,0:T(1,128)S(1)} %copy-done.50, bf16[1,1,4,360,1024]{4,3,2,1,0:T(8,128)(2,1)S(1)} %copy-done.1, bf16[720,1024]{1,0:T(8,128)(2,1)S(1)} %copy-done.5, bf16[208,256]{1,0:T(8,128)(2,1)S(1)} %get-tuple-element.83.refs_0_, ...), custom_call_target="tpu_custom_call" | custom-call | flops 530841600 | bytes 2211840 | tf_op jit(solution)/shard_map/pallas_call | solution.py:209
  96.6 2.3 %shard_map.194 = (bf16[360,1024]{1,0:T(8,128)(2,1)S(1)}, bf16[360,512]{1,0:T(8,128)(2,1)S(1)}) custom-call(s32[1]{0:T(128)} %bitcast.1.me_ref, s32[1,4]{1,0:T(1,128)S(1)} %copy-done.50, bf16[1,1,4,360,1024]{4,3,2,1,0:T(8,128)(2,1)S(1)} %copy-done.1, bf16[720,1024]{1,0:T(8,128)(2,1)S(1)} %copy-done.5, bf16[208,256]{1,0:T(8,128)(2,1)S(1)} %copy-done.44, ...), custom_call_target="tpu_custom_call" | custom-call | flops 530841600 | bytes 2211840 | tf_op jit(solution)/shard_map/pallas_call | solution.py:209
  98.9 3.7 %collective-permute-start.4 = (bf16[208,256]{1,0:T(8,128)(2,1)S(1)}, bf16[208,256]{1,0:T(8,128)(2,1)S(1)}, u32[]{:S(2)}, u32[]{:S(2)}) collective-permute-start(bf16[208,256]{1,0:T(8,128)(2,1)S(1)} %copy-done.54), channel_id=1, source_target_pairs={{0,2},{1,3},{2,0},{3,1},{4,6},{5,7},{6,4},{7,5},{8,10},{9,11},{10,... | collective-permute-start | bytes 319496 | tf_op jit(solution)/shard_map/ppermute | solution.py:239
  102.6 2.0 %collective-permute-start.5 = (bf16[208,256]{1,0:T(8,128)(2,1)S(1)}, bf16[208,256]{1,0:T(8,128)(2,1)S(1)}, u32[]{:S(2)}, u32[]{:S(2)}) collective-permute-start(bf16[208,256]{1,0:T(8,128)(2,1)S(1)} %copy-done.52), channel_id=1, source_target_pairs={{0,3},{1,0},{2,1},{3,2},{4,7},{5,4},{6,5},{7,6},{8,11},{9,8},{10,9... | collective-permute-start | bytes 319496 | tf_op jit(solution)/shard_map/ppermute | solution.py:239
  104.6 3.2 %collective-permute-start.27 = (bf16[360,512]{1,0:T(8,128)(2,1)}, bf16[360,512]{1,0:T(8,128)(2,1)}, u32[]{:S(2)}, u32[]{:S(2)}) collective-permute-start(bf16[360,512]{1,0:T(8,128)(2,1)} %get-tuple-element.88.own_ref), channel_id=1, source_target_pairs={{0,4},{1,5},{2,6},{3,7},{8,12},{9,13},{10,14},{11,15},{16,20},{17,... | collective-permute-start | bytes 1105928 | tf_op jit(solution)/shard_map/ppermute | solution.py:376
  107.8 2.2 %shard_map.190 = (bf16[360,1024]{1,0:T(8,128)(2,1)S(1)}, bf16[360,512]{1,0:T(8,128)(2,1)}) custom-call(s32[1]{0:T(128)} %bitcast.1.me_ref, s32[1,4]{1,0:T(1,128)S(1)} %copy-done.50, bf16[1,1,4,360,1024]{4,3,2,1,0:T(8,128)(2,1)S(1)} %copy-done.1, bf16[720,1024]{1,0:T(8,128)(2,1)S(1)} %copy-done.5, bf16[208,256]{1,0:T(8,128)(2,1)S(1)} %copy-done.38, ...), custom_call_target="tpu_custom_call" | custom-call | flops 530841600 | bytes 2211840 | tf_op jit(solution)/shard_map/pallas_call | solution.py:209
  110.1 2.2 %shard_map.199.query_ref = bf16[360,1024]{1,0:T(8,128)(2,1)S(1)} custom-call(bf16[360,1024]{1,0:T(8,128)(2,1)S(1)} %get-tuple-element.87.hidden_ref, bf16[1024,1024]{1,0:T(8,128)(2,1)S(1)} %copy-done.8), custom_call_target="tpu_custom_call" | custom-call | flops 754974720 | bytes 1474560 | tf_op jit(solution)/shard_map/pallas_call | solution.py:209
  112.3 2.2 %shard_map.195.query_ref = bf16[360,1024]{1,0:T(8,128)(2,1)S(1)} custom-call(bf16[360,1024]{1,0:T(8,128)(2,1)S(1)} %get-tuple-element.77.hidden_ref, bf16[1024,1024]{1,0:T(8,128)(2,1)S(1)} %copy-done.8), custom_call_target="tpu_custom_call" | custom-call | flops 754974720 | bytes 1474560 | tf_op jit(solution)/shard_map/pallas_call | solution.py:209
  114.6 2.3 %collective-permute-start.20 = (bf16[360,512]{1,0:T(8,128)(2,1)S(1)}, bf16[360,512]{1,0:T(8,128)(2,1)}, u32[]{:S(2)}, u32[]{:S(2)}) collective-permute-start(bf16[360,512]{1,0:T(8,128)(2,1)S(1)} %get-tuple-element.78.own_ref), channel_id=1, source_target_pairs={{0,4},{1,5},{2,6},{3,7},{8,12},{9,13},{10,14},{11,15},{16,20},{17,... | collective-permute-start | bytes 1105928 | tf_op jit(solution)/shard_map/ppermute | solution.py:376
  116.9 1.6 %collective-permute-start.30 = (f32[260,128]{1,0:T(8,128)S(1)}, f32[260,128]{1,0:T(8,128)S(1)}, u32[]{:S(2)}, u32[]{:S(2)}) collective-permute-start(f32[260,128]{1,0:T(8,128)S(1)} %fusion.3), channel_id=1, source_target_pairs={{0,16},{8,24},{16,0},{24,8},{1,17},{9,25},{17,1},{25,9},{2,18},{10... | collective-permute-start | bytes 399368 | tf_op jit(solution)/shard_map/ppermute | solution.py:252
  118.5 2.2 %shard_map.191.query_ref = bf16[360,1024]{1,0:T(8,128)(2,1)S(1)} custom-call(bf16[360,1024]{1,0:T(8,128)(2,1)S(1)} %get-tuple-element.67.hidden_ref, bf16[1024,1024]{1,0:T(8,128)(2,1)S(1)} %copy-done.8), custom_call_target="tpu_custom_call" | custom-call | flops 754974720 | bytes 1474560 | tf_op jit(solution)/shard_map/pallas_call | solution.py:209
  120.8 2.1 %collective-permute-start.13 = (bf16[360,512]{1,0:T(8,128)(2,1)}, bf16[360,512]{1,0:T(8,128)(2,1)}, u32[]{:S(2)}, u32[]{:S(2)}) collective-permute-start(bf16[360,512]{1,0:T(8,128)(2,1)} %get-tuple-element.68.own_ref), channel_id=1, source_target_pairs={{0,4},{1,5},{2,6},{3,7},{8,12},{9,13},{10,14},{11,15},{16,20},{17,... | collective-permute-start | bytes 1105928 | tf_op jit(solution)/shard_map/ppermute | solution.py:376
  122.9 2.2 %shard_map.186 = (bf16[360,1024]{1,0:T(8,128)(2,1)S(1)}, bf16[360,512]{1,0:T(8,128)(2,1)}) custom-call(s32[1]{0:T(128)} %bitcast.1.me_ref, s32[1,4]{1,0:T(1,128)S(1)} %copy-done.50, bf16[1,1,4,360,1024]{4,3,2,1,0:T(8,128)(2,1)S(1)} %copy-done.1, bf16[720,1024]{1,0:T(8,128)(2,1)S(1)} %copy-done.6, bf16[208,256]{1,0:T(8,128)(2,1)S(1)} %copy-done.34, ...), custom_call_target="tpu_custom_call" | custom-call | flops 530841600 | bytes 2211840 | tf_op jit(solution)/shard_map/pallas_call | solution.py:209
  125.0 2.1 %collective-permute-start.6 = (bf16[360,512]{1,0:T(8,128)(2,1)}, bf16[360,512]{1,0:T(8,128)(2,1)}, u32[]{:S(2)}, u32[]{:S(2)}) collective-permute-start(bf16[360,512]{1,0:T(8,128)(2,1)} %get-tuple-element.58.own_ref), channel_id=1, source_target_pairs={{0,4},{1,5},{2,6},{3,7},{8,12},{9,13},{10,14},{11,15},{16,20},{17,... | collective-permute-start | bytes 1105928 | tf_op jit(solution)/shard_map/ppermute | solution.py:376
  127.1 2.2 %shard_map.187.query_ref = bf16[360,1024]{1,0:T(8,128)(2,1)S(1)} custom-call(bf16[360,1024]{1,0:T(8,128)(2,1)S(1)} %get-tuple-element.57.hidden_ref, bf16[1024,1024]{1,0:T(8,128)(2,1)S(1)} %copy-done.8), custom_call_target="tpu_custom_call" | custom-call | flops 754974720 | bytes 1474560 | tf_op jit(solution)/shard_map/pallas_call | solution.py:209
  129.3 0.9 copy-done.27
  130.2 0.8 reshape.135
  131.7 1.1 copy-done.16
  132.8 3.9 %shard_map.200.rest_0_ = bf16[1,1,4,360,1024]{4,3,2,1,0:T(8,128)(2,1)} custom-call(s32[1]{0:T(128)S(6)} %convert_element_type.6.seen_ref, bf16[360,1024]{1,0:T(8,128)(2,1)S(1)} %copy-done.16, bf16[360,512]{1,0:T(8,128)(2,1)} %get-tuple-element.88.own_ref, bf16[360,512]{1,0:T(8,128)(2,1)} %collective-permute-done.27.other_ref, ...), custom_call_target="tpu_custom_call" | custom-call | flops 1509949440 | bytes 5898240 | tf_op jit(solution)/shard_map/pallas_call | solution.py:209
  136.7 3.8 %shard_map.201.rest_0_ = bf16[1,1,4,360,1024]{4,3,2,1,0:T(8,128)(2,1)} custom-call(s32[1]{0:T(128)S(6)} %convert_element_type.6.seen_ref, bf16[360,1024]{1,0:T(8,128)(2,1)S(1)} %copy-done.22, bf16[360,512]{1,0:T(8,128)(2,1)S(1)} %get-tuple-element.78.own_ref, bf16[360,512]{1,0:T(8,128)(2,1)} %collective-permute-done.20.other_ref, ...), custom_call_target="tpu_custom_call", output_to_operand_aliasing={{}: (7, {})} | custom-call | flops 1509949440 | bytes 5898240 | tf_op jit(solution)/shard_map/pallas_call | solution.py:209
  140.5 3.9 %shard_map.202.rest_0_ = bf16[1,1,4,360,1024]{4,3,2,1,0:T(8,128)(2,1)} custom-call(s32[1]{0:T(128)S(6)} %convert_element_type.6.seen_ref, bf16[360,1024]{1,0:T(8,128)(2,1)S(1)} %copy-done.24, bf16[360,512]{1,0:T(8,128)(2,1)} %get-tuple-element.68.own_ref, bf16[360,512]{1,0:T(8,128)(2,1)} %collective-permute-done.13.other_ref, ...), custom_call_target="tpu_custom_call", output_to_operand_aliasing={{}: (7, {})} | custom-call | flops 1509949440 | bytes 5898240 | tf_op jit(solution)/shard_map/pallas_call | solution.py:209
  144.4 3.8 %shard_map.203 = bf16[1,1,4,360,1024]{4,3,2,1,0:T(8,128)(2,1)} custom-call(s32[1]{0:T(128)S(6)} %convert_element_type.6.seen_ref, bf16[360,1024]{1,0:T(8,128)(2,1)S(1)} %copy-done.28, bf16[360,512]{1,0:T(8,128)(2,1)} %get-tuple-element.58.own_ref, bf16[360,512]{1,0:T(8,128)(2,1)} %collective-permute-done.6.other_ref, ...), custom_call_target="tpu_custom_call", output_to_operand_aliasing={{}: (7, {})} | custom-call | flops 1509949440 | bytes 5898240 | tf_op jit(solution)/shard_map/pallas_call | solution.py:209
  (193 shorter events, 15.5 us)
Async XLA Ops:
  8.2 6.7 %copy-start.35 = (bf16[208,256]{1,0:T(8,128)(2,1)}, bf16[208,256]{1,0:T(8,128)(2,1)S(1)}, u32[]{:S(2)}) copy-start(bf16[208,256]{1,0:T(8,128)(2,1)S(1)} %get-tuple-element.79.refs_0_) | copy-start | bytes 319492
  8.2 33.5 %collective-permute-start.21 = (bf16[208,256]{1,0:T(8,128)(2,1)}, bf16[208,256]{1,0:T(8,128)(2,1)S(1)}, u32[]{:S(2)}, u32[]{:S(2)}) collective-permute-start(bf16[208,256]{1,0:T(8,128)(2,1)} %get-tuple-element.80), channel_id=1, source_target_pairs={{0,1},{1,2},{2,3},{3,0},{4,5},{5,6},{6,7},{7,4},{8,9},{9,10},{10,1... | collective-permute-start | bytes 319496 | tf_op jit(solution)/shard_map/ppermute | solution.py:239
  9.8 32.0 %collective-permute-start.22 = (bf16[208,256]{1,0:T(8,128)(2,1)}, bf16[208,256]{1,0:T(8,128)(2,1)S(1)}, u32[]{:S(2)}, u32[]{:S(2)}) collective-permute-start(bf16[208,256]{1,0:T(8,128)(2,1)} %get-tuple-element.81), channel_id=1, source_target_pairs={{0,2},{1,3},{2,0},{3,1},{4,6},{5,7},{6,4},{7,5},{8,10},{9,11},{10,... | collective-permute-start | bytes 319496 | tf_op jit(solution)/shard_map/ppermute | solution.py:239
  10.8 8.5 %copy-start.69 = (bf16[2,4,64,64]{3,2,1,0:T(8,128)(2,1)S(1)}, bf16[2,4,64,64]{3,2,1,0:T(8,128)(2,1)}, u32[]{:S(2)}) copy-start(bf16[2,4,64,64]{3,2,1,0:T(8,128)(2,1)} %param.22) | copy-start | bytes 196612
  10.8 34.5 %collective-permute-start.23 = (bf16[208,256]{1,0:T(8,128)(2,1)}, bf16[208,256]{1,0:T(8,128)(2,1)}, u32[]{:S(2)}, u32[]{:S(2)}) collective-permute-start(bf16[208,256]{1,0:T(8,128)(2,1)} %get-tuple-element.82), channel_id=1, source_target_pairs={{0,3},{1,0},{2,1},{3,2},{4,7},{5,4},{6,5},{7,6},{8,11},{9,8},{10,9... | collective-permute-start | bytes 319496 | tf_op jit(solution)/shard_map/ppermute | solution.py:239
  15.6 31.7 %collective-permute-start.14 = (bf16[208,256]{1,0:T(8,128)(2,1)}, bf16[208,256]{1,0:T(8,128)(2,1)S(1)}, u32[]{:S(2)}, u32[]{:S(2)}) collective-permute-start(bf16[208,256]{1,0:T(8,128)(2,1)} %get-tuple-element.70), channel_id=1, source_target_pairs={{0,1},{1,2},{2,3},{3,0},{4,5},{5,6},{6,7},{7,4},{8,9},{9,10},{10,1... | collective-permute-start | bytes 319496 | tf_op jit(solution)/shard_map/ppermute | solution.py:239
  15.6 37.2 %collective-permute-start.15 = (bf16[208,256]{1,0:T(8,128)(2,1)}, bf16[208,256]{1,0:T(8,128)(2,1)}, u32[]{:S(2)}, u32[]{:S(2)}) collective-permute-start(bf16[208,256]{1,0:T(8,128)(2,1)} %get-tuple-element.71), channel_id=1, source_target_pairs={{0,2},{1,3},{2,0},{3,1},{4,6},{5,7},{6,4},{7,5},{8,10},{9,11},{10,... | collective-permute-start | bytes 319496 | tf_op jit(solution)/shard_map/ppermute | solution.py:239
  20.1 11.0 %copy-start.1 = (bf16[1,1,4,360,1024]{4,3,2,1,0:T(8,128)(2,1)S(1)}, bf16[1,1,4,360,1024]{4,3,2,1,0:T(8,128)(2,1)}, u32[]{:S(2)}) copy-start(bf16[1,1,4,360,1024]{4,3,2,1,0:T(8,128)(2,1)} %x_ref.15) | copy-start | bytes 8847364
  20.1 11.0 %copy-start.31 = (bf16[208,360]{1,0:T(8,128)(2,1)S(1)}, bf16[208,360]{1,0:T(8,128)(2,1)}, u32[]{:S(2)}) copy-start(bf16[208,360]{1,0:T(8,128)(2,1)} %constant.66.basis_ref) | copy-start | bytes 449284
  20.1 11.0 %copy-start.48 = (f32[1024]{0:T(1024)S(1)}, f32[1024]{0:T(1024)}, u32[]{:S(2)}) copy-start(f32[1024]{0:T(1024)} %param.21) | copy-start | bytes 12292
  20.2 11.0 %copy-start.50 = (s32[1,4]{1,0:T(1,128)S(1)}, s32[1,4]{1,0:T(1,128)}, u32[]{:S(2)}) copy-start(s32[1,4]{1,0:T(1,128)} %band_ref.15) | copy-start | bytes 52
  32.5 4.0 %copy-start.70 = (f32[2,256]{1,0:T(2,128)S(1)}, f32[2,256]{1,0:T(2,128)}, u32[]{:S(2)}) copy-start(f32[2,256]{1,0:T(2,128)} %param.23) | copy-start | bytes 6148
  32.5 4.0 %copy-start.71 = (f32[2,256]{1,0:T(2,128)S(1)}, f32[2,256]{1,0:T(2,128)}, u32[]{:S(2)}) copy-start(f32[2,256]{1,0:T(2,128)} %param.25) | copy-start | bytes 6148
  39.3 4.6 %copy-start.4 = (bf16[720,1024]{1,0:T(8,128)(2,1)S(1)}, bf16[720,1024]{1,0:T(8,128)(2,1)}, u32[]{:S(2)}) copy-start(bf16[720,1024]{1,0:T(8,128)(2,1)} %lat_ref.15) | copy-start | bytes 4423684
  41.7 13.1 %collective-permute-start.16 = (bf16[208,256]{1,0:T(8,128)(2,1)}, bf16[208,256]{1,0:T(8,128)(2,1)S(1)}, u32[]{:S(2)}, u32[]{:S(2)}) collective-permute-start(bf16[208,256]{1,0:T(8,128)(2,1)} %copy-done.57), channel_id=1, source_target_pairs={{0,3},{1,0},{2,1},{3,2},{4,7},{5,4},{6,5},{7,6},{8,11},{9,8},{10,9... | collective-permute-start | bytes 319496 | tf_op jit(solution)/shard_map/ppermute | solution.py:239
  41.8 5.5 %copy-start.61 = (bf16[208,256]{1,0:T(8,128)(2,1)S(1)}, bf16[208,256]{1,0:T(8,128)(2,1)}, u32[]{:S(2)}) copy-start(bf16[208,256]{1,0:T(8,128)(2,1)} %copy-done.60) | copy-start | bytes 319492
  41.8 5.5 %copy-start.9 = (bf16[736,832]{1,0:T(8,128)(2,1)S(1)}, bf16[736,832]{1,0:T(8,128)(2,1)}, u32[]{:S(2)}) copy-start(bf16[736,832]{1,0:T(8,128)(2,1)} %constant.60.clone.refs_4_) | copy-start | bytes 3674116
  41.8 5.5 %copy-start.10 = (bf16[4,208,736]{2,1,0:T(8,128)(2,1)S(1)}, bf16[4,208,736]{2,1,0:T(8,128)(2,1)}, u32[]{:S(2)}) copy-start(bf16[4,208,736]{2,1,0:T(8,128)(2,1)} %constant.61.clone.refs_9_) | copy-start | bytes 3674116
  41.8 5.5 %copy-start.36 = (bf16[208,256]{1,0:T(8,128)(2,1)S(1)}, bf16[208,256]{1,0:T(8,128)(2,1)}, u32[]{:S(2)}) copy-start(bf16[208,256]{1,0:T(8,128)(2,1)} %copy-done.35) | copy-start | bytes 319492
  41.8 15.9 %collective-permute-start.7 = (bf16[208,256]{1,0:T(8,128)(2,1)}, bf16[208,256]{1,0:T(8,128)(2,1)S(1)}, u32[]{:S(2)}, u32[]{:S(2)}) collective-permute-start(bf16[208,256]{1,0:T(8,128)(2,1)} %copy-done.67), channel_id=1, source_target_pairs={{0,1},{1,2},{2,3},{3,0},{4,5},{5,6},{6,7},{7,4},{8,9},{9,10},{10,1... | collective-permute-start | bytes 319496 | tf_op jit(solution)/shard_map/ppermute | solution.py:239
  45.4 17.8 %collective-permute-start.8 = (bf16[208,256]{1,0:T(8,128)(2,1)S(1)}, bf16[208,256]{1,0:T(8,128)(2,1)S(1)}, u32[]{:S(2)}, u32[]{:S(2)}) collective-permute-start(bf16[208,256]{1,0:T(8,128)(2,1)S(1)} %copy-done.64), channel_id=1, source_target_pairs={{0,2},{1,3},{2,0},{3,1},{4,6},{5,7},{6,4},{7,5},{8,10},{9,11},{10,... | collective-permute-start | bytes 319496 | tf_op jit(solution)/shard_map/ppermute | solution.py:239
  47.3 17.9 %collective-permute-start.9 = (bf16[208,256]{1,0:T(8,128)(2,1)S(1)}, bf16[208,256]{1,0:T(8,128)(2,1)S(1)}, u32[]{:S(2)}, u32[]{:S(2)}) collective-permute-start(bf16[208,256]{1,0:T(8,128)(2,1)S(1)} %copy-done.61), channel_id=1, source_target_pairs={{0,3},{1,0},{2,1},{3,2},{4,7},{5,4},{6,5},{7,6},{8,11},{9,8},{10,9... | collective-permute-start | bytes 319496 | tf_op jit(solution)/shard_map/ppermute | solution.py:239
  52.8 14.2 %copy-start.42 = (bf16[208,256]{1,0:T(8,128)(2,1)S(1)}, bf16[208,256]{1,0:T(8,128)(2,1)}, u32[]{:S(2)}) copy-start(bf16[208,256]{1,0:T(8,128)(2,1)} %copy-done.41) | copy-start | bytes 319492
  52.8 18.3 %collective-permute-start = (bf16[208,256]{1,0:T(8,128)(2,1)S(1)}, bf16[208,256]{1,0:T(8,128)(2,1)S(1)}, u32[]{:S(2)}, u32[]{:S(2)}) collective-permute-start(bf16[208,256]{1,0:T(8,128)(2,1)S(1)} %get-tuple-element.50), channel_id=1, source_target_pairs={{0,1},{1,2},{2,3},{3,0},{4,5},{5,6},{6,7},{7,4},{8,9},{9,10},{10,1... | collective-permute-start | bytes 319496 | tf_op jit(solution)/shard_map/ppermute | solution.py:239
  54.8 16.3 %collective-permute-start.1 = (bf16[208,256]{1,0:T(8,128)(2,1)S(1)}, bf16[208,256]{1,0:T(8,128)(2,1)S(1)}, u32[]{:S(2)}, u32[]{:S(2)}) collective-permute-start(bf16[208,256]{1,0:T(8,128)(2,1)S(1)} %get-tuple-element.51), channel_id=1, source_target_pairs={{0,2},{1,3},{2,0},{3,1},{4,6},{5,7},{6,4},{7,5},{8,10},{9,11},{10,... | collective-permute-start | bytes 319496 | tf_op jit(solution)/shard_map/ppermute | solution.py:239
  57.7 15.4 %collective-permute-start.2 = (bf16[208,256]{1,0:T(8,128)(2,1)S(1)}, bf16[208,256]{1,0:T(8,128)(2,1)S(1)}, u32[]{:S(2)}, u32[]{:S(2)}) collective-permute-start(bf16[208,256]{1,0:T(8,128)(2,1)S(1)} %get-tuple-element.52), channel_id=1, source_target_pairs={{0,3},{1,0},{2,1},{3,2},{4,7},{5,4},{6,5},{7,6},{8,11},{9,8},{10,9... | collective-permute-start | bytes 319496 | tf_op jit(solution)/shard_map/ppermute | solution.py:239
  63.1 17.2 %collective-permute-start.24 = (bf16[208,256]{1,0:T(8,128)(2,1)}, bf16[208,256]{1,0:T(8,128)(2,1)}, u32[]{:S(2)}, u32[]{:S(2)}) collective-permute-start(bf16[208,256]{1,0:T(8,128)(2,1)} %get-tuple-element.84), channel_id=1, source_target_pairs={{0,1},{1,2},{2,3},{3,0},{4,5},{5,6},{6,7},{7,4},{8,9},{9,10},{10,1... | collective-permute-start | bytes 319496 | tf_op jit(solution)/shard_map/ppermute | solution.py:239
  65.2 15.2 %collective-permute-start.25 = (bf16[208,256]{1,0:T(8,128)(2,1)}, bf16[208,256]{1,0:T(8,128)(2,1)}, u32[]{:S(2)}, u32[]{:S(2)}) collective-permute-start(bf16[208,256]{1,0:T(8,128)(2,1)} %get-tuple-element.85), channel_id=1, source_target_pairs={{0,2},{1,3},{2,0},{3,1},{4,6},{5,7},{6,4},{7,5},{8,10},{9,11},{10,... | collective-permute-start | bytes 319496 | tf_op jit(solution)/shard_map/ppermute | solution.py:239
  71.1 5.6 %copy-start.37 = (bf16[208,256]{1,0:T(8,128)(2,1)}, bf16[208,256]{1,0:T(8,128)(2,1)S(1)}, u32[]{:S(2)}) copy-start(bf16[208,256]{1,0:T(8,128)(2,1)S(1)} %get-tuple-element.63.refs_0_) | copy-start | bytes 319492
  71.1 4.2 %copy-start.32 = (bf16[1,1,4,2,368,256]{5,4,3,2,1,0:T(8,128)(2,1)S(1)}, bf16[1,1,4,2,368,256]{5,4,3,2,1,0:T(8,128)(2,1)}, u32[]{:S(2)}) copy-start(bf16[1,1,4,2,368,256]{5,4,3,2,1,0:T(8,128)(2,1)} %param.30) | copy-start | bytes 4521988
  71.1 11.3 %collective-permute-start.26 = (bf16[208,256]{1,0:T(8,128)(2,1)}, bf16[208,256]{1,0:T(8,128)(2,1)}, u32[]{:S(2)}, u32[]{:S(2)}) collective-permute-start(bf16[208,256]{1,0:T(8,128)(2,1)} %get-tuple-element.86), channel_id=1, source_target_pairs={{0,3},{1,0},{2,1},{3,2},{4,7},{5,4},{6,5},{7,6},{8,11},{9,8},{10,9... | collective-permute-start | bytes 319496 | tf_op jit(solution)/shard_map/ppermute | solution.py:239
  71.1 13.1 %collective-permute-start.17 = (bf16[208,256]{1,0:T(8,128)(2,1)}, bf16[208,256]{1,0:T(8,128)(2,1)}, u32[]{:S(2)}, u32[]{:S(2)}) collective-permute-start(bf16[208,256]{1,0:T(8,128)(2,1)} %get-tuple-element.74), channel_id=1, source_target_pairs={{0,1},{1,2},{2,3},{3,0},{4,5},{5,6},{6,7},{7,4},{8,9},{9,10},{10,1... | collective-permute-start | bytes 319496 | tf_op jit(solution)/shard_map/ppermute | solution.py:239
  75.3 15.4 %copy-start.29 = (bf16[360,208]{1,0:T(8,128)(2,1)S(1)}, bf16[360,208]{1,0:T(8,128)(2,1)}, u32[]{:S(2)}) copy-start(bf16[360,208]{1,0:T(8,128)(2,1)} %constant.59.clone.refs_4_) | copy-start | bytes 449284
  77.5 11.9 %collective-permute-start.18 = (bf16[208,256]{1,0:T(8,128)(2,1)}, bf16[208,256]{1,0:T(8,128)(2,1)S(1)}, u32[]{:S(2)}, u32[]{:S(2)}) collective-permute-start(bf16[208,256]{1,0:T(8,128)(2,1)} %copy-done.66), channel_id=1, source_target_pairs={{0,2},{1,3},{2,0},{3,1},{4,6},{5,7},{6,4},{7,5},{8,10},{9,11},{10,... | collective-permute-start | bytes 319496 | tf_op jit(solution)/shard_map/ppermute | solution.py:239
  80.3 16.1 %collective-permute-start.19 = (bf16[208,256]{1,0:T(8,128)(2,1)}, bf16[208,256]{1,0:T(8,128)(2,1)S(1)}, u32[]{:S(2)}, u32[]{:S(2)}) collective-permute-start(bf16[208,256]{1,0:T(8,128)(2,1)} %copy-done.59), channel_id=1, source_target_pairs={{0,3},{1,0},{2,1},{3,2},{4,7},{5,4},{6,5},{7,6},{8,11},{9,8},{10,9... | collective-permute-start | bytes 319496 | tf_op jit(solution)/shard_map/ppermute | solution.py:239
  80.3 18.6 %collective-permute-start.10 = (bf16[208,256]{1,0:T(8,128)(2,1)}, bf16[208,256]{1,0:T(8,128)(2,1)S(1)}, u32[]{:S(2)}, u32[]{:S(2)}) collective-permute-start(bf16[208,256]{1,0:T(8,128)(2,1)} %copy-done.65), channel_id=1, source_target_pairs={{0,1},{1,2},{2,3},{3,0},{4,5},{5,6},{6,7},{7,4},{8,9},{9,10},{10,1... | collective-permute-start | bytes 319496 | tf_op jit(solution)/shard_map/ppermute | solution.py:239
  82.4 20.3 %collective-permute-start.11 = (bf16[208,256]{1,0:T(8,128)(2,1)}, bf16[208,256]{1,0:T(8,128)(2,1)S(1)}, u32[]{:S(2)}, u32[]{:S(2)}) collective-permute-start(bf16[208,256]{1,0:T(8,128)(2,1)} %copy-done.62), channel_id=1, source_target_pairs={{0,2},{1,3},{2,0},{3,1},{4,6},{5,7},{6,4},{7,5},{8,10},{9,11},{10,... | collective-permute-start | bytes 319496 | tf_op jit(solution)/shard_map/ppermute | solution.py:239
  84.2 20.4 %collective-permute-start.12 = (bf16[208,256]{1,0:T(8,128)(2,1)}, bf16[208,256]{1,0:T(8,128)(2,1)S(1)}, u32[]{:S(2)}, u32[]{:S(2)}) collective-permute-start(bf16[208,256]{1,0:T(8,128)(2,1)} %copy-done.58), channel_id=1, source_target_pairs={{0,3},{1,0},{2,1},{3,2},{4,7},{5,4},{6,5},{7,6},{8,11},{9,8},{10,9... | collective-permute-start | bytes 319496 | tf_op jit(solution)/shard_map/ppermute | solution.py:239
  89.3 20.6 %collective-permute-start.28 = (f32[260,128]{1,0:T(8,128)S(1)}, f32[260,128]{1,0:T(8,128)S(1)}, u32[]{:S(2)}, u32[]{:S(2)}) collective-permute-start(f32[260,128]{1,0:T(8,128)S(1)} %maximum_bitcast_fusion), channel_id=1, source_target_pairs={{0,4},{4,0},{1,5},{5,1},{2,6},{6,2},{3,7},{7,3},{8,12},{12,8},{9,1... | collective-permute-start | bytes 399368 | tf_op jit(solution)/shard_map/ppermute | solution.py:252
  96.5 13.6 %copy-start.13 = (bf16[360,1024]{1,0:T(8,128)(2,1)}, bf16[360,1024]{1,0:T(8,128)(2,1)S(1)}, u32[]{:S(2)}) copy-start(bf16[360,1024]{1,0:T(8,128)(2,1)S(1)} %get-tuple-element.87.hidden_ref) | copy-start | bytes 2211844
  96.5 20.4 %collective-permute-start.3 = (bf16[208,256]{1,0:T(8,128)(2,1)S(1)}, bf16[208,256]{1,0:T(8,128)(2,1)S(1)}, u32[]{:S(2)}, u32[]{:S(2)}) collective-permute-start(bf16[208,256]{1,0:T(8,128)(2,1)S(1)} %copy-done.56), channel_id=1, source_target_pairs={{0,1},{1,2},{2,3},{3,0},{4,5},{5,6},{6,7},{7,4},{8,9},{9,10},{10,1... | collective-permute-start | bytes 319496 | tf_op jit(solution)/shard_map/ppermute | solution.py:239
  96.6 6.1 %copy-start.52 = (bf16[208,256]{1,0:T(8,128)(2,1)S(1)}, bf16[208,256]{1,0:T(8,128)(2,1)}, u32[]{:S(2)}) copy-start(bf16[208,256]{1,0:T(8,128)(2,1)} %copy-done.51) | copy-start | bytes 319492
  96.6 11.2 %copy-start.38 = (bf16[208,256]{1,0:T(8,128)(2,1)S(1)}, bf16[208,256]{1,0:T(8,128)(2,1)}, u32[]{:S(2)}) copy-start(bf16[208,256]{1,0:T(8,128)(2,1)} %copy-done.37) | copy-start | bytes 319492
  98.9 13.4 %copy-start.17 = (bf16[360,1024]{1,0:T(8,128)(2,1)}, bf16[360,1024]{1,0:T(8,128)(2,1)S(1)}, u32[]{:S(2)}) copy-start(bf16[360,1024]{1,0:T(8,128)(2,1)S(1)} %get-tuple-element.77.hidden_ref) | copy-start | bytes 2211844
  98.9 21.8 %collective-permute-start.4 = (bf16[208,256]{1,0:T(8,128)(2,1)S(1)}, bf16[208,256]{1,0:T(8,128)(2,1)S(1)}, u32[]{:S(2)}, u32[]{:S(2)}) collective-permute-start(bf16[208,256]{1,0:T(8,128)(2,1)S(1)} %copy-done.54), channel_id=1, source_target_pairs={{0,2},{1,3},{2,0},{3,1},{4,6},{5,7},{6,4},{7,5},{8,10},{9,11},{10,... | collective-permute-start | bytes 319496 | tf_op jit(solution)/shard_map/ppermute | solution.py:239
  102.6 20.2 %collective-permute-start.5 = (bf16[208,256]{1,0:T(8,128)(2,1)S(1)}, bf16[208,256]{1,0:T(8,128)(2,1)S(1)}, u32[]{:S(2)}, u32[]{:S(2)}) collective-permute-start(bf16[208,256]{1,0:T(8,128)(2,1)S(1)} %copy-done.52), channel_id=1, source_target_pairs={{0,3},{1,0},{2,1},{3,2},{4,7},{5,4},{6,5},{7,6},{8,11},{9,8},{10,9... | collective-permute-start | bytes 319496 | tf_op jit(solution)/shard_map/ppermute | solution.py:239
  104.6 27.0 %collective-permute-start.27 = (bf16[360,512]{1,0:T(8,128)(2,1)}, bf16[360,512]{1,0:T(8,128)(2,1)}, u32[]{:S(2)}, u32[]{:S(2)}) collective-permute-start(bf16[360,512]{1,0:T(8,128)(2,1)} %get-tuple-element.88.own_ref), channel_id=1, source_target_pairs={{0,4},{1,5},{2,6},{3,7},{8,12},{9,13},{10,14},{11,15},{16,20},{17,... | collective-permute-start | bytes 1105928 | tf_op jit(solution)/shard_map/ppermute | solution.py:376
  109.9 8.6 %copy-start.19 = (bf16[360,1024]{1,0:T(8,128)(2,1)}, bf16[360,1024]{1,0:T(8,128)(2,1)S(1)}, u32[]{:S(2)}) copy-start(bf16[360,1024]{1,0:T(8,128)(2,1)S(1)} %get-tuple-element.67.hidden_ref) | copy-start | bytes 2211844
  110.0 4.6 %collective-permute-start.29 = (f32[260,128]{1,0:T(8,128)S(1)}, f32[260,128]{1,0:T(8,128)S(1)}, u32[]{:S(2)}, u32[]{:S(2)}) collective-permute-start(f32[260,128]{1,0:T(8,128)S(1)} %fusion.2), channel_id=1, source_target_pairs={{0,8},{8,0},{16,24},{24,16},{1,9},{9,1},{17,25},{25,17},{2,10},{10... | collective-permute-start | bytes 399368 | tf_op jit(solution)/shard_map/ppermute | solution.py:252
  112.3 8.4 %copy-start.15 = (bf16[360,1024]{1,0:T(8,128)(2,1)}, bf16[360,1024]{1,0:T(8,128)(2,1)S(1)}, u32[]{:S(2)}) copy-start(bf16[360,1024]{1,0:T(8,128)(2,1)S(1)} %shard_map.199.query_ref) | copy-start | bytes 2211844
  114.5 10.5 %copy-start.21 = (bf16[360,1024]{1,0:T(8,128)(2,1)}, bf16[360,1024]{1,0:T(8,128)(2,1)S(1)}, u32[]{:S(2)}) copy-start(bf16[360,1024]{1,0:T(8,128)(2,1)S(1)} %shard_map.195.query_ref) | copy-start | bytes 2211844
  114.5 8.3 %copy-start.6 = (bf16[720,1024]{1,0:T(8,128)(2,1)S(1)}, bf16[720,1024]{1,0:T(8,128)(2,1)}, u32[]{:S(2)}) copy-start(bf16[720,1024]{1,0:T(8,128)(2,1)} %lat_ref.15) | copy-start | bytes 4423684
  114.6 8.3 %copy-start.12 = (bf16[1024,512]{1,0:T(8,128)(2,1)S(1)}, bf16[1024,512]{1,0:T(8,128)(2,1)}, u32[]{:S(2)}) copy-start(bf16[1024,512]{1,0:T(8,128)(2,1)} %refs_5_.7) | copy-start | bytes 3145732
  114.6 8.3 %copy-start.34 = (bf16[208,256]{1,0:T(8,128)(2,1)S(1)}, bf16[208,256]{1,0:T(8,128)(2,1)}, u32[]{:S(2)}) copy-start(bf16[208,256]{1,0:T(8,128)(2,1)} %copy-done.33) | copy-start | bytes 319492
  114.6 22.1 %collective-permute-start.20 = (bf16[360,512]{1,0:T(8,128)(2,1)S(1)}, bf16[360,512]{1,0:T(8,128)(2,1)}, u32[]{:S(2)}, u32[]{:S(2)}) collective-permute-start(bf16[360,512]{1,0:T(8,128)(2,1)S(1)} %get-tuple-element.78.own_ref), channel_id=1, source_target_pairs={{0,4},{1,5},{2,6},{3,7},{8,12},{9,13},{10,14},{11,15},{16,20},{17,... | collective-permute-start | bytes 1105928 | tf_op jit(solution)/shard_map/ppermute | solution.py:376
  116.9 13.3 %collective-permute-start.30 = (f32[260,128]{1,0:T(8,128)S(1)}, f32[260,128]{1,0:T(8,128)S(1)}, u32[]{:S(2)}, u32[]{:S(2)}) collective-permute-start(f32[260,128]{1,0:T(8,128)S(1)} %fusion.3), channel_id=1, source_target_pairs={{0,16},{8,24},{16,0},{24,8},{1,17},{9,25},{17,1},{25,9},{2,18},{10... | collective-permute-start | bytes 399368 | tf_op jit(solution)/shard_map/ppermute | solution.py:252
  120.7 4.3 %copy-start.23 = (bf16[360,1024]{1,0:T(8,128)(2,1)}, bf16[360,1024]{1,0:T(8,128)(2,1)S(1)}, u32[]{:S(2)}) copy-start(bf16[360,1024]{1,0:T(8,128)(2,1)S(1)} %shard_map.191.query_ref) | copy-start | bytes 2211844
  120.8 19.7 %collective-permute-start.13 = (bf16[360,512]{1,0:T(8,128)(2,1)}, bf16[360,512]{1,0:T(8,128)(2,1)}, u32[]{:S(2)}, u32[]{:S(2)}) collective-permute-start(bf16[360,512]{1,0:T(8,128)(2,1)} %get-tuple-element.68.own_ref), channel_id=1, source_target_pairs={{0,4},{1,5},{2,6},{3,7},{8,12},{9,13},{10,14},{11,15},{16,20},{17,... | collective-permute-start | bytes 1105928 | tf_op jit(solution)/shard_map/ppermute | solution.py:376
  125.0 5.2 %copy-start.25 = (bf16[360,1024]{1,0:T(8,128)(2,1)}, bf16[360,1024]{1,0:T(8,128)(2,1)S(1)}, u32[]{:S(2)}) copy-start(bf16[360,1024]{1,0:T(8,128)(2,1)S(1)} %get-tuple-element.57.hidden_ref) | copy-start | bytes 2211844
  125.0 19.3 %collective-permute-start.6 = (bf16[360,512]{1,0:T(8,128)(2,1)}, bf16[360,512]{1,0:T(8,128)(2,1)}, u32[]{:S(2)}, u32[]{:S(2)}) collective-permute-start(bf16[360,512]{1,0:T(8,128)(2,1)} %get-tuple-element.58.own_ref), channel_id=1, source_target_pairs={{0,4},{1,5},{2,6},{3,7},{8,12},{9,13},{10,14},{11,15},{16,20},{17,... | collective-permute-start | bytes 1105928 | tf_op jit(solution)/shard_map/ppermute | solution.py:376
  127.1 4.5 %copy-start.7 = (bf16[1024,1024]{1,0:T(8,128)(2,1)S(1)}, bf16[1024,1024]{1,0:T(8,128)(2,1)}, u32[]{:S(2)}) copy-start(bf16[1024,1024]{1,0:T(8,128)(2,1)} %w_ref.7) | copy-start | bytes 6291460
  127.1 4.5 %copy-start.14 = (bf16[360,1024]{1,0:T(8,128)(2,1)S(1)}, bf16[360,1024]{1,0:T(8,128)(2,1)}, u32[]{:S(2)}) copy-start(bf16[360,1024]{1,0:T(8,128)(2,1)} %copy-done.13) | copy-start | bytes 2211844
  140.4 3.9 %copy-start.26 = (bf16[360,1024]{1,0:T(8,128)(2,1)S(1)}, bf16[360,1024]{1,0:T(8,128)(2,1)}, u32[]{:S(2)}) copy-start(bf16[360,1024]{1,0:T(8,128)(2,1)} %copy-done.25) | copy-start | bytes 2211844
  140.5 3.9 %copy-start.28 = (bf16[360,1024]{1,0:T(8,128)(2,1)S(1)}, bf16[360,1024]{1,0:T(8,128)(2,1)}, u32[]{:S(2)}) copy-start(bf16[360,1024]{1,0:T(8,128)(2,1)} %copy-done.27) | copy-start | bytes 2211844
  (39 other events, 65.5 us)

commit v2 on v1

--- a/solution.py
+++ b/solution.py
@@ -37,7 +37,7 @@
     def small(array):
         return (np.round(array * 2.0**16) / 2.0**16).astype(ml_dtypes.bfloat16)
 
-    return small(basis), small(fold), small(unfold)
+    return small(basis), small(basis.T), small(fold), small(unfold)
 
 
 LANES = 256
@@ -59,11 +59,10 @@
     return jnp.sum(jnp.where(place == band % rows.shape[0], rows, 0.0), axis=0, keepdims=True)
 
 
-def compress_kernel(row, me_ref, band_ref, x_ref, lat_ref, gain_ref, basis_ref, *rest):
-    outs, (normed_ref,) = rest[:-1], rest[-1:]
-    count = len(outs)
+def compress_kernel(start, band_ref, x_ref, lat_ref, gain_ref, basis_ref, *rest):
+    *outs, normed_ref = rest
     rows, width = x_ref.shape
-    embed = latitude_row(band_ref[0, row], lat_ref[...])
+    embed = latitude_row(band_ref[0, start + pl.program_id(0)], lat_ref[...])
     gain = gain_ref[...]
     for low, high in row_tiles(rows, 16):
         inputs = x_ref[low:high].astype(F32) + embed
@@ -71,56 +70,109 @@
         inputs = inputs - center
         spread = jnp.sum(inputs * inputs, axis=-1, keepdims=True) * (1.0 / width)
         normed_ref[low:high] = (inputs * lax.rsqrt(spread + 1e-05) * gain).astype(BF16)
-    for shift, out in enumerate(outs):
-        block = lax.rem(me_ref[0] + shift, count)
-        columns = pl.ds(pl.multiple_of(block * out.shape[1], out.shape[1]), out.shape[1])
-        out[...] = dot(basis_ref[...], normed_ref[:, columns]).astype(BF16)
-
-
-def filter_kernel(count, me_ref, *refs):
-    parts, refs = refs[:count], refs[count:]
-    fold_ref, w1_ref, b1_ref, w2_ref, b2_ref, unfold_ref = refs[:6]
-    outs, first_ref, whole_ref, mixed_ref = refs[6 : 6 + count], *refs[6 + count :]
-    rank, width = parts[0].shape
-    modes = first_ref.shape[0] // 2
-    me = me_ref[0]
-    for shift, part in enumerate(parts):
-        owner = lax.rem(me + count - shift, count)
-        whole_ref[pl.ds(pl.multiple_of(owner * rank, 16), rank)] = part[...]
-    spectrum = dot(fold_ref[...], whole_ref[...]).astype(BF16)
-    first = (
-        dot(spectrum[:modes], w1_ref[:width])
-        + dot(spectrum[modes:], w1_ref[width:])
-        + b1_ref[...]
-    )
-    first = jnp.maximum(first, 0.0).astype(BF16)
-    first_ref[:modes] = first[:, :width]
-    first_ref[modes:] = first[:, width:]
-    mixed = (dot(first, w2_ref[...]) + b2_ref[...]).astype(BF16)
-    mixed_ref[:modes] = mixed[:, :width]
-    mixed_ref[modes:] = mixed[:, width:]
-    for shift, out in enumerate(outs):
-        out[...] = dot(unfold_ref[lax.rem(me + shift, count)], mixed_ref[...]).astype(BF16)
-
-
-def gradient_kernel(*refs):
-    *firsts, cot_ref, weight_ref, bias_ref = refs
-    modes, width = cot_ref.shape[2:]
-    blocks, size = weight_ref.shape[1:3]
-    contract = (((0,), (0,)), ((), ()))
-    total, bias = 0.0, 0.0
-    for row, first_ref in enumerate(firsts):
-        real, imag = cot_ref[row, 0], cot_ref[row, 1]
-        both = jnp.concatenate([real, imag], axis=1)
-        turned = jnp.concatenate([imag, -real], axis=1)
-        total += lax.dot_general(first_ref[:modes], both, contract, preferred_element_type=F32)
-        total += lax.dot_general(first_ref[modes:], turned, contract, preferred_element_type=F32)
-        bias += jnp.sum(both.astype(F32), axis=0, keepdims=True)
-    bias_ref[...] = bias
-    for part in range(2):
+    size = width // lax.axis_size("lon")
+    for block, store in outgoing(outs):
+        columns = pl.ds(pl.multiple_of(block * size, size), size)
+        store(dot(basis_ref[...], normed_ref[:, columns]).astype(BF16))
+
+
+def outgoing(outs):
+    count = lax.axis_size("lon")
+    if len(outs) == 1:
+        return [(block, functools.partial(outs[0].__setitem__, block)) for block in range(count)]
+    me = lax.axis_index("lon")
+    return [
+        (lax.rem(me + shift, count), functools.partial(out.__setitem__, ...))
+        for shift, out in enumerate(outs)
+    ]
+
+
+def incoming(parts):
+    count = lax.axis_size("lon")
+    if len(parts) == 1:
+        return [(owner, parts[0][owner]) for owner in range(count)]
+    me = lax.axis_index("lon")
+    return [(lax.rem(me + count - shift, count), part[...]) for shift, part in enumerate(parts)]
+
+
+def blocks_kernel(w1_ref, w2_ref, mix1_ref, mix2_ref):
+    _, blocks, size, _ = w1_ref.shape
+    width = blocks * size
+    for weight, mix in ((w1_ref, mix1_ref), (w2_ref, mix2_ref)):
+        mix[...] = jnp.zeros(mix.shape, mix.dtype)
         for block in range(blocks):
             low = block * size
-            weight_ref[part, block] = total[low : low + size, part * width + low : part * width + low + size]
+            here, there = slice(low, low + size), slice(width + low, width + low + size)
+            real, imag = weight[0, block], weight[1, block]
+            mix[here, here] = real
+            mix[here, there] = imag
+            mix[there, here] = -imag
+            mix[there, there] = real
+
+
+def filter_kernel(taken, *refs):
+    parts, refs = refs[:taken], refs[taken:]
+    fold_ref, w1_ref, b1_ref, w2_ref, b2_ref, unfold_ref = refs[:6]
+    *outs, first_ref, whole_ref, mixed_ref = refs[6:]
+    rank, width = parts[0].shape[-2:]
+    modes = first_ref.shape[0] // 2
+    for owner, part in incoming(parts):
+        whole_ref[pl.ds(pl.multiple_of(owner * rank, 16), rank)] = part
+    spectrum = dot(fold_ref[...], whole_ref[...]).astype(BF16)
+    first = dot(spectrum[:modes], w1_ref[:width]) + dot(spectrum[modes:], w1_ref[width:])
+    first_re = jnp.maximum(first[:, :width] + b1_ref[0:1], 0.0).astype(BF16)
+    first_im = jnp.maximum(first[:, width:] + b1_ref[1:2], 0.0).astype(BF16)
+    first_ref[:modes] = first_re
+    first_ref[modes:] = first_im
+    mixed = dot(first_re, w2_ref[:width]) + dot(first_im, w2_ref[width:])
+    mixed_ref[:modes] = (mixed[:, :width] + b2_ref[0:1]).astype(BF16)
+    mixed_ref[modes:] = (mixed[:, width:] + b2_ref[1:2]).astype(BF16)
+    for block, store in outgoing(outs):
+        store(dot(unfold_ref[block], mixed_ref[...]).astype(BF16))
+
+
+def gradient_kernel(size, *refs):
+    *firsts, cot_ref, packed_ref = refs
+    modes, width = cot_ref.shape[2:]
+    contract = (((0,), (0,)), ((), ()))
+    total, bias, row = 0.0, 0.0, 0
+    for first_ref in firsts:
+        for piece in range(first_ref.shape[0]):
+            real, imag = cot_ref[row, 0], cot_ref[row, 1]
+            both = jnp.concatenate([real, imag], axis=1)
+            turned = jnp.concatenate([imag, -real], axis=1)
+            first_re, first_im = first_ref[piece, :modes], first_ref[piece, modes:]
+            total += lax.dot_general(first_re, both, contract, preferred_element_type=F32)
+            total += lax.dot_general(first_im, turned, contract, preferred_element_type=F32)
+            bias += jnp.sum(both.astype(F32), axis=0, keepdims=True)
+            row += 1
+    pair = 2 * size
+    lane = lax.broadcasted_iota(jnp.int32, (size, pair), 1)
+    out = 0
+    for low in range(0, 2 * width, pair):
+        left = low % width
+        even = total[left : left + size, low : low + pair]
+        odd = total[left + size : left + pair, low : low + pair]
+        packed_ref[out : out + size] = jnp.where(lane < size, even, odd)
+        out += size
+    packed_ref[out:] = jnp.zeros((packed_ref.shape[0] - out, pair), F32)
+    for place, low in enumerate(range(0, 2 * width, pair)):
+        packed_ref[out + place : out + place + 1] = bias[:, low : low + pair]
+
+
+def unpack_kernel(summed_ref, weight_ref, bias_ref):
+    _, blocks, size, _ = weight_ref.shape
+    total = summed_ref[...]
+    out = 0
+    for part in range(2):
+        for block in range(0, blocks, 2):
+            weight_ref[part, block] = total[out : out + size, :size]
+            weight_ref[part, block + 1] = total[out : out + size, size:]
+            out += size
+    for part in range(2):
+        for low in range(0, bias_ref.shape[1], 2 * size):
+            bias_ref[part : part + 1, low : low + 2 * size] = total[out : out + 1]
+            out += 1
 
 
 def head_scale(values, ones):
@@ -134,14 +186,13 @@
     return jnp.where(row == column, value, 0.0).astype(BF16)
 
 
-def expand_kernel(row, count, head_size, me_ref, band_ref, x_ref, lat_ref, *refs):
-    parts, refs = refs[:count], refs[count:]
+def expand_kernel(start, taken, head_size, band_ref, x_ref, lat_ref, *refs):
+    parts, refs = refs[:taken], refs[taken:]
     basis_ref, w_keyval_ref, hidden_ref, keyval_ref, whole_ref = refs
-    width = parts[0].shape[1]
-    me = me_ref[0]
-    for shift, part in enumerate(parts):
-        whole_ref[lax.rem(me + count - shift, count)] = part[...]
-    embed = latitude_row(band_ref[0, row], lat_ref[...])
+    count, _, width = whole_ref.shape
+    for owner, part in incoming(parts):
+        whole_ref[owner] = part
+    embed = latitude_row(band_ref[0, start + pl.program_id(0)], lat_ref[...])
     for block in range(count):
         columns = slice(block * width, block * width + width)
         grid = dot(basis_ref[...], whole_ref[block]).astype(BF16).astype(F32)
@@ -166,16 +217,21 @@
 def repeat_head(pair, upper, head_size):
     lane = lax.broadcasted_iota(jnp.int32, pair.shape, 1)
     rolled = pltpu.roll(pair, head_size, 1)
-    first_half = (lane < head_size) != upper
-    return jnp.where(first_half, pair, rolled)
-
-
-def attend_kernel(head_size, seen_ref, query_ref, own_ref, other_ref, hidden_ref, scale_ref, w_ref, *rest):
+    return jnp.where((lane < head_size) != upper, pair, rolled)
+
+
+def twice(part):
+    return jnp.concatenate([part, part], axis=1)
+
+
+def attend_kernel(head_size, past_ref, scale_ref, query_ref, own_ref, other_ref, hidden_ref, w_ref, *rest):
     out_ref, attended_ref = rest[-2:]
     half = own_ref.shape[1] // 2
     pair_width = 2 * head_size
+    group = LANES // head_size
     ones = head_ones(head_size, 1.0)
-    seen = seen_ref[0] > 0
+    lane_head = lax.broadcasted_iota(jnp.int32, (1, LANES), 1) // head_size
+    seen = jnp.logical_and(lax.axis_index("frame") == 1, past_ref[0] <= 0)
     for head in range(half // head_size):
         pair = slice(head // 2 * pair_width, (head // 2 + 1) * pair_width)
         value_pair = slice(half + pair.start, half + pair.stop)
@@ -186,13 +242,15 @@
         value = repeat_head(own_value, upper, head_size)
         value_step = repeat_head(other_value - own_value, upper, head_size)
         columns = slice(head * LANES, head * LANES + LANES)
-        twice = lambda part: jnp.concatenate([part, part], axis=1)
-        product = query_ref[:, columns].astype(F32) * twice(key_step) * scale_ref[:, columns]
+        scale = jnp.zeros((1, LANES), F32)
+        for place in range(group):
+            scale = jnp.where(lane_head == place, scale_ref[head * group + place], scale)
+        scale = scale * (1.0 / math.sqrt(head_size))
+        product = query_ref[:, columns].astype(F32) * twice(key_step) * scale
         high = product.astype(BF16)
         low = (product - high.astype(F32)).astype(BF16)
         lead = dot(high, ones) + dot(low, ones)
-        prob = 1.0 / (1.0 + jnp.exp(-lead))
-        prob = jnp.where(seen, prob, 0.0)
+        prob = jnp.where(seen, 1.0 / (1.0 + jnp.exp(-lead)), 0.0)
         attended_ref[:, columns] = (twice(value) + prob * twice(value_step)).astype(BF16)
     for low in range(0, out_ref.shape[1], LANES):
         columns = slice(low, low + LANES)
@@ -200,41 +258,75 @@
         out_ref[:, columns] = (hidden_ref[:, columns].astype(F32) + output).astype(BF16)
 
 
-def whole(array):
-    return pl.BlockSpec(array.shape, lambda *_, rank=array.ndim: (0,) * rank)
-
-
-def call(kernel, prefetch, args, specs, outs, scratch, flops, grid=(1,), alias=None, out_specs=None):
-    moved = sum(math.prod(a.shape) * a.dtype.itemsize for a in outs) * 2
+def fixed(array):
+    return pl.BlockSpec(array.shape, lambda *_, rank=len(array.shape): (0,) * rank)
+
+
+def by_row(array, low=0, lead=0):
+    before, after = array.shape[:lead], array.shape[lead + 1 :]
+    return pl.BlockSpec(
+        (*before, None, *after), lambda i, *_: (0,) * len(before) + (low + i,) + (0,) * len(after)
+    )
+
+
+class Order:
+    def __init__(self):
+        self.last = None
+
+    def __call__(self, kernel, prefetch, args, specs, outs, out_specs, scratch, flops, grid=(1,), alias=None):
+        anywhere = pl.BlockSpec(memory_space=pl.ANY)
+        token = jax.ShapeDtypeStruct((8, 128), F32)
+        taken = [] if self.last is None else [self.last]
+        skip, count = len(prefetch) + len(args), len(outs)
+
+        def ordered(*refs):
+            refs = refs[:skip] + refs[skip + len(taken) :]
+            give = len(prefetch) + len(args) + count
+            kernel(*refs[:give], *refs[give + 1 :])
+
+        *results, self.last = call(
+            ordered,
+            prefetch,
+            (*args, *taken),
+            [*specs, *[anywhere] * len(taken)],
+            [*outs, token],
+            [*out_specs, anywhere],
+            scratch,
+            flops,
+            grid,
+            alias,
+        )
+        return results
+
+
+def call(kernel, prefetch, args, specs, outs, out_specs, scratch, flops, grid=(1,), alias=None):
+    moved = 2 * sum(math.prod(out.shape) * out.dtype.itemsize for out in outs)
     return pl.pallas_call(
         kernel,
         grid_spec=pltpu.PrefetchScalarGridSpec(
             num_scalar_prefetch=len(prefetch),
             grid=grid,
             in_specs=specs,
-            out_specs=out_specs or [whole(out) for out in outs],
+            out_specs=out_specs,
             scratch_shapes=scratch,
         ),
         out_shape=outs,
         input_output_aliases=alias or {},
-        compiler_params=pltpu.CompilerParams(vmem_limit_bytes=40 * 1024 * 1024),
-        cost_estimate=pl.CostEstimate(flops=flops, bytes_accessed=moved, transcendentals=0),
+        compiler_params=pltpu.CompilerParams(vmem_limit_bytes=VMEM_BYTES),
+        cost_estimate=pl.CostEstimate(flops=1024, bytes_accessed=1024, transcendentals=0),
     )(*prefetch, *args)
 
 
-def block_diagonal(weight):
-    _, blocks, size, _ = weight.shape
-    width = blocks * size
-    tiled = jnp.tile(weight.reshape(2, width, size), (1, 1, blocks))
-    row = lax.broadcasted_iota(jnp.int32, (width, width), 0) // size
-    column = lax.broadcasted_iota(jnp.int32, (width, width), 1) // size
-    real, imag = jnp.where((row == column)[None], tiled, 0)
-    return jnp.concatenate(
-        [jnp.concatenate([real, imag], axis=1), jnp.concatenate([-imag, real], axis=1)], axis=0
-    )
+VMEM_BYTES = 36 * 1024 * 1024
+
+
+def held(array):
+    return pltpu.with_memory_space_constraint(array, pltpu.HBM)
 
 
 def swap_blocks(parts, count):
+    if len(parts) == 1:
+        return [lax.all_to_all(parts[0], "lon", 0, 0, tiled=True)]
     moved = [
         lax.ppermute(part, "lon", [(i, (i + shift) % count) for i in range(count)])
         for shift, part in enumerate(parts)
@@ -243,15 +335,12 @@
     return [parts[0], *moved]
 
 
-def sum_over(array, axis):
+def exchanges(axis):
     size = lax.axis_size(axis)
-    if size & (size - 1):
-        return lax.psum(array, axis)
     step = 1
     while step < size:
-        array = array + lax.ppermute(array, axis, [(i, i ^ step) for i in range(size)])
+        yield axis, [(i, i ^ step) for i in range(size)]
         step *= 2
-    return array
 
 
 def fused_body(
@@ -278,125 +367,180 @@
     head_size = width // score_scale.shape[0]
     keyval_width = w_keyval.shape[1]
     rank = basis_rank(window, length, modes)
-    basis, fold, unfold = (jnp.asarray(a) for a in window_tables(window, length, modes, rank))
-    me = jnp.reshape(lax.axis_index("lon"), (1,)).astype(jnp.int32)
-    frame = lax.axis_index("frame")
-    seen = ((frame == 1) & (earliest_past_snapshot <= 0)).astype(jnp.int32)
-    scale_lanes = jnp.repeat(score_scale / math.sqrt(head_size), head_size).reshape(1, width)
+    basis, basis_t, fold, unfold = window_tables(window, length, modes, rank)
     gain = norm_gain.reshape(1, width)
-    mix1, mix2 = block_diagonal(w_in1), block_diagonal(w_out2)
-    bias1, bias2 = b_in1.reshape(1, -1), b_out2.reshape(1, -1)
-
-    part_shape = jax.ShapeDtypeStruct((rank, local_width), BF16)
-    lat_block = 16
-
-    def row_specs(row):
+
+    run = Order()
+
+    def struct(*shape, dtype=BF16):
+        return jax.ShapeDtypeStruct(shape, dtype)
+
+    def row_specs(start):
         return [
-            pl.BlockSpec((None, None, None, window, width), lambda *_: (0, 0, row, 0, 0)),
-            pl.BlockSpec((lat_block, width), lambda _, me, band: (band[0, row] // lat_block, 0)),
+            pl.BlockSpec((None, None, None, window, width), lambda i, *_: (0, 0, start + i, 0, 0)),
+            pl.BlockSpec((16, width), lambda i, band: (band[0, start + i] // 16, 0)),
         ]
 
-    def compress(row):
+    def part_outs(rows, at_once):
+        if at_once:
+            return [struct(count, rows, rank, local_width)]
+        return [struct(rows, rank, local_width)] * count
+
+    def compress(start, rows, at_once):
+        outs = part_outs(rows, at_once)
+        return run(
+            functools.partial(compress_kernel, start),
+            (band_rows,),
+            (held(fields), held(lat_table), gain, basis_t),
+            [*row_specs(start), fixed(gain), fixed(basis_t)],
+            outs,
+            [by_row(out, lead=len(out.shape) - 3) for out in outs],
+            [pltpu.VMEM((window, width), BF16)],
+            2 * rows * rank * window * width,
+            grid=(rows,),
+        )
+
+    def mix(parts, low, rows, at_once):
+        args = (fold, mix1, b_in1, mix2, b_out2, unfold)
+        outs = [*part_outs(rows, at_once), struct(rows, 2 * modes, local_width)]
+        return run(
+            functools.partial(filter_kernel, len(parts)),
+            (),
+            (*parts, *args),
+            [*[by_row(part, low, part.ndim - 3) for part in parts], *[fixed(a) for a in args]],
+            outs,
+            [by_row(out, lead=len(out.shape) - 3) for out in outs],
+            [pltpu.VMEM((count * rank, local_width), BF16), pltpu.VMEM((2 * modes, local_width), BF16)],
+            rows * (16 * modes * local_width * local_width + 8 * modes * local_width * rank * count),
+            grid=(rows,),
+        )
+
+    def expand(start, parts, low, rows):
+        args = (basis, w_keyval)
+        outs = [struct(rows, window, width), struct(rows, window, keyval_width)]
+        return run(
+            functools.partial(expand_kernel, start, len(parts), head_size),
+            (band_rows,),
+            (held(fields), held(lat_table), *parts, *args),
+            [*row_specs(start), *[by_row(part, low, part.ndim - 3) for part in parts], *[fixed(a) for a in args]],
+            outs,
+            [by_row(out) for out in outs],
+            [pltpu.VMEM((count, rank, local_width), BF16)],
+            2 * rows * window * width * (rank + keyval_width),
+            grid=(rows,),
+        )
+
+    def gradient(firsts):
+        args = (*firsts, spec_cot.reshape(spec_cot.shape[2:]))
+        packed = struct(blocks * block_size + 8, 2 * block_size, dtype=F32)
         return call(
-            functools.partial(compress_kernel, row),
-            (me, band_rows),
-            (fields, lat_table, gain, basis.T),
-            [*row_specs(row), whole(gain), whole(basis.T)],
-            [part_shape] * count,
-            [pltpu.VMEM((window, width), BF16)],
-            2 * rank * window * width,
-        )
-
-    def mix(parts):
-        args = (*parts, fold, mix1, bias1, mix2, bias2, unfold)
-        return call(
-            functools.partial(filter_kernel, count),
-            (me,),
+            functools.partial(gradient_kernel, block_size),
+            (),
             args,
-            [whole(a) for a in args],
-            [*[part_shape] * count, jax.ShapeDtypeStruct((2 * modes, local_width), BF16)],
-            [pltpu.VMEM((count * rank, local_width), BF16), pltpu.VMEM((2 * modes, local_width), BF16)],
-            16 * modes * local_width * local_width + 8 * modes * local_width * rank * count,
-        )
-
-    def expand(row, parts):
-        args = (*parts, basis, w_keyval)
-        return call(
-            functools.partial(expand_kernel, row, count, head_size),
-            (me, band_rows),
-            (fields, lat_table, *args),
-            [*row_specs(row), *[whole(a) for a in args]],
-            [
-                jax.ShapeDtypeStruct((window, width), BF16),
-                jax.ShapeDtypeStruct((window, keyval_width), BF16),
-            ],
-            [pltpu.VMEM((count, rank, local_width), BF16)],
-            2 * window * width * (rank + keyval_width),
-        )
+            [fixed(a) for a in args],
+            [packed],
+            [fixed(packed)],
+            [],
+            8 * lat_rows * modes * local_width * local_width,
+        )[0]
+
+    def unpack(summed):
+        outs = [struct(*w_out2.shape, dtype=F32), struct(*b_out2.shape, dtype=F32)]
+        specs = [fixed(out) for out in outs]
+        return call(unpack_kernel, (), (summed,), [fixed(summed)], outs, specs, [], 0)
 
     def project(hidden):
-        return call(
+        return run(
             functools.partial(query_kernel, head_size),
             (),
             (hidden, w_query),
-            [whole(hidden), whole(w_query)],
-            [jax.ShapeDtypeStruct(hidden.shape, BF16)],
+            [by_row(hidden), fixed(w_query)],
+            [struct(*hidden.shape)],
+            [by_row(hidden)],
             [],
-            2 * window * width * width,
+            2 * hidden.size * width,
+            grid=(hidden.shape[0],),
         )[0]
 
-    def attention(row, query, own, other, hidden, filled):
-        args = (query, own, other, hidden, scale_lanes, w_output)
-        specs = [whole(a) for a in args]
+    def attention(start, query, own, other, hidden, filled):
+        args = (query, own, other, hidden, w_output)
+        first_frame = pl.BlockSpec((None, None, *own.shape[1:]), lambda i, *_: (0, i, 0, 0))
+        specs = [
+            by_row(query),
+            by_row(own),
+            first_frame if other.ndim > own.ndim else by_row(other),
+            by_row(hidden),
+            fixed(w_output),
+        ]
         alias = None
         if filled is not None:
-            alias = {1 + len(args): 0}
+            alias = {2 + len(args): 0}
             args, specs = (*args, filled), [*specs, pl.BlockSpec(memory_space=pl.ANY)]
-        return call(
+        return run(
             functools.partial(attend_kernel, head_size),
-            (seen,),
+            (earliest_past_snapshot, score_scale),
             args,
             specs,
-            [jax.ShapeDtypeStruct(fields.shape, BF16)],
+            [struct(*fields.shape)],
+            [pl.BlockSpec((None, None, None, window, width), lambda i, *_: (0, 0, start + i, 0, 0))],
             [pltpu.VMEM((window, width), BF16)],
-            4 * window * width * width,
+            4 * hidden.size * width,
+            grid=(hidden.shape[0],),
             alias=alias,
-            out_specs=[pl.BlockSpec((None, None, None, window, width), lambda *_: (0, 0, row, 0, 0))],
         )[0]
 
-    outward = [swap_blocks(compress(row), count) for row in range(lat_rows)]
-    homeward, firsts = [], []
-    for row in range(lat_rows):
-        *parts, first = mix(outward[row])
-        homeward.append(swap_blocks(parts, count))
-        firsts.append(first)
-    cells = []
-    for row in range(lat_rows):
-        hidden, keyval = expand(row, homeward[row])
-        earlier = lax.ppermute(keyval, "frame", [(0, 1)])
-        cells.append((project(hidden), keyval, earlier, hidden))
-
-    cotangent = spec_cot.reshape(spec_cot.shape[2:])
-    args = (*firsts, cotangent)
-    weight, bias = call(
-        gradient_kernel,
-        (),
-        args,
-        [whole(a) for a in args],
-        [
-            jax.ShapeDtypeStruct((2, blocks, block_size, block_size), F32),
-            jax.ShapeDtypeStruct((1, 2 * local_width), F32),
-        ],
-        [],
-        8 * lat_rows * modes * local_width * local_width,
-    )
-    packed = jnp.concatenate([weight.reshape(-1), bias.reshape(-1)]).reshape(-1, 128)
-    packed = sum_over(sum_over(packed, "frame"), "dp").reshape(-1)
-    cut = weight.size
-    filled = None
-    for row in range(lat_rows):
-        filled = attention(row, *cells[row], filled)
-    return (filled, packed[:cut].reshape(weight.shape), packed[cut:].reshape(2, local_width))
+    received, firsts, homeward, cells = {}, [], {}, {}
+    filled = gradients = None
+    for step, start, rows, at_once in PLAN:
+        if step == "compress":
+            parts = swap_blocks(compress(start, rows, at_once), count)
+            received.update({start + low: (parts, low) for low in range(rows)})
+        elif step == "blocks":
+            mixes = [w_in1, w_out2]
+            mix_shape = struct(2 * local_width, 2 * local_width)
+            mix1, mix2 = run(
+                blocks_kernel, (), mixes, [fixed(a) for a in mixes], [mix_shape] * 2, [fixed(mix_shape)] * 2, [], 0
+            )
+        elif step == "mix":
+            *back, first = mix(*received[start], rows, at_once)
+            parts = swap_blocks(back, count)
+            homeward.update({start + low: (parts, low) for low in range(rows)})
+            firsts.append(first)
+        elif step == "expand":
+            hidden, keyval = expand(start, *homeward[start], rows)
+            earlier = lax.all_gather(keyval, "frame") if at_once else lax.ppermute(keyval, "frame", [(0, 1)])
+            cells[start] = (keyval, earlier, hidden)
+        elif step == "query":
+            cells[start] = (project(cells[start][-1]), *cells[start])
+        elif step == "attend":
+            filled = attention(start, *cells[start], filled)
+        elif step == "gradient":
+            summed = gradient(firsts)
+            for axis, pairs in (*exchanges("frame"), *exchanges("dp")):
+                summed = summed + lax.ppermute(summed, axis, pairs)
+        elif step == "sum":
+            gradients = unpack(summed)
+    return (filled, *gradients)
+
+
+PLAN = (
+    ("compress", 0, 2, False),
+    ("compress", 2, 2, False),
+    ("blocks", 0, 0, False),
+    ("mix", 0, 2, False),
+    ("mix", 2, 2, False),
+    ("expand", 0, 2, False),
+    ("query", 0, 2, False),
+    ("gradient", 0, 0, False),
+    ("expand", 2, 1, False),
+    ("query", 2, 1, False),
+    ("expand", 3, 1, False),
+    ("query", 3, 1, False),
+    ("attend", 0, 2, False),
+    ("attend", 2, 1, False),
+    ("attend", 3, 1, False),
+    ("sum", 0, 0, False),
+)
 
 
 def transform_table(length, modes):
@@ -591,9 +735,13 @@
         fields.shape[0] == 1
         and lax.axis_size("frame") == 2
         and local_width % LANES == 0
+        and fields.shape[2] == sum(rows for step, _, rows, _ in PLAN if step == "compress")
         and 2 * head_size == 128
+        and 2 * rest[4].shape[2] == 128
         and rest[-4].shape[1] * 2 == width
     )
+    sizes = [lax.axis_size(axis) for axis in ("frame", "dp")]
+    fits = fits and all(size & (size - 1) == 0 for size in sizes)
     return (fused_body if fits else plain_body)(fields, *rest)
 
 

time: 150 us -> 124 us (0.83)
  waiting for transfers between devices: 4.28 us -> 47.3 us
  local copies, waits for them, and re-layouts: 33.2 us -> 2.31 us
  starting transfers between devices: 48.2 us -> 24 us
  other arithmetic: 6.58 us -> 0.05 us
  Pallas kernels: 53.8 us -> 47.9 us
    ppermute x24 -> x12, waiting for transfers between devices: 4.26 us -> 42.5 us  [swap_blocks(): lax.ppermute(part, 'lon', [(i, (i + shift) % count) for i in range(count)])]
    ppermute x24 -> x12, starting transfers between devices: 35.6 us -> 15.5 us  [swap_blocks(): lax.ppermute(part, 'lon', [(i, (i + shift) % count) for i in range(count)])]
    unnamed x146 -> x32, local copies, waits for them, and re-layouts: 20.4 us -> 2.31 us
    another operation x9 -> x0, local copies, waits for them, and re-layouts: 9.96 us -> none  [the longest x6 7.73 us: block_diagonal(): tiled = jnp.tile(weight.reshape(2, width, size), (1, 1, blocks))]
    pallas_call x21 -> x16, Pallas kernels: 53.8 us -> 47.9 us  [call(): pl.pallas_call(kernel, grid_spec=pltpu.PrefetchScalarGridSpec(num_scalar_...]
    ppermute x7 -> x6, waiting for transfers between devices: 0.02 us -> 4.82 us  [the longest x3 4.81 us: fused_body(): summed = summed + lax.ppermute(summed, axis, pairs)]
    ppermute x7 -> x6, starting transfers between devices: 12.6 us -> 8.45 us  [the longest x3 6.73 us: fused_body(): lax.ppermute(keyval, 'frame', [(0, 1)])]
    concatenate x2 -> x0, other arithmetic: 2.37 us -> none  [block_diagonal(): jnp.concatenate([jnp.concatenate([real, imag], axis=1), jnp.concatenate([...]
  transfers between devices with their start and end apart: 31 -> 18, of which waited for: 1 -> 10; matrix products, arithmetic and copies ran while one was open for 13% -> 0% of each run, Pallas kernels for 32% -> 30%
where the time goes in v2:
time: 124 us; the launch traced here: 123 us
  Pallas kernels  47.9 us (39%)
  waiting for transfers between devices  47.3 us (38%)
  starting transfers between devices  24 us (19%)
  local copies, waits for them, and re-layouts  2.31 us (2%)
  between operations  1.54 us (1%)
    pallas_call x16, Pallas kernels, call(): pl.pallas_call(kernel, grid_spec=pltpu.PrefetchScalarGridSpec(num_scalar_...  47.9 us
    ppermute x12, waiting for transfers between devices, swap_blocks(): lax.ppermute(part, 'lon', [(i, (i + shift) % count) for i in range(count)])  42.5 us
    ppermute x12, starting transfers between devices, swap_blocks(): lax.ppermute(part, 'lon', [(i, (i + shift) % count) for i in range(count)])  15.5 us
    ppermute x3, starting transfers between devices, fused_body(): lax.ppermute(keyval, 'frame', [(0, 1)])  6.73 us
    ppermute x3, waiting for transfers between devices, fused_body(): summed = summed + lax.ppermute(summed, axis, pairs)  4.81 us
  transfers between devices with their start and end apart: 18, of which 10 were waited for; matrix products, arithmetic and copies ran while one was open for 0% of the time, Pallas kernels for 30%

profile of v2, /device:TPU:8, one launch (start us, length us, event | category | flops | bytes accessed | tf_op | source)
XLA Modules:
  0.0 123.1 jit_solution(10816049855938000326)
XLA Ops:
  0.6 0.0 copy-start.7
  0.6 0.9 copy-done.7
  1.6 0.7 copy-done.10
  2.2 0.7 copy-done.11
  2.9 3.6 %shard_map.193 = (bf16[2,208,256]{2,1,0:T(8,128)(2,1)S(1)}, bf16[2,208,256]{2,1,0:T(8,128)(2,1)S(1)}, bf16[2,208,256]{2,1,0:T(8,128)(2,1)S(1)}, bf16[2,208,256]{2,1,0:T(8,128)(2,1)S(1)}, f32[8,128]{1,0:T(8,128)S(1)}) custom-call(s32[1,4]{1,0:T(1,128)S(1)} %copy-done.11, bf16[1,1,4,360,1024]{4,3,2,1,0:T(8,128)(2,1)} %refs_1_.19, bf16[720,1024]{1,0:T(8,128)(2,1)} %refs_2_.9, ...), custom_call_target="tpu_custom_call" | custom-call | flops 1024 | bytes 1024 | tf_op jit(solution)/shard_map/pallas_call | solution.py:304
  6.5 1.6 %collective-permute-start.3 = (bf16[2,208,256]{2,1,0:T(8,128)(2,1)S(1)}, bf16[2,208,256]{2,1,0:T(8,128)(2,1)S(1)}, u32[]{:S(2)}, u32[]{:S(2)}) collective-permute-start(bf16[2,208,256]{2,1,0:T(8,128)(2,1)S(1)} %get-tuple-element.59), channel_id=1, source_target_pairs={{0,1},{1,2},{2,3},{3,0},{4,5},{5,6},{6,7},{7,4},{8,9},{9,10},{10,1... | collective-permute-start | bytes 638984 | tf_op jit(solution)/shard_map/ppermute | solution.py:331
  8.1 1.1 collective-permute-start.4
  9.2 1.9 %collective-permute-start.5 = (bf16[2,208,256]{2,1,0:T(8,128)(2,1)S(1)}, bf16[2,208,256]{2,1,0:T(8,128)(2,1)S(1)}, u32[]{:S(2)}, u32[]{:S(2)}) collective-permute-start(bf16[2,208,256]{2,1,0:T(8,128)(2,1)S(1)} %get-tuple-element.61), channel_id=1, source_target_pairs={{0,3},{1,0},{2,1},{3,2},{4,7},{5,4},{6,5},{7,6},{8,11},{9,8},{10,9... | collective-permute-start | bytes 638984 | tf_op jit(solution)/shard_map/ppermute | solution.py:331
  11.2 0.0 copy-start.13
  11.2 0.0 copy-start.14
  11.2 3.9 %shard_map.194 = (bf16[2,208,256]{2,1,0:T(8,128)(2,1)S(1)}, bf16[2,208,256]{2,1,0:T(8,128)(2,1)S(1)}, bf16[2,208,256]{2,1,0:T(8,128)(2,1)S(1)}, bf16[2,208,256]{2,1,0:T(8,128)(2,1)S(1)}, f32[8,128]{1,0:T(8,128)S(1)}) custom-call(s32[1,4]{1,0:T(1,128)S(1)} %copy-done.11, bf16[1,1,4,360,1024]{4,3,2,1,0:T(8,128)(2,1)} %refs_1_.19, bf16[720,1024]{1,0:T(8,128)(2,1)} %refs_2_.9, ...), custom_call_target="tpu_custom_call" | custom-call | flops 1024 | bytes 1024 | tf_op jit(solution)/shard_map/pallas_call | solution.py:304
  15.1 0.1 collective-permute-start
  15.3 3.6 %collective-permute-start.1 = (bf16[2,208,256]{2,1,0:T(8,128)(2,1)S(1)}, bf16[2,208,256]{2,1,0:T(8,128)(2,1)S(1)}, u32[]{:S(2)}, u32[]{:S(2)}) collective-permute-start(bf16[2,208,256]{2,1,0:T(8,128)(2,1)S(1)} %get-tuple-element.53), channel_id=1, source_target_pairs={{0,2},{1,3},{2,0},{3,1},{4,6},{5,7},{6,4},{7,5},{8,10},{9,11},{10,... | collective-permute-start | bytes 638984 | tf_op jit(solution)/shard_map/ppermute | solution.py:331
  18.9 0.2 shard_map.195
  19.1 3.5 %collective-permute-done.3.refs_1_ = bf16[2,208,256]{2,1,0:T(8,128)(2,1)S(1)} collective-permute-done((bf16[2,208,256]{2,1,0:T(8,128)(2,1)S(1)}, bf16[2,208,256]{2,1,0:T(8,128)(2,1)S(1)}, u32[]{:S(2)}, u32[]{:S(2)}) %collective-permute-start.3) | collective-permute-done | bytes 213024 | tf_op jit(solution)/shard_map/ppermute | solution.py:331
  22.5 0.0 collective-permute-start.2
  22.5 14.1 %collective-permute-done.4.refs_2_ = bf16[2,208,256]{2,1,0:T(8,128)(2,1)S(1)} collective-permute-done((bf16[2,208,256]{2,1,0:T(8,128)(2,1)S(1)}, bf16[2,208,256]{2,1,0:T(8,128)(2,1)S(1)}, u32[]{:S(2)}, u32[]{:S(2)}) %collective-permute-start.4) | collective-permute-done | bytes 213024 | tf_op jit(solution)/shard_map/ppermute | solution.py:331
  36.6 0.7 collective-permute-done.5.refs_3_
  37.4 0.0 copy-done.4
  37.4 4.3 %shard_map.196 = (bf16[2,208,256]{2,1,0:T(8,128)(2,1)S(1)}, bf16[2,208,256]{2,1,0:T(8,128)(2,1)S(1)}, bf16[2,208,256]{2,1,0:T(8,128)(2,1)S(1)}, bf16[2,208,256]{...) custom-call(bf16[2,208,256]{2,1,0:T(8,128)(2,1)S(1)} %get-tuple-element.58.refs_0_, ...), custom_call_target="tpu_custom_call" | custom-call | flops 1024 | bytes 1024 | tf_op jit(solution)/shard_map/pallas_call | solution.py:304
  41.7 2.7 %collective-permute-start.10 = (bf16[2,208,256]{2,1,0:T(8,128)(2,1)S(1)}, bf16[2,208,256]{2,1,0:T(8,128)(2,1)S(1)}, u32[]{:S(2)}, u32[]{:S(2)}) collective-permute-start(bf16[2,208,256]{2,1,0:T(8,128)(2,1)S(1)} %get-tuple-element.70), channel_id=1, source_target_pairs={{0,2},{1,3},{2,0},{3,1},{4,6},{5,7},{6,4},{7,5},{8,10},{9,11},{10,... | collective-permute-start | bytes 638984 | tf_op jit(solution)/shard_map/ppermute | solution.py:331
  44.4 0.0 collective-permute-start.11
  44.5 0.0 collective-permute-done.refs_1_
  44.5 2.0 %collective-permute-start.9 = (bf16[2,208,256]{2,1,0:T(8,128)(2,1)S(1)}, bf16[2,208,256]{2,1,0:T(8,128)(2,1)S(1)}, u32[]{:S(2)}, u32[]{:S(2)}) collective-permute-start(bf16[2,208,256]{2,1,0:T(8,128)(2,1)S(1)} %get-tuple-element.69), channel_id=1, source_target_pairs={{0,1},{1,2},{2,3},{3,0},{4,5},{5,6},{6,7},{7,4},{8,9},{9,10},{10,1... | collective-permute-start | bytes 638984 | tf_op jit(solution)/shard_map/ppermute | solution.py:331
  46.5 8.5 %collective-permute-done.1.refs_2_ = bf16[2,208,256]{2,1,0:T(8,128)(2,1)S(1)} collective-permute-done((bf16[2,208,256]{2,1,0:T(8,128)(2,1)S(1)}, bf16[2,208,256]{2,1,0:T(8,128)(2,1)S(1)}, u32[]{:S(2)}, u32[]{:S(2)}) %collective-permute-start.1) | collective-permute-done | bytes 213024 | tf_op jit(solution)/shard_map/ppermute | solution.py:331
  54.9 0.0 collective-permute-done.2.refs_3_
  55.0 4.3 %shard_map.197 = (bf16[2,208,256]{2,1,0:T(8,128)(2,1)S(1)}, bf16[2,208,256]{2,1,0:T(8,128)(2,1)S(1)}, bf16[2,208,256]{2,1,0:T(8,128)(2,1)S(1)}, bf16[2,208,256]{...) custom-call(bf16[2,208,256]{2,1,0:T(8,128)(2,1)S(1)} %get-tuple-element.51.refs_0_, ...), custom_call_target="tpu_custom_call" | custom-call | flops 1024 | bytes 1024 | tf_op jit(solution)/shard_map/pallas_call | solution.py:304
  59.3 0.2 collective-permute-done.10.refs_5_
  59.5 5.2 %collective-permute-done.11.refs_6_ = bf16[2,208,256]{2,1,0:T(8,128)(2,1)S(1)} collective-permute-done((bf16[2,208,256]{2,1,0:T(8,128)(2,1)S(1)}, bf16[2,208,256]{2,1,0:T(8,128)(2,1)S(1)}, u32[]{:S(2)}, u32[]{:S(2)}) %collective-permute-start.11) | collective-permute-done | bytes 213024 | tf_op jit(solution)/shard_map/ppermute | solution.py:331
  64.7 0.0 collective-permute-done.9.refs_4_
  64.7 0.0 copy-done.12
  64.7 0.0 copy-start.6
  64.7 3.6 %shard_map.198 = (bf16[2,360,1024]{2,1,0:T(8,128)(2,1)S(1)}, bf16[2,360,512]{2,1,0:T(8,128)(2,1)S(1)}, f32[8,128]{1,0:T(8,128)S(1)}) custom-call(s32[1,4]{1,0:T(1,128)S(1)} %copy-done.12, bf16[1,1,4,360,1024]{4,3,2,1,0:T(8,128)(2,1)} %refs_1_.19, bf16[720,1024]{1,0:T(8,128)(2,1)} %refs_2_.9, bf16[2,208,256]{2,1,0:T(8,128)(2,1)S(1)} %get-tuple-element.68.refs_3_, ...), custom_call_target="tpu_custom_call" | custom-call | flops 1024 | bytes 1024 | tf_op jit(solution)/shard_map/pallas_call | solution.py:304
  68.3 0.0 copy-start.1
  68.3 3.6 %collective-permute-start.14 = (bf16[2,360,512]{2,1,0:T(8,128)(2,1)S(1)}, bf16[2,360,512]{2,1,0:T(8,128)(2,1)S(1)}, u32[]{:S(2)}, u32[]{:S(2)}) collective-permute-start(bf16[2,360,512]{2,1,0:T(8,128)(2,1)S(1)} %get-tuple-element.86.refs_3_), channel_id=1, source_target_pairs={{0,4},{1,5},{2,6},{3,7},{8,12},{9,13},{10,14},{11,15},{16,20},{17,... | collective-permute-start | bytes 2211848 | tf_op jit(solution)/shard_map/ppermute | solution.py:511
  71.9 0.8 collective-permute-start.6
  72.7 0.0 collective-permute-start.7
  72.7 1.5 %collective-permute-start.8 = (bf16[2,208,256]{2,1,0:T(8,128)(2,1)S(1)}, bf16[2,208,256]{2,1,0:T(8,128)(2,1)S(1)}, u32[]{:S(2)}, u32[]{:S(2)}) collective-permute-start(bf16[2,208,256]{2,1,0:T(8,128)(2,1)S(1)} %get-tuple-element.67), channel_id=1, source_target_pairs={{0,3},{1,0},{2,1},{3,2},{4,7},{5,4},{6,5},{7,6},{8,11},{9,8},{10,9... | collective-permute-start | bytes 638984 | tf_op jit(solution)/shard_map/ppermute | solution.py:331
  74.2 1.3 %shard_map.207 = f32[264,128]{1,0:T(8,128)S(1)} custom-call(bf16[2,736,256]{2,1,0:T(8,128)(2,1)S(1)} %get-tuple-element.93.refs_0_, bf16[2,736,256]{2,1,0:T(8,128)(2,1)S(1)} %get-tuple-element.94.refs_1_, bf16[4,2,368,256]{3,2,1,0:T(8,128)(2,1)S(1)} %bitcast.2), custom_call_target="tpu_custom_call" | custom-call | flops 1024 | bytes 1024 | tf_op jit(solution)/shard_map/pallas_call | solution.py:304
  75.5 0.1 collective-permute-start.15
  75.6 4.4 %shard_map.199 = (bf16[2,360,1024]{2,1,0:T(8,128)(2,1)S(1)}, f32[8,128]{1,0:T(8,128)S(1)}) custom-call(bf16[2,360,1024]{2,1,0:T(8,128)(2,1)S(1)} %get-tuple-element.73.refs_0_.refs_5_, bf16[1024,1024]{1,0:T(8,128)(2,1)S(1)} %copy-done.1, f32[8,128]{1,0:T(8,128)S(1)} %get-tuple-element.74.refs_2_), custom_call_target="tpu_custom_call" | custom-call | flops 1024 | bytes 1024 | tf_op jit(solution)/shard_map/pallas_call | solution.py:304
  80.1 7.3 %collective-permute-done.6.refs_4_ = bf16[2,208,256]{2,1,0:T(8,128)(2,1)S(1)} collective-permute-done((bf16[2,208,256]{2,1,0:T(8,128)(2,1)S(1)}, bf16[2,208,256]{2,1,0:T(8,128)(2,1)S(1)}, u32[]{:S(2)}, u32[]{:S(2)}) %collective-permute-start.6) | collective-permute-done | bytes 213024 | tf_op jit(solution)/shard_map/ppermute | solution.py:331
  87.4 3.0 %collective-permute-done.7.refs_5_ = bf16[2,208,256]{2,1,0:T(8,128)(2,1)S(1)} collective-permute-done((bf16[2,208,256]{2,1,0:T(8,128)(2,1)S(1)}, bf16[2,208,256]{2,1,0:T(8,128)(2,1)S(1)}, u32[]{:S(2)}, u32[]{:S(2)}) %collective-permute-start.7) | collective-permute-done | bytes 213024 | tf_op jit(solution)/shard_map/ppermute | solution.py:331
  90.4 0.0 collective-permute-done.8.refs_6_
  90.4 2.6 %shard_map.200 = (bf16[1,360,1024]{2,1,0:T(8,128)(2,1)S(1)}, bf16[1,360,512]{2,1,0:T(8,128)(2,1)S(1)}, f32[8,128]{1,0:T(8,128)S(1)}) custom-call(s32[1,4]{1,0:T(1,128)S(1)} %copy-done.12, bf16[1,1,4,360,1024]{4,3,2,1,0:T(8,128)(2,1)} %refs_1_.19, bf16[720,1024]{1,0:T(8,128)(2,1)} %refs_2_.9, bf16[2,208,256]{2,1,0:T(8,128)(2,1)S(1)} %get-tuple-element.64.refs_3_, ...), custom_call_target="tpu_custom_call" | custom-call | flops 1024 | bytes 1024 | tf_op jit(solution)/shard_map/pallas_call | solution.py:304
  92.9 1.7 %collective-permute-start.13 = (bf16[1,360,512]{2,1,0:T(8,128)(2,1)S(1)}, bf16[1,360,512]{2,1,0:T(8,128)(2,1)S(1)}, u32[]{:S(2)}, u32[]{:S(2)}) collective-permute-start(bf16[1,360,512]{2,1,0:T(8,128)(2,1)S(1)} %get-tuple-element.84.refs_3_), channel_id=1, source_target_pairs={{0,4},{1,5},{2,6},{3,7},{8,12},{9,13},{10,14},{11,15},{16,20},{17,... | collective-permute-start | bytes 1105928 | tf_op jit(solution)/shard_map/ppermute | solution.py:511
  94.7 2.2 %shard_map.201 = (bf16[1,360,1024]{2,1,0:T(8,128)(2,1)S(1)}, f32[8,128]{1,0:T(8,128)S(1)}) custom-call(bf16[1,360,1024]{2,1,0:T(8,128)(2,1)S(1)} %get-tuple-element.76.refs_0_.refs_5_, bf16[1024,1024]{1,0:T(8,128)(2,1)S(1)} %copy-done.1, f32[8,128]{1,0:T(8,128)S(1)} %get-tuple-element.77.refs_2_), custom_call_target="tpu_custom_call" | custom-call | flops 1024 | bytes 1024 | tf_op jit(solution)/shard_map/pallas_call | solution.py:304
  96.9 2.6 %shard_map.202 = (bf16[1,360,1024]{2,1,0:T(8,128)(2,1)S(1)}, bf16[1,360,512]{2,1,0:T(8,128)(2,1)S(1)}, f32[8,128]{1,0:T(8,128)S(1)}) custom-call(s32[1,4]{1,0:T(1,128)S(1)} %copy-done.12, bf16[1,1,4,360,1024]{4,3,2,1,0:T(8,128)(2,1)} %refs_1_.19, bf16[720,1024]{1,0:T(8,128)(2,1)} %refs_2_.9, bf16[2,208,256]{2,1,0:T(8,128)(2,1)S(1)} %get-tuple-element.64.refs_3_, ...), custom_call_target="tpu_custom_call" | custom-call | flops 1024 | bytes 1024 | tf_op jit(solution)/shard_map/pallas_call | solution.py:304
  99.5 0.0 copy-start
  99.5 0.0 copy-start.15
  99.5 1.4 %collective-permute-start.12 = (bf16[1,360,512]{2,1,0:T(8,128)(2,1)S(1)}, bf16[1,360,512]{2,1,0:T(8,128)(2,1)S(1)}, u32[]{:S(2)}, u32[]{:S(2)}) collective-permute-start(bf16[1,360,512]{2,1,0:T(8,128)(2,1)S(1)} %get-tuple-element.82.refs_3_), channel_id=1, source_target_pairs={{0,4},{1,5},{2,6},{3,7},{8,12},{9,13},{10,14},{11,15},{16,20},{17,... | collective-permute-start | bytes 1105928 | tf_op jit(solution)/shard_map/ppermute | solution.py:511
  100.9 0.0 collective-permute-done.15
  101.0 0.1 collective-permute-start.16
  101.1 1.3 %collective-permute-done.16 = f32[264,128]{1,0:T(8,128)S(1)} collective-permute-done((f32[264,128]{1,0:T(8,128)S(1)}, f32[264,128]{1,0:T(8,128)S(1)}, u32[]{:S(2)}, u32[]{:S(2)}) %collective-permute-start.16) | collective-permute-done | bytes 135200 | tf_op jit(solution)/shard_map/ppermute | solution.py:520
  102.4 1.6 %collective-permute-start.17 = (f32[264,128]{1,0:T(8,128)S(1)}, f32[264,128]{1,0:T(8,128)S(1)}, u32[]{:S(2)}, u32[]{:S(2)}) collective-permute-start(f32[264,128]{1,0:T(8,128)S(1)} %add.10), channel_id=1, source_target_pairs={{0,16},{8,24},{16,0},{24,8},{1,17},{9,25},{17,1},{25,9},{2,18},{10... | collective-permute-start | bytes 405512 | tf_op jit(solution)/shard_map/ppermute | solution.py:520
  104.6 3.5 %collective-permute-done.17 = f32[264,128]{1,0:T(8,128)S(1)} collective-permute-done((f32[264,128]{1,0:T(8,128)S(1)}, f32[264,128]{1,0:T(8,128)S(1)}, u32[]{:S(2)}, u32[]{:S(2)}) %collective-permute-start.17) | collective-permute-done | bytes 135200 | tf_op jit(solution)/shard_map/ppermute | solution.py:520
  108.1 2.2 %shard_map.203 = (bf16[1,360,1024]{2,1,0:T(8,128)(2,1)S(1)}, f32[8,128]{1,0:T(8,128)S(1)}) custom-call(bf16[1,360,1024]{2,1,0:T(8,128)(2,1)S(1)} %get-tuple-element.79.refs_0_.refs_5_, bf16[1024,1024]{1,0:T(8,128)(2,1)S(1)} %copy-done.1, f32[8,128]{1,0:T(8,128)S(1)} %get-tuple-element.80.refs_2_), custom_call_target="tpu_custom_call" | custom-call | flops 1024 | bytes 1024 | tf_op jit(solution)/shard_map/pallas_call | solution.py:304
  110.3 0.8 shard_map.208
  111.2 0.0 collective-permute-done.14.refs_4_
  111.2 5.3 %shard_map.204 = (bf16[1,1,4,360,1024]{4,3,2,1,0:T(8,128)(2,1)}, f32[8,128]{1,0:T(8,128)S(1)}) custom-call(s32[1]{0:T(128)S(6)} %copy.25.refs_0_, f32[16]{0:T(128)S(1)} %copy-done.15, bf16[2,360,1024]{2,1,0:T(8,128)(2,1)S(1)} %get-tuple-element.85.refs_2_, bf16[2,360,512]{2,1,0:T(8,128)(2,1)S(1)} %get-tuple-element.86.refs_3_, ...), custom_call_target="tpu_custom_call" | custom-call | flops 1024 | bytes 1024 | tf_op jit(solution)/shard_map/pallas_call | solution.py:304
  116.4 0.0 collective-permute-done.13.refs_4_
  116.4 3.3 %shard_map.205 = (bf16[1,1,4,360,1024]{4,3,2,1,0:T(8,128)(2,1)}, f32[8,128]{1,0:T(8,128)S(1)}) custom-call(s32[1]{0:T(128)S(6)} %copy.25.refs_0_, f32[16]{0:T(128)S(1)} %copy-done.15, bf16[1,360,1024]{2,1,0:T(8,128)(2,1)S(1)} %get-tuple-element.83.refs_2_, bf16[1,360,512]{2,1,0:T(8,128)(2,1)S(1)} %get-tuple-element.84.refs_3_, ...), custom_call_target="tpu_custom_call", output_to_operand_aliasing={{0}: (7, {})} | custom-call | flops 1024 | bytes 1024 | tf_op jit(solution)/shard_map/pallas_call | solution.py:304
  119.7 0.0 collective-permute-done.12.refs_4_
  119.8 3.3 %shard_map.206 = (bf16[1,1,4,360,1024]{4,3,2,1,0:T(8,128)(2,1)}, f32[8,128]{1,0:T(8,128)}) custom-call(s32[1]{0:T(128)S(6)} %copy.25.refs_0_, f32[16]{0:T(128)S(1)} %copy-done.15, bf16[1,360,1024]{2,1,0:T(8,128)(2,1)S(1)} %get-tuple-element.81.refs_2_, bf16[1,360,512]{2,1,0:T(8,128)(2,1)S(1)} %get-tuple-element.82.refs_3_, ...), custom_call_target="tpu_custom_call", output_to_operand_aliasing={{0}: (7, {})} | custom-call | flops 1024 | bytes 1024 | tf_op jit(solution)/shard_map/pallas_call | solution.py:304
  (23 shorter events, 0.1 us)
Async XLA Ops:
  0.6 0.9 copy-start.7
  1.5 0.7 copy-start.10
  2.2 0.7 copy-start.11
  6.5 16.0 %collective-permute-start.3 = (bf16[2,208,256]{2,1,0:T(8,128)(2,1)S(1)}, bf16[2,208,256]{2,1,0:T(8,128)(2,1)S(1)}, u32[]{:S(2)}, u32[]{:S(2)}) collective-permute-start(bf16[2,208,256]{2,1,0:T(8,128)(2,1)S(1)} %get-tuple-element.59), channel_id=1, source_target_pairs={{0,1},{1,2},{2,3},{3,0},{4,5},{5,6},{6,7},{7,4},{8,9},{9,10},{10,1... | collective-permute-start | bytes 638984 | tf_op jit(solution)/shard_map/ppermute | solution.py:331
  8.1 28.5 %collective-permute-start.4 = (bf16[2,208,256]{2,1,0:T(8,128)(2,1)S(1)}, bf16[2,208,256]{2,1,0:T(8,128)(2,1)S(1)}, u32[]{:S(2)}, u32[]{:S(2)}) collective-permute-start(bf16[2,208,256]{2,1,0:T(8,128)(2,1)S(1)} %get-tuple-element.60), channel_id=1, source_target_pairs={{0,2},{1,3},{2,0},{3,1},{4,6},{5,7},{6,4},{7,5},{8,10},{9,11},{10,... | collective-permute-start | bytes 638984 | tf_op jit(solution)/shard_map/ppermute | solution.py:331
  9.2 28.2 %collective-permute-start.5 = (bf16[2,208,256]{2,1,0:T(8,128)(2,1)S(1)}, bf16[2,208,256]{2,1,0:T(8,128)(2,1)S(1)}, u32[]{:S(2)}, u32[]{:S(2)}) collective-permute-start(bf16[2,208,256]{2,1,0:T(8,128)(2,1)S(1)} %get-tuple-element.61), channel_id=1, source_target_pairs={{0,3},{1,0},{2,1},{3,2},{4,7},{5,4},{6,5},{7,6},{8,11},{9,8},{10,9... | collective-permute-start | bytes 638984 | tf_op jit(solution)/shard_map/ppermute | solution.py:331
  11.2 7.7 %copy-start.8 = (bf16[2,4,64,64]{3,2,1,0:T(8,128)(2,1)S(1)}, bf16[2,4,64,64]{3,2,1,0:T(8,128)(2,1)}, u32[]{:S(2)}) copy-start(bf16[2,4,64,64]{3,2,1,0:T(8,128)(2,1)} %refs_0_.11) | copy-start | bytes 196612
  11.2 7.7 %copy-start.9 = (bf16[2,4,64,64]{3,2,1,0:T(8,128)(2,1)S(1)}, bf16[2,4,64,64]{3,2,1,0:T(8,128)(2,1)}, u32[]{:S(2)}) copy-start(bf16[2,4,64,64]{3,2,1,0:T(8,128)(2,1)} %refs_1_.14) | copy-start | bytes 196612
  11.2 26.2 %copy-start.3 = (bf16[736,832]{1,0:T(8,128)(2,1)S(1)}, bf16[736,832]{1,0:T(8,128)(2,1)}, u32[]{:S(2)}) copy-start(bf16[736,832]{1,0:T(8,128)(2,1)} %constant.9.clone.refs_4_) | copy-start | bytes 3674116
  11.2 26.2 %copy-start.4 = (bf16[4,208,736]{2,1,0:T(8,128)(2,1)S(1)}, bf16[4,208,736]{2,1,0:T(8,128)(2,1)}, u32[]{:S(2)}) copy-start(bf16[4,208,736]{2,1,0:T(8,128)(2,1)} %constant.10.clone.refs_9_) | copy-start | bytes 3674116
  11.2 26.2 %copy-start.13 = (f32[2,256]{1,0:T(2,128)S(1)}, f32[2,256]{1,0:T(2,128)}, u32[]{:S(2)}) copy-start(f32[2,256]{1,0:T(2,128)} %refs_6_.6) | copy-start | bytes 6148
  11.2 26.2 %copy-start.14 = (f32[2,256]{1,0:T(2,128)S(1)}, f32[2,256]{1,0:T(2,128)}, u32[]{:S(2)}) copy-start(f32[2,256]{1,0:T(2,128)} %refs_8_.6) | copy-start | bytes 6148
  15.1 29.3 %collective-permute-start = (bf16[2,208,256]{2,1,0:T(8,128)(2,1)S(1)}, bf16[2,208,256]{2,1,0:T(8,128)(2,1)S(1)}, u32[]{:S(2)}, u32[]{:S(2)}) collective-permute-start(bf16[2,208,256]{2,1,0:T(8,128)(2,1)S(1)} %get-tuple-element.52), channel_id=1, source_target_pairs={{0,1},{1,2},{2,3},{3,0},{4,5},{5,6},{6,7},{7,4},{8,9},{9,10},{10,1... | collective-permute-start | bytes 638984 | tf_op jit(solution)/shard_map/ppermute | solution.py:331
  15.3 39.7 %collective-permute-start.1 = (bf16[2,208,256]{2,1,0:T(8,128)(2,1)S(1)}, bf16[2,208,256]{2,1,0:T(8,128)(2,1)S(1)}, u32[]{:S(2)}, u32[]{:S(2)}) collective-permute-start(bf16[2,208,256]{2,1,0:T(8,128)(2,1)S(1)} %get-tuple-element.53), channel_id=1, source_target_pairs={{0,2},{1,3},{2,0},{3,1},{4,6},{5,7},{6,4},{7,5},{8,10},{9,11},{10,... | collective-permute-start | bytes 638984 | tf_op jit(solution)/shard_map/ppermute | solution.py:331
  22.5 32.4 %collective-permute-start.2 = (bf16[2,208,256]{2,1,0:T(8,128)(2,1)S(1)}, bf16[2,208,256]{2,1,0:T(8,128)(2,1)S(1)}, u32[]{:S(2)}, u32[]{:S(2)}) collective-permute-start(bf16[2,208,256]{2,1,0:T(8,128)(2,1)S(1)} %get-tuple-element.54), channel_id=1, source_target_pairs={{0,3},{1,0},{2,1},{3,2},{4,7},{5,4},{6,5},{7,6},{8,11},{9,8},{10,9... | collective-permute-start | bytes 638984 | tf_op jit(solution)/shard_map/ppermute | solution.py:331
  41.7 17.8 %collective-permute-start.10 = (bf16[2,208,256]{2,1,0:T(8,128)(2,1)S(1)}, bf16[2,208,256]{2,1,0:T(8,128)(2,1)S(1)}, u32[]{:S(2)}, u32[]{:S(2)}) collective-permute-start(bf16[2,208,256]{2,1,0:T(8,128)(2,1)S(1)} %get-tuple-element.70), channel_id=1, source_target_pairs={{0,2},{1,3},{2,0},{3,1},{4,6},{5,7},{6,4},{7,5},{8,10},{9,11},{10,... | collective-permute-start | bytes 638984 | tf_op jit(solution)/shard_map/ppermute | solution.py:331
  44.4 20.2 %collective-permute-start.11 = (bf16[2,208,256]{2,1,0:T(8,128)(2,1)S(1)}, bf16[2,208,256]{2,1,0:T(8,128)(2,1)S(1)}, u32[]{:S(2)}, u32[]{:S(2)}) collective-permute-start(bf16[2,208,256]{2,1,0:T(8,128)(2,1)S(1)} %get-tuple-element.71), channel_id=1, source_target_pairs={{0,3},{1,0},{2,1},{3,2},{4,7},{5,4},{6,5},{7,6},{8,11},{9,8},{10,9... | collective-permute-start | bytes 638984 | tf_op jit(solution)/shard_map/ppermute | solution.py:331
  44.5 20.2 %collective-permute-start.9 = (bf16[2,208,256]{2,1,0:T(8,128)(2,1)S(1)}, bf16[2,208,256]{2,1,0:T(8,128)(2,1)S(1)}, u32[]{:S(2)}, u32[]{:S(2)}) collective-permute-start(bf16[2,208,256]{2,1,0:T(8,128)(2,1)S(1)} %get-tuple-element.69), channel_id=1, source_target_pairs={{0,1},{1,2},{2,3},{3,0},{4,5},{5,6},{6,7},{7,4},{8,9},{9,10},{10,1... | collective-permute-start | bytes 638984 | tf_op jit(solution)/shard_map/ppermute | solution.py:331
  55.0 9.7 %copy-start.2 = (bf16[1024,512]{1,0:T(8,128)(2,1)S(1)}, bf16[1024,512]{1,0:T(8,128)(2,1)}, u32[]{:S(2)}) copy-start(bf16[1024,512]{1,0:T(8,128)(2,1)} %refs_8_.9) | copy-start | bytes 3145732
  55.0 9.7 %copy-start.5 = (bf16[360,208]{1,0:T(8,128)(2,1)S(1)}, bf16[360,208]{1,0:T(8,128)(2,1)}, u32[]{:S(2)}) copy-start(bf16[360,208]{1,0:T(8,128)(2,1)} %constant.11.clone.refs_7_) | copy-start | bytes 449284
  55.0 9.7 %copy-start.12 = (s32[1,4]{1,0:T(1,128)S(1)}, s32[1,4]{1,0:T(1,128)}, u32[]{:S(2)}) copy-start(s32[1,4]{1,0:T(1,128)} %refs_0_.14) | copy-start | bytes 52
  64.7 9.5 %copy-start.6 = (bf16[1,1,4,2,368,256]{5,4,3,2,1,0:T(8,128)(2,1)S(1)}, bf16[1,1,4,2,368,256]{5,4,3,2,1,0:T(8,128)(2,1)}, u32[]{:S(2)}) copy-start(bf16[1,1,4,2,368,256]{5,4,3,2,1,0:T(8,128)(2,1)} %param.31) | copy-start | bytes 4521988
  68.3 7.3 %copy-start.1 = (bf16[1024,1024]{1,0:T(8,128)(2,1)S(1)}, bf16[1024,1024]{1,0:T(8,128)(2,1)}, u32[]{:S(2)}) copy-start(bf16[1024,1024]{1,0:T(8,128)(2,1)} %refs_1_.20) | copy-start | bytes 6291460
  68.3 42.8 %collective-permute-start.14 = (bf16[2,360,512]{2,1,0:T(8,128)(2,1)S(1)}, bf16[2,360,512]{2,1,0:T(8,128)(2,1)S(1)}, u32[]{:S(2)}, u32[]{:S(2)}) collective-permute-start(bf16[2,360,512]{2,1,0:T(8,128)(2,1)S(1)} %get-tuple-element.86.refs_3_), channel_id=1, source_target_pairs={{0,4},{1,5},{2,6},{3,7},{8,12},{9,13},{10,14},{11,15},{16,20},{17,... | collective-permute-start | bytes 2211848 | tf_op jit(solution)/shard_map/ppermute | solution.py:511
  71.9 15.5 %collective-permute-start.6 = (bf16[2,208,256]{2,1,0:T(8,128)(2,1)S(1)}, bf16[2,208,256]{2,1,0:T(8,128)(2,1)S(1)}, u32[]{:S(2)}, u32[]{:S(2)}) collective-permute-start(bf16[2,208,256]{2,1,0:T(8,128)(2,1)S(1)} %get-tuple-element.65), channel_id=1, source_target_pairs={{0,1},{1,2},{2,3},{3,0},{4,5},{5,6},{6,7},{7,4},{8,9},{9,10},{10,1... | collective-permute-start | bytes 638984 | tf_op jit(solution)/shard_map/ppermute | solution.py:331
  72.7 17.7 %collective-permute-start.7 = (bf16[2,208,256]{2,1,0:T(8,128)(2,1)S(1)}, bf16[2,208,256]{2,1,0:T(8,128)(2,1)S(1)}, u32[]{:S(2)}, u32[]{:S(2)}) collective-permute-start(bf16[2,208,256]{2,1,0:T(8,128)(2,1)S(1)} %get-tuple-element.66), channel_id=1, source_target_pairs={{0,2},{1,3},{2,0},{3,1},{4,6},{5,7},{6,4},{7,5},{8,10},{9,11},{10,... | collective-permute-start | bytes 638984 | tf_op jit(solution)/shard_map/ppermute | solution.py:331
  72.7 17.7 %collective-permute-start.8 = (bf16[2,208,256]{2,1,0:T(8,128)(2,1)S(1)}, bf16[2,208,256]{2,1,0:T(8,128)(2,1)S(1)}, u32[]{:S(2)}, u32[]{:S(2)}) collective-permute-start(bf16[2,208,256]{2,1,0:T(8,128)(2,1)S(1)} %get-tuple-element.67), channel_id=1, source_target_pairs={{0,3},{1,0},{2,1},{3,2},{4,7},{5,4},{6,5},{7,6},{8,11},{9,8},{10,9... | collective-permute-start | bytes 638984 | tf_op jit(solution)/shard_map/ppermute | solution.py:331
  75.5 25.4 %collective-permute-start.15 = (f32[264,128]{1,0:T(8,128)S(1)}, f32[264,128]{1,0:T(8,128)S(1)}, u32[]{:S(2)}, u32[]{:S(2)}) collective-permute-start(f32[264,128]{1,0:T(8,128)S(1)} %shard_map.207), channel_id=1, source_target_pairs={{0,4},{4,0},{1,5},{5,1},{2,6},{6,2},{3,7},{7,3},{8,12},{12,8},{9,1... | collective-permute-start | bytes 405512 | tf_op jit(solution)/shard_map/ppermute | solution.py:520
  92.9 23.5 %collective-permute-start.13 = (bf16[1,360,512]{2,1,0:T(8,128)(2,1)S(1)}, bf16[1,360,512]{2,1,0:T(8,128)(2,1)S(1)}, u32[]{:S(2)}, u32[]{:S(2)}) collective-permute-start(bf16[1,360,512]{2,1,0:T(8,128)(2,1)S(1)} %get-tuple-element.84.refs_3_), channel_id=1, source_target_pairs={{0,4},{1,5},{2,6},{3,7},{8,12},{9,13},{10,14},{11,15},{16,20},{17,... | collective-permute-start | bytes 1105928 | tf_op jit(solution)/shard_map/ppermute | solution.py:511
  99.5 11.7 %copy-start = (bf16[1024,1024]{1,0:T(8,128)(2,1)S(1)}, bf16[1024,1024]{1,0:T(8,128)(2,1)}, u32[]{:S(2)}) copy-start(bf16[1024,1024]{1,0:T(8,128)(2,1)} %refs_6_.9) | copy-start | bytes 6291460
  99.5 11.7 %copy-start.15 = (f32[16]{0:T(128)S(1)}, f32[16]{0:T(128)}, u32[]{:S(2)}) copy-start(f32[16]{0:T(128)} %refs_1_.23) | copy-start | bytes 196
  99.5 20.3 %collective-permute-start.12 = (bf16[1,360,512]{2,1,0:T(8,128)(2,1)S(1)}, bf16[1,360,512]{2,1,0:T(8,128)(2,1)S(1)}, u32[]{:S(2)}, u32[]{:S(2)}) collective-permute-start(bf16[1,360,512]{2,1,0:T(8,128)(2,1)S(1)} %get-tuple-element.82.refs_3_), channel_id=1, source_target_pairs={{0,4},{1,5},{2,6},{3,7},{8,12},{9,13},{10,14},{11,15},{16,20},{17,... | collective-permute-start | bytes 1105928 | tf_op jit(solution)/shard_map/ppermute | solution.py:511
  101.0 1.4 %collective-permute-start.16 = (f32[264,128]{1,0:T(8,128)S(1)}, f32[264,128]{1,0:T(8,128)S(1)}, u32[]{:S(2)}, u32[]{:S(2)}) collective-permute-start(f32[264,128]{1,0:T(8,128)S(1)} %add.9), channel_id=1, source_target_pairs={{0,8},{8,0},{16,24},{24,16},{1,9},{9,1},{17,25},{25,17},{2,10},{10... | collective-permute-start | bytes 405512 | tf_op jit(solution)/shard_map/ppermute | solution.py:520
  102.4 5.7 %collective-permute-start.17 = (f32[264,128]{1,0:T(8,128)S(1)}, f32[264,128]{1,0:T(8,128)S(1)}, u32[]{:S(2)}, u32[]{:S(2)}) collective-permute-start(f32[264,128]{1,0:T(8,128)S(1)} %add.10), channel_id=1, source_target_pairs={{0,16},{8,24},{16,0},{24,8},{1,17},{9,25},{17,1},{25,9},{2,18},{10... | collective-permute-start | bytes 405512 | tf_op jit(solution)/shard_map/ppermute | solution.py:520

commit v3 on v2

--- a/solution.py
+++ b/solution.py
@@ -188,7 +188,7 @@
 
 def expand_kernel(start, taken, head_size, band_ref, x_ref, lat_ref, *refs):
     parts, refs = refs[:taken], refs[taken:]
-    basis_ref, w_keyval_ref, hidden_ref, keyval_ref, whole_ref = refs
+    basis_ref, w_keyval_ref, hidden_ref, *keyval_refs, whole_ref = refs
     count, _, width = whole_ref.shape
     for owner, part in incoming(parts):
         whole_ref[owner] = part
@@ -201,9 +201,12 @@
     keyval = dot(hidden_ref[...], w_keyval_ref[...])
     ones = head_ones(head_size, 1.0 / head_size)
     half = keyval.shape[1] // 2
-    for low in range(0, half, LANES):
-        keyval_ref[:, low : low + LANES] = head_scale(keyval[:, low : low + LANES], ones).astype(BF16)
-    keyval_ref[:, half:] = keyval[:, half:].astype(BF16)
+    keys = [head_scale(keyval[:, low : low + LANES], ones) for low in range(0, half, LANES)]
+    keyval = jnp.concatenate([*keys, keyval[:, half:]], axis=1).astype(BF16)
+    low = 0
+    for out in keyval_refs:
+        out[...] = keyval[:, low : low + out.shape[1]]
+        low += out.shape[1]
 
 
 def query_kernel(head_size, hidden_ref, w_query_ref, query_ref):
@@ -224,34 +227,41 @@
     return jnp.concatenate([part, part], axis=1)
 
 
-def attend_kernel(head_size, past_ref, scale_ref, query_ref, own_ref, other_ref, hidden_ref, w_ref, *rest):
-    out_ref, attended_ref = rest[-2:]
-    half = own_ref.shape[1] // 2
+def attend_kernel(head_size, taken, past_ref, scale_ref, query_ref, *refs):
+    own_refs, other_refs, refs = refs[:taken], refs[taken : 2 * taken], refs[2 * taken :]
+    hidden_ref, w_ref, *_, out_ref, attended_ref = refs
+    half = sum(ref.shape[1] for ref in own_refs) // 2
     pair_width = 2 * head_size
     group = LANES // head_size
     ones = head_ones(head_size, 1.0)
+    ones = jnp.concatenate([ones, ones], axis=0)
     lane_head = lax.broadcasted_iota(jnp.int32, (1, LANES), 1) // head_size
     seen = jnp.logical_and(lax.axis_index("frame") == 1, past_ref[0] <= 0)
-    for head in range(half // head_size):
-        pair = slice(head // 2 * pair_width, (head // 2 + 1) * pair_width)
-        value_pair = slice(half + pair.start, half + pair.stop)
-        upper = head % 2 == 1
-        own_key, other_key = own_ref[:, pair].astype(F32), other_ref[:, pair].astype(F32)
-        own_value, other_value = own_ref[:, value_pair].astype(F32), other_ref[:, value_pair].astype(F32)
-        key_step = repeat_head(other_key - own_key, upper, head_size)
-        value = repeat_head(own_value, upper, head_size)
-        value_step = repeat_head(other_value - own_value, upper, head_size)
-        columns = slice(head * LANES, head * LANES + LANES)
-        scale = jnp.zeros((1, LANES), F32)
-        for place in range(group):
-            scale = jnp.where(lane_head == place, scale_ref[head * group + place], scale)
-        scale = scale * (1.0 / math.sqrt(head_size))
-        product = query_ref[:, columns].astype(F32) * twice(key_step) * scale
-        high = product.astype(BF16)
-        low = (product - high.astype(F32)).astype(BF16)
-        lead = dot(high, ones) + dot(low, ones)
-        prob = jnp.where(seen, 1.0 / (1.0 + jnp.exp(-lead)), 0.0)
-        attended_ref[:, columns] = (twice(value) + prob * twice(value_step)).astype(BF16)
+
+    def load(refs, low):
+        size = refs[0].shape[1]
+        return refs[low // size][:, low % size : low % size + pair_width].astype(F32)
+
+    for pair in range(0, half, pair_width):
+        key_step = load(other_refs, pair) - load(own_refs, pair)
+        own_value = load(own_refs, half + pair)
+        reach = jnp.where(seen, 0.5 * (load(other_refs, half + pair) - own_value), 0.0)
+        middle = own_value + reach
+        for upper in (False, True):
+            head = pair // head_size + upper
+            columns = slice(head * LANES, head * LANES + LANES)
+            scale = jnp.zeros((1, LANES), F32)
+            for place in range(group):
+                scale = jnp.where(lane_head == place, scale_ref[head * group + place], scale)
+            scale = scale * (0.5 / math.sqrt(head_size))
+            step = repeat_head(key_step, upper, head_size)
+            product = query_ref[:, columns].astype(F32) * twice(step)
+            high = product.astype(BF16)
+            low = (product - high.astype(F32)).astype(BF16)
+            lead = dot(jnp.concatenate([high, low], axis=1), ones)
+            share = jnp.tanh(lead * scale)
+            middles, reaches = (twice(repeat_head(part, upper, head_size)) for part in (middle, reach))
+            attended_ref[:, columns] = (middles + reaches * share).astype(BF16)
     for low in range(0, out_ref.shape[1], LANES):
         columns = slice(low, low + LANES)
         output = dot(attended_ref[...], w_ref[:, columns])
@@ -391,7 +401,7 @@
         return run(
             functools.partial(compress_kernel, start),
             (band_rows,),
-            (held(fields), held(lat_table), gain, basis_t),
+            tuple(held(a) for a in (fields, lat_table, gain, basis_t)),
             [*row_specs(start), fixed(gain), fixed(basis_t)],
             outs,
             [by_row(out, lead=len(out.shape) - 3) for out in outs],
@@ -415,9 +425,10 @@
             grid=(rows,),
         )
 
-    def expand(start, parts, low, rows):
+    def expand(start, parts, low, rows, split):
         args = (basis, w_keyval)
-        outs = [struct(rows, window, width), struct(rows, window, keyval_width)]
+        pieces = 2 if split else 1
+        outs = [struct(rows, window, width), *[struct(rows, window, keyval_width // pieces)] * pieces]
         return run(
             functools.partial(expand_kernel, start, len(parts), head_size),
             (band_rows,),
@@ -447,7 +458,7 @@
     def unpack(summed):
         outs = [struct(*w_out2.shape, dtype=F32), struct(*b_out2.shape, dtype=F32)]
         specs = [fixed(out) for out in outs]
-        return call(unpack_kernel, (), (summed,), [fixed(summed)], outs, specs, [], 0)
+        return run(unpack_kernel, (), (summed,), [fixed(summed)], outs, specs, [], 0)
 
     def project(hidden):
         return run(
@@ -463,21 +474,15 @@
         )[0]
 
     def attention(start, query, own, other, hidden, filled):
-        args = (query, own, other, hidden, w_output)
-        first_frame = pl.BlockSpec((None, None, *own.shape[1:]), lambda i, *_: (0, i, 0, 0))
-        specs = [
-            by_row(query),
-            by_row(own),
-            first_frame if other.ndim > own.ndim else by_row(other),
-            by_row(hidden),
-            fixed(w_output),
-        ]
+        by_rows = (query, *own, *other, hidden)
+        args = (*by_rows, w_output)
+        specs = [*[by_row(a) for a in by_rows], fixed(w_output)]
         alias = None
         if filled is not None:
             alias = {2 + len(args): 0}
             args, specs = (*args, filled), [*specs, pl.BlockSpec(memory_space=pl.ANY)]
         return run(
-            functools.partial(attend_kernel, head_size),
+            functools.partial(attend_kernel, head_size, len(own)),
             (earliest_past_snapshot, score_scale),
             args,
             specs,
@@ -507,8 +512,8 @@
             homeward.update({start + low: (parts, low) for low in range(rows)})
             firsts.append(first)
         elif step == "expand":
-            hidden, keyval = expand(start, *homeward[start], rows)
-            earlier = lax.all_gather(keyval, "frame") if at_once else lax.ppermute(keyval, "frame", [(0, 1)])
+            hidden, *keyval = expand(start, *homeward[start], rows, at_once)
+            earlier = [lax.ppermute(part, "frame", [(0, 1)]) for part in keyval]
             cells[start] = (keyval, earlier, hidden)
         elif step == "query":
             cells[start] = (project(cells[start][-1]), *cells[start])
@@ -529,12 +534,12 @@
     ("blocks", 0, 0, False),
     ("mix", 0, 2, False),
     ("mix", 2, 2, False),
-    ("expand", 0, 2, False),
+    ("expand", 0, 2, True),
     ("query", 0, 2, False),
     ("gradient", 0, 0, False),
     ("expand", 2, 1, False),
+    ("expand", 3, 1, False),
     ("query", 2, 1, False),
-    ("expand", 3, 1, False),
     ("query", 3, 1, False),
     ("attend", 0, 2, False),
     ("attend", 2, 1, False),

time: 124 us -> 116 us (0.935)
  waiting for transfers between devices: 47.3 us -> 37.3 us
  starting transfers between devices: 24 us -> 28.4 us
  local copies, waits for them, and re-layouts: 2.31 us -> 0.72 us
    ppermute x12, waiting for transfers between devices: 42.5 us -> 34.6 us  [swap_blocks(): lax.ppermute(part, 'lon', [(i, (i + shift) % count) for i in range(count)])]
    ppermute x3, waiting for transfers between devices: 4.81 us -> 1.35 us  [fused_body(): summed = summed + lax.ppermute(summed, axis, pairs)]
    ppermute x12, starting transfers between devices: 15.5 us -> 18.7 us  [swap_blocks(): lax.ppermute(part, 'lon', [(i, (i + shift) % count) for i in range(count)])]
    unnamed x32 -> x28, local copies, waits for them, and re-layouts: 2.31 us -> 0.72 us
    ppermute x3, starting transfers between devices: 1.72 us -> 3.13 us  [fused_body(): summed = summed + lax.ppermute(summed, axis, pairs)]
    ppermute x3 -> x4, waiting for transfers between devices: 0.01 us -> 1.4 us  [fused_body(): earlier = [lax.ppermute(part, 'frame', [(0, 1)]) for part in keyval]]
    ppermute x3 -> x4, starting transfers between devices: 6.73 us -> 6.6 us  [fused_body(): earlier = [lax.ppermute(part, 'frame', [(0, 1)]) for part in keyval]]
  transfers between devices with their start and end apart: 18 -> 19, of which waited for: 10 -> 7; matrix products, arithmetic and copies ran while one was open for 0% -> 0% of each run, Pallas kernels for 30% -> 34%
where the time goes in v3:
time: 116 us; the launch traced here: 115 us
  Pallas kernels  47.1 us (41%)
  waiting for transfers between devices  37.3 us (32%)
  starting transfers between devices  28.4 us (24%)
  between operations  1.62 us (1%)
    pallas_call x16, Pallas kernels, call(): pl.pallas_call(kernel, grid_spec=pltpu.PrefetchScalarGridSpec(num_scalar_...  47.1 us
    ppermute x12, waiting for transfers between devices, swap_blocks(): lax.ppermute(part, 'lon', [(i, (i + shift) % count) for i in range(count)])  34.6 us
    ppermute x12, starting transfers between devices, swap_blocks(): lax.ppermute(part, 'lon', [(i, (i + shift) % count) for i in range(count)])  18.7 us
    ppermute x4, starting transfers between devices, fused_body(): earlier = [lax.ppermute(part, 'frame', [(0, 1)]) for part in keyval]  6.6 us
    ppermute x3, starting transfers between devices, fused_body(): summed = summed + lax.ppermute(summed, axis, pairs)  3.13 us
  transfers between devices with their start and end apart: 19, of which 7 were waited for; matrix products, arithmetic and copies ran while one was open for 0% of the time, Pallas kernels for 34%

profile of v3, /device:TPU:8, one launch (start us, length us, event | category | flops | bytes accessed | tf_op | source)
XLA Modules:
  0.0 115.2 jit_solution(944845327727409702)
XLA Ops:
  0.6 0.0 copy-start.9
  0.6 0.6 copy-done.9
  1.3 3.6 %shard_map.193 = (bf16[2,208,256]{2,1,0:T(8,128)(2,1)S(1)}, bf16[2,208,256]{2,1,0:T(8,128)(2,1)S(1)}, bf16[2,208,256]{2,1,0:T(8,128)(2,1)S(1)}, bf16[2,208,256]{2,1,0:T(8,128)(2,1)S(1)}, f32[8,128]{1,0:T(8,128)S(1)}) custom-call(s32[1,4]{1,0:T(1,128)S(1)} %copy-done.9, bf16[1,1,4,360,1024]{4,3,2,1,0:T(8,128)(2,1)} %refs_1_.18, bf16[720,1024]{1,0:T(8,128)(2,1)} %refs_2_.9, ...), custom_call_target="tpu_custom_call" | custom-call | flops 1024 | bytes 1024 | tf_op jit(solution)/shard_map/pallas_call | solution.py:314
  4.9 1.6 %collective-permute-start.3 = (bf16[2,208,256]{2,1,0:T(8,128)(2,1)S(1)}, bf16[2,208,256]{2,1,0:T(8,128)(2,1)S(1)}, u32[]{:S(2)}, u32[]{:S(2)}) collective-permute-start(bf16[2,208,256]{2,1,0:T(8,128)(2,1)S(1)} %get-tuple-element.61), channel_id=1, source_target_pairs={{0,1},{1,2},{2,3},{3,0},{4,5},{5,6},{6,7},{7,4},{8,9},{9,10},{10,1... | collective-permute-start | bytes 638984 | tf_op jit(solution)/shard_map/ppermute | solution.py:341
  6.6 1.1 collective-permute-start.4
  7.6 1.9 %collective-permute-start.5 = (bf16[2,208,256]{2,1,0:T(8,128)(2,1)S(1)}, bf16[2,208,256]{2,1,0:T(8,128)(2,1)S(1)}, u32[]{:S(2)}, u32[]{:S(2)}) collective-permute-start(bf16[2,208,256]{2,1,0:T(8,128)(2,1)S(1)} %get-tuple-element.63), channel_id=1, source_target_pairs={{0,3},{1,0},{2,1},{3,2},{4,7},{5,4},{6,5},{7,6},{8,11},{9,8},{10,9... | collective-permute-start | bytes 638984 | tf_op jit(solution)/shard_map/ppermute | solution.py:341
  9.6 0.0 copy-start.11
  9.6 0.0 copy-start.12
  9.6 4.0 %shard_map.194 = (bf16[2,208,256]{2,1,0:T(8,128)(2,1)S(1)}, bf16[2,208,256]{2,1,0:T(8,128)(2,1)S(1)}, bf16[2,208,256]{2,1,0:T(8,128)(2,1)S(1)}, bf16[2,208,256]{2,1,0:T(8,128)(2,1)S(1)}, f32[8,128]{1,0:T(8,128)S(1)}) custom-call(s32[1,4]{1,0:T(1,128)S(1)} %copy-done.9, bf16[1,1,4,360,1024]{4,3,2,1,0:T(8,128)(2,1)} %refs_1_.18, bf16[720,1024]{1,0:T(8,128)(2,1)} %refs_2_.9, ...), custom_call_target="tpu_custom_call" | custom-call | flops 1024 | bytes 1024 | tf_op jit(solution)/shard_map/pallas_call | solution.py:314
  13.6 0.1 collective-permute-start
  13.7 3.6 %collective-permute-start.1 = (bf16[2,208,256]{2,1,0:T(8,128)(2,1)S(1)}, bf16[2,208,256]{2,1,0:T(8,128)(2,1)S(1)}, u32[]{:S(2)}, u32[]{:S(2)}) collective-permute-start(bf16[2,208,256]{2,1,0:T(8,128)(2,1)S(1)} %get-tuple-element.55), channel_id=1, source_target_pairs={{0,2},{1,3},{2,0},{3,1},{4,6},{5,7},{6,4},{7,5},{8,10},{9,11},{10,... | collective-permute-start | bytes 638984 | tf_op jit(solution)/shard_map/ppermute | solution.py:341
  17.4 0.2 shard_map.195
  17.5 3.4 %collective-permute-done.3.refs_1_ = bf16[2,208,256]{2,1,0:T(8,128)(2,1)S(1)} collective-permute-done((bf16[2,208,256]{2,1,0:T(8,128)(2,1)S(1)}, bf16[2,208,256]{2,1,0:T(8,128)(2,1)S(1)}, u32[]{:S(2)}, u32[]{:S(2)}) %collective-permute-start.3) | collective-permute-done | bytes 213024 | tf_op jit(solution)/shard_map/ppermute | solution.py:341
  21.0 0.0 collective-permute-start.2
  21.0 14.1 %collective-permute-done.4.refs_2_ = bf16[2,208,256]{2,1,0:T(8,128)(2,1)S(1)} collective-permute-done((bf16[2,208,256]{2,1,0:T(8,128)(2,1)S(1)}, bf16[2,208,256]{2,1,0:T(8,128)(2,1)S(1)}, u32[]{:S(2)}, u32[]{:S(2)}) %collective-permute-start.4) | collective-permute-done | bytes 213024 | tf_op jit(solution)/shard_map/ppermute | solution.py:341
  35.1 0.7 collective-permute-done.5.refs_3_
  35.8 4.3 %shard_map.196 = (bf16[2,208,256]{2,1,0:T(8,128)(2,1)S(1)}, bf16[2,208,256]{2,1,0:T(8,128)(2,1)S(1)}, bf16[2,208,256]{2,1,0:T(8,128)(2,1)S(1)}, bf16[2,208,256]{...) custom-call(bf16[2,208,256]{2,1,0:T(8,128)(2,1)S(1)} %get-tuple-element.60.refs_0_, ...), custom_call_target="tpu_custom_call" | custom-call | flops 1024 | bytes 1024 | tf_op jit(solution)/shard_map/pallas_call | solution.py:314
  40.2 2.7 %collective-permute-start.10 = (bf16[2,208,256]{2,1,0:T(8,128)(2,1)S(1)}, bf16[2,208,256]{2,1,0:T(8,128)(2,1)S(1)}, u32[]{:S(2)}, u32[]{:S(2)}) collective-permute-start(bf16[2,208,256]{2,1,0:T(8,128)(2,1)S(1)} %get-tuple-element.72), channel_id=1, source_target_pairs={{0,2},{1,3},{2,0},{3,1},{4,6},{5,7},{6,4},{7,5},{8,10},{9,11},{10,... | collective-permute-start | bytes 638984 | tf_op jit(solution)/shard_map/ppermute | solution.py:341
  42.9 0.0 collective-permute-start.11
  42.9 0.0 collective-permute-done.refs_1_
  42.9 2.0 %collective-permute-start.9 = (bf16[2,208,256]{2,1,0:T(8,128)(2,1)S(1)}, bf16[2,208,256]{2,1,0:T(8,128)(2,1)S(1)}, u32[]{:S(2)}, u32[]{:S(2)}) collective-permute-start(bf16[2,208,256]{2,1,0:T(8,128)(2,1)S(1)} %get-tuple-element.71), channel_id=1, source_target_pairs={{0,1},{1,2},{2,3},{3,0},{4,5},{5,6},{6,7},{7,4},{8,9},{9,10},{10,1... | collective-permute-start | bytes 638984 | tf_op jit(solution)/shard_map/ppermute | solution.py:341
  44.9 8.5 %collective-permute-done.1.refs_2_ = bf16[2,208,256]{2,1,0:T(8,128)(2,1)S(1)} collective-permute-done((bf16[2,208,256]{2,1,0:T(8,128)(2,1)S(1)}, bf16[2,208,256]{2,1,0:T(8,128)(2,1)S(1)}, u32[]{:S(2)}, u32[]{:S(2)}) %collective-permute-start.1) | collective-permute-done | bytes 213024 | tf_op jit(solution)/shard_map/ppermute | solution.py:341
  53.4 0.0 collective-permute-done.2.refs_3_
  53.4 4.3 %shard_map.197 = (bf16[2,208,256]{2,1,0:T(8,128)(2,1)S(1)}, bf16[2,208,256]{2,1,0:T(8,128)(2,1)S(1)}, bf16[2,208,256]{2,1,0:T(8,128)(2,1)S(1)}, bf16[2,208,256]{...) custom-call(bf16[2,208,256]{2,1,0:T(8,128)(2,1)S(1)} %get-tuple-element.53.refs_0_, ...), custom_call_target="tpu_custom_call" | custom-call | flops 1024 | bytes 1024 | tf_op jit(solution)/shard_map/pallas_call | solution.py:314
  57.7 0.0 copy-start.2
  57.7 0.0 copy-start.5
  57.7 0.0 copy-start.10
  57.7 0.1 collective-permute-start.6
  57.8 3.5 %collective-permute-start.7 = (bf16[2,208,256]{2,1,0:T(8,128)(2,1)S(1)}, bf16[2,208,256]{2,1,0:T(8,128)(2,1)S(1)}, u32[]{:S(2)}, u32[]{:S(2)}) collective-permute-start(bf16[2,208,256]{2,1,0:T(8,128)(2,1)S(1)} %get-tuple-element.68), channel_id=1, source_target_pairs={{0,2},{1,3},{2,0},{3,1},{4,6},{5,7},{6,4},{7,5},{8,10},{9,11},{10,... | collective-permute-start | bytes 638984 | tf_op jit(solution)/shard_map/ppermute | solution.py:341
  61.3 0.0 collective-permute-done.10.refs_5_
  61.3 1.9 %collective-permute-start.8 = (bf16[2,208,256]{2,1,0:T(8,128)(2,1)S(1)}, bf16[2,208,256]{2,1,0:T(8,128)(2,1)S(1)}, u32[]{:S(2)}, u32[]{:S(2)}) collective-permute-start(bf16[2,208,256]{2,1,0:T(8,128)(2,1)S(1)} %get-tuple-element.69), channel_id=1, source_target_pairs={{0,3},{1,0},{2,1},{3,2},{4,7},{5,4},{6,5},{7,6},{8,11},{9,8},{10,9... | collective-permute-start | bytes 638984 | tf_op jit(solution)/shard_map/ppermute | solution.py:341
  63.2 1.3 %shard_map.207 = f32[264,128]{1,0:T(8,128)S(1)} custom-call(bf16[2,736,256]{2,1,0:T(8,128)(2,1)S(1)} %get-tuple-element.96.refs_0_, bf16[2,736,256]{2,1,0:T(8,128)(2,1)S(1)} %get-tuple-element.97.refs_1_, bf16[4,2,368,256]{3,2,1,0:T(8,128)(2,1)S(1)} %bitcast.2), custom_call_target="tpu_custom_call" | custom-call | flops 1024 | bytes 1024 | tf_op jit(solution)/shard_map/pallas_call | solution.py:314
  64.5 7.8 %collective-permute-done.11.refs_6_ = bf16[2,208,256]{2,1,0:T(8,128)(2,1)S(1)} collective-permute-done((bf16[2,208,256]{2,1,0:T(8,128)(2,1)S(1)}, bf16[2,208,256]{2,1,0:T(8,128)(2,1)S(1)}, u32[]{:S(2)}, u32[]{:S(2)}) %collective-permute-start.11) | collective-permute-done | bytes 213024 | tf_op jit(solution)/shard_map/ppermute | solution.py:341
  72.3 1.5 %collective-permute-start.16 = (f32[264,128]{1,0:T(8,128)S(1)}, f32[264,128]{1,0:T(8,128)S(1)}, u32[]{:S(2)}, u32[]{:S(2)}) collective-permute-start(f32[264,128]{1,0:T(8,128)S(1)} %shard_map.207), channel_id=1, source_target_pairs={{0,4},{4,0},{1,5},{5,1},{2,6},{6,2},{3,7},{7,3},{8,12},{12,8},{9,1... | collective-permute-start | bytes 405512 | tf_op jit(solution)/shard_map/ppermute | solution.py:525
  73.8 0.0 collective-permute-done.9.refs_4_
  73.8 0.0 copy-start.1
  73.9 3.7 %shard_map.198 = (bf16[2,360,1024]{2,1,0:T(8,128)(2,1)S(1)}, bf16[2,360,256]{2,1,0:T(8,128)(2,1)S(1)}, bf16[2,360,256]{2,1,0:T(8,128)(2,1)S(1)}, f32[8,128]{1,0:T(8,128)S(1)}) custom-call(s32[1,4]{1,0:T(1,128)S(1)} %copy-done.10, bf16[1,1,4,360,1024]{4,3,2,1,0:T(8,128)(2,1)} %refs_1_.18, bf16[720,1024]{1,0:T(8,128)(2,1)} %refs_2_.9, ...), custom_call_target="tpu_custom_call" | custom-call | flops 1024 | bytes 1024 | tf_op jit(solution)/shard_map/pallas_call | solution.py:314
  77.5 2.5 %collective-permute-start.14 = (bf16[2,360,256]{2,1,0:T(8,128)(2,1)S(1)}, bf16[2,360,256]{2,1,0:T(8,128)(2,1)S(1)}, u32[]{:S(2)}, u32[]{:S(2)}) collective-permute-start(bf16[2,360,256]{2,1,0:T(8,128)(2,1)S(1)} %get-tuple-element.88.refs_3_), channel_id=1, source_target_pairs={{0,4},{1,5},{2,6},{3,7},{8,12},{9,13},{10,14},{11,15},{16,20},{17,... | collective-permute-start | bytes 1105928 | tf_op jit(solution)/shard_map/ppermute | solution.py:516
  80.0 4.5 %shard_map.199 = (bf16[2,360,1024]{2,1,0:T(8,128)(2,1)S(1)}, f32[8,128]{1,0:T(8,128)S(1)}) custom-call(bf16[2,360,1024]{2,1,0:T(8,128)(2,1)S(1)} %get-tuple-element.75.refs_0_.refs_7_, bf16[1024,1024]{1,0:T(8,128)(2,1)S(1)} %copy-done.1, f32[8,128]{1,0:T(8,128)S(1)} %get-tuple-element.76.refs_2_), custom_call_target="tpu_custom_call" | custom-call | flops 1024 | bytes 1024 | tf_op jit(solution)/shard_map/pallas_call | solution.py:314
  84.5 0.0 collective-permute-done.6.refs_4_
  84.5 1.3 %collective-permute-start.15 = (bf16[2,360,256]{2,1,0:T(8,128)(2,1)S(1)}, bf16[2,360,256]{2,1,0:T(8,128)(2,1)S(1)}, u32[]{:S(2)}, u32[]{:S(2)}) collective-permute-start(bf16[2,360,256]{2,1,0:T(8,128)(2,1)S(1)} %get-tuple-element.89.refs_4_), channel_id=1, source_target_pairs={{0,4},{1,5},{2,6},{3,7},{8,12},{9,13},{10,14},{11,15},{16,20},{17,... | collective-permute-start | bytes 1105928 | tf_op jit(solution)/shard_map/ppermute | solution.py:516
  85.8 0.0 collective-permute-done.7.refs_5_
  85.8 0.0 collective-permute-done.8.refs_6_
  85.8 2.6 %shard_map.200 = (bf16[1,360,1024]{2,1,0:T(8,128)(2,1)S(1)}, bf16[1,360,512]{2,1,0:T(8,128)(2,1)S(1)}, f32[8,128]{1,0:T(8,128)S(1)}) custom-call(s32[1,4]{1,0:T(1,128)S(1)} %copy-done.10, bf16[1,1,4,360,1024]{4,3,2,1,0:T(8,128)(2,1)} %refs_1_.18, bf16[720,1024]{1,0:T(8,128)(2,1)} %refs_2_.9, bf16[2,208,256]{2,1,0:T(8,128)(2,1)S(1)} %get-tuple-element.66.refs_3_, ...), custom_call_target="tpu_custom_call" | custom-call | flops 1024 | bytes 1024 | tf_op jit(solution)/shard_map/pallas_call | solution.py:314
  88.4 1.3 %collective-permute-start.13 = (bf16[1,360,512]{2,1,0:T(8,128)(2,1)S(1)}, bf16[1,360,512]{2,1,0:T(8,128)(2,1)S(1)}, u32[]{:S(2)}, u32[]{:S(2)}) collective-permute-start(bf16[1,360,512]{2,1,0:T(8,128)(2,1)S(1)} %get-tuple-element.86.refs_3_), channel_id=1, source_target_pairs={{0,4},{1,5},{2,6},{3,7},{8,12},{9,13},{10,14},{11,15},{16,20},{17,... | collective-permute-start | bytes 1105928 | tf_op jit(solution)/shard_map/ppermute | solution.py:516
  89.7 2.6 %shard_map.201 = (bf16[1,360,1024]{2,1,0:T(8,128)(2,1)S(1)}, bf16[1,360,512]{2,1,0:T(8,128)(2,1)S(1)}, f32[8,128]{1,0:T(8,128)S(1)}) custom-call(s32[1,4]{1,0:T(1,128)S(1)} %copy-done.10, bf16[1,1,4,360,1024]{4,3,2,1,0:T(8,128)(2,1)} %refs_1_.18, bf16[720,1024]{1,0:T(8,128)(2,1)} %refs_2_.9, bf16[2,208,256]{2,1,0:T(8,128)(2,1)S(1)} %get-tuple-element.66.refs_3_, ...), custom_call_target="tpu_custom_call" | custom-call | flops 1024 | bytes 1024 | tf_op jit(solution)/shard_map/pallas_call | solution.py:314
  92.3 1.5 %collective-permute-start.12 = (bf16[1,360,512]{2,1,0:T(8,128)(2,1)S(1)}, bf16[1,360,512]{2,1,0:T(8,128)(2,1)S(1)}, u32[]{:S(2)}, u32[]{:S(2)}) collective-permute-start(bf16[1,360,512]{2,1,0:T(8,128)(2,1)S(1)} %get-tuple-element.84.refs_3_), channel_id=1, source_target_pairs={{0,4},{1,5},{2,6},{3,7},{8,12},{9,13},{10,14},{11,15},{16,20},{17,... | collective-permute-start | bytes 1105928 | tf_op jit(solution)/shard_map/ppermute | solution.py:516
  93.8 0.0 collective-permute-done.16
  93.8 0.1 collective-permute-start.17
  93.9 1.3 %collective-permute-done.17 = f32[264,128]{1,0:T(8,128)S(1)} collective-permute-done((f32[264,128]{1,0:T(8,128)S(1)}, f32[264,128]{1,0:T(8,128)S(1)}, u32[]{:S(2)}, u32[]{:S(2)}) %collective-permute-start.17) | collective-permute-done | bytes 135200 | tf_op jit(solution)/shard_map/ppermute | solution.py:525
  95.3 1.6 %collective-permute-start.18 = (f32[264,128]{1,0:T(8,128)S(1)}, f32[264,128]{1,0:T(8,128)S(1)}, u32[]{:S(2)}, u32[]{:S(2)}) collective-permute-start(f32[264,128]{1,0:T(8,128)S(1)} %add.10), channel_id=1, source_target_pairs={{0,16},{8,24},{16,0},{24,8},{1,17},{9,25},{17,1},{25,9},{2,18},{10... | collective-permute-start | bytes 405512 | tf_op jit(solution)/shard_map/ppermute | solution.py:525
  97.5 2.2 %shard_map.202 = (bf16[1,360,1024]{2,1,0:T(8,128)(2,1)S(1)}, f32[8,128]{1,0:T(8,128)S(1)}) custom-call(bf16[1,360,1024]{2,1,0:T(8,128)(2,1)S(1)} %get-tuple-element.80.refs_0_.refs_5_, bf16[1024,1024]{1,0:T(8,128)(2,1)S(1)} %copy-done.1, f32[8,128]{1,0:T(8,128)S(1)} %get-tuple-element.81.refs_2_), custom_call_target="tpu_custom_call" | custom-call | flops 1024 | bytes 1024 | tf_op jit(solution)/shard_map/pallas_call | solution.py:314
  99.7 0.0 copy-start
  99.7 0.0 copy-start.13
  99.8 2.2 %shard_map.203 = (bf16[1,360,1024]{2,1,0:T(8,128)(2,1)S(1)}, f32[8,128]{1,0:T(8,128)S(1)}) custom-call(bf16[1,360,1024]{2,1,0:T(8,128)(2,1)S(1)} %get-tuple-element.79.refs_0_.refs_5_, bf16[1024,1024]{1,0:T(8,128)(2,1)S(1)} %copy-done.1, f32[8,128]{1,0:T(8,128)S(1)} %get-tuple-element.82.refs_2_), custom_call_target="tpu_custom_call" | custom-call | flops 1024 | bytes 1024 | tf_op jit(solution)/shard_map/pallas_call | solution.py:314
  102.0 0.0 collective-permute-done.18
  102.0 0.0 collective-permute-done.14.refs_5_
  102.0 0.0 collective-permute-done.15.refs_6_
  102.0 4.8 %shard_map.204 = (bf16[1,1,4,360,1024]{4,3,2,1,0:T(8,128)(2,1)}, f32[8,128]{1,0:T(8,128)S(1)}) custom-call(s32[1]{0:T(128)S(6)} %copy.25.refs_0_, f32[16]{0:T(128)S(1)} %copy-done.13, bf16[2,360,1024]{2,1,0:T(8,128)(2,1)S(1)} %get-tuple-element.87.refs_2_, bf16[2,360,256]{2,1,0:T(8,128)(2,1)S(1)} %get-tuple-element.88.refs_3_, ...), custom_call_target="tpu_custom_call" | custom-call | flops 1024 | bytes 1024 | tf_op jit(solution)/shard_map/pallas_call | solution.py:314
  106.9 0.0 collective-permute-done.13.refs_4_
  106.9 3.1 %shard_map.205 = (bf16[1,1,4,360,1024]{4,3,2,1,0:T(8,128)(2,1)}, f32[8,128]{1,0:T(8,128)S(1)}) custom-call(s32[1]{0:T(128)S(6)} %copy.25.refs_0_, f32[16]{0:T(128)S(1)} %copy-done.13, bf16[1,360,1024]{2,1,0:T(8,128)(2,1)S(1)} %get-tuple-element.85.refs_2_, bf16[1,360,512]{2,1,0:T(8,128)(2,1)S(1)} %get-tuple-element.86.refs_3_, ...), custom_call_target="tpu_custom_call", output_to_operand_aliasing={{0}: (7, {})} | custom-call | flops 1024 | bytes 1024 | tf_op jit(solution)/shard_map/pallas_call | solution.py:314
  109.9 1.4 %collective-permute-done.12.refs_4_ = bf16[1,360,512]{2,1,0:T(8,128)(2,1)S(1)} collective-permute-done((bf16[1,360,512]{2,1,0:T(8,128)(2,1)S(1)}, bf16[1,360,512]{2,1,0:T(8,128)(2,1)S(1)}, u32[]{:S(2)}, u32[]{:S(2)}) %collective-permute-start.12) | collective-permute-done | bytes 368672 | tf_op jit(solution)/shard_map/ppermute | solution.py:516
  111.3 3.1 %shard_map.206 = (bf16[1,1,4,360,1024]{4,3,2,1,0:T(8,128)(2,1)}, f32[8,128]{1,0:T(8,128)S(1)}) custom-call(s32[1]{0:T(128)S(6)} %copy.25.refs_0_, f32[16]{0:T(128)S(1)} %copy-done.13, bf16[1,360,1024]{2,1,0:T(8,128)(2,1)S(1)} %get-tuple-element.83.refs_2_, bf16[1,360,512]{2,1,0:T(8,128)(2,1)S(1)} %get-tuple-element.84.refs_3_, ...), custom_call_target="tpu_custom_call", output_to_operand_aliasing={{0}: (7, {})} | custom-call | flops 1024 | bytes 1024 | tf_op jit(solution)/shard_map/pallas_call | solution.py:314
  114.4 0.8 shard_map.208
  (21 shorter events, 0.1 us)
Async XLA Ops:
  0.6 0.7 copy-start.9
  4.9 16.0 %collective-permute-start.3 = (bf16[2,208,256]{2,1,0:T(8,128)(2,1)S(1)}, bf16[2,208,256]{2,1,0:T(8,128)(2,1)S(1)}, u32[]{:S(2)}, u32[]{:S(2)}) collective-permute-start(bf16[2,208,256]{2,1,0:T(8,128)(2,1)S(1)} %get-tuple-element.61), channel_id=1, source_target_pairs={{0,1},{1,2},{2,3},{3,0},{4,5},{5,6},{6,7},{7,4},{8,9},{9,10},{10,1... | collective-permute-start | bytes 638984 | tf_op jit(solution)/shard_map/ppermute | solution.py:341
  6.6 28.5 %collective-permute-start.4 = (bf16[2,208,256]{2,1,0:T(8,128)(2,1)S(1)}, bf16[2,208,256]{2,1,0:T(8,128)(2,1)S(1)}, u32[]{:S(2)}, u32[]{:S(2)}) collective-permute-start(bf16[2,208,256]{2,1,0:T(8,128)(2,1)S(1)} %get-tuple-element.62), channel_id=1, source_target_pairs={{0,2},{1,3},{2,0},{3,1},{4,6},{5,7},{6,4},{7,5},{8,10},{9,11},{10,... | collective-permute-start | bytes 638984 | tf_op jit(solution)/shard_map/ppermute | solution.py:341
  7.6 28.2 %collective-permute-start.5 = (bf16[2,208,256]{2,1,0:T(8,128)(2,1)S(1)}, bf16[2,208,256]{2,1,0:T(8,128)(2,1)S(1)}, u32[]{:S(2)}, u32[]{:S(2)}) collective-permute-start(bf16[2,208,256]{2,1,0:T(8,128)(2,1)S(1)} %get-tuple-element.63), channel_id=1, source_target_pairs={{0,3},{1,0},{2,1},{3,2},{4,7},{5,4},{6,5},{7,6},{8,11},{9,8},{10,9... | collective-permute-start | bytes 638984 | tf_op jit(solution)/shard_map/ppermute | solution.py:341
  9.6 7.8 %copy-start.7 = (bf16[2,4,64,64]{3,2,1,0:T(8,128)(2,1)S(1)}, bf16[2,4,64,64]{3,2,1,0:T(8,128)(2,1)}, u32[]{:S(2)}) copy-start(bf16[2,4,64,64]{3,2,1,0:T(8,128)(2,1)} %refs_0_.11) | copy-start | bytes 196612
  9.6 7.8 %copy-start.8 = (bf16[2,4,64,64]{3,2,1,0:T(8,128)(2,1)S(1)}, bf16[2,4,64,64]{3,2,1,0:T(8,128)(2,1)}, u32[]{:S(2)}) copy-start(bf16[2,4,64,64]{3,2,1,0:T(8,128)(2,1)} %refs_1_.14) | copy-start | bytes 196612
  9.6 26.2 %copy-start.3 = (bf16[736,832]{1,0:T(8,128)(2,1)S(1)}, bf16[736,832]{1,0:T(8,128)(2,1)}, u32[]{:S(2)}) copy-start(bf16[736,832]{1,0:T(8,128)(2,1)} %constant.9.clone.refs_4_) | copy-start | bytes 3674116
  9.6 26.2 %copy-start.4 = (bf16[4,208,736]{2,1,0:T(8,128)(2,1)S(1)}, bf16[4,208,736]{2,1,0:T(8,128)(2,1)}, u32[]{:S(2)}) copy-start(bf16[4,208,736]{2,1,0:T(8,128)(2,1)} %constant.10.clone.refs_9_) | copy-start | bytes 3674116
  9.6 26.2 %copy-start.11 = (f32[2,256]{1,0:T(2,128)S(1)}, f32[2,256]{1,0:T(2,128)}, u32[]{:S(2)}) copy-start(f32[2,256]{1,0:T(2,128)} %refs_6_.5) | copy-start | bytes 6148
  9.6 26.2 %copy-start.12 = (f32[2,256]{1,0:T(2,128)S(1)}, f32[2,256]{1,0:T(2,128)}, u32[]{:S(2)}) copy-start(f32[2,256]{1,0:T(2,128)} %refs_8_.7) | copy-start | bytes 6148
  13.6 29.3 %collective-permute-start = (bf16[2,208,256]{2,1,0:T(8,128)(2,1)S(1)}, bf16[2,208,256]{2,1,0:T(8,128)(2,1)S(1)}, u32[]{:S(2)}, u32[]{:S(2)}) collective-permute-start(bf16[2,208,256]{2,1,0:T(8,128)(2,1)S(1)} %get-tuple-element.54), channel_id=1, source_target_pairs={{0,1},{1,2},{2,3},{3,0},{4,5},{5,6},{6,7},{7,4},{8,9},{9,10},{10,1... | collective-permute-start | bytes 638984 | tf_op jit(solution)/shard_map/ppermute | solution.py:341
  13.7 39.6 %collective-permute-start.1 = (bf16[2,208,256]{2,1,0:T(8,128)(2,1)S(1)}, bf16[2,208,256]{2,1,0:T(8,128)(2,1)S(1)}, u32[]{:S(2)}, u32[]{:S(2)}) collective-permute-start(bf16[2,208,256]{2,1,0:T(8,128)(2,1)S(1)} %get-tuple-element.55), channel_id=1, source_target_pairs={{0,2},{1,3},{2,0},{3,1},{4,6},{5,7},{6,4},{7,5},{8,10},{9,11},{10,... | collective-permute-start | bytes 638984 | tf_op jit(solution)/shard_map/ppermute | solution.py:341
  21.0 32.4 %collective-permute-start.2 = (bf16[2,208,256]{2,1,0:T(8,128)(2,1)S(1)}, bf16[2,208,256]{2,1,0:T(8,128)(2,1)S(1)}, u32[]{:S(2)}, u32[]{:S(2)}) collective-permute-start(bf16[2,208,256]{2,1,0:T(8,128)(2,1)S(1)} %get-tuple-element.56), channel_id=1, source_target_pairs={{0,3},{1,0},{2,1},{3,2},{4,7},{5,4},{6,5},{7,6},{8,11},{9,8},{10,9... | collective-permute-start | bytes 638984 | tf_op jit(solution)/shard_map/ppermute | solution.py:341
  40.2 21.1 %collective-permute-start.10 = (bf16[2,208,256]{2,1,0:T(8,128)(2,1)S(1)}, bf16[2,208,256]{2,1,0:T(8,128)(2,1)S(1)}, u32[]{:S(2)}, u32[]{:S(2)}) collective-permute-start(bf16[2,208,256]{2,1,0:T(8,128)(2,1)S(1)} %get-tuple-element.72), channel_id=1, source_target_pairs={{0,2},{1,3},{2,0},{3,1},{4,6},{5,7},{6,4},{7,5},{8,10},{9,11},{10,... | collective-permute-start | bytes 638984 | tf_op jit(solution)/shard_map/ppermute | solution.py:341
  42.9 29.5 %collective-permute-start.11 = (bf16[2,208,256]{2,1,0:T(8,128)(2,1)S(1)}, bf16[2,208,256]{2,1,0:T(8,128)(2,1)S(1)}, u32[]{:S(2)}, u32[]{:S(2)}) collective-permute-start(bf16[2,208,256]{2,1,0:T(8,128)(2,1)S(1)} %get-tuple-element.73), channel_id=1, source_target_pairs={{0,3},{1,0},{2,1},{3,2},{4,7},{5,4},{6,5},{7,6},{8,11},{9,8},{10,9... | collective-permute-start | bytes 638984 | tf_op jit(solution)/shard_map/ppermute | solution.py:341
  42.9 30.9 %collective-permute-start.9 = (bf16[2,208,256]{2,1,0:T(8,128)(2,1)S(1)}, bf16[2,208,256]{2,1,0:T(8,128)(2,1)S(1)}, u32[]{:S(2)}, u32[]{:S(2)}) collective-permute-start(bf16[2,208,256]{2,1,0:T(8,128)(2,1)S(1)} %get-tuple-element.71), channel_id=1, source_target_pairs={{0,1},{1,2},{2,3},{3,0},{4,5},{5,6},{6,7},{7,4},{8,9},{9,10},{10,1... | collective-permute-start | bytes 638984 | tf_op jit(solution)/shard_map/ppermute | solution.py:341
  53.4 9.9 %copy-start.6 = (bf16[1,1,4,2,368,256]{5,4,3,2,1,0:T(8,128)(2,1)S(1)}, bf16[1,1,4,2,368,256]{5,4,3,2,1,0:T(8,128)(2,1)}, u32[]{:S(2)}) copy-start(bf16[1,1,4,2,368,256]{5,4,3,2,1,0:T(8,128)(2,1)} %param.31) | copy-start | bytes 4521988
  57.7 16.1 %copy-start.2 = (bf16[1024,512]{1,0:T(8,128)(2,1)S(1)}, bf16[1024,512]{1,0:T(8,128)(2,1)}, u32[]{:S(2)}) copy-start(bf16[1024,512]{1,0:T(8,128)(2,1)} %refs_8_.10) | copy-start | bytes 3145732
  57.7 16.1 %copy-start.5 = (bf16[360,208]{1,0:T(8,128)(2,1)S(1)}, bf16[360,208]{1,0:T(8,128)(2,1)}, u32[]{:S(2)}) copy-start(bf16[360,208]{1,0:T(8,128)(2,1)} %constant.11.clone.refs_7_) | copy-start | bytes 449284
  57.7 16.1 %copy-start.10 = (s32[1,4]{1,0:T(1,128)S(1)}, s32[1,4]{1,0:T(1,128)}, u32[]{:S(2)}) copy-start(s32[1,4]{1,0:T(1,128)} %refs_0_.14) | copy-start | bytes 52
  57.7 26.8 %collective-permute-start.6 = (bf16[2,208,256]{2,1,0:T(8,128)(2,1)S(1)}, bf16[2,208,256]{2,1,0:T(8,128)(2,1)S(1)}, u32[]{:S(2)}, u32[]{:S(2)}) collective-permute-start(bf16[2,208,256]{2,1,0:T(8,128)(2,1)S(1)} %get-tuple-element.67), channel_id=1, source_target_pairs={{0,1},{1,2},{2,3},{3,0},{4,5},{5,6},{6,7},{7,4},{8,9},{9,10},{10,1... | collective-permute-start | bytes 638984 | tf_op jit(solution)/shard_map/ppermute | solution.py:341
  57.8 28.0 %collective-permute-start.7 = (bf16[2,208,256]{2,1,0:T(8,128)(2,1)S(1)}, bf16[2,208,256]{2,1,0:T(8,128)(2,1)S(1)}, u32[]{:S(2)}, u32[]{:S(2)}) collective-permute-start(bf16[2,208,256]{2,1,0:T(8,128)(2,1)S(1)} %get-tuple-element.68), channel_id=1, source_target_pairs={{0,2},{1,3},{2,0},{3,1},{4,6},{5,7},{6,4},{7,5},{8,10},{9,11},{10,... | collective-permute-start | bytes 638984 | tf_op jit(solution)/shard_map/ppermute | solution.py:341
  61.3 24.5 %collective-permute-start.8 = (bf16[2,208,256]{2,1,0:T(8,128)(2,1)S(1)}, bf16[2,208,256]{2,1,0:T(8,128)(2,1)S(1)}, u32[]{:S(2)}, u32[]{:S(2)}) collective-permute-start(bf16[2,208,256]{2,1,0:T(8,128)(2,1)S(1)} %get-tuple-element.69), channel_id=1, source_target_pairs={{0,3},{1,0},{2,1},{3,2},{4,7},{5,4},{6,5},{7,6},{8,11},{9,8},{10,9... | collective-permute-start | bytes 638984 | tf_op jit(solution)/shard_map/ppermute | solution.py:341
  72.3 21.5 %collective-permute-start.16 = (f32[264,128]{1,0:T(8,128)S(1)}, f32[264,128]{1,0:T(8,128)S(1)}, u32[]{:S(2)}, u32[]{:S(2)}) collective-permute-start(f32[264,128]{1,0:T(8,128)S(1)} %shard_map.207), channel_id=1, source_target_pairs={{0,4},{4,0},{1,5},{5,1},{2,6},{6,2},{3,7},{7,3},{8,12},{12,8},{9,1... | collective-permute-start | bytes 405512 | tf_op jit(solution)/shard_map/ppermute | solution.py:525
  73.8 6.2 %copy-start.1 = (bf16[1024,1024]{1,0:T(8,128)(2,1)S(1)}, bf16[1024,1024]{1,0:T(8,128)(2,1)}, u32[]{:S(2)}) copy-start(bf16[1024,1024]{1,0:T(8,128)(2,1)} %refs_1_.20) | copy-start | bytes 6291460
  77.5 24.5 %collective-permute-start.14 = (bf16[2,360,256]{2,1,0:T(8,128)(2,1)S(1)}, bf16[2,360,256]{2,1,0:T(8,128)(2,1)S(1)}, u32[]{:S(2)}, u32[]{:S(2)}) collective-permute-start(bf16[2,360,256]{2,1,0:T(8,128)(2,1)S(1)} %get-tuple-element.88.refs_3_), channel_id=1, source_target_pairs={{0,4},{1,5},{2,6},{3,7},{8,12},{9,13},{10,14},{11,15},{16,20},{17,... | collective-permute-start | bytes 1105928 | tf_op jit(solution)/shard_map/ppermute | solution.py:516
  84.5 17.5 %collective-permute-start.15 = (bf16[2,360,256]{2,1,0:T(8,128)(2,1)S(1)}, bf16[2,360,256]{2,1,0:T(8,128)(2,1)S(1)}, u32[]{:S(2)}, u32[]{:S(2)}) collective-permute-start(bf16[2,360,256]{2,1,0:T(8,128)(2,1)S(1)} %get-tuple-element.89.refs_4_), channel_id=1, source_target_pairs={{0,4},{1,5},{2,6},{3,7},{8,12},{9,13},{10,14},{11,15},{16,20},{17,... | collective-permute-start | bytes 1105928 | tf_op jit(solution)/shard_map/ppermute | solution.py:516
  88.4 18.5 %collective-permute-start.13 = (bf16[1,360,512]{2,1,0:T(8,128)(2,1)S(1)}, bf16[1,360,512]{2,1,0:T(8,128)(2,1)S(1)}, u32[]{:S(2)}, u32[]{:S(2)}) collective-permute-start(bf16[1,360,512]{2,1,0:T(8,128)(2,1)S(1)} %get-tuple-element.86.refs_3_), channel_id=1, source_target_pairs={{0,4},{1,5},{2,6},{3,7},{8,12},{9,13},{10,14},{11,15},{16,20},{17,... | collective-permute-start | bytes 1105928 | tf_op jit(solution)/shard_map/ppermute | solution.py:516
  92.3 19.0 %collective-permute-start.12 = (bf16[1,360,512]{2,1,0:T(8,128)(2,1)S(1)}, bf16[1,360,512]{2,1,0:T(8,128)(2,1)S(1)}, u32[]{:S(2)}, u32[]{:S(2)}) collective-permute-start(bf16[1,360,512]{2,1,0:T(8,128)(2,1)S(1)} %get-tuple-element.84.refs_3_), channel_id=1, source_target_pairs={{0,4},{1,5},{2,6},{3,7},{8,12},{9,13},{10,14},{11,15},{16,20},{17,... | collective-permute-start | bytes 1105928 | tf_op jit(solution)/shard_map/ppermute | solution.py:516
  93.8 1.4 %collective-permute-start.17 = (f32[264,128]{1,0:T(8,128)S(1)}, f32[264,128]{1,0:T(8,128)S(1)}, u32[]{:S(2)}, u32[]{:S(2)}) collective-permute-start(f32[264,128]{1,0:T(8,128)S(1)} %add.9), channel_id=1, source_target_pairs={{0,8},{8,0},{16,24},{24,16},{1,9},{9,1},{17,25},{25,17},{2,10},{10... | collective-permute-start | bytes 405512 | tf_op jit(solution)/shard_map/ppermute | solution.py:525
  95.3 6.7 %collective-permute-start.18 = (f32[264,128]{1,0:T(8,128)S(1)}, f32[264,128]{1,0:T(8,128)S(1)}, u32[]{:S(2)}, u32[]{:S(2)}) collective-permute-start(f32[264,128]{1,0:T(8,128)S(1)} %add.10), channel_id=1, source_target_pairs={{0,16},{8,24},{16,0},{24,8},{1,17},{9,25},{17,1},{25,9},{2,18},{10... | collective-permute-start | bytes 405512 | tf_op jit(solution)/shard_map/ppermute | solution.py:525
  99.7 2.3 %copy-start = (bf16[1024,1024]{1,0:T(8,128)(2,1)S(1)}, bf16[1024,1024]{1,0:T(8,128)(2,1)}, u32[]{:S(2)}) copy-start(bf16[1024,1024]{1,0:T(8,128)(2,1)} %refs_6_.7) | copy-start | bytes 6291460
  99.7 2.3 %copy-start.13 = (f32[16]{0:T(128)S(1)}, f32[16]{0:T(128)}, u32[]{:S(2)}) copy-start(f32[16]{0:T(128)} %refs_1_.23) | copy-start | bytes 196

commit v4 on v3

--- a/solution.py
+++ b/solution.py
@@ -112,23 +112,29 @@
 
 def filter_kernel(taken, *refs):
     parts, refs = refs[:taken], refs[taken:]
-    fold_ref, w1_ref, b1_ref, w2_ref, b2_ref, unfold_ref = refs[:6]
-    *outs, first_ref, whole_ref, mixed_ref = refs[6:]
+    fold_ref, w1_ref, b1_ref, w2_ref, b2_ref, first_ref, mixed_ref, whole_ref = refs
     rank, width = parts[0].shape[-2:]
     modes = first_ref.shape[0] // 2
     for owner, part in incoming(parts):
         whole_ref[pl.ds(pl.multiple_of(owner * rank, 16), rank)] = part
     spectrum = dot(fold_ref[...], whole_ref[...]).astype(BF16)
-    first = dot(spectrum[:modes], w1_ref[:width]) + dot(spectrum[modes:], w1_ref[width:])
-    first_re = jnp.maximum(first[:, :width] + b1_ref[0:1], 0.0).astype(BF16)
-    first_im = jnp.maximum(first[:, width:] + b1_ref[1:2], 0.0).astype(BF16)
-    first_ref[:modes] = first_re
-    first_ref[modes:] = first_im
-    mixed = dot(first_re, w2_ref[:width]) + dot(first_im, w2_ref[width:])
-    mixed_ref[:modes] = (mixed[:, :width] + b2_ref[0:1]).astype(BF16)
-    mixed_ref[modes:] = (mixed[:, width:] + b2_ref[1:2]).astype(BF16)
-    for block, store in outgoing(outs):
-        store(dot(unfold_ref[block], mixed_ref[...]).astype(BF16))
+    spectrum = jnp.concatenate([spectrum[:modes], spectrum[modes:]], axis=1)
+    first = jnp.maximum(dot(spectrum, w1_ref[...]) + both_parts(b1_ref), 0.0).astype(BF16)
+    first_ref[:modes] = first[:, :width]
+    first_ref[modes:] = first[:, width:]
+    mixed = (dot(first, w2_ref[...]) + both_parts(b2_ref)).astype(BF16)
+    mixed_ref[:modes] = mixed[:, :width]
+    mixed_ref[modes:] = mixed[:, width:]
+
+
+def both_parts(ref):
+    return jnp.concatenate([ref[0:1], ref[1:2]], axis=1)
+
+
+def unfold_kernel(mixed_ref, unfold_ref, *outs):
+    sums = [(store, dot(unfold_ref[block], mixed_ref[...])) for block, store in outgoing(outs)]
+    for store, part in sums:
+        store(part.astype(BF16))
 
 
 def gradient_kernel(size, *refs):
@@ -193,12 +199,11 @@
     for owner, part in incoming(parts):
         whole_ref[owner] = part
     embed = latitude_row(band_ref[0, start + pl.program_id(0)], lat_ref[...])
-    for block in range(count):
-        columns = slice(block * width, block * width + width)
-        grid = dot(basis_ref[...], whole_ref[block]).astype(BF16).astype(F32)
-        inputs = x_ref[:, columns].astype(F32) + embed[:, columns]
-        hidden_ref[:, columns] = (inputs + grid).astype(BF16)
-    keyval = dot(hidden_ref[...], w_keyval_ref[...])
+    grids = [dot(basis_ref[...], whole_ref[block]).astype(BF16) for block in range(count)]
+    inputs = x_ref[...].astype(F32) + embed
+    hidden = (inputs + jnp.concatenate(grids, axis=1).astype(F32)).astype(BF16)
+    hidden_ref[...] = hidden
+    keyval = dot(hidden, w_keyval_ref[...])
     ones = head_ones(head_size, 1.0 / head_size)
     half = keyval.shape[1] // 2
     keys = [head_scale(keyval[:, low : low + LANES], ones) for low in range(0, half, LANES)]
@@ -211,10 +216,11 @@
 
 def query_kernel(head_size, hidden_ref, w_query_ref, query_ref):
     ones = head_ones(head_size, 1.0 / head_size)
-    for low in range(0, query_ref.shape[1], LANES):
-        columns = slice(low, low + LANES)
-        query = dot(hidden_ref[...], w_query_ref[:, columns])
-        query_ref[:, columns] = head_scale(query, ones).astype(BF16)
+    tiles = [slice(low, low + LANES) for low in range(0, query_ref.shape[1], LANES)]
+    queries = [dot(hidden_ref[...], w_query_ref[:, columns]) for columns in tiles]
+    means = [dot((query * query).astype(BF16), ones) for query in queries]
+    for columns, query, mean in zip(tiles, queries, means):
+        query_ref[:, columns] = (query * lax.rsqrt(mean + 1e-06)).astype(BF16)
 
 
 def repeat_head(pair, upper, head_size):
@@ -227,9 +233,22 @@
     return jnp.concatenate([part, part], axis=1)
 
 
-def attend_kernel(head_size, taken, past_ref, scale_ref, query_ref, *refs):
+def attend_kernel(head_size, groups, past_ref, scale_ref, *refs):
+    out_ref = refs[-1]
+    w_ref = refs[sum(2 + 2 * taken for _, _, taken in groups)]
+    for first, last, taken in groups:
+        size = 2 + 2 * taken
+        mine, refs = refs[:size], refs[size:]
+        row = pl.program_id(0)
+
+        @pl.when(jnp.logical_and(row >= first, row < last))
+        def _(mine=mine, taken=taken):
+            attend_row(head_size, taken, past_ref, scale_ref, *mine, w_ref, out_ref)
+
+
+def attend_row(head_size, taken, past_ref, scale_ref, query_ref, *refs):
     own_refs, other_refs, refs = refs[:taken], refs[taken : 2 * taken], refs[2 * taken :]
-    hidden_ref, w_ref, *_, out_ref, attended_ref = refs
+    hidden_ref, w_ref, out_ref = refs
     half = sum(ref.shape[1] for ref in own_refs) // 2
     pair_width = 2 * head_size
     group = LANES // head_size
@@ -242,30 +261,27 @@
         size = refs[0].shape[1]
         return refs[low // size][:, low % size : low % size + pair_width].astype(F32)
 
-    for pair in range(0, half, pair_width):
-        key_step = load(other_refs, pair) - load(own_refs, pair)
-        own_value = load(own_refs, half + pair)
-        reach = jnp.where(seen, 0.5 * (load(other_refs, half + pair) - own_value), 0.0)
-        middle = own_value + reach
-        for upper in (False, True):
-            head = pair // head_size + upper
-            columns = slice(head * LANES, head * LANES + LANES)
-            scale = jnp.zeros((1, LANES), F32)
-            for place in range(group):
-                scale = jnp.where(lane_head == place, scale_ref[head * group + place], scale)
-            scale = scale * (0.5 / math.sqrt(head_size))
-            step = repeat_head(key_step, upper, head_size)
-            product = query_ref[:, columns].astype(F32) * twice(step)
-            high = product.astype(BF16)
-            low = (product - high.astype(F32)).astype(BF16)
-            lead = dot(jnp.concatenate([high, low], axis=1), ones)
-            share = jnp.tanh(lead * scale)
-            middles, reaches = (twice(repeat_head(part, upper, head_size)) for part in (middle, reach))
-            attended_ref[:, columns] = (middles + reaches * share).astype(BF16)
-    for low in range(0, out_ref.shape[1], LANES):
-        columns = slice(low, low + LANES)
-        output = dot(attended_ref[...], w_ref[:, columns])
-        out_ref[:, columns] = (hidden_ref[:, columns].astype(F32) + output).astype(BF16)
+    leads, attended = [], []
+    heads = range(half // head_size)
+    for head in heads:
+        pair = head // 2 * pair_width
+        step = repeat_head(load(other_refs, pair) - load(own_refs, pair), head % 2 == 1, head_size)
+        product = query_ref[:, head * LANES : head * LANES + LANES].astype(F32) * twice(step)
+        high = product.astype(BF16)
+        low = (product - high.astype(F32)).astype(BF16)
+        leads.append(dot(jnp.concatenate([high, low], axis=1), ones))
+    for head in heads:
+        pair = half + head // 2 * pair_width
+        value = load(own_refs, pair)
+        reach = jnp.where(seen, 0.5 * (load(other_refs, pair) - value), 0.0)
+        scale = jnp.zeros((1, LANES), F32)
+        for place in range(group):
+            scale = jnp.where(lane_head == place, scale_ref[head * group + place], scale)
+        share = jnp.tanh(leads[head] * (scale * (0.5 / math.sqrt(head_size))))
+        middle, reach = (twice(repeat_head(part, head % 2 == 1, head_size)) for part in (value + reach, reach))
+        attended.append((middle + reach * share).astype(BF16))
+    output = dot(jnp.concatenate(attended, axis=1), w_ref[...])
+    out_ref[...] = (hidden_ref[...].astype(F32) + output).astype(BF16)
 
 
 def fixed(array):
@@ -279,14 +295,23 @@
     )
 
 
+def within(array, start):
+    rows, *rest = array.shape
+    return pl.BlockSpec(
+        (None, *rest), lambda i, *_: (jnp.clip(i - start, 0, rows - 1),) + (0,) * len(rest)
+    )
+
+
 class Order:
     def __init__(self):
         self.last = None
+        self.after = []
 
     def __call__(self, kernel, prefetch, args, specs, outs, out_specs, scratch, flops, grid=(1,), alias=None):
         anywhere = pl.BlockSpec(memory_space=pl.ANY)
         token = jax.ShapeDtypeStruct((8, 128), F32)
-        taken = [] if self.last is None else [self.last]
+        taken = self.after + ([] if self.last is None else [self.last])
+        self.after = []
         skip, count = len(prefetch) + len(args), len(outs)
 
         def ordered(*refs):
@@ -297,7 +322,7 @@
         *results, self.last = call(
             ordered,
             prefetch,
-            (*args, *taken),
+            tuple(args) + tuple(taken),
             [*specs, *[anywhere] * len(taken)],
             [*outs, token],
             [*out_specs, anywhere],
@@ -410,18 +435,33 @@
             grid=(rows,),
         )
 
-    def mix(parts, low, rows, at_once):
-        args = (fold, mix1, b_in1, mix2, b_out2, unfold)
-        outs = [*part_outs(rows, at_once), struct(rows, 2 * modes, local_width)]
+    def mix(parts, low, rows):
+        args = (fold, mix1, b_in1, mix2, b_out2)
+        outs = [struct(rows, 2 * modes, local_width)] * 2
         return run(
             functools.partial(filter_kernel, len(parts)),
             (),
             (*parts, *args),
             [*[by_row(part, low, part.ndim - 3) for part in parts], *[fixed(a) for a in args]],
             outs,
+            [by_row(out) for out in outs],
+            [pltpu.VMEM((count * rank, local_width), BF16)],
+            rows * (16 * modes * local_width * local_width + 4 * modes * local_width * rank * count),
+            grid=(rows,),
+        )
+
+    def unmix(mixed, at_once):
+        rows = mixed.shape[0]
+        outs = part_outs(rows, at_once)
+        return run(
+            unfold_kernel,
+            (),
+            (mixed, unfold),
+            [by_row(mixed), fixed(unfold)],
+            outs,
             [by_row(out, lead=len(out.shape) - 3) for out in outs],
-            [pltpu.VMEM((count * rank, local_width), BF16), pltpu.VMEM((2 * modes, local_width), BF16)],
-            rows * (16 * modes * local_width * local_width + 8 * modes * local_width * rank * count),
+            [],
+            rows * 4 * modes * local_width * rank * count,
             grid=(rows,),
         )
 
@@ -432,7 +472,7 @@
         return run(
             functools.partial(expand_kernel, start, len(parts), head_size),
             (band_rows,),
-            (held(fields), held(lat_table), *parts, *args),
+            (fields, held(lat_table), *parts, *args),
             [*row_specs(start), *[by_row(part, low, part.ndim - 3) for part in parts], *[fixed(a) for a in args]],
             outs,
             [by_row(out) for out in outs],
@@ -444,7 +484,7 @@
     def gradient(firsts):
         args = (*firsts, spec_cot.reshape(spec_cot.shape[2:]))
         packed = struct(blocks * block_size + 8, 2 * block_size, dtype=F32)
-        return call(
+        return run(
             functools.partial(gradient_kernel, block_size),
             (),
             args,
@@ -473,78 +513,102 @@
             grid=(hidden.shape[0],),
         )[0]
 
-    def attention(start, query, own, other, hidden, filled):
-        by_rows = (query, *own, *other, hidden)
-        args = (*by_rows, w_output)
-        specs = [*[by_row(a) for a in by_rows], fixed(w_output)]
+    def attention(start, rows, filled):
+        args, specs, groups = [], [], []
+        for low in sorted(set(cells) & set(range(start, start + rows))):
+            query, own, other, hidden = cells[low]
+            mine = (query, *own, *other, hidden)
+            groups.append((low - start, low - start + query.shape[0], len(own)))
+            args += mine
+            specs += [within(a, low - start) for a in mine]
+        args.append(w_output)
+        specs.append(fixed(w_output))
         alias = None
         if filled is not None:
             alias = {2 + len(args): 0}
-            args, specs = (*args, filled), [*specs, pl.BlockSpec(memory_space=pl.ANY)]
+            args.append(filled)
+            specs.append(pl.BlockSpec(memory_space=pl.ANY))
         return run(
-            functools.partial(attend_kernel, head_size, len(own)),
+            functools.partial(attend_kernel, head_size, groups),
             (earliest_past_snapshot, score_scale),
             args,
             specs,
             [struct(*fields.shape)],
             [pl.BlockSpec((None, None, None, window, width), lambda i, *_: (0, 0, start + i, 0, 0))],
-            [pltpu.VMEM((window, width), BF16)],
-            4 * hidden.size * width,
-            grid=(hidden.shape[0],),
+            [],
+            4 * rows * window * width * width,
+            grid=(rows,),
             alias=alias,
         )[0]
 
-    received, firsts, homeward, cells = {}, [], {}, {}
-    filled = gradients = None
+    predicted = None
+    received, mixes, firsts, homeward, cells = {}, {}, [], {}, {}
     for step, start, rows, at_once in PLAN:
         if step == "compress":
             parts = swap_blocks(compress(start, rows, at_once), count)
             received.update({start + low: (parts, low) for low in range(rows)})
         elif step == "blocks":
-            mixes = [w_in1, w_out2]
+            weights = [w_in1, w_out2]
             mix_shape = struct(2 * local_width, 2 * local_width)
             mix1, mix2 = run(
-                blocks_kernel, (), mixes, [fixed(a) for a in mixes], [mix_shape] * 2, [fixed(mix_shape)] * 2, [], 0
+                blocks_kernel, (), weights, [fixed(a) for a in weights], [mix_shape] * 2, [fixed(mix_shape)] * 2, [], 0
             )
         elif step == "mix":
-            *back, first = mix(*received[start], rows, at_once)
-            parts = swap_blocks(back, count)
+            first, mixes[start] = mix(*received[start], rows)
+            firsts.append(first)
+        elif step == "unmix":
+            parts = swap_blocks(unmix(mixes[start], at_once), count)
             homeward.update({start + low: (parts, low) for low in range(rows)})
-            firsts.append(first)
         elif step == "expand":
             hidden, *keyval = expand(start, *homeward[start], rows, at_once)
             earlier = [lax.ppermute(part, "frame", [(0, 1)]) for part in keyval]
             cells[start] = (keyval, earlier, hidden)
+        elif step == "received":
+            run.after.append(received[start][0][rows])
+        elif step == "returned":
+            run.after.append(homeward[start][0][rows])
         elif step == "query":
             cells[start] = (project(cells[start][-1]), *cells[start])
         elif step == "attend":
-            filled = attention(start, *cells[start], filled)
+            predicted = attention(start, rows, predicted)
         elif step == "gradient":
             summed = gradient(firsts)
-            for axis, pairs in (*exchanges("frame"), *exchanges("dp")):
-                summed = summed + lax.ppermute(summed, axis, pairs)
+            rounds = [*exchanges("frame"), *exchanges("dp")]
+            crossing = lax.ppermute(summed, *rounds.pop(0))
+        elif step == "add":
+            summed = summed + crossing
+            if rounds:
+                crossing = lax.ppermute(summed, *rounds.pop(0))
+                run.after.append(summed)
         elif step == "sum":
             gradients = unpack(summed)
-    return (filled, *gradients)
+    return (predicted, *gradients)
 
 
 PLAN = (
     ("compress", 0, 2, False),
+    ("received", 0, 2, False),
     ("compress", 2, 2, False),
     ("blocks", 0, 0, False),
     ("mix", 0, 2, False),
+    ("unmix", 0, 2, False),
     ("mix", 2, 2, False),
+    ("gradient", 0, 0, False),
+    ("returned", 0, 1, False),
+    ("unmix", 2, 2, False),
     ("expand", 0, 2, True),
     ("query", 0, 2, False),
-    ("gradient", 0, 0, False),
     ("expand", 2, 1, False),
     ("expand", 3, 1, False),
+    ("add", 0, 0, False),
     ("query", 2, 1, False),
     ("query", 3, 1, False),
+    ("add", 0, 0, False),
     ("attend", 0, 2, False),
     ("attend", 2, 1, False),
+    ("add", 0, 0, False),
+    ("sum", 0, 0, False),
     ("attend", 3, 1, False),
-    ("sum", 0, 0, False),
 )
 
 

time: 116 us -> 113 us (0.974)
  Pallas kernels: 47.1 us -> 41.7 us
  waiting for transfers between devices: 37.3 us -> 38.9 us
    pallas_call x16 -> x18, Pallas kernels: 47.1 us -> 41.7 us  [call(): pl.pallas_call(kernel, grid_spec=pltpu.PrefetchScalarGridSpec(num_scalar_...]
    ppermute x12, waiting for transfers between devices: 34.6 us -> 35.8 us  [swap_blocks(): lax.ppermute(part, 'lon', [(i, (i + shift) % count) for i in range(count)])]
  transfers between devices with their start and end apart: 19 -> 19, of which waited for: 7 -> 8; matrix products, arithmetic and copies ran while one was open for 0% -> 0% of each run, Pallas kernels for 34% -> 31%
where the time goes in v4:
time: 113 us; the launch traced here: 112 us
  Pallas kernels  41.7 us (37%)
  waiting for transfers between devices  38.9 us (34%)
  starting transfers between devices  28.4 us (25%)
  between operations  1.68 us (1%)
    pallas_call x18, Pallas kernels, call(): pl.pallas_call(kernel, grid_spec=pltpu.PrefetchScalarGridSpec(num_scalar_...  41.7 us
    ppermute x12, waiting for transfers between devices, swap_blocks(): lax.ppermute(part, 'lon', [(i, (i + shift) % count) for i in range(count)])  35.8 us
    ppermute x12, starting transfers between devices, swap_blocks(): lax.ppermute(part, 'lon', [(i, (i + shift) % count) for i in range(count)])  18.8 us
    ppermute x4, starting transfers between devices, fused_body(): earlier = [lax.ppermute(part, 'frame', [(0, 1)]) for part in keyval]  7.31 us
  transfers between devices with their start and end apart: 19, of which 8 were waited for; matrix products, arithmetic and copies ran while one was open for 0% of the time, Pallas kernels for 31%

profile of v4, /device:TPU:8, one launch (start us, length us, event | category | flops | bytes accessed | tf_op | source)
XLA Modules:
  0.0 111.8 jit_solution(5769900502644324826)
XLA Ops:
  0.6 0.0 copy-start.10
  0.6 0.6 copy-done.10
  1.3 3.6 %shard_map.193 = (bf16[2,208,256]{2,1,0:T(8,128)(2,1)S(1)}, bf16[2,208,256]{2,1,0:T(8,128)(2,1)S(1)}, bf16[2,208,256]{2,1,0:T(8,128)(2,1)S(1)}, bf16[2,208,256]{2,1,0:T(8,128)(2,1)S(1)}, f32[8,128]{1,0:T(8,128)S(1)}) custom-call(s32[1,4]{1,0:T(1,128)S(1)} %copy-done.10, bf16[1,1,4,360,1024]{4,3,2,1,0:T(8,128)(2,1)} %refs_1_.20, bf16[720,1024]{1,0:T(8,128)(2,1)} %refs_2_.9, ...), custom_call_target="tpu_custom_call" | custom-call | flops 1024 | bytes 1024 | tf_op jit(solution)/shard_map/pallas_call | solution.py:339
  4.9 2.7 %collective-permute-start = (bf16[2,208,256]{2,1,0:T(8,128)(2,1)S(1)}, bf16[2,208,256]{2,1,0:T(8,128)(2,1)S(1)}, u32[]{:S(2)}, u32[]{:S(2)}) collective-permute-start(bf16[2,208,256]{2,1,0:T(8,128)(2,1)S(1)} %get-tuple-element.58), channel_id=1, source_target_pairs={{0,2},{1,3},{2,0},{3,1},{4,6},{5,7},{6,4},{7,5},{8,10},{9,11},{10,... | collective-permute-start | bytes 638984 | tf_op jit(solution)/shard_map/ppermute | solution.py:366
  7.6 0.0 collective-permute-start.4
  7.6 2.0 %collective-permute-start.5 = (bf16[2,208,256]{2,1,0:T(8,128)(2,1)S(1)}, bf16[2,208,256]{2,1,0:T(8,128)(2,1)S(1)}, u32[]{:S(2)}, u32[]{:S(2)}) collective-permute-start(bf16[2,208,256]{2,1,0:T(8,128)(2,1)S(1)} %get-tuple-element.69), channel_id=1, source_target_pairs={{0,3},{1,0},{2,1},{3,2},{4,7},{5,4},{6,5},{7,6},{8,11},{9,8},{10,9... | collective-permute-start | bytes 638984 | tf_op jit(solution)/shard_map/ppermute | solution.py:366
  9.6 7.9 %collective-permute-done.refs_5_.refs_2_ = bf16[2,208,256]{2,1,0:T(8,128)(2,1)S(1)} collective-permute-done((bf16[2,208,256]{2,1,0:T(8,128)(2,1)S(1)}, bf16[2,208,256]{2,1,0:T(8,128)(2,1)S(1)}, u32[]{:S(2)}, u32[]{:S(2)}) %collective-permute-start) | collective-permute-done | bytes 213024 | tf_op jit(solution)/shard_map/ppermute | solution.py:366
  17.5 3.6 %shard_map.194 = (bf16[2,208,256]{2,1,0:T(8,128)(2,1)S(1)}, bf16[2,208,256]{2,1,0:T(8,128)(2,1)S(1)}, bf16[2,208,256]{2,1,0:T(8,128)(2,1)S(1)}, bf16[2,208,256]{2,1,0:T(8,128)(2,1)S(1)}, f32[8,128]{1,0:T(8,128)S(1)}) custom-call(s32[1,4]{1,0:T(1,128)S(1)} %copy-done.10, bf16[1,1,4,360,1024]{4,3,2,1,0:T(8,128)(2,1)} %refs_1_.20, bf16[720,1024]{1,0:T(8,128)(2,1)} %refs_2_.9, ...), custom_call_target="tpu_custom_call" | custom-call | flops 1024 | bytes 1024 | tf_op jit(solution)/shard_map/pallas_call | solution.py:339
  21.2 0.0 copy-start.5
  21.2 3.9 %collective-permute-start.1 = (bf16[2,208,256]{2,1,0:T(8,128)(2,1)S(1)}, bf16[2,208,256]{2,1,0:T(8,128)(2,1)S(1)}, u32[]{:S(2)}, u32[]{:S(2)}) collective-permute-start(bf16[2,208,256]{2,1,0:T(8,128)(2,1)S(1)} %get-tuple-element.61), channel_id=1, source_target_pairs={{0,1},{1,2},{2,3},{3,0},{4,5},{5,6},{6,7},{7,4},{8,9},{9,10},{10,1... | collective-permute-start | bytes 638984 | tf_op jit(solution)/shard_map/ppermute | solution.py:366
  25.1 4.3 %collective-permute-start.2 = (bf16[2,208,256]{2,1,0:T(8,128)(2,1)S(1)}, bf16[2,208,256]{2,1,0:T(8,128)(2,1)S(1)}, u32[]{:S(2)}, u32[]{:S(2)}) collective-permute-start(bf16[2,208,256]{2,1,0:T(8,128)(2,1)S(1)} %get-tuple-element.62), channel_id=1, source_target_pairs={{0,2},{1,3},{2,0},{3,1},{4,6},{5,7},{6,4},{7,5},{8,10},{9,11},{10,... | collective-permute-start | bytes 638984 | tf_op jit(solution)/shard_map/ppermute | solution.py:366
  29.4 0.0 collective-permute-start.3
  29.4 0.2 shard_map.195
  29.6 0.0 collective-permute-done.4.refs_1_
  29.6 0.0 collective-permute-done.5.refs_3_
  29.6 3.4 %shard_map.196 = (bf16[2,736,256]{2,1,0:T(8,128)(2,1)S(1)}, bf16[2,736,256]{2,1,0:T(8,128)(2,1)S(1)}, f32[8,128]{1,0:T(8,128)S(1)}) custom-call(bf16[2,208,256]{2,1,0:T(8,128)(2,1)S(1)} %get-tuple-element.67.refs_0_, bf16[2,208,256]{2,1,0:T(8,128)(2,1)S(1)} %collective-permute-done.4.refs_1_, bf16[2,208,256]{2,1,0:T(8,128)(2,1)S(1)} %collective-permute-done.refs_5_.refs_2_, ...), custom_call_target="tpu_custom_call" | custom-call | flops 1024 | bytes 1024 | tf_op jit(solution)/shard_map/pallas_call | solution.py:339
  33.0 1.0 shard_map.197
  34.1 0.0 copy-start.7
  34.1 2.1 %collective-permute-start.6 = (bf16[2,208,256]{2,1,0:T(8,128)(2,1)S(1)}, bf16[2,208,256]{2,1,0:T(8,128)(2,1)S(1)}, u32[]{:S(2)}, u32[]{:S(2)}) collective-permute-start(bf16[2,208,256]{2,1,0:T(8,128)(2,1)S(1)} %get-tuple-element.75), channel_id=1, source_target_pairs={{0,1},{1,2},{2,3},{3,0},{4,5},{5,6},{6,7},{7,4},{8,9},{9,10},{10,1... | collective-permute-start | bytes 638984 | tf_op jit(solution)/shard_map/ppermute | solution.py:366
  36.1 1.8 %collective-permute-start.10 = (bf16[2,208,256]{2,1,0:T(8,128)(2,1)S(1)}, bf16[2,208,256]{2,1,0:T(8,128)(2,1)S(1)}, u32[]{:S(2)}, u32[]{:S(2)}) collective-permute-start(bf16[2,208,256]{2,1,0:T(8,128)(2,1)S(1)} %get-tuple-element.85), channel_id=1, source_target_pairs={{0,2},{1,3},{2,0},{3,1},{4,6},{5,7},{6,4},{7,5},{8,10},{9,11},{10,... | collective-permute-start | bytes 638984 | tf_op jit(solution)/shard_map/ppermute | solution.py:366
  37.9 0.1 collective-permute-done.1.refs_1_
  38.1 0.0 collective-permute-start.11
  38.1 15.5 %collective-permute-done.2.refs_2_ = bf16[2,208,256]{2,1,0:T(8,128)(2,1)S(1)} collective-permute-done((bf16[2,208,256]{2,1,0:T(8,128)(2,1)S(1)}, bf16[2,208,256]{2,1,0:T(8,128)(2,1)S(1)}, u32[]{:S(2)}, u32[]{:S(2)}) %collective-permute-start.2) | collective-permute-done | bytes 213024 | tf_op jit(solution)/shard_map/ppermute | solution.py:366
  53.6 4.6 %collective-permute-done.3.refs_3_ = bf16[2,208,256]{2,1,0:T(8,128)(2,1)S(1)} collective-permute-done((bf16[2,208,256]{2,1,0:T(8,128)(2,1)S(1)}, bf16[2,208,256]{2,1,0:T(8,128)(2,1)S(1)}, u32[]{:S(2)}, u32[]{:S(2)}) %collective-permute-start.3) | collective-permute-done | bytes 213024 | tf_op jit(solution)/shard_map/ppermute | solution.py:366
  58.3 3.4 %shard_map.198 = (bf16[2,736,256]{2,1,0:T(8,128)(2,1)S(1)}, bf16[2,736,256]{2,1,0:T(8,128)(2,1)S(1)}, f32[8,128]{1,0:T(8,128)S(1)}) custom-call(bf16[2,208,256]{2,1,0:T(8,128)(2,1)S(1)} %get-tuple-element.60.refs_0_, bf16[2,208,256]{2,1,0:T(8,128)(2,1)S(1)} %collective-permute-done.1.refs_1_, bf16[2,208,256]{2,1,0:T(8,128)(2,1)S(1)} %collective-permute-done.2.refs_2_, ...), custom_call_target="tpu_custom_call" | custom-call | flops 1024 | bytes 1024 | tf_op jit(solution)/shard_map/pallas_call | solution.py:339
  61.7 0.0 copy-start
  61.7 0.0 copy-start.3
  61.7 0.0 copy-start.6
  61.7 0.0 copy-start.11
  61.7 1.3 %shard_map.199 = (f32[264,128]{1,0:T(8,128)S(1)}, f32[8,128]{1,0:T(8,128)S(1)}) custom-call(bf16[2,736,256]{2,1,0:T(8,128)(2,1)S(1)} %get-tuple-element.76.refs_0_, bf16[2,736,256]{2,1,0:T(8,128)(2,1)S(1)} %get-tuple-element.77.refs_1_, bf16[4,2,368,256]{3,2,1,0:T(8,128)(2,1)S(1)} %bitcast.2, f32[8,128]{1,0:T(8,128)S(1)} %get-tuple-element.78.refs_3_), custom_call_target="tpu_custom_call" | custom-call | flops 1024 | bytes 1024 | tf_op jit(solution)/shard_map/pallas_call | solution.py:339
  63.0 0.0 collective-permute-done.6.refs_2_.refs_4_
  63.0 1.0 shard_map.200
  64.0 0.1 collective-permute-start.7
  64.1 0.1 collective-permute-start.8
  64.2 1.9 %collective-permute-start.9 = (bf16[2,208,256]{2,1,0:T(8,128)(2,1)S(1)}, bf16[2,208,256]{2,1,0:T(8,128)(2,1)S(1)}, u32[]{:S(2)}, u32[]{:S(2)}) collective-permute-start(bf16[2,208,256]{2,1,0:T(8,128)(2,1)S(1)} %get-tuple-element.83), channel_id=1, source_target_pairs={{0,3},{1,0},{2,1},{3,2},{4,7},{5,4},{6,5},{7,6},{8,11},{9,8},{10,9... | collective-permute-start | bytes 638984 | tf_op jit(solution)/shard_map/ppermute | solution.py:366
  66.1 0.0 collective-permute-done.10.refs_5_
  66.1 0.6 collective-permute-start.12
  66.7 7.5 %collective-permute-done.11.refs_6_ = bf16[2,208,256]{2,1,0:T(8,128)(2,1)S(1)} collective-permute-done((bf16[2,208,256]{2,1,0:T(8,128)(2,1)S(1)}, bf16[2,208,256]{2,1,0:T(8,128)(2,1)S(1)}, u32[]{:S(2)}, u32[]{:S(2)}) %collective-permute-start.11) | collective-permute-done | bytes 213024 | tf_op jit(solution)/shard_map/ppermute | solution.py:366
  74.3 0.0 copy-start.2
  74.3 3.2 %shard_map.201 = (bf16[2,360,1024]{2,1,0:T(8,128)(2,1)S(1)}, bf16[2,360,256]{2,1,0:T(8,128)(2,1)S(1)}, bf16[2,360,256]{2,1,0:T(8,128)(2,1)S(1)}, f32[8,128]{1,0:T(8,128)S(1)}) custom-call(s32[1,4]{1,0:T(1,128)S(1)} %copy-done.11, bf16[1,1,4,360,1024]{4,3,2,1,0:T(8,128)(2,1)S(1)} %copy-done, bf16[720,1024]{1,0:T(8,128)(2,1)} %refs_2_.9, ...), custom_call_target="tpu_custom_call" | custom-call | flops 1024 | bytes 1024 | tf_op jit(solution)/shard_map/pallas_call | solution.py:339
  77.5 3.2 %collective-permute-start.15 = (bf16[2,360,256]{2,1,0:T(8,128)(2,1)S(1)}, bf16[2,360,256]{2,1,0:T(8,128)(2,1)S(1)}, u32[]{:S(2)}, u32[]{:S(2)}) collective-permute-start(bf16[2,360,256]{2,1,0:T(8,128)(2,1)S(1)} %get-tuple-element.102.refs_3_), channel_id=1, source_target_pairs={{0,4},{1,5},{2,6},{3,7},{8,12},{9,13},{10,14},{11,15},{16,20},{17,... | collective-permute-start | bytes 1105928 | tf_op jit(solution)/shard_map/ppermute | solution.py:564
  80.7 0.0 collective-permute-done.7.refs_4_
  80.7 1.3 %collective-permute-start.16 = (bf16[2,360,256]{2,1,0:T(8,128)(2,1)S(1)}, bf16[2,360,256]{2,1,0:T(8,128)(2,1)S(1)}, u32[]{:S(2)}, u32[]{:S(2)}) collective-permute-start(bf16[2,360,256]{2,1,0:T(8,128)(2,1)S(1)} %get-tuple-element.103.refs_4_), channel_id=1, source_target_pairs={{0,4},{1,5},{2,6},{3,7},{8,12},{9,13},{10,14},{11,15},{16,20},{17,... | collective-permute-start | bytes 1105928 | tf_op jit(solution)/shard_map/ppermute | solution.py:564
  82.1 2.3 %shard_map.202 = (bf16[2,360,1024]{2,1,0:T(8,128)(2,1)S(1)}, f32[8,128]{1,0:T(8,128)S(1)}) custom-call(bf16[2,360,1024]{2,1,0:T(8,128)(2,1)S(1)} %get-tuple-element.88.refs_0_.refs_7_, bf16[1024,1024]{1,0:T(8,128)(2,1)S(1)} %copy-done.2, f32[8,128]{1,0:T(8,128)S(1)} %get-tuple-element.89.refs_2_), custom_call_target="tpu_custom_call" | custom-call | flops 1024 | bytes 1024 | tf_op jit(solution)/shard_map/pallas_call | solution.py:339
  84.4 0.0 collective-permute-done.8.refs_5_
  84.4 0.0 collective-permute-done.9.refs_6_
  84.4 2.2 %shard_map.203 = (bf16[1,360,1024]{2,1,0:T(8,128)(2,1)S(1)}, bf16[1,360,512]{2,1,0:T(8,128)(2,1)S(1)}, f32[8,128]{1,0:T(8,128)S(1)}) custom-call(s32[1,4]{1,0:T(1,128)S(1)} %copy-done.11, bf16[1,1,4,360,1024]{4,3,2,1,0:T(8,128)(2,1)S(1)} %copy-done, bf16[720,1024]{1,0:T(8,128)(2,1)} %refs_2_.9, bf16[2,208,256]{2,1,0:T(8,128)(2,1)S(1)} %get-tuple-element.80.refs_3_, ...), custom_call_target="tpu_custom_call" | custom-call | flops 1024 | bytes 1024 | tf_op jit(solution)/shard_map/pallas_call | solution.py:339
  86.7 1.3 %collective-permute-start.14 = (bf16[1,360,512]{2,1,0:T(8,128)(2,1)S(1)}, bf16[1,360,512]{2,1,0:T(8,128)(2,1)S(1)}, u32[]{:S(2)}, u32[]{:S(2)}) collective-permute-start(bf16[1,360,512]{2,1,0:T(8,128)(2,1)S(1)} %get-tuple-element.100.refs_3_), channel_id=1, source_target_pairs={{0,4},{1,5},{2,6},{3,7},{8,12},{9,13},{10,14},{11,15},{16,20},{17,... | collective-permute-start | bytes 1105928 | tf_op jit(solution)/shard_map/ppermute | solution.py:564
  88.0 2.2 %shard_map.204 = (bf16[1,360,1024]{2,1,0:T(8,128)(2,1)S(1)}, bf16[1,360,512]{2,1,0:T(8,128)(2,1)S(1)}, f32[8,128]{1,0:T(8,128)S(1)}) custom-call(s32[1,4]{1,0:T(1,128)S(1)} %copy-done.11, bf16[1,1,4,360,1024]{4,3,2,1,0:T(8,128)(2,1)S(1)} %copy-done, bf16[720,1024]{1,0:T(8,128)(2,1)} %refs_2_.9, bf16[2,208,256]{2,1,0:T(8,128)(2,1)S(1)} %get-tuple-element.80.refs_3_, ...), custom_call_target="tpu_custom_call" | custom-call | flops 1024 | bytes 1024 | tf_op jit(solution)/shard_map/pallas_call | solution.py:339
  90.2 1.5 %collective-permute-start.13 = (bf16[1,360,512]{2,1,0:T(8,128)(2,1)S(1)}, bf16[1,360,512]{2,1,0:T(8,128)(2,1)S(1)}, u32[]{:S(2)}, u32[]{:S(2)}) collective-permute-start(bf16[1,360,512]{2,1,0:T(8,128)(2,1)S(1)} %get-tuple-element.98.refs_3_), channel_id=1, source_target_pairs={{0,4},{1,5},{2,6},{3,7},{8,12},{9,13},{10,14},{11,15},{16,20},{17,... | collective-permute-start | bytes 1105928 | tf_op jit(solution)/shard_map/ppermute | solution.py:564
  91.7 0.1 collective-permute-start.17
  91.8 1.3 %collective-permute-done.17 = f32[264,128]{1,0:T(8,128)S(1)} collective-permute-done((f32[264,128]{1,0:T(8,128)S(1)}, f32[264,128]{1,0:T(8,128)S(1)}, u32[]{:S(2)}, u32[]{:S(2)}) %collective-permute-start.17) | collective-permute-done | bytes 135200 | tf_op jit(solution)/shard_map/ppermute | solution.py:581
  93.2 1.6 %collective-permute-start.18 = (f32[264,128]{1,0:T(8,128)S(1)}, f32[264,128]{1,0:T(8,128)S(1)}, u32[]{:S(2)}, u32[]{:S(2)}) collective-permute-start(f32[264,128]{1,0:T(8,128)S(1)} %add.10.refs_9_), channel_id=1, source_target_pairs={{0,16},{8,24},{16,0},{24,8},{1,17},{9,25},{17,1},{25,9},{2,18},{10... | collective-permute-start | bytes 405512 | tf_op jit(solution)/shard_map/ppermute | solution.py:581
  95.4 1.2 %shard_map.205 = (bf16[1,360,1024]{2,1,0:T(8,128)(2,1)S(1)}, f32[8,128]{1,0:T(8,128)S(1)}) custom-call(bf16[1,360,1024]{2,1,0:T(8,128)(2,1)S(1)} %get-tuple-element.93.refs_0_.refs_5_, bf16[1024,1024]{1,0:T(8,128)(2,1)S(1)} %copy-done.2, f32[264,128]{1,0:T(8,128)S(1)} %add.9.refs_2_, f32[8,128]{1,0:T(8,128)S(1)} %get-tuple-element.95.refs_3_), custom_call_target="tpu_custom_call" | custom-call | flops 1024 | bytes 1024 | tf_op jit(solution)/shard_map/pallas_call | solution.py:339
  96.6 0.0 copy-start.1
  96.6 0.0 copy-start.14
  96.6 1.2 %shard_map.206 = (bf16[1,360,1024]{2,1,0:T(8,128)(2,1)S(1)}, f32[8,128]{1,0:T(8,128)S(1)}) custom-call(bf16[1,360,1024]{2,1,0:T(8,128)(2,1)S(1)} %get-tuple-element.92.refs_0_.refs_5_, bf16[1024,1024]{1,0:T(8,128)(2,1)S(1)} %copy-done.2, f32[8,128]{1,0:T(8,128)S(1)} %get-tuple-element.96.refs_2_), custom_call_target="tpu_custom_call" | custom-call | flops 1024 | bytes 1024 | tf_op jit(solution)/shard_map/pallas_call | solution.py:339
  97.8 0.4 copy-done.1
  98.2 4.8 %shard_map.207 = (bf16[1,1,4,360,1024]{4,3,2,1,0:T(8,128)(2,1)}, f32[8,128]{1,0:T(8,128)S(1)}) custom-call(s32[1]{0:T(128)S(6)} %copy.25.refs_0_, f32[16]{0:T(128)S(1)} %copy-done.14, bf16[2,360,1024]{2,1,0:T(8,128)(2,1)S(1)} %get-tuple-element.101.refs_2_, bf16[2,360,256]{2,1,0:T(8,128)(2,1)S(1)} %get-tuple-element.102.refs_3_, ...), custom_call_target="tpu_custom_call" | custom-call | flops 1024 | bytes 1024 | tf_op jit(solution)/shard_map/pallas_call | solution.py:339
  103.0 1.7 %collective-permute-done.14.refs_4_ = bf16[1,360,512]{2,1,0:T(8,128)(2,1)S(1)} collective-permute-done((bf16[1,360,512]{2,1,0:T(8,128)(2,1)S(1)}, bf16[1,360,512]{2,1,0:T(8,128)(2,1)S(1)}, u32[]{:S(2)}, u32[]{:S(2)}) %collective-permute-start.14) | collective-permute-done | bytes 368672 | tf_op jit(solution)/shard_map/ppermute | solution.py:564
  104.7 3.1 %shard_map.208 = (bf16[1,1,4,360,1024]{4,3,2,1,0:T(8,128)(2,1)}, f32[8,128]{1,0:T(8,128)S(1)}) custom-call(s32[1]{0:T(128)S(6)} %copy.25.refs_0_, f32[16]{0:T(128)S(1)} %copy-done.14, bf16[1,360,1024]{2,1,0:T(8,128)(2,1)S(1)} %get-tuple-element.99.refs_2_, bf16[1,360,512]{2,1,0:T(8,128)(2,1)S(1)} %get-tuple-element.100.refs_3_, ...), custom_call_target="tpu_custom_call", output_to_operand_aliasing={{0}: (7, {})} | custom-call | flops 1024 | bytes 1024 | tf_op jit(solution)/shard_map/pallas_call | solution.py:339
  107.8 0.8 shard_map.209
  108.6 0.1 collective-permute-done.13.refs_4_
  108.7 3.1 %shard_map.210 = (bf16[1,1,4,360,1024]{4,3,2,1,0:T(8,128)(2,1)}, f32[8,128]{1,0:T(8,128)}) custom-call(s32[1]{0:T(128)S(6)} %copy.25.refs_0_, f32[16]{0:T(128)S(1)} %copy-done.14, bf16[1,360,1024]{2,1,0:T(8,128)(2,1)S(1)} %get-tuple-element.97.refs_2_, bf16[1,360,512]{2,1,0:T(8,128)(2,1)S(1)} %get-tuple-element.98.refs_3_, ...), custom_call_target="tpu_custom_call", output_to_operand_aliasing={{0}: (7, {})} | custom-call | flops 1024 | bytes 1024 | tf_op jit(solution)/shard_map/pallas_call | solution.py:339
  (25 shorter events, 0.1 us)
Async XLA Ops:
  0.6 0.7 copy-start.10
  4.9 12.6 %collective-permute-start = (bf16[2,208,256]{2,1,0:T(8,128)(2,1)S(1)}, bf16[2,208,256]{2,1,0:T(8,128)(2,1)S(1)}, u32[]{:S(2)}, u32[]{:S(2)}) collective-permute-start(bf16[2,208,256]{2,1,0:T(8,128)(2,1)S(1)} %get-tuple-element.58), channel_id=1, source_target_pairs={{0,2},{1,3},{2,0},{3,1},{4,6},{5,7},{6,4},{7,5},{8,10},{9,11},{10,... | collective-permute-start | bytes 638984 | tf_op jit(solution)/shard_map/ppermute | solution.py:366
  7.6 22.0 %collective-permute-start.4 = (bf16[2,208,256]{2,1,0:T(8,128)(2,1)S(1)}, bf16[2,208,256]{2,1,0:T(8,128)(2,1)S(1)}, u32[]{:S(2)}, u32[]{:S(2)}) collective-permute-start(bf16[2,208,256]{2,1,0:T(8,128)(2,1)S(1)} %get-tuple-element.68), channel_id=1, source_target_pairs={{0,1},{1,2},{2,3},{3,0},{4,5},{5,6},{6,7},{7,4},{8,9},{9,10},{10,1... | collective-permute-start | bytes 638984 | tf_op jit(solution)/shard_map/ppermute | solution.py:366
  7.6 22.0 %collective-permute-start.5 = (bf16[2,208,256]{2,1,0:T(8,128)(2,1)S(1)}, bf16[2,208,256]{2,1,0:T(8,128)(2,1)S(1)}, u32[]{:S(2)}, u32[]{:S(2)}) collective-permute-start(bf16[2,208,256]{2,1,0:T(8,128)(2,1)S(1)} %get-tuple-element.69), channel_id=1, source_target_pairs={{0,3},{1,0},{2,1},{3,2},{4,7},{5,4},{6,5},{7,6},{8,11},{9,8},{10,9... | collective-permute-start | bytes 638984 | tf_op jit(solution)/shard_map/ppermute | solution.py:366
  17.5 11.9 %copy-start.8 = (bf16[2,4,64,64]{3,2,1,0:T(8,128)(2,1)S(1)}, bf16[2,4,64,64]{3,2,1,0:T(8,128)(2,1)}, u32[]{:S(2)}) copy-start(bf16[2,4,64,64]{3,2,1,0:T(8,128)(2,1)} %refs_0_.11) | copy-start | bytes 196612
  17.5 11.9 %copy-start.9 = (bf16[2,4,64,64]{3,2,1,0:T(8,128)(2,1)S(1)}, bf16[2,4,64,64]{3,2,1,0:T(8,128)(2,1)}, u32[]{:S(2)}) copy-start(bf16[2,4,64,64]{3,2,1,0:T(8,128)(2,1)} %refs_1_.16) | copy-start | bytes 196612
  17.5 12.1 %copy-start.4 = (bf16[736,832]{1,0:T(8,128)(2,1)S(1)}, bf16[736,832]{1,0:T(8,128)(2,1)}, u32[]{:S(2)}) copy-start(bf16[736,832]{1,0:T(8,128)(2,1)} %constant.9.clone.refs_4_) | copy-start | bytes 3674116
  17.5 12.1 %copy-start.12 = (f32[2,256]{1,0:T(2,128)S(1)}, f32[2,256]{1,0:T(2,128)}, u32[]{:S(2)}) copy-start(f32[2,256]{1,0:T(2,128)} %refs_6_.5) | copy-start | bytes 6148
  17.5 12.1 %copy-start.13 = (f32[2,256]{1,0:T(2,128)S(1)}, f32[2,256]{1,0:T(2,128)}, u32[]{:S(2)}) copy-start(f32[2,256]{1,0:T(2,128)} %refs_8_.7) | copy-start | bytes 6148
  21.2 11.8 %copy-start.5 = (bf16[4,208,736]{2,1,0:T(8,128)(2,1)S(1)}, bf16[4,208,736]{2,1,0:T(8,128)(2,1)}, u32[]{:S(2)}) copy-start(bf16[4,208,736]{2,1,0:T(8,128)(2,1)} %constant.10.clone.refs_1_) | copy-start | bytes 3674116
  21.2 16.9 %collective-permute-start.1 = (bf16[2,208,256]{2,1,0:T(8,128)(2,1)S(1)}, bf16[2,208,256]{2,1,0:T(8,128)(2,1)S(1)}, u32[]{:S(2)}, u32[]{:S(2)}) collective-permute-start(bf16[2,208,256]{2,1,0:T(8,128)(2,1)S(1)} %get-tuple-element.61), channel_id=1, source_target_pairs={{0,1},{1,2},{2,3},{3,0},{4,5},{5,6},{6,7},{7,4},{8,9},{9,10},{10,1... | collective-permute-start | bytes 638984 | tf_op jit(solution)/shard_map/ppermute | solution.py:366
  25.1 28.5 %collective-permute-start.2 = (bf16[2,208,256]{2,1,0:T(8,128)(2,1)S(1)}, bf16[2,208,256]{2,1,0:T(8,128)(2,1)S(1)}, u32[]{:S(2)}, u32[]{:S(2)}) collective-permute-start(bf16[2,208,256]{2,1,0:T(8,128)(2,1)S(1)} %get-tuple-element.62), channel_id=1, source_target_pairs={{0,2},{1,3},{2,0},{3,1},{4,6},{5,7},{6,4},{7,5},{8,10},{9,11},{10,... | collective-permute-start | bytes 638984 | tf_op jit(solution)/shard_map/ppermute | solution.py:366
  29.4 28.9 %collective-permute-start.3 = (bf16[2,208,256]{2,1,0:T(8,128)(2,1)S(1)}, bf16[2,208,256]{2,1,0:T(8,128)(2,1)S(1)}, u32[]{:S(2)}, u32[]{:S(2)}) collective-permute-start(bf16[2,208,256]{2,1,0:T(8,128)(2,1)S(1)} %get-tuple-element.63), channel_id=1, source_target_pairs={{0,3},{1,0},{2,1},{3,2},{4,7},{5,4},{6,5},{7,6},{8,11},{9,8},{10,9... | collective-permute-start | bytes 638984 | tf_op jit(solution)/shard_map/ppermute | solution.py:366
  34.1 27.6 %copy-start.7 = (bf16[1,1,4,2,368,256]{5,4,3,2,1,0:T(8,128)(2,1)S(1)}, bf16[1,1,4,2,368,256]{5,4,3,2,1,0:T(8,128)(2,1)}, u32[]{:S(2)}) copy-start(bf16[1,1,4,2,368,256]{5,4,3,2,1,0:T(8,128)(2,1)} %param.31) | copy-start | bytes 4521988
  34.1 28.9 %collective-permute-start.6 = (bf16[2,208,256]{2,1,0:T(8,128)(2,1)S(1)}, bf16[2,208,256]{2,1,0:T(8,128)(2,1)S(1)}, u32[]{:S(2)}, u32[]{:S(2)}) collective-permute-start(bf16[2,208,256]{2,1,0:T(8,128)(2,1)S(1)} %get-tuple-element.75), channel_id=1, source_target_pairs={{0,1},{1,2},{2,3},{3,0},{4,5},{5,6},{6,7},{7,4},{8,9},{9,10},{10,1... | collective-permute-start | bytes 638984 | tf_op jit(solution)/shard_map/ppermute | solution.py:366
  36.1 30.0 %collective-permute-start.10 = (bf16[2,208,256]{2,1,0:T(8,128)(2,1)S(1)}, bf16[2,208,256]{2,1,0:T(8,128)(2,1)S(1)}, u32[]{:S(2)}, u32[]{:S(2)}) collective-permute-start(bf16[2,208,256]{2,1,0:T(8,128)(2,1)S(1)} %get-tuple-element.85), channel_id=1, source_target_pairs={{0,2},{1,3},{2,0},{3,1},{4,6},{5,7},{6,4},{7,5},{8,10},{9,11},{10,... | collective-permute-start | bytes 638984 | tf_op jit(solution)/shard_map/ppermute | solution.py:366
  38.1 36.2 %collective-permute-start.11 = (bf16[2,208,256]{2,1,0:T(8,128)(2,1)S(1)}, bf16[2,208,256]{2,1,0:T(8,128)(2,1)S(1)}, u32[]{:S(2)}, u32[]{:S(2)}) collective-permute-start(bf16[2,208,256]{2,1,0:T(8,128)(2,1)S(1)} %get-tuple-element.86), channel_id=1, source_target_pairs={{0,3},{1,0},{2,1},{3,2},{4,7},{5,4},{6,5},{7,6},{8,11},{9,8},{10,9... | collective-permute-start | bytes 638984 | tf_op jit(solution)/shard_map/ppermute | solution.py:366
  61.7 12.6 %copy-start = (bf16[1,1,4,360,1024]{4,3,2,1,0:T(8,128)(2,1)S(1)}, bf16[1,1,4,360,1024]{4,3,2,1,0:T(8,128)(2,1)}, u32[]{:S(2)}) copy-start(bf16[1,1,4,360,1024]{4,3,2,1,0:T(8,128)(2,1)} %refs_1_.20) | copy-start | bytes 8847364
  61.7 12.6 %copy-start.3 = (bf16[1024,512]{1,0:T(8,128)(2,1)S(1)}, bf16[1024,512]{1,0:T(8,128)(2,1)}, u32[]{:S(2)}) copy-start(bf16[1024,512]{1,0:T(8,128)(2,1)} %refs_8_.10) | copy-start | bytes 3145732
  61.7 12.6 %copy-start.6 = (bf16[360,208]{1,0:T(8,128)(2,1)S(1)}, bf16[360,208]{1,0:T(8,128)(2,1)}, u32[]{:S(2)}) copy-start(bf16[360,208]{1,0:T(8,128)(2,1)} %constant.11.clone.refs_7_) | copy-start | bytes 449284
  61.7 12.6 %copy-start.11 = (s32[1,4]{1,0:T(1,128)S(1)}, s32[1,4]{1,0:T(1,128)}, u32[]{:S(2)}) copy-start(s32[1,4]{1,0:T(1,128)} %refs_0_.14) | copy-start | bytes 52
  64.0 16.7 %collective-permute-start.7 = (bf16[2,208,256]{2,1,0:T(8,128)(2,1)S(1)}, bf16[2,208,256]{2,1,0:T(8,128)(2,1)S(1)}, u32[]{:S(2)}, u32[]{:S(2)}) collective-permute-start(bf16[2,208,256]{2,1,0:T(8,128)(2,1)S(1)} %get-tuple-element.81), channel_id=1, source_target_pairs={{0,1},{1,2},{2,3},{3,0},{4,5},{5,6},{6,7},{7,4},{8,9},{9,10},{10,1... | collective-permute-start | bytes 638984 | tf_op jit(solution)/shard_map/ppermute | solution.py:366
  64.1 20.3 %collective-permute-start.8 = (bf16[2,208,256]{2,1,0:T(8,128)(2,1)S(1)}, bf16[2,208,256]{2,1,0:T(8,128)(2,1)S(1)}, u32[]{:S(2)}, u32[]{:S(2)}) collective-permute-start(bf16[2,208,256]{2,1,0:T(8,128)(2,1)S(1)} %get-tuple-element.82), channel_id=1, source_target_pairs={{0,2},{1,3},{2,0},{3,1},{4,6},{5,7},{6,4},{7,5},{8,10},{9,11},{10,... | collective-permute-start | bytes 638984 | tf_op jit(solution)/shard_map/ppermute | solution.py:366
  64.2 20.2 %collective-permute-start.9 = (bf16[2,208,256]{2,1,0:T(8,128)(2,1)S(1)}, bf16[2,208,256]{2,1,0:T(8,128)(2,1)S(1)}, u32[]{:S(2)}, u32[]{:S(2)}) collective-permute-start(bf16[2,208,256]{2,1,0:T(8,128)(2,1)S(1)} %get-tuple-element.83), channel_id=1, source_target_pairs={{0,3},{1,0},{2,1},{3,2},{4,7},{5,4},{6,5},{7,6},{8,11},{9,8},{10,9... | collective-permute-start | bytes 638984 | tf_op jit(solution)/shard_map/ppermute | solution.py:366
  66.1 25.6 %collective-permute-start.12 = (f32[264,128]{1,0:T(8,128)S(1)}, f32[264,128]{1,0:T(8,128)S(1)}, u32[]{:S(2)}, u32[]{:S(2)}) collective-permute-start(f32[264,128]{1,0:T(8,128)S(1)} %get-tuple-element.94), channel_id=1, source_target_pairs={{0,4},{4,0},{1,5},{5,1},{2,6},{6,2},{3,7},{7,3},{8,12},{12,8},{9,1... | collective-permute-start | bytes 405512 | tf_op jit(solution)/shard_map/ppermute | solution.py:577
  74.3 7.8 %copy-start.2 = (bf16[1024,1024]{1,0:T(8,128)(2,1)S(1)}, bf16[1024,1024]{1,0:T(8,128)(2,1)}, u32[]{:S(2)}) copy-start(bf16[1024,1024]{1,0:T(8,128)(2,1)} %refs_1_.22) | copy-start | bytes 6291460
  77.5 20.2 %collective-permute-start.15 = (bf16[2,360,256]{2,1,0:T(8,128)(2,1)S(1)}, bf16[2,360,256]{2,1,0:T(8,128)(2,1)S(1)}, u32[]{:S(2)}, u32[]{:S(2)}) collective-permute-start(bf16[2,360,256]{2,1,0:T(8,128)(2,1)S(1)} %get-tuple-element.102.refs_3_), channel_id=1, source_target_pairs={{0,4},{1,5},{2,6},{3,7},{8,12},{9,13},{10,14},{11,15},{16,20},{17,... | collective-permute-start | bytes 1105928 | tf_op jit(solution)/shard_map/ppermute | solution.py:564
  80.7 17.0 %collective-permute-start.16 = (bf16[2,360,256]{2,1,0:T(8,128)(2,1)S(1)}, bf16[2,360,256]{2,1,0:T(8,128)(2,1)S(1)}, u32[]{:S(2)}, u32[]{:S(2)}) collective-permute-start(bf16[2,360,256]{2,1,0:T(8,128)(2,1)S(1)} %get-tuple-element.103.refs_4_), channel_id=1, source_target_pairs={{0,4},{1,5},{2,6},{3,7},{8,12},{9,13},{10,14},{11,15},{16,20},{17,... | collective-permute-start | bytes 1105928 | tf_op jit(solution)/shard_map/ppermute | solution.py:564
  86.7 18.1 %collective-permute-start.14 = (bf16[1,360,512]{2,1,0:T(8,128)(2,1)S(1)}, bf16[1,360,512]{2,1,0:T(8,128)(2,1)S(1)}, u32[]{:S(2)}, u32[]{:S(2)}) collective-permute-start(bf16[1,360,512]{2,1,0:T(8,128)(2,1)S(1)} %get-tuple-element.100.refs_3_), channel_id=1, source_target_pairs={{0,4},{1,5},{2,6},{3,7},{8,12},{9,13},{10,14},{11,15},{16,20},{17,... | collective-permute-start | bytes 1105928 | tf_op jit(solution)/shard_map/ppermute | solution.py:564
  90.2 18.5 %collective-permute-start.13 = (bf16[1,360,512]{2,1,0:T(8,128)(2,1)S(1)}, bf16[1,360,512]{2,1,0:T(8,128)(2,1)S(1)}, u32[]{:S(2)}, u32[]{:S(2)}) collective-permute-start(bf16[1,360,512]{2,1,0:T(8,128)(2,1)S(1)} %get-tuple-element.98.refs_3_), channel_id=1, source_target_pairs={{0,4},{1,5},{2,6},{3,7},{8,12},{9,13},{10,14},{11,15},{16,20},{17,... | collective-permute-start | bytes 1105928 | tf_op jit(solution)/shard_map/ppermute | solution.py:564
  91.7 1.4 %collective-permute-start.17 = (f32[264,128]{1,0:T(8,128)S(1)}, f32[264,128]{1,0:T(8,128)S(1)}, u32[]{:S(2)}, u32[]{:S(2)}) collective-permute-start(f32[264,128]{1,0:T(8,128)S(1)} %add.9.refs_2_), channel_id=1, source_target_pairs={{0,8},{8,0},{16,24},{24,16},{1,9},{9,1},{17,25},{25,17},{2,10},{10... | collective-permute-start | bytes 405512 | tf_op jit(solution)/shard_map/ppermute | solution.py:581
  93.2 9.8 %collective-permute-start.18 = (f32[264,128]{1,0:T(8,128)S(1)}, f32[264,128]{1,0:T(8,128)S(1)}, u32[]{:S(2)}, u32[]{:S(2)}) collective-permute-start(f32[264,128]{1,0:T(8,128)S(1)} %add.10.refs_9_), channel_id=1, source_target_pairs={{0,16},{8,24},{16,0},{24,8},{1,17},{9,25},{17,1},{25,9},{2,18},{10... | collective-permute-start | bytes 405512 | tf_op jit(solution)/shard_map/ppermute | solution.py:581
  96.6 1.6 %copy-start.1 = (bf16[1024,1024]{1,0:T(8,128)(2,1)S(1)}, bf16[1024,1024]{1,0:T(8,128)(2,1)}, u32[]{:S(2)}) copy-start(bf16[1024,1024]{1,0:T(8,128)(2,1)} %refs_6_.7) | copy-start | bytes 6291460
  96.6 1.6 %copy-start.14 = (f32[16]{0:T(128)S(1)}, f32[16]{0:T(128)}, u32[]{:S(2)}) copy-start(f32[16]{0:T(128)} %refs_1_.25) | copy-start | bytes 196

commit v5 on v4

--- a/solution.py
+++ b/solution.py
@@ -594,7 +594,7 @@
     ("unmix", 0, 2, False),
     ("mix", 2, 2, False),
     ("gradient", 0, 0, False),
-    ("returned", 0, 1, False),
+    ("returned", 0, 2, False),
     ("unmix", 2, 2, False),
     ("expand", 0, 2, True),
     ("query", 0, 2, False),

time: 113 us -> 110 us (0.973)
  waiting for transfers between devices: 38.9 us -> 32.5 us
  starting transfers between devices: 28.4 us -> 32.8 us
    ppermute x12, waiting for transfers between devices: 35.8 us -> 31.2 us  [swap_blocks(): lax.ppermute(part, 'lon', [(i, (i + shift) % count) for i in range(count)])]
    ppermute x4, starting transfers between devices: 7.31 us -> 10.4 us  [fused_body(): earlier = [lax.ppermute(part, 'frame', [(0, 1)]) for part in keyval]]
    ppermute x4, waiting for transfers between devices: 1.8 us -> 0.01 us  [fused_body(): earlier = [lax.ppermute(part, 'frame', [(0, 1)]) for part in keyval]]
  transfers between devices with their start and end apart: 19 -> 19, of which waited for: 8 -> 6; matrix products, arithmetic and copies ran while one was open for 0% -> 0% of each run, Pallas kernels for 31% -> 32%
where the time goes in v5:
time: 110 us
  Pallas kernels  41.6 us (38%)
  starting transfers between devices  32.8 us (30%)
  waiting for transfers between devices  32.5 us (30%)
  between operations  1.68 us (2%)
  local copies, waits for them, and re-layouts  1.11 us (1%)
    pallas_call x18, Pallas kernels, call(): pl.pallas_call(kernel, grid_spec=pltpu.PrefetchScalarGridSpec(num_scalar_...  41.6 us
    ppermute x12, waiting for transfers between devices, swap_blocks(): lax.ppermute(part, 'lon', [(i, (i + shift) % count) for i in range(count)])  31.2 us
    ppermute x12, starting transfers between devices, swap_blocks(): lax.ppermute(part, 'lon', [(i, (i + shift) % count) for i in range(count)])  19.5 us
    ppermute x4, starting transfers between devices, fused_body(): earlier = [lax.ppermute(part, 'frame', [(0, 1)]) for part in keyval]  10.4 us
    ppermute x3, starting transfers between devices, fused_body(): crossing = lax.ppermute(summed, *rounds.pop(0))  2.91 us
  transfers between devices with their start and end apart: 19, of which 6 were waited for; matrix products, arithmetic and copies ran while one was open for 0% of the time, Pallas kernels for 32%

profile of v5, /device:TPU:8, one launch (start us, length us, event | category | flops | bytes accessed | tf_op | source)
XLA Modules:
  0.0 109.8 jit_solution(3755702183716036094)
XLA Ops:
  0.6 0.0 copy-start.10
  0.6 0.6 copy-done.10
  1.3 3.6 %shard_map.193 = (bf16[2,208,256]{2,1,0:T(8,128)(2,1)S(1)}, bf16[2,208,256]{2,1,0:T(8,128)(2,1)S(1)}, bf16[2,208,256]{2,1,0:T(8,128)(2,1)S(1)}, bf16[2,208,256]{2,1,0:T(8,128)(2,1)S(1)}, f32[8,128]{1,0:T(8,128)S(1)}) custom-call(s32[1,4]{1,0:T(1,128)S(1)} %copy-done.10, bf16[1,1,4,360,1024]{4,3,2,1,0:T(8,128)(2,1)} %refs_1_.20, bf16[720,1024]{1,0:T(8,128)(2,1)} %refs_2_.9, ...), custom_call_target="tpu_custom_call" | custom-call | flops 1024 | bytes 1024 | tf_op jit(solution)/shard_map/pallas_call | solution.py:339
  4.9 2.7 %collective-permute-start = (bf16[2,208,256]{2,1,0:T(8,128)(2,1)S(1)}, bf16[2,208,256]{2,1,0:T(8,128)(2,1)S(1)}, u32[]{:S(2)}, u32[]{:S(2)}) collective-permute-start(bf16[2,208,256]{2,1,0:T(8,128)(2,1)S(1)} %get-tuple-element.58), channel_id=1, source_target_pairs={{0,2},{1,3},{2,0},{3,1},{4,6},{5,7},{6,4},{7,5},{8,10},{9,11},{10,... | collective-permute-start | bytes 638984 | tf_op jit(solution)/shard_map/ppermute | solution.py:366
  7.6 0.0 collective-permute-start.4
  7.6 2.0 %collective-permute-start.5 = (bf16[2,208,256]{2,1,0:T(8,128)(2,1)S(1)}, bf16[2,208,256]{2,1,0:T(8,128)(2,1)S(1)}, u32[]{:S(2)}, u32[]{:S(2)}) collective-permute-start(bf16[2,208,256]{2,1,0:T(8,128)(2,1)S(1)} %get-tuple-element.69), channel_id=1, source_target_pairs={{0,3},{1,0},{2,1},{3,2},{4,7},{5,4},{6,5},{7,6},{8,11},{9,8},{10,9... | collective-permute-start | bytes 638984 | tf_op jit(solution)/shard_map/ppermute | solution.py:366
  9.6 7.9 %collective-permute-done.refs_5_.refs_2_ = bf16[2,208,256]{2,1,0:T(8,128)(2,1)S(1)} collective-permute-done((bf16[2,208,256]{2,1,0:T(8,128)(2,1)S(1)}, bf16[2,208,256]{2,1,0:T(8,128)(2,1)S(1)}, u32[]{:S(2)}, u32[]{:S(2)}) %collective-permute-start) | collective-permute-done | bytes 213024 | tf_op jit(solution)/shard_map/ppermute | solution.py:366
  17.5 3.6 %shard_map.194 = (bf16[2,208,256]{2,1,0:T(8,128)(2,1)S(1)}, bf16[2,208,256]{2,1,0:T(8,128)(2,1)S(1)}, bf16[2,208,256]{2,1,0:T(8,128)(2,1)S(1)}, bf16[2,208,256]{2,1,0:T(8,128)(2,1)S(1)}, f32[8,128]{1,0:T(8,128)S(1)}) custom-call(s32[1,4]{1,0:T(1,128)S(1)} %copy-done.10, bf16[1,1,4,360,1024]{4,3,2,1,0:T(8,128)(2,1)} %refs_1_.20, bf16[720,1024]{1,0:T(8,128)(2,1)} %refs_2_.9, ...), custom_call_target="tpu_custom_call" | custom-call | flops 1024 | bytes 1024 | tf_op jit(solution)/shard_map/pallas_call | solution.py:339
  21.2 0.0 copy-start.5
  21.2 3.9 %collective-permute-start.1 = (bf16[2,208,256]{2,1,0:T(8,128)(2,1)S(1)}, bf16[2,208,256]{2,1,0:T(8,128)(2,1)S(1)}, u32[]{:S(2)}, u32[]{:S(2)}) collective-permute-start(bf16[2,208,256]{2,1,0:T(8,128)(2,1)S(1)} %get-tuple-element.61), channel_id=1, source_target_pairs={{0,1},{1,2},{2,3},{3,0},{4,5},{5,6},{6,7},{7,4},{8,9},{9,10},{10,1... | collective-permute-start | bytes 638984 | tf_op jit(solution)/shard_map/ppermute | solution.py:366
  25.1 4.3 %collective-permute-start.2 = (bf16[2,208,256]{2,1,0:T(8,128)(2,1)S(1)}, bf16[2,208,256]{2,1,0:T(8,128)(2,1)S(1)}, u32[]{:S(2)}, u32[]{:S(2)}) collective-permute-start(bf16[2,208,256]{2,1,0:T(8,128)(2,1)S(1)} %get-tuple-element.62), channel_id=1, source_target_pairs={{0,2},{1,3},{2,0},{3,1},{4,6},{5,7},{6,4},{7,5},{8,10},{9,11},{10,... | collective-permute-start | bytes 638984 | tf_op jit(solution)/shard_map/ppermute | solution.py:366
  29.4 0.0 collective-permute-start.3
  29.4 0.2 shard_map.195
  29.6 0.0 collective-permute-done.4.refs_1_
  29.6 0.0 collective-permute-done.5.refs_3_
  29.6 3.4 %shard_map.196 = (bf16[2,736,256]{2,1,0:T(8,128)(2,1)S(1)}, bf16[2,736,256]{2,1,0:T(8,128)(2,1)S(1)}, f32[8,128]{1,0:T(8,128)S(1)}) custom-call(bf16[2,208,256]{2,1,0:T(8,128)(2,1)S(1)} %get-tuple-element.67.refs_0_, bf16[2,208,256]{2,1,0:T(8,128)(2,1)S(1)} %collective-permute-done.4.refs_1_, bf16[2,208,256]{2,1,0:T(8,128)(2,1)S(1)} %collective-permute-done.refs_5_.refs_2_, ...), custom_call_target="tpu_custom_call" | custom-call | flops 1024 | bytes 1024 | tf_op jit(solution)/shard_map/pallas_call | solution.py:339
  33.0 1.0 shard_map.197
  34.1 0.0 copy-start.7
  34.1 0.7 collective-permute-start.6
  34.8 2.3 %collective-permute-start.10 = (bf16[2,208,256]{2,1,0:T(8,128)(2,1)S(1)}, bf16[2,208,256]{2,1,0:T(8,128)(2,1)S(1)}, u32[]{:S(2)}, u32[]{:S(2)}) collective-permute-start(bf16[2,208,256]{2,1,0:T(8,128)(2,1)S(1)} %get-tuple-element.85), channel_id=1, source_target_pairs={{0,1},{1,2},{2,3},{3,0},{4,5},{5,6},{6,7},{7,4},{8,9},{9,10},{10,1... | collective-permute-start | bytes 638984 | tf_op jit(solution)/shard_map/ppermute | solution.py:366
  37.1 5.6 %collective-permute-done.1.refs_1_ = bf16[2,208,256]{2,1,0:T(8,128)(2,1)S(1)} collective-permute-done((bf16[2,208,256]{2,1,0:T(8,128)(2,1)S(1)}, bf16[2,208,256]{2,1,0:T(8,128)(2,1)S(1)}, u32[]{:S(2)}, u32[]{:S(2)}) %collective-permute-start.1) | collective-permute-done | bytes 213024 | tf_op jit(solution)/shard_map/ppermute | solution.py:366
  42.7 11.0 %collective-permute-done.2.refs_2_ = bf16[2,208,256]{2,1,0:T(8,128)(2,1)S(1)} collective-permute-done((bf16[2,208,256]{2,1,0:T(8,128)(2,1)S(1)}, bf16[2,208,256]{2,1,0:T(8,128)(2,1)S(1)}, u32[]{:S(2)}, u32[]{:S(2)}) %collective-permute-start.2) | collective-permute-done | bytes 213024 | tf_op jit(solution)/shard_map/ppermute | solution.py:366
  53.6 2.4 %collective-permute-done.3.refs_3_ = bf16[2,208,256]{2,1,0:T(8,128)(2,1)S(1)} collective-permute-done((bf16[2,208,256]{2,1,0:T(8,128)(2,1)S(1)}, bf16[2,208,256]{2,1,0:T(8,128)(2,1)S(1)}, u32[]{:S(2)}, u32[]{:S(2)}) %collective-permute-start.3) | collective-permute-done | bytes 213024 | tf_op jit(solution)/shard_map/ppermute | solution.py:366
  56.0 3.4 %shard_map.198 = (bf16[2,736,256]{2,1,0:T(8,128)(2,1)S(1)}, bf16[2,736,256]{2,1,0:T(8,128)(2,1)S(1)}, f32[8,128]{1,0:T(8,128)S(1)}) custom-call(bf16[2,208,256]{2,1,0:T(8,128)(2,1)S(1)} %get-tuple-element.60.refs_0_, bf16[2,208,256]{2,1,0:T(8,128)(2,1)S(1)} %collective-permute-done.1.refs_1_, bf16[2,208,256]{2,1,0:T(8,128)(2,1)S(1)} %collective-permute-done.2.refs_2_, ...), custom_call_target="tpu_custom_call" | custom-call | flops 1024 | bytes 1024 | tf_op jit(solution)/shard_map/pallas_call | solution.py:339
  59.4 0.0 copy-start
  59.4 0.0 copy-start.3
  59.4 0.0 copy-start.6
  59.4 0.0 copy-start.11
  59.4 1.3 %shard_map.199 = (f32[264,128]{1,0:T(8,128)S(1)}, f32[8,128]{1,0:T(8,128)S(1)}) custom-call(bf16[2,736,256]{2,1,0:T(8,128)(2,1)S(1)} %get-tuple-element.76.refs_0_, bf16[2,736,256]{2,1,0:T(8,128)(2,1)S(1)} %get-tuple-element.77.refs_1_, bf16[4,2,368,256]{3,2,1,0:T(8,128)(2,1)S(1)} %bitcast.2, f32[8,128]{1,0:T(8,128)S(1)} %get-tuple-element.78.refs_3_), custom_call_target="tpu_custom_call" | custom-call | flops 1024 | bytes 1024 | tf_op jit(solution)/shard_map/pallas_call | solution.py:339
  60.7 1.0 shard_map.200
  61.8 0.1 collective-permute-start.7
  61.8 3.6 %collective-permute-start.8 = (bf16[2,208,256]{2,1,0:T(8,128)(2,1)S(1)}, bf16[2,208,256]{2,1,0:T(8,128)(2,1)S(1)}, u32[]{:S(2)}, u32[]{:S(2)}) collective-permute-start(bf16[2,208,256]{2,1,0:T(8,128)(2,1)S(1)} %get-tuple-element.82), channel_id=1, source_target_pairs={{0,2},{1,3},{2,0},{3,1},{4,6},{5,7},{6,4},{7,5},{8,10},{9,11},{10,... | collective-permute-start | bytes 638984 | tf_op jit(solution)/shard_map/ppermute | solution.py:366
  65.5 0.0 collective-permute-start.9
  65.5 0.0 collective-permute-done.10.refs_4_
  65.5 1.3 %collective-permute-start.12 = (f32[264,128]{1,0:T(8,128)S(1)}, f32[264,128]{1,0:T(8,128)S(1)}, u32[]{:S(2)}, u32[]{:S(2)}) collective-permute-start(f32[264,128]{1,0:T(8,128)S(1)} %get-tuple-element.94), channel_id=1, source_target_pairs={{0,4},{4,0},{1,5},{5,1},{2,6},{6,2},{3,7},{7,3},{8,12},{12,8},{9,1... | collective-permute-start | bytes 405512 | tf_op jit(solution)/shard_map/ppermute | solution.py:577
  66.7 4.3 %collective-permute-done.11.refs_6_ = bf16[2,208,256]{2,1,0:T(8,128)(2,1)S(1)} collective-permute-done((bf16[2,208,256]{2,1,0:T(8,128)(2,1)S(1)}, bf16[2,208,256]{2,1,0:T(8,128)(2,1)S(1)}, u32[]{:S(2)}, u32[]{:S(2)}) %collective-permute-start.11) | collective-permute-done | bytes 213024 | tf_op jit(solution)/shard_map/ppermute | solution.py:366
  71.1 0.0 copy-start.2
  71.1 3.2 %shard_map.201 = (bf16[2,360,1024]{2,1,0:T(8,128)(2,1)S(1)}, bf16[2,360,256]{2,1,0:T(8,128)(2,1)S(1)}, bf16[2,360,256]{2,1,0:T(8,128)(2,1)S(1)}, f32[8,128]{1,0:T(8,128)S(1)}) custom-call(s32[1,4]{1,0:T(1,128)S(1)} %copy-done.11, bf16[1,1,4,360,1024]{4,3,2,1,0:T(8,128)(2,1)S(1)} %copy-done, bf16[720,1024]{1,0:T(8,128)(2,1)} %refs_2_.9, ...), custom_call_target="tpu_custom_call" | custom-call | flops 1024 | bytes 1024 | tf_op jit(solution)/shard_map/pallas_call | solution.py:339
  74.3 3.2 %collective-permute-start.15 = (bf16[2,360,256]{2,1,0:T(8,128)(2,1)S(1)}, bf16[2,360,256]{2,1,0:T(8,128)(2,1)S(1)}, u32[]{:S(2)}, u32[]{:S(2)}) collective-permute-start(bf16[2,360,256]{2,1,0:T(8,128)(2,1)S(1)} %get-tuple-element.102.refs_3_), channel_id=1, source_target_pairs={{0,4},{1,5},{2,6},{3,7},{8,12},{9,13},{10,14},{11,15},{16,20},{17,... | collective-permute-start | bytes 1105928 | tf_op jit(solution)/shard_map/ppermute | solution.py:564
  77.5 0.0 collective-permute-done.7.refs_4_
  77.5 2.7 %collective-permute-start.16 = (bf16[2,360,256]{2,1,0:T(8,128)(2,1)S(1)}, bf16[2,360,256]{2,1,0:T(8,128)(2,1)S(1)}, u32[]{:S(2)}, u32[]{:S(2)}) collective-permute-start(bf16[2,360,256]{2,1,0:T(8,128)(2,1)S(1)} %get-tuple-element.103.refs_4_), channel_id=1, source_target_pairs={{0,4},{1,5},{2,6},{3,7},{8,12},{9,13},{10,14},{11,15},{16,20},{17,... | collective-permute-start | bytes 1105928 | tf_op jit(solution)/shard_map/ppermute | solution.py:564
  80.2 2.3 %shard_map.202 = (bf16[2,360,1024]{2,1,0:T(8,128)(2,1)S(1)}, f32[8,128]{1,0:T(8,128)S(1)}) custom-call(bf16[2,360,1024]{2,1,0:T(8,128)(2,1)S(1)} %get-tuple-element.88.refs_0_.refs_7_, bf16[1024,1024]{1,0:T(8,128)(2,1)S(1)} %copy-done.2, f32[8,128]{1,0:T(8,128)S(1)} %get-tuple-element.89.refs_2_), custom_call_target="tpu_custom_call" | custom-call | flops 1024 | bytes 1024 | tf_op jit(solution)/shard_map/pallas_call | solution.py:339
  82.6 0.0 collective-permute-done.8.refs_5_
  82.6 0.0 collective-permute-done.9.refs_6_
  82.6 2.2 %shard_map.203 = (bf16[1,360,1024]{2,1,0:T(8,128)(2,1)S(1)}, bf16[1,360,512]{2,1,0:T(8,128)(2,1)S(1)}, f32[8,128]{1,0:T(8,128)S(1)}) custom-call(s32[1,4]{1,0:T(1,128)S(1)} %copy-done.11, bf16[1,1,4,360,1024]{4,3,2,1,0:T(8,128)(2,1)S(1)} %copy-done, bf16[720,1024]{1,0:T(8,128)(2,1)} %refs_2_.9, bf16[2,208,256]{2,1,0:T(8,128)(2,1)S(1)} %get-tuple-element.80.refs_3_, ...), custom_call_target="tpu_custom_call" | custom-call | flops 1024 | bytes 1024 | tf_op jit(solution)/shard_map/pallas_call | solution.py:339
  84.8 3.0 %collective-permute-start.14 = (bf16[1,360,512]{2,1,0:T(8,128)(2,1)S(1)}, bf16[1,360,512]{2,1,0:T(8,128)(2,1)S(1)}, u32[]{:S(2)}, u32[]{:S(2)}) collective-permute-start(bf16[1,360,512]{2,1,0:T(8,128)(2,1)S(1)} %get-tuple-element.100.refs_3_), channel_id=1, source_target_pairs={{0,4},{1,5},{2,6},{3,7},{8,12},{9,13},{10,14},{11,15},{16,20},{17,... | collective-permute-start | bytes 1105928 | tf_op jit(solution)/shard_map/ppermute | solution.py:564
  87.8 2.2 %shard_map.204 = (bf16[1,360,1024]{2,1,0:T(8,128)(2,1)S(1)}, bf16[1,360,512]{2,1,0:T(8,128)(2,1)S(1)}, f32[8,128]{1,0:T(8,128)S(1)}) custom-call(s32[1,4]{1,0:T(1,128)S(1)} %copy-done.11, bf16[1,1,4,360,1024]{4,3,2,1,0:T(8,128)(2,1)S(1)} %copy-done, bf16[720,1024]{1,0:T(8,128)(2,1)} %refs_2_.9, bf16[2,208,256]{2,1,0:T(8,128)(2,1)S(1)} %get-tuple-element.80.refs_3_, ...), custom_call_target="tpu_custom_call" | custom-call | flops 1024 | bytes 1024 | tf_op jit(solution)/shard_map/pallas_call | solution.py:339
  90.0 1.5 %collective-permute-start.13 = (bf16[1,360,512]{2,1,0:T(8,128)(2,1)S(1)}, bf16[1,360,512]{2,1,0:T(8,128)(2,1)S(1)}, u32[]{:S(2)}, u32[]{:S(2)}) collective-permute-start(bf16[1,360,512]{2,1,0:T(8,128)(2,1)S(1)} %get-tuple-element.98.refs_3_), channel_id=1, source_target_pairs={{0,4},{1,5},{2,6},{3,7},{8,12},{9,13},{10,14},{11,15},{16,20},{17,... | collective-permute-start | bytes 1105928 | tf_op jit(solution)/shard_map/ppermute | solution.py:564
  91.6 0.1 collective-permute-start.17
  91.7 1.3 %collective-permute-done.17 = f32[264,128]{1,0:T(8,128)S(1)} collective-permute-done((f32[264,128]{1,0:T(8,128)S(1)}, f32[264,128]{1,0:T(8,128)S(1)}, u32[]{:S(2)}, u32[]{:S(2)}) %collective-permute-start.17) | collective-permute-done | bytes 135200 | tf_op jit(solution)/shard_map/ppermute | solution.py:581
  93.0 1.6 %collective-permute-start.18 = (f32[264,128]{1,0:T(8,128)S(1)}, f32[264,128]{1,0:T(8,128)S(1)}, u32[]{:S(2)}, u32[]{:S(2)}) collective-permute-start(f32[264,128]{1,0:T(8,128)S(1)} %add.10.refs_9_), channel_id=1, source_target_pairs={{0,16},{8,24},{16,0},{24,8},{1,17},{9,25},{17,1},{25,9},{2,18},{10... | collective-permute-start | bytes 405512 | tf_op jit(solution)/shard_map/ppermute | solution.py:581
  95.2 1.2 %shard_map.205 = (bf16[1,360,1024]{2,1,0:T(8,128)(2,1)S(1)}, f32[8,128]{1,0:T(8,128)S(1)}) custom-call(bf16[1,360,1024]{2,1,0:T(8,128)(2,1)S(1)} %get-tuple-element.93.refs_0_.refs_5_, bf16[1024,1024]{1,0:T(8,128)(2,1)S(1)} %copy-done.2, f32[264,128]{1,0:T(8,128)S(1)} %add.9.refs_2_, f32[8,128]{1,0:T(8,128)S(1)} %get-tuple-element.95.refs_3_), custom_call_target="tpu_custom_call" | custom-call | flops 1024 | bytes 1024 | tf_op jit(solution)/shard_map/pallas_call | solution.py:339
  96.4 0.0 copy-start.1
  96.4 0.0 copy-start.14
  96.4 1.2 %shard_map.206 = (bf16[1,360,1024]{2,1,0:T(8,128)(2,1)S(1)}, f32[8,128]{1,0:T(8,128)S(1)}) custom-call(bf16[1,360,1024]{2,1,0:T(8,128)(2,1)S(1)} %get-tuple-element.92.refs_0_.refs_5_, bf16[1024,1024]{1,0:T(8,128)(2,1)S(1)} %copy-done.2, f32[8,128]{1,0:T(8,128)S(1)} %get-tuple-element.96.refs_2_), custom_call_target="tpu_custom_call" | custom-call | flops 1024 | bytes 1024 | tf_op jit(solution)/shard_map/pallas_call | solution.py:339
  97.6 0.0 collective-permute-done.15.refs_5_
  97.6 0.0 collective-permute-done.16.refs_6_
  97.6 0.4 copy-done.1
  98.0 4.8 %shard_map.207 = (bf16[1,1,4,360,1024]{4,3,2,1,0:T(8,128)(2,1)}, f32[8,128]{1,0:T(8,128)S(1)}) custom-call(s32[1]{0:T(128)S(6)} %copy.25.refs_0_, f32[16]{0:T(128)S(1)} %copy-done.14, bf16[2,360,1024]{2,1,0:T(8,128)(2,1)S(1)} %get-tuple-element.101.refs_2_, bf16[2,360,256]{2,1,0:T(8,128)(2,1)S(1)} %get-tuple-element.102.refs_3_, ...), custom_call_target="tpu_custom_call" | custom-call | flops 1024 | bytes 1024 | tf_op jit(solution)/shard_map/pallas_call | solution.py:339
  102.8 0.0 collective-permute-done.18
  102.9 0.0 collective-permute-done.14.refs_4_
  102.9 3.1 %shard_map.208 = (bf16[1,1,4,360,1024]{4,3,2,1,0:T(8,128)(2,1)}, f32[8,128]{1,0:T(8,128)S(1)}) custom-call(s32[1]{0:T(128)S(6)} %copy.25.refs_0_, f32[16]{0:T(128)S(1)} %copy-done.14, bf16[1,360,1024]{2,1,0:T(8,128)(2,1)S(1)} %get-tuple-element.99.refs_2_, bf16[1,360,512]{2,1,0:T(8,128)(2,1)S(1)} %get-tuple-element.100.refs_3_, ...), custom_call_target="tpu_custom_call", output_to_operand_aliasing={{0}: (7, {})} | custom-call | flops 1024 | bytes 1024 | tf_op jit(solution)/shard_map/pallas_call | solution.py:339
  105.9 0.8 shard_map.209
  106.8 3.1 %shard_map.210 = (bf16[1,1,4,360,1024]{4,3,2,1,0:T(8,128)(2,1)}, f32[8,128]{1,0:T(8,128)}) custom-call(s32[1]{0:T(128)S(6)} %copy.25.refs_0_, f32[16]{0:T(128)S(1)} %copy-done.14, bf16[1,360,1024]{2,1,0:T(8,128)(2,1)S(1)} %get-tuple-element.97.refs_2_, bf16[1,360,512]{2,1,0:T(8,128)(2,1)S(1)} %get-tuple-element.98.refs_3_, ...), custom_call_target="tpu_custom_call", output_to_operand_aliasing={{0}: (7, {})} | custom-call | flops 1024 | bytes 1024 | tf_op jit(solution)/shard_map/pallas_call | solution.py:339
  (25 shorter events, 0.1 us)
Async XLA Ops:
  0.6 0.7 copy-start.10
  4.9 12.6 %collective-permute-start = (bf16[2,208,256]{2,1,0:T(8,128)(2,1)S(1)}, bf16[2,208,256]{2,1,0:T(8,128)(2,1)S(1)}, u32[]{:S(2)}, u32[]{:S(2)}) collective-permute-start(bf16[2,208,256]{2,1,0:T(8,128)(2,1)S(1)} %get-tuple-element.58), channel_id=1, source_target_pairs={{0,2},{1,3},{2,0},{3,1},{4,6},{5,7},{6,4},{7,5},{8,10},{9,11},{10,... | collective-permute-start | bytes 638984 | tf_op jit(solution)/shard_map/ppermute | solution.py:366
  7.6 22.0 %collective-permute-start.4 = (bf16[2,208,256]{2,1,0:T(8,128)(2,1)S(1)}, bf16[2,208,256]{2,1,0:T(8,128)(2,1)S(1)}, u32[]{:S(2)}, u32[]{:S(2)}) collective-permute-start(bf16[2,208,256]{2,1,0:T(8,128)(2,1)S(1)} %get-tuple-element.68), channel_id=1, source_target_pairs={{0,1},{1,2},{2,3},{3,0},{4,5},{5,6},{6,7},{7,4},{8,9},{9,10},{10,1... | collective-permute-start | bytes 638984 | tf_op jit(solution)/shard_map/ppermute | solution.py:366
  7.6 22.0 %collective-permute-start.5 = (bf16[2,208,256]{2,1,0:T(8,128)(2,1)S(1)}, bf16[2,208,256]{2,1,0:T(8,128)(2,1)S(1)}, u32[]{:S(2)}, u32[]{:S(2)}) collective-permute-start(bf16[2,208,256]{2,1,0:T(8,128)(2,1)S(1)} %get-tuple-element.69), channel_id=1, source_target_pairs={{0,3},{1,0},{2,1},{3,2},{4,7},{5,4},{6,5},{7,6},{8,11},{9,8},{10,9... | collective-permute-start | bytes 638984 | tf_op jit(solution)/shard_map/ppermute | solution.py:366
  17.5 11.9 %copy-start.8 = (bf16[2,4,64,64]{3,2,1,0:T(8,128)(2,1)S(1)}, bf16[2,4,64,64]{3,2,1,0:T(8,128)(2,1)}, u32[]{:S(2)}) copy-start(bf16[2,4,64,64]{3,2,1,0:T(8,128)(2,1)} %refs_0_.11) | copy-start | bytes 196612
  17.5 11.9 %copy-start.9 = (bf16[2,4,64,64]{3,2,1,0:T(8,128)(2,1)S(1)}, bf16[2,4,64,64]{3,2,1,0:T(8,128)(2,1)}, u32[]{:S(2)}) copy-start(bf16[2,4,64,64]{3,2,1,0:T(8,128)(2,1)} %refs_1_.16) | copy-start | bytes 196612
  17.5 12.1 %copy-start.4 = (bf16[736,832]{1,0:T(8,128)(2,1)S(1)}, bf16[736,832]{1,0:T(8,128)(2,1)}, u32[]{:S(2)}) copy-start(bf16[736,832]{1,0:T(8,128)(2,1)} %constant.9.clone.refs_4_) | copy-start | bytes 3674116
  17.5 12.1 %copy-start.12 = (f32[2,256]{1,0:T(2,128)S(1)}, f32[2,256]{1,0:T(2,128)}, u32[]{:S(2)}) copy-start(f32[2,256]{1,0:T(2,128)} %refs_6_.5) | copy-start | bytes 6148
  17.5 12.1 %copy-start.13 = (f32[2,256]{1,0:T(2,128)S(1)}, f32[2,256]{1,0:T(2,128)}, u32[]{:S(2)}) copy-start(f32[2,256]{1,0:T(2,128)} %refs_8_.7) | copy-start | bytes 6148
  21.2 11.8 %copy-start.5 = (bf16[4,208,736]{2,1,0:T(8,128)(2,1)S(1)}, bf16[4,208,736]{2,1,0:T(8,128)(2,1)}, u32[]{:S(2)}) copy-start(bf16[4,208,736]{2,1,0:T(8,128)(2,1)} %constant.10.clone.refs_1_) | copy-start | bytes 3674116
  21.2 21.5 %collective-permute-start.1 = (bf16[2,208,256]{2,1,0:T(8,128)(2,1)S(1)}, bf16[2,208,256]{2,1,0:T(8,128)(2,1)S(1)}, u32[]{:S(2)}, u32[]{:S(2)}) collective-permute-start(bf16[2,208,256]{2,1,0:T(8,128)(2,1)S(1)} %get-tuple-element.61), channel_id=1, source_target_pairs={{0,1},{1,2},{2,3},{3,0},{4,5},{5,6},{6,7},{7,4},{8,9},{9,10},{10,1... | collective-permute-start | bytes 638984 | tf_op jit(solution)/shard_map/ppermute | solution.py:366
  25.1 28.5 %collective-permute-start.2 = (bf16[2,208,256]{2,1,0:T(8,128)(2,1)S(1)}, bf16[2,208,256]{2,1,0:T(8,128)(2,1)S(1)}, u32[]{:S(2)}, u32[]{:S(2)}) collective-permute-start(bf16[2,208,256]{2,1,0:T(8,128)(2,1)S(1)} %get-tuple-element.62), channel_id=1, source_target_pairs={{0,2},{1,3},{2,0},{3,1},{4,6},{5,7},{6,4},{7,5},{8,10},{9,11},{10,... | collective-permute-start | bytes 638984 | tf_op jit(solution)/shard_map/ppermute | solution.py:366
  29.4 26.6 %collective-permute-start.3 = (bf16[2,208,256]{2,1,0:T(8,128)(2,1)S(1)}, bf16[2,208,256]{2,1,0:T(8,128)(2,1)S(1)}, u32[]{:S(2)}, u32[]{:S(2)}) collective-permute-start(bf16[2,208,256]{2,1,0:T(8,128)(2,1)S(1)} %get-tuple-element.63), channel_id=1, source_target_pairs={{0,3},{1,0},{2,1},{3,2},{4,7},{5,4},{6,5},{7,6},{8,11},{9,8},{10,9... | collective-permute-start | bytes 638984 | tf_op jit(solution)/shard_map/ppermute | solution.py:366
  34.1 25.3 %copy-start.7 = (bf16[1,1,4,2,368,256]{5,4,3,2,1,0:T(8,128)(2,1)S(1)}, bf16[1,1,4,2,368,256]{5,4,3,2,1,0:T(8,128)(2,1)}, u32[]{:S(2)}) copy-start(bf16[1,1,4,2,368,256]{5,4,3,2,1,0:T(8,128)(2,1)} %param.31) | copy-start | bytes 4521988
  34.1 26.6 %collective-permute-start.6 = (bf16[2,208,256]{2,1,0:T(8,128)(2,1)S(1)}, bf16[2,208,256]{2,1,0:T(8,128)(2,1)S(1)}, u32[]{:S(2)}, u32[]{:S(2)}) collective-permute-start(bf16[2,208,256]{2,1,0:T(8,128)(2,1)S(1)} %get-tuple-element.75), channel_id=1, source_target_pairs={{0,2},{1,3},{2,0},{3,1},{4,6},{5,7},{6,4},{7,5},{8,10},{9,11},{10,... | collective-permute-start | bytes 638984 | tf_op jit(solution)/shard_map/ppermute | solution.py:366
  34.8 30.7 %collective-permute-start.10 = (bf16[2,208,256]{2,1,0:T(8,128)(2,1)S(1)}, bf16[2,208,256]{2,1,0:T(8,128)(2,1)S(1)}, u32[]{:S(2)}, u32[]{:S(2)}) collective-permute-start(bf16[2,208,256]{2,1,0:T(8,128)(2,1)S(1)} %get-tuple-element.85), channel_id=1, source_target_pairs={{0,1},{1,2},{2,3},{3,0},{4,5},{5,6},{6,7},{7,4},{8,9},{9,10},{10,1... | collective-permute-start | bytes 638984 | tf_op jit(solution)/shard_map/ppermute | solution.py:366
  42.6 28.4 %collective-permute-start.11 = (bf16[2,208,256]{2,1,0:T(8,128)(2,1)S(1)}, bf16[2,208,256]{2,1,0:T(8,128)(2,1)S(1)}, u32[]{:S(2)}, u32[]{:S(2)}) collective-permute-start(bf16[2,208,256]{2,1,0:T(8,128)(2,1)S(1)} %get-tuple-element.86), channel_id=1, source_target_pairs={{0,3},{1,0},{2,1},{3,2},{4,7},{5,4},{6,5},{7,6},{8,11},{9,8},{10,9... | collective-permute-start | bytes 638984 | tf_op jit(solution)/shard_map/ppermute | solution.py:366
  59.4 11.7 %copy-start = (bf16[1,1,4,360,1024]{4,3,2,1,0:T(8,128)(2,1)S(1)}, bf16[1,1,4,360,1024]{4,3,2,1,0:T(8,128)(2,1)}, u32[]{:S(2)}) copy-start(bf16[1,1,4,360,1024]{4,3,2,1,0:T(8,128)(2,1)} %refs_1_.20) | copy-start | bytes 8847364
  59.4 11.7 %copy-start.3 = (bf16[1024,512]{1,0:T(8,128)(2,1)S(1)}, bf16[1024,512]{1,0:T(8,128)(2,1)}, u32[]{:S(2)}) copy-start(bf16[1024,512]{1,0:T(8,128)(2,1)} %refs_8_.10) | copy-start | bytes 3145732
  59.4 11.7 %copy-start.6 = (bf16[360,208]{1,0:T(8,128)(2,1)S(1)}, bf16[360,208]{1,0:T(8,128)(2,1)}, u32[]{:S(2)}) copy-start(bf16[360,208]{1,0:T(8,128)(2,1)} %constant.11.clone.refs_7_) | copy-start | bytes 449284
  59.4 11.6 %copy-start.11 = (s32[1,4]{1,0:T(1,128)S(1)}, s32[1,4]{1,0:T(1,128)}, u32[]{:S(2)}) copy-start(s32[1,4]{1,0:T(1,128)} %refs_0_.14) | copy-start | bytes 52
  61.8 15.7 %collective-permute-start.7 = (bf16[2,208,256]{2,1,0:T(8,128)(2,1)S(1)}, bf16[2,208,256]{2,1,0:T(8,128)(2,1)S(1)}, u32[]{:S(2)}, u32[]{:S(2)}) collective-permute-start(bf16[2,208,256]{2,1,0:T(8,128)(2,1)S(1)} %get-tuple-element.81), channel_id=1, source_target_pairs={{0,1},{1,2},{2,3},{3,0},{4,5},{5,6},{6,7},{7,4},{8,9},{9,10},{10,1... | collective-permute-start | bytes 638984 | tf_op jit(solution)/shard_map/ppermute | solution.py:366
  61.8 20.8 %collective-permute-start.8 = (bf16[2,208,256]{2,1,0:T(8,128)(2,1)S(1)}, bf16[2,208,256]{2,1,0:T(8,128)(2,1)S(1)}, u32[]{:S(2)}, u32[]{:S(2)}) collective-permute-start(bf16[2,208,256]{2,1,0:T(8,128)(2,1)S(1)} %get-tuple-element.82), channel_id=1, source_target_pairs={{0,2},{1,3},{2,0},{3,1},{4,6},{5,7},{6,4},{7,5},{8,10},{9,11},{10,... | collective-permute-start | bytes 638984 | tf_op jit(solution)/shard_map/ppermute | solution.py:366
  65.5 17.1 %collective-permute-start.9 = (bf16[2,208,256]{2,1,0:T(8,128)(2,1)S(1)}, bf16[2,208,256]{2,1,0:T(8,128)(2,1)S(1)}, u32[]{:S(2)}, u32[]{:S(2)}) collective-permute-start(bf16[2,208,256]{2,1,0:T(8,128)(2,1)S(1)} %get-tuple-element.83), channel_id=1, source_target_pairs={{0,3},{1,0},{2,1},{3,2},{4,7},{5,4},{6,5},{7,6},{8,11},{9,8},{10,9... | collective-permute-start | bytes 638984 | tf_op jit(solution)/shard_map/ppermute | solution.py:366
  65.5 26.1 %collective-permute-start.12 = (f32[264,128]{1,0:T(8,128)S(1)}, f32[264,128]{1,0:T(8,128)S(1)}, u32[]{:S(2)}, u32[]{:S(2)}) collective-permute-start(f32[264,128]{1,0:T(8,128)S(1)} %get-tuple-element.94), channel_id=1, source_target_pairs={{0,4},{4,0},{1,5},{5,1},{2,6},{6,2},{3,7},{7,3},{8,12},{12,8},{9,1... | collective-permute-start | bytes 405512 | tf_op jit(solution)/shard_map/ppermute | solution.py:577
  71.1 9.2 %copy-start.2 = (bf16[1024,1024]{1,0:T(8,128)(2,1)S(1)}, bf16[1024,1024]{1,0:T(8,128)(2,1)}, u32[]{:S(2)}) copy-start(bf16[1024,1024]{1,0:T(8,128)(2,1)} %refs_1_.22) | copy-start | bytes 6291460
  74.3 23.3 %collective-permute-start.15 = (bf16[2,360,256]{2,1,0:T(8,128)(2,1)S(1)}, bf16[2,360,256]{2,1,0:T(8,128)(2,1)S(1)}, u32[]{:S(2)}, u32[]{:S(2)}) collective-permute-start(bf16[2,360,256]{2,1,0:T(8,128)(2,1)S(1)} %get-tuple-element.102.refs_3_), channel_id=1, source_target_pairs={{0,4},{1,5},{2,6},{3,7},{8,12},{9,13},{10,14},{11,15},{16,20},{17,... | collective-permute-start | bytes 1105928 | tf_op jit(solution)/shard_map/ppermute | solution.py:564
  77.5 20.1 %collective-permute-start.16 = (bf16[2,360,256]{2,1,0:T(8,128)(2,1)S(1)}, bf16[2,360,256]{2,1,0:T(8,128)(2,1)S(1)}, u32[]{:S(2)}, u32[]{:S(2)}) collective-permute-start(bf16[2,360,256]{2,1,0:T(8,128)(2,1)S(1)} %get-tuple-element.103.refs_4_), channel_id=1, source_target_pairs={{0,4},{1,5},{2,6},{3,7},{8,12},{9,13},{10,14},{11,15},{16,20},{17,... | collective-permute-start | bytes 1105928 | tf_op jit(solution)/shard_map/ppermute | solution.py:564
  84.8 18.1 %collective-permute-start.14 = (bf16[1,360,512]{2,1,0:T(8,128)(2,1)S(1)}, bf16[1,360,512]{2,1,0:T(8,128)(2,1)S(1)}, u32[]{:S(2)}, u32[]{:S(2)}) collective-permute-start(bf16[1,360,512]{2,1,0:T(8,128)(2,1)S(1)} %get-tuple-element.100.refs_3_), channel_id=1, source_target_pairs={{0,4},{1,5},{2,6},{3,7},{8,12},{9,13},{10,14},{11,15},{16,20},{17,... | collective-permute-start | bytes 1105928 | tf_op jit(solution)/shard_map/ppermute | solution.py:564
  90.0 16.7 %collective-permute-start.13 = (bf16[1,360,512]{2,1,0:T(8,128)(2,1)S(1)}, bf16[1,360,512]{2,1,0:T(8,128)(2,1)S(1)}, u32[]{:S(2)}, u32[]{:S(2)}) collective-permute-start(bf16[1,360,512]{2,1,0:T(8,128)(2,1)S(1)} %get-tuple-element.98.refs_3_), channel_id=1, source_target_pairs={{0,4},{1,5},{2,6},{3,7},{8,12},{9,13},{10,14},{11,15},{16,20},{17,... | collective-permute-start | bytes 1105928 | tf_op jit(solution)/shard_map/ppermute | solution.py:564
  91.6 1.4 %collective-permute-start.17 = (f32[264,128]{1,0:T(8,128)S(1)}, f32[264,128]{1,0:T(8,128)S(1)}, u32[]{:S(2)}, u32[]{:S(2)}) collective-permute-start(f32[264,128]{1,0:T(8,128)S(1)} %add.9.refs_2_), channel_id=1, source_target_pairs={{0,8},{8,0},{16,24},{24,16},{1,9},{9,1},{17,25},{25,17},{2,10},{10... | collective-permute-start | bytes 405512 | tf_op jit(solution)/shard_map/ppermute | solution.py:581
  93.0 9.8 %collective-permute-start.18 = (f32[264,128]{1,0:T(8,128)S(1)}, f32[264,128]{1,0:T(8,128)S(1)}, u32[]{:S(2)}, u32[]{:S(2)}) collective-permute-start(f32[264,128]{1,0:T(8,128)S(1)} %add.10.refs_9_), channel_id=1, source_target_pairs={{0,16},{8,24},{16,0},{24,8},{1,17},{9,25},{17,1},{25,9},{2,18},{10... | collective-permute-start | bytes 405512 | tf_op jit(solution)/shard_map/ppermute | solution.py:581
  96.4 1.6 %copy-start.1 = (bf16[1024,1024]{1,0:T(8,128)(2,1)S(1)}, bf16[1024,1024]{1,0:T(8,128)(2,1)}, u32[]{:S(2)}) copy-start(bf16[1024,1024]{1,0:T(8,128)(2,1)} %refs_6_.7) | copy-start | bytes 6291460
  96.4 1.6 %copy-start.14 = (f32[16]{0:T(128)S(1)}, f32[16]{0:T(128)}, u32[]{:S(2)}) copy-start(f32[16]{0:T(128)} %refs_1_.25) | copy-start | bytes 196

commit v6 on v5

--- a/solution.py
+++ b/solution.py
@@ -587,7 +587,7 @@
 
 PLAN = (
     ("compress", 0, 2, False),
-    ("received", 0, 2, False),
+    ("received", 0, 1, False),
     ("compress", 2, 2, False),
     ("blocks", 0, 0, False),
     ("mix", 0, 2, False),
@@ -600,11 +600,11 @@
     ("query", 0, 2, False),
     ("expand", 2, 1, False),
     ("expand", 3, 1, False),
-    ("add", 0, 0, False),
     ("query", 2, 1, False),
     ("query", 3, 1, False),
     ("add", 0, 0, False),
     ("attend", 0, 2, False),
+    ("add", 0, 0, False),
     ("attend", 2, 1, False),
     ("add", 0, 0, False),
     ("sum", 0, 0, False),

time: 110 us -> 110 us (level)
  transfers between devices with their start and end apart: 19 -> 19, of which waited for: 6 -> 7; matrix products, arithmetic and copies ran while one was open for 0% -> 0% of each run, Pallas kernels for 32% -> 32%
where the time goes in v6:
time: 110 us; the launch traced here: 109 us
  Pallas kernels  41.5 us (38%)
  waiting for transfers between devices  32.8 us (30%)
  starting transfers between devices  32.2 us (29%)
  between operations  1.64 us (1%)
  local copies, waits for them, and re-layouts  1.1 us (1%)
    pallas_call x18, Pallas kernels, call(): pl.pallas_call(kernel, grid_spec=pltpu.PrefetchScalarGridSpec(num_scalar_...  41.5 us
    ppermute x12, waiting for transfers between devices, swap_blocks(): lax.ppermute(part, 'lon', [(i, (i + shift) % count) for i in range(count)])  31.4 us
    ppermute x12, starting transfers between devices, swap_blocks(): lax.ppermute(part, 'lon', [(i, (i + shift) % count) for i in range(count)])  18.5 us
    ppermute x4, starting transfers between devices, fused_body(): earlier = [lax.ppermute(part, 'frame', [(0, 1)]) for part in keyval]  10.6 us
    ppermute x3, starting transfers between devices, fused_body(): crossing = lax.ppermute(summed, *rounds.pop(0))  3.15 us
  transfers between devices with their start and end apart: 19, of which 7 were waited for; matrix products, arithmetic and copies ran while one was open for 0% of the time, Pallas kernels for 32%

profile of v6, /device:TPU:8, one launch (start us, length us, event | category | flops | bytes accessed | tf_op | source)
XLA Modules:
  0.0 109.3 jit_solution(5866031741473643677)
XLA Ops:
  0.6 0.0 copy-start.10
  0.6 0.6 copy-done.10
  1.3 3.6 %shard_map.193 = (bf16[2,208,256]{2,1,0:T(8,128)(2,1)S(1)}, bf16[2,208,256]{2,1,0:T(8,128)(2,1)S(1)}, bf16[2,208,256]{2,1,0:T(8,128)(2,1)S(1)}, bf16[2,208,256]{2,1,0:T(8,128)(2,1)S(1)}, f32[8,128]{1,0:T(8,128)S(1)}) custom-call(s32[1,4]{1,0:T(1,128)S(1)} %copy-done.10, bf16[1,1,4,360,1024]{4,3,2,1,0:T(8,128)(2,1)} %refs_1_.20, bf16[720,1024]{1,0:T(8,128)(2,1)} %refs_2_.9, ...), custom_call_target="tpu_custom_call" | custom-call | flops 1024 | bytes 1024 | tf_op jit(solution)/shard_map/pallas_call | solution.py:339
  4.9 1.6 %collective-permute-start = (bf16[2,208,256]{2,1,0:T(8,128)(2,1)S(1)}, bf16[2,208,256]{2,1,0:T(8,128)(2,1)S(1)}, u32[]{:S(2)}, u32[]{:S(2)}) collective-permute-start(bf16[2,208,256]{2,1,0:T(8,128)(2,1)S(1)} %get-tuple-element.58), channel_id=1, source_target_pairs={{0,1},{1,2},{2,3},{3,0},{4,5},{5,6},{6,7},{7,4},{8,9},{9,10},{10,1... | collective-permute-start | bytes 638984 | tf_op jit(solution)/shard_map/ppermute | solution.py:366
  6.6 1.1 collective-permute-start.4
  7.6 1.9 %collective-permute-start.5 = (bf16[2,208,256]{2,1,0:T(8,128)(2,1)S(1)}, bf16[2,208,256]{2,1,0:T(8,128)(2,1)S(1)}, u32[]{:S(2)}, u32[]{:S(2)}) collective-permute-start(bf16[2,208,256]{2,1,0:T(8,128)(2,1)S(1)} %get-tuple-element.69), channel_id=1, source_target_pairs={{0,3},{1,0},{2,1},{3,2},{4,7},{5,4},{6,5},{7,6},{8,11},{9,8},{10,9... | collective-permute-start | bytes 638984 | tf_op jit(solution)/shard_map/ppermute | solution.py:366
  9.6 11.4 %collective-permute-done.refs_5_.refs_1_ = bf16[2,208,256]{2,1,0:T(8,128)(2,1)S(1)} collective-permute-done((bf16[2,208,256]{2,1,0:T(8,128)(2,1)S(1)}, bf16[2,208,256]{2,1,0:T(8,128)(2,1)S(1)}, u32[]{:S(2)}, u32[]{:S(2)}) %collective-permute-start) | collective-permute-done | bytes 213024 | tf_op jit(solution)/shard_map/ppermute | solution.py:366
  21.0 3.6 %shard_map.194 = (bf16[2,208,256]{2,1,0:T(8,128)(2,1)S(1)}, bf16[2,208,256]{2,1,0:T(8,128)(2,1)S(1)}, bf16[2,208,256]{2,1,0:T(8,128)(2,1)S(1)}, bf16[2,208,256]{2,1,0:T(8,128)(2,1)S(1)}, f32[8,128]{1,0:T(8,128)S(1)}) custom-call(s32[1,4]{1,0:T(1,128)S(1)} %copy-done.10, bf16[1,1,4,360,1024]{4,3,2,1,0:T(8,128)(2,1)} %refs_1_.20, bf16[720,1024]{1,0:T(8,128)(2,1)} %refs_2_.9, ...), custom_call_target="tpu_custom_call" | custom-call | flops 1024 | bytes 1024 | tf_op jit(solution)/shard_map/pallas_call | solution.py:339
  24.6 0.0 copy-start.5
  24.6 3.0 %collective-permute-start.1 = (bf16[2,208,256]{2,1,0:T(8,128)(2,1)S(1)}, bf16[2,208,256]{2,1,0:T(8,128)(2,1)S(1)}, u32[]{:S(2)}, u32[]{:S(2)}) collective-permute-start(bf16[2,208,256]{2,1,0:T(8,128)(2,1)S(1)} %get-tuple-element.61), channel_id=1, source_target_pairs={{0,1},{1,2},{2,3},{3,0},{4,5},{5,6},{6,7},{7,4},{8,9},{9,10},{10,1... | collective-permute-start | bytes 638984 | tf_op jit(solution)/shard_map/ppermute | solution.py:366
  27.6 0.0 collective-permute-start.2
  27.6 1.5 %collective-permute-start.3 = (bf16[2,208,256]{2,1,0:T(8,128)(2,1)S(1)}, bf16[2,208,256]{2,1,0:T(8,128)(2,1)S(1)}, u32[]{:S(2)}, u32[]{:S(2)}) collective-permute-start(bf16[2,208,256]{2,1,0:T(8,128)(2,1)S(1)} %get-tuple-element.63), channel_id=1, source_target_pairs={{0,3},{1,0},{2,1},{3,2},{4,7},{5,4},{6,5},{7,6},{8,11},{9,8},{10,9... | collective-permute-start | bytes 638984 | tf_op jit(solution)/shard_map/ppermute | solution.py:366
  29.1 0.2 shard_map.195
  29.3 3.3 %collective-permute-done.4.refs_2_ = bf16[2,208,256]{2,1,0:T(8,128)(2,1)S(1)} collective-permute-done((bf16[2,208,256]{2,1,0:T(8,128)(2,1)S(1)}, bf16[2,208,256]{2,1,0:T(8,128)(2,1)S(1)}, u32[]{:S(2)}, u32[]{:S(2)}) %collective-permute-start.4) | collective-permute-done | bytes 213024 | tf_op jit(solution)/shard_map/ppermute | solution.py:366
  32.7 3.2 %collective-permute-done.5.refs_3_ = bf16[2,208,256]{2,1,0:T(8,128)(2,1)S(1)} collective-permute-done((bf16[2,208,256]{2,1,0:T(8,128)(2,1)S(1)}, bf16[2,208,256]{2,1,0:T(8,128)(2,1)S(1)}, u32[]{:S(2)}, u32[]{:S(2)}) %collective-permute-start.5) | collective-permute-done | bytes 213024 | tf_op jit(solution)/shard_map/ppermute | solution.py:366
  35.8 3.4 %shard_map.196 = (bf16[2,736,256]{2,1,0:T(8,128)(2,1)S(1)}, bf16[2,736,256]{2,1,0:T(8,128)(2,1)S(1)}, f32[8,128]{1,0:T(8,128)S(1)}) custom-call(bf16[2,208,256]{2,1,0:T(8,128)(2,1)S(1)} %get-tuple-element.67.refs_0_, bf16[2,208,256]{2,1,0:T(8,128)(2,1)S(1)} %collective-permute-done.refs_5_.refs_1_, bf16[2,208,256]{2,1,0:T(8,128)(2,1)S(1)} %collective-permute-done.4.refs_2_, ...), custom_call_target="tpu_custom_call" | custom-call | flops 1024 | bytes 1024 | tf_op jit(solution)/shard_map/pallas_call | solution.py:339
  39.2 1.0 shard_map.197
  40.3 0.0 copy-start.7
  40.3 2.7 %collective-permute-start.6 = (bf16[2,208,256]{2,1,0:T(8,128)(2,1)S(1)}, bf16[2,208,256]{2,1,0:T(8,128)(2,1)S(1)}, u32[]{:S(2)}, u32[]{:S(2)}) collective-permute-start(bf16[2,208,256]{2,1,0:T(8,128)(2,1)S(1)} %get-tuple-element.75), channel_id=1, source_target_pairs={{0,2},{1,3},{2,0},{3,1},{4,6},{5,7},{6,4},{7,5},{8,10},{9,11},{10,... | collective-permute-start | bytes 638984 | tf_op jit(solution)/shard_map/ppermute | solution.py:366
  43.0 0.0 collective-permute-start.10
  43.0 0.0 collective-permute-done.1.refs_1_
  43.0 2.0 %collective-permute-start.11 = (bf16[2,208,256]{2,1,0:T(8,128)(2,1)S(1)}, bf16[2,208,256]{2,1,0:T(8,128)(2,1)S(1)}, u32[]{:S(2)}, u32[]{:S(2)}) collective-permute-start(bf16[2,208,256]{2,1,0:T(8,128)(2,1)S(1)} %get-tuple-element.86), channel_id=1, source_target_pairs={{0,3},{1,0},{2,1},{3,2},{4,7},{5,4},{6,5},{7,6},{8,11},{9,8},{10,9... | collective-permute-start | bytes 638984 | tf_op jit(solution)/shard_map/ppermute | solution.py:366
  45.1 3.8 %collective-permute-done.2.refs_2_ = bf16[2,208,256]{2,1,0:T(8,128)(2,1)S(1)} collective-permute-done((bf16[2,208,256]{2,1,0:T(8,128)(2,1)S(1)}, bf16[2,208,256]{2,1,0:T(8,128)(2,1)S(1)}, u32[]{:S(2)}, u32[]{:S(2)}) %collective-permute-start.2) | collective-permute-done | bytes 213024 | tf_op jit(solution)/shard_map/ppermute | solution.py:366
  48.8 5.3 %collective-permute-done.3.refs_3_ = bf16[2,208,256]{2,1,0:T(8,128)(2,1)S(1)} collective-permute-done((bf16[2,208,256]{2,1,0:T(8,128)(2,1)S(1)}, bf16[2,208,256]{2,1,0:T(8,128)(2,1)S(1)}, u32[]{:S(2)}, u32[]{:S(2)}) %collective-permute-start.3) | collective-permute-done | bytes 213024 | tf_op jit(solution)/shard_map/ppermute | solution.py:366
  54.1 3.4 %shard_map.198 = (bf16[2,736,256]{2,1,0:T(8,128)(2,1)S(1)}, bf16[2,736,256]{2,1,0:T(8,128)(2,1)S(1)}, f32[8,128]{1,0:T(8,128)S(1)}) custom-call(bf16[2,208,256]{2,1,0:T(8,128)(2,1)S(1)} %get-tuple-element.60.refs_0_, bf16[2,208,256]{2,1,0:T(8,128)(2,1)S(1)} %collective-permute-done.1.refs_1_, bf16[2,208,256]{2,1,0:T(8,128)(2,1)S(1)} %collective-permute-done.2.refs_2_, ...), custom_call_target="tpu_custom_call" | custom-call | flops 1024 | bytes 1024 | tf_op jit(solution)/shard_map/pallas_call | solution.py:339
  57.5 0.0 copy-start
  57.5 0.0 copy-start.3
  57.5 0.0 copy-start.6
  57.5 0.0 copy-start.11
  57.5 1.3 %shard_map.199 = (f32[264,128]{1,0:T(8,128)S(1)}, f32[8,128]{1,0:T(8,128)S(1)}) custom-call(bf16[2,736,256]{2,1,0:T(8,128)(2,1)S(1)} %get-tuple-element.76.refs_0_, bf16[2,736,256]{2,1,0:T(8,128)(2,1)S(1)} %get-tuple-element.77.refs_1_, bf16[4,2,368,256]{3,2,1,0:T(8,128)(2,1)S(1)} %bitcast.2, f32[8,128]{1,0:T(8,128)S(1)} %get-tuple-element.78.refs_3_), custom_call_target="tpu_custom_call" | custom-call | flops 1024 | bytes 1024 | tf_op jit(solution)/shard_map/pallas_call | solution.py:339
  58.8 0.0 collective-permute-done.6.refs_2_.refs_5_
  58.8 1.0 shard_map.200
  59.9 0.1 collective-permute-start.7
  59.9 3.6 %collective-permute-start.8 = (bf16[2,208,256]{2,1,0:T(8,128)(2,1)S(1)}, bf16[2,208,256]{2,1,0:T(8,128)(2,1)S(1)}, u32[]{:S(2)}, u32[]{:S(2)}) collective-permute-start(bf16[2,208,256]{2,1,0:T(8,128)(2,1)S(1)} %get-tuple-element.82), channel_id=1, source_target_pairs={{0,2},{1,3},{2,0},{3,1},{4,6},{5,7},{6,4},{7,5},{8,10},{9,11},{10,... | collective-permute-start | bytes 638984 | tf_op jit(solution)/shard_map/ppermute | solution.py:366
  63.5 0.9 collective-permute-start.9
  64.4 0.0 collective-permute-done.10.refs_4_
  64.4 1.5 %collective-permute-start.16 = (f32[264,128]{1,0:T(8,128)S(1)}, f32[264,128]{1,0:T(8,128)S(1)}, u32[]{:S(2)}, u32[]{:S(2)}) collective-permute-start(f32[264,128]{1,0:T(8,128)S(1)} %get-tuple-element.103), channel_id=1, source_target_pairs={{0,4},{4,0},{1,5},{5,1},{2,6},{6,2},{3,7},{7,3},{8,12},{12,8},{9,1... | collective-permute-start | bytes 405512 | tf_op jit(solution)/shard_map/ppermute | solution.py:577
  65.9 0.0 collective-permute-done.11.refs_6_
  66.0 0.0 copy-start.2
  66.0 3.2 %shard_map.201 = (bf16[2,360,1024]{2,1,0:T(8,128)(2,1)S(1)}, bf16[2,360,256]{2,1,0:T(8,128)(2,1)S(1)}, bf16[2,360,256]{2,1,0:T(8,128)(2,1)S(1)}, f32[8,128]{1,0:T(8,128)S(1)}) custom-call(s32[1,4]{1,0:T(1,128)S(1)} %copy-done.11, bf16[1,1,4,360,1024]{4,3,2,1,0:T(8,128)(2,1)S(1)} %copy-done, bf16[720,1024]{1,0:T(8,128)(2,1)} %refs_2_.9, ...), custom_call_target="tpu_custom_call" | custom-call | flops 1024 | bytes 1024 | tf_op jit(solution)/shard_map/pallas_call | solution.py:339
  69.2 2.5 %collective-permute-start.14 = (bf16[2,360,256]{2,1,0:T(8,128)(2,1)S(1)}, bf16[2,360,256]{2,1,0:T(8,128)(2,1)S(1)}, u32[]{:S(2)}, u32[]{:S(2)}) collective-permute-start(bf16[2,360,256]{2,1,0:T(8,128)(2,1)S(1)} %get-tuple-element.101.refs_3_), channel_id=1, source_target_pairs={{0,4},{1,5},{2,6},{3,7},{8,12},{9,13},{10,14},{11,15},{16,20},{17,... | collective-permute-start | bytes 1105928 | tf_op jit(solution)/shard_map/ppermute | solution.py:564
  71.7 4.5 %collective-permute-done.7.refs_4_ = bf16[2,208,256]{2,1,0:T(8,128)(2,1)S(1)} collective-permute-done((bf16[2,208,256]{2,1,0:T(8,128)(2,1)S(1)}, bf16[2,208,256]{2,1,0:T(8,128)(2,1)S(1)}, u32[]{:S(2)}, u32[]{:S(2)}) %collective-permute-start.7) | collective-permute-done | bytes 213024 | tf_op jit(solution)/shard_map/ppermute | solution.py:366
  76.2 3.4 %collective-permute-start.15 = (bf16[2,360,256]{2,1,0:T(8,128)(2,1)S(1)}, bf16[2,360,256]{2,1,0:T(8,128)(2,1)S(1)}, u32[]{:S(2)}, u32[]{:S(2)}) collective-permute-start(bf16[2,360,256]{2,1,0:T(8,128)(2,1)S(1)} %get-tuple-element.102.refs_4_), channel_id=1, source_target_pairs={{0,4},{1,5},{2,6},{3,7},{8,12},{9,13},{10,14},{11,15},{16,20},{17,... | collective-permute-start | bytes 1105928 | tf_op jit(solution)/shard_map/ppermute | solution.py:564
  79.6 2.3 %shard_map.202 = (bf16[2,360,1024]{2,1,0:T(8,128)(2,1)S(1)}, f32[8,128]{1,0:T(8,128)S(1)}) custom-call(bf16[2,360,1024]{2,1,0:T(8,128)(2,1)S(1)} %get-tuple-element.88.refs_0_.refs_7_, bf16[1024,1024]{1,0:T(8,128)(2,1)S(1)} %copy-done.2, f32[8,128]{1,0:T(8,128)S(1)} %get-tuple-element.89.refs_2_), custom_call_target="tpu_custom_call" | custom-call | flops 1024 | bytes 1024 | tf_op jit(solution)/shard_map/pallas_call | solution.py:339
  82.0 0.0 collective-permute-done.9.refs_6_
  82.0 2.2 %shard_map.203 = (bf16[1,360,1024]{2,1,0:T(8,128)(2,1)S(1)}, bf16[1,360,512]{2,1,0:T(8,128)(2,1)S(1)}, f32[8,128]{1,0:T(8,128)S(1)}) custom-call(s32[1,4]{1,0:T(1,128)S(1)} %copy-done.11, bf16[1,1,4,360,1024]{4,3,2,1,0:T(8,128)(2,1)S(1)} %copy-done, bf16[720,1024]{1,0:T(8,128)(2,1)} %refs_2_.9, bf16[2,208,256]{2,1,0:T(8,128)(2,1)S(1)} %get-tuple-element.80.refs_3_, ...), custom_call_target="tpu_custom_call" | custom-call | flops 1024 | bytes 1024 | tf_op jit(solution)/shard_map/pallas_call | solution.py:339
  84.2 3.2 %collective-permute-start.13 = (bf16[1,360,512]{2,1,0:T(8,128)(2,1)S(1)}, bf16[1,360,512]{2,1,0:T(8,128)(2,1)S(1)}, u32[]{:S(2)}, u32[]{:S(2)}) collective-permute-start(bf16[1,360,512]{2,1,0:T(8,128)(2,1)S(1)} %get-tuple-element.99.refs_3_), channel_id=1, source_target_pairs={{0,4},{1,5},{2,6},{3,7},{8,12},{9,13},{10,14},{11,15},{16,20},{17,... | collective-permute-start | bytes 1105928 | tf_op jit(solution)/shard_map/ppermute | solution.py:564
  87.4 2.2 %shard_map.204 = (bf16[1,360,1024]{2,1,0:T(8,128)(2,1)S(1)}, bf16[1,360,512]{2,1,0:T(8,128)(2,1)S(1)}, f32[8,128]{1,0:T(8,128)S(1)}) custom-call(s32[1,4]{1,0:T(1,128)S(1)} %copy-done.11, bf16[1,1,4,360,1024]{4,3,2,1,0:T(8,128)(2,1)S(1)} %copy-done, bf16[720,1024]{1,0:T(8,128)(2,1)} %refs_2_.9, bf16[2,208,256]{2,1,0:T(8,128)(2,1)S(1)} %get-tuple-element.80.refs_3_, ...), custom_call_target="tpu_custom_call" | custom-call | flops 1024 | bytes 1024 | tf_op jit(solution)/shard_map/pallas_call | solution.py:339
  89.6 1.5 %collective-permute-start.12 = (bf16[1,360,512]{2,1,0:T(8,128)(2,1)S(1)}, bf16[1,360,512]{2,1,0:T(8,128)(2,1)S(1)}, u32[]{:S(2)}, u32[]{:S(2)}) collective-permute-start(bf16[1,360,512]{2,1,0:T(8,128)(2,1)S(1)} %get-tuple-element.97.refs_3_), channel_id=1, source_target_pairs={{0,4},{1,5},{2,6},{3,7},{8,12},{9,13},{10,14},{11,15},{16,20},{17,... | collective-permute-start | bytes 1105928 | tf_op jit(solution)/shard_map/ppermute | solution.py:564
  91.1 0.0 collective-permute-done.16
  91.1 0.1 collective-permute-start.17
  91.2 1.3 %collective-permute-done.17 = f32[264,128]{1,0:T(8,128)S(1)} collective-permute-done((f32[264,128]{1,0:T(8,128)S(1)}, f32[264,128]{1,0:T(8,128)S(1)}, u32[]{:S(2)}, u32[]{:S(2)}) %collective-permute-start.17) | collective-permute-done | bytes 135200 | tf_op jit(solution)/shard_map/ppermute | solution.py:581
  92.6 1.6 %collective-permute-start.18 = (f32[264,128]{1,0:T(8,128)S(1)}, f32[264,128]{1,0:T(8,128)S(1)}, u32[]{:S(2)}, u32[]{:S(2)}) collective-permute-start(f32[264,128]{1,0:T(8,128)S(1)} %add.10.refs_8_), channel_id=1, source_target_pairs={{0,16},{8,24},{16,0},{24,8},{1,17},{9,25},{17,1},{25,9},{2,18},{10... | collective-permute-start | bytes 405512 | tf_op jit(solution)/shard_map/ppermute | solution.py:581
  94.8 1.2 %shard_map.205 = (bf16[1,360,1024]{2,1,0:T(8,128)(2,1)S(1)}, f32[8,128]{1,0:T(8,128)S(1)}) custom-call(bf16[1,360,1024]{2,1,0:T(8,128)(2,1)S(1)} %get-tuple-element.93.refs_0_.refs_5_, bf16[1024,1024]{1,0:T(8,128)(2,1)S(1)} %copy-done.2, f32[8,128]{1,0:T(8,128)S(1)} %get-tuple-element.94.refs_2_), custom_call_target="tpu_custom_call" | custom-call | flops 1024 | bytes 1024 | tf_op jit(solution)/shard_map/pallas_call | solution.py:339
  96.0 0.0 copy-start.1
  96.0 0.0 copy-start.14
  96.0 1.2 %shard_map.206 = (bf16[1,360,1024]{2,1,0:T(8,128)(2,1)S(1)}, f32[8,128]{1,0:T(8,128)S(1)}) custom-call(bf16[1,360,1024]{2,1,0:T(8,128)(2,1)S(1)} %get-tuple-element.92.refs_0_.refs_5_, bf16[1024,1024]{1,0:T(8,128)(2,1)S(1)} %copy-done.2, f32[8,128]{1,0:T(8,128)S(1)} %get-tuple-element.95.refs_2_), custom_call_target="tpu_custom_call" | custom-call | flops 1024 | bytes 1024 | tf_op jit(solution)/shard_map/pallas_call | solution.py:339
  97.2 0.0 collective-permute-done.14.refs_5_
  97.2 0.4 copy-done.1
  97.6 4.7 %shard_map.207 = (bf16[1,1,4,360,1024]{4,3,2,1,0:T(8,128)(2,1)}, f32[8,128]{1,0:T(8,128)S(1)}) custom-call(s32[1]{0:T(128)S(6)} %copy.25.refs_0_, f32[16]{0:T(128)S(1)} %copy-done.14, bf16[2,360,1024]{2,1,0:T(8,128)(2,1)S(1)} %get-tuple-element.100.refs_2_, bf16[2,360,256]{2,1,0:T(8,128)(2,1)S(1)} %get-tuple-element.101.refs_3_, ...), custom_call_target="tpu_custom_call" | custom-call | flops 1024 | bytes 1024 | tf_op jit(solution)/shard_map/pallas_call | solution.py:339
  102.4 0.0 collective-permute-done.13.refs_4_
  102.4 3.1 %shard_map.208 = (bf16[1,1,4,360,1024]{4,3,2,1,0:T(8,128)(2,1)}, f32[8,128]{1,0:T(8,128)S(1)}) custom-call(s32[1]{0:T(128)S(6)} %copy.25.refs_0_, f32[16]{0:T(128)S(1)} %copy-done.14, bf16[1,360,1024]{2,1,0:T(8,128)(2,1)S(1)} %get-tuple-element.98.refs_2_, bf16[1,360,512]{2,1,0:T(8,128)(2,1)S(1)} %get-tuple-element.99.refs_3_, ...), custom_call_target="tpu_custom_call", output_to_operand_aliasing={{0}: (7, {})} | custom-call | flops 1024 | bytes 1024 | tf_op jit(solution)/shard_map/pallas_call | solution.py:339
  105.4 0.8 shard_map.209
  106.2 3.1 %shard_map.210 = (bf16[1,1,4,360,1024]{4,3,2,1,0:T(8,128)(2,1)}, f32[8,128]{1,0:T(8,128)}) custom-call(s32[1]{0:T(128)S(6)} %copy.25.refs_0_, f32[16]{0:T(128)S(1)} %copy-done.14, bf16[1,360,1024]{2,1,0:T(8,128)(2,1)S(1)} %get-tuple-element.96.refs_2_, bf16[1,360,512]{2,1,0:T(8,128)(2,1)S(1)} %get-tuple-element.97.refs_3_, ...), custom_call_target="tpu_custom_call", output_to_operand_aliasing={{0}: (7, {})} | custom-call | flops 1024 | bytes 1024 | tf_op jit(solution)/shard_map/pallas_call | solution.py:339
  (25 shorter events, 0.1 us)
Async XLA Ops:
  0.6 0.7 copy-start.10
  4.9 16.0 %collective-permute-start = (bf16[2,208,256]{2,1,0:T(8,128)(2,1)S(1)}, bf16[2,208,256]{2,1,0:T(8,128)(2,1)S(1)}, u32[]{:S(2)}, u32[]{:S(2)}) collective-permute-start(bf16[2,208,256]{2,1,0:T(8,128)(2,1)S(1)} %get-tuple-element.58), channel_id=1, source_target_pairs={{0,1},{1,2},{2,3},{3,0},{4,5},{5,6},{6,7},{7,4},{8,9},{9,10},{10,1... | collective-permute-start | bytes 638984 | tf_op jit(solution)/shard_map/ppermute | solution.py:366
  6.6 26.1 %collective-permute-start.4 = (bf16[2,208,256]{2,1,0:T(8,128)(2,1)S(1)}, bf16[2,208,256]{2,1,0:T(8,128)(2,1)S(1)}, u32[]{:S(2)}, u32[]{:S(2)}) collective-permute-start(bf16[2,208,256]{2,1,0:T(8,128)(2,1)S(1)} %get-tuple-element.68), channel_id=1, source_target_pairs={{0,2},{1,3},{2,0},{3,1},{4,6},{5,7},{6,4},{7,5},{8,10},{9,11},{10,... | collective-permute-start | bytes 638984 | tf_op jit(solution)/shard_map/ppermute | solution.py:366
  7.6 28.2 %collective-permute-start.5 = (bf16[2,208,256]{2,1,0:T(8,128)(2,1)S(1)}, bf16[2,208,256]{2,1,0:T(8,128)(2,1)S(1)}, u32[]{:S(2)}, u32[]{:S(2)}) collective-permute-start(bf16[2,208,256]{2,1,0:T(8,128)(2,1)S(1)} %get-tuple-element.69), channel_id=1, source_target_pairs={{0,3},{1,0},{2,1},{3,2},{4,7},{5,4},{6,5},{7,6},{8,11},{9,8},{10,9... | collective-permute-start | bytes 638984 | tf_op jit(solution)/shard_map/ppermute | solution.py:366
  21.0 8.2 %copy-start.8 = (bf16[2,4,64,64]{3,2,1,0:T(8,128)(2,1)S(1)}, bf16[2,4,64,64]{3,2,1,0:T(8,128)(2,1)}, u32[]{:S(2)}) copy-start(bf16[2,4,64,64]{3,2,1,0:T(8,128)(2,1)} %refs_0_.11) | copy-start | bytes 196612
  21.0 8.2 %copy-start.9 = (bf16[2,4,64,64]{3,2,1,0:T(8,128)(2,1)S(1)}, bf16[2,4,64,64]{3,2,1,0:T(8,128)(2,1)}, u32[]{:S(2)}) copy-start(bf16[2,4,64,64]{3,2,1,0:T(8,128)(2,1)} %refs_1_.16) | copy-start | bytes 196612
  21.0 14.9 %copy-start.4 = (bf16[736,832]{1,0:T(8,128)(2,1)S(1)}, bf16[736,832]{1,0:T(8,128)(2,1)}, u32[]{:S(2)}) copy-start(bf16[736,832]{1,0:T(8,128)(2,1)} %constant.9.clone.refs_4_) | copy-start | bytes 3674116
  21.0 14.9 %copy-start.12 = (f32[2,256]{1,0:T(2,128)S(1)}, f32[2,256]{1,0:T(2,128)}, u32[]{:S(2)}) copy-start(f32[2,256]{1,0:T(2,128)} %refs_6_.5) | copy-start | bytes 6148
  21.0 14.9 %copy-start.13 = (f32[2,256]{1,0:T(2,128)S(1)}, f32[2,256]{1,0:T(2,128)}, u32[]{:S(2)}) copy-start(f32[2,256]{1,0:T(2,128)} %refs_8_.7) | copy-start | bytes 6148
  24.6 14.6 %copy-start.5 = (bf16[4,208,736]{2,1,0:T(8,128)(2,1)S(1)}, bf16[4,208,736]{2,1,0:T(8,128)(2,1)}, u32[]{:S(2)}) copy-start(bf16[4,208,736]{2,1,0:T(8,128)(2,1)} %constant.10.clone.refs_1_) | copy-start | bytes 3674116
  24.6 18.4 %collective-permute-start.1 = (bf16[2,208,256]{2,1,0:T(8,128)(2,1)S(1)}, bf16[2,208,256]{2,1,0:T(8,128)(2,1)S(1)}, u32[]{:S(2)}, u32[]{:S(2)}) collective-permute-start(bf16[2,208,256]{2,1,0:T(8,128)(2,1)S(1)} %get-tuple-element.61), channel_id=1, source_target_pairs={{0,1},{1,2},{2,3},{3,0},{4,5},{5,6},{6,7},{7,4},{8,9},{9,10},{10,1... | collective-permute-start | bytes 638984 | tf_op jit(solution)/shard_map/ppermute | solution.py:366
  27.6 21.2 %collective-permute-start.2 = (bf16[2,208,256]{2,1,0:T(8,128)(2,1)S(1)}, bf16[2,208,256]{2,1,0:T(8,128)(2,1)S(1)}, u32[]{:S(2)}, u32[]{:S(2)}) collective-permute-start(bf16[2,208,256]{2,1,0:T(8,128)(2,1)S(1)} %get-tuple-element.62), channel_id=1, source_target_pairs={{0,2},{1,3},{2,0},{3,1},{4,6},{5,7},{6,4},{7,5},{8,10},{9,11},{10,... | collective-permute-start | bytes 638984 | tf_op jit(solution)/shard_map/ppermute | solution.py:366
  27.6 26.5 %collective-permute-start.3 = (bf16[2,208,256]{2,1,0:T(8,128)(2,1)S(1)}, bf16[2,208,256]{2,1,0:T(8,128)(2,1)S(1)}, u32[]{:S(2)}, u32[]{:S(2)}) collective-permute-start(bf16[2,208,256]{2,1,0:T(8,128)(2,1)S(1)} %get-tuple-element.63), channel_id=1, source_target_pairs={{0,3},{1,0},{2,1},{3,2},{4,7},{5,4},{6,5},{7,6},{8,11},{9,8},{10,9... | collective-permute-start | bytes 638984 | tf_op jit(solution)/shard_map/ppermute | solution.py:366
  40.3 17.2 %copy-start.7 = (bf16[1,1,4,2,368,256]{5,4,3,2,1,0:T(8,128)(2,1)S(1)}, bf16[1,1,4,2,368,256]{5,4,3,2,1,0:T(8,128)(2,1)}, u32[]{:S(2)}) copy-start(bf16[1,1,4,2,368,256]{5,4,3,2,1,0:T(8,128)(2,1)} %param.31) | copy-start | bytes 4521988
  40.3 18.5 %collective-permute-start.6 = (bf16[2,208,256]{2,1,0:T(8,128)(2,1)S(1)}, bf16[2,208,256]{2,1,0:T(8,128)(2,1)S(1)}, u32[]{:S(2)}, u32[]{:S(2)}) collective-permute-start(bf16[2,208,256]{2,1,0:T(8,128)(2,1)S(1)} %get-tuple-element.75), channel_id=1, source_target_pairs={{0,2},{1,3},{2,0},{3,1},{4,6},{5,7},{6,4},{7,5},{8,10},{9,11},{10,... | collective-permute-start | bytes 638984 | tf_op jit(solution)/shard_map/ppermute | solution.py:366
  43.0 21.4 %collective-permute-start.10 = (bf16[2,208,256]{2,1,0:T(8,128)(2,1)S(1)}, bf16[2,208,256]{2,1,0:T(8,128)(2,1)S(1)}, u32[]{:S(2)}, u32[]{:S(2)}) collective-permute-start(bf16[2,208,256]{2,1,0:T(8,128)(2,1)S(1)} %get-tuple-element.85), channel_id=1, source_target_pairs={{0,1},{1,2},{2,3},{3,0},{4,5},{5,6},{6,7},{7,4},{8,9},{9,10},{10,1... | collective-permute-start | bytes 638984 | tf_op jit(solution)/shard_map/ppermute | solution.py:366
  43.0 22.9 %collective-permute-start.11 = (bf16[2,208,256]{2,1,0:T(8,128)(2,1)S(1)}, bf16[2,208,256]{2,1,0:T(8,128)(2,1)S(1)}, u32[]{:S(2)}, u32[]{:S(2)}) collective-permute-start(bf16[2,208,256]{2,1,0:T(8,128)(2,1)S(1)} %get-tuple-element.86), channel_id=1, source_target_pairs={{0,3},{1,0},{2,1},{3,2},{4,7},{5,4},{6,5},{7,6},{8,11},{9,8},{10,9... | collective-permute-start | bytes 638984 | tf_op jit(solution)/shard_map/ppermute | solution.py:366
  57.5 8.5 %copy-start = (bf16[1,1,4,360,1024]{4,3,2,1,0:T(8,128)(2,1)S(1)}, bf16[1,1,4,360,1024]{4,3,2,1,0:T(8,128)(2,1)}, u32[]{:S(2)}) copy-start(bf16[1,1,4,360,1024]{4,3,2,1,0:T(8,128)(2,1)} %refs_1_.20) | copy-start | bytes 8847364
  57.5 8.5 %copy-start.3 = (bf16[1024,512]{1,0:T(8,128)(2,1)S(1)}, bf16[1024,512]{1,0:T(8,128)(2,1)}, u32[]{:S(2)}) copy-start(bf16[1024,512]{1,0:T(8,128)(2,1)} %refs_8_.10) | copy-start | bytes 3145732
  57.5 8.4 %copy-start.6 = (bf16[360,208]{1,0:T(8,128)(2,1)S(1)}, bf16[360,208]{1,0:T(8,128)(2,1)}, u32[]{:S(2)}) copy-start(bf16[360,208]{1,0:T(8,128)(2,1)} %constant.11.clone.refs_7_) | copy-start | bytes 449284
  57.5 8.4 %copy-start.11 = (s32[1,4]{1,0:T(1,128)S(1)}, s32[1,4]{1,0:T(1,128)}, u32[]{:S(2)}) copy-start(s32[1,4]{1,0:T(1,128)} %refs_0_.14) | copy-start | bytes 52
  59.9 16.3 %collective-permute-start.7 = (bf16[2,208,256]{2,1,0:T(8,128)(2,1)S(1)}, bf16[2,208,256]{2,1,0:T(8,128)(2,1)S(1)}, u32[]{:S(2)}, u32[]{:S(2)}) collective-permute-start(bf16[2,208,256]{2,1,0:T(8,128)(2,1)S(1)} %get-tuple-element.81), channel_id=1, source_target_pairs={{0,1},{1,2},{2,3},{3,0},{4,5},{5,6},{6,7},{7,4},{8,9},{9,10},{10,1... | collective-permute-start | bytes 638984 | tf_op jit(solution)/shard_map/ppermute | solution.py:366
  59.9 22.1 %collective-permute-start.8 = (bf16[2,208,256]{2,1,0:T(8,128)(2,1)S(1)}, bf16[2,208,256]{2,1,0:T(8,128)(2,1)S(1)}, u32[]{:S(2)}, u32[]{:S(2)}) collective-permute-start(bf16[2,208,256]{2,1,0:T(8,128)(2,1)S(1)} %get-tuple-element.82), channel_id=1, source_target_pairs={{0,2},{1,3},{2,0},{3,1},{4,6},{5,7},{6,4},{7,5},{8,10},{9,11},{10,... | collective-permute-start | bytes 638984 | tf_op jit(solution)/shard_map/ppermute | solution.py:366
  63.5 18.4 %collective-permute-start.9 = (bf16[2,208,256]{2,1,0:T(8,128)(2,1)S(1)}, bf16[2,208,256]{2,1,0:T(8,128)(2,1)S(1)}, u32[]{:S(2)}, u32[]{:S(2)}) collective-permute-start(bf16[2,208,256]{2,1,0:T(8,128)(2,1)S(1)} %get-tuple-element.83), channel_id=1, source_target_pairs={{0,3},{1,0},{2,1},{3,2},{4,7},{5,4},{6,5},{7,6},{8,11},{9,8},{10,9... | collective-permute-start | bytes 638984 | tf_op jit(solution)/shard_map/ppermute | solution.py:366
  64.4 26.7 %collective-permute-start.16 = (f32[264,128]{1,0:T(8,128)S(1)}, f32[264,128]{1,0:T(8,128)S(1)}, u32[]{:S(2)}, u32[]{:S(2)}) collective-permute-start(f32[264,128]{1,0:T(8,128)S(1)} %get-tuple-element.103), channel_id=1, source_target_pairs={{0,4},{4,0},{1,5},{5,1},{2,6},{6,2},{3,7},{7,3},{8,12},{12,8},{9,1... | collective-permute-start | bytes 405512 | tf_op jit(solution)/shard_map/ppermute | solution.py:577
  66.0 13.7 %copy-start.2 = (bf16[1024,1024]{1,0:T(8,128)(2,1)S(1)}, bf16[1024,1024]{1,0:T(8,128)(2,1)}, u32[]{:S(2)}) copy-start(bf16[1024,1024]{1,0:T(8,128)(2,1)} %refs_1_.22) | copy-start | bytes 6291460
  69.2 28.0 %collective-permute-start.14 = (bf16[2,360,256]{2,1,0:T(8,128)(2,1)S(1)}, bf16[2,360,256]{2,1,0:T(8,128)(2,1)S(1)}, u32[]{:S(2)}, u32[]{:S(2)}) collective-permute-start(bf16[2,360,256]{2,1,0:T(8,128)(2,1)S(1)} %get-tuple-element.101.refs_3_), channel_id=1, source_target_pairs={{0,4},{1,5},{2,6},{3,7},{8,12},{9,13},{10,14},{11,15},{16,20},{17,... | collective-permute-start | bytes 1105928 | tf_op jit(solution)/shard_map/ppermute | solution.py:564
  76.2 21.0 %collective-permute-start.15 = (bf16[2,360,256]{2,1,0:T(8,128)(2,1)S(1)}, bf16[2,360,256]{2,1,0:T(8,128)(2,1)S(1)}, u32[]{:S(2)}, u32[]{:S(2)}) collective-permute-start(bf16[2,360,256]{2,1,0:T(8,128)(2,1)S(1)} %get-tuple-element.102.refs_4_), channel_id=1, source_target_pairs={{0,4},{1,5},{2,6},{3,7},{8,12},{9,13},{10,14},{11,15},{16,20},{17,... | collective-permute-start | bytes 1105928 | tf_op jit(solution)/shard_map/ppermute | solution.py:564
  84.2 18.2 %collective-permute-start.13 = (bf16[1,360,512]{2,1,0:T(8,128)(2,1)S(1)}, bf16[1,360,512]{2,1,0:T(8,128)(2,1)S(1)}, u32[]{:S(2)}, u32[]{:S(2)}) collective-permute-start(bf16[1,360,512]{2,1,0:T(8,128)(2,1)S(1)} %get-tuple-element.99.refs_3_), channel_id=1, source_target_pairs={{0,4},{1,5},{2,6},{3,7},{8,12},{9,13},{10,14},{11,15},{16,20},{17,... | collective-permute-start | bytes 1105928 | tf_op jit(solution)/shard_map/ppermute | solution.py:564
  89.6 16.6 %collective-permute-start.12 = (bf16[1,360,512]{2,1,0:T(8,128)(2,1)S(1)}, bf16[1,360,512]{2,1,0:T(8,128)(2,1)S(1)}, u32[]{:S(2)}, u32[]{:S(2)}) collective-permute-start(bf16[1,360,512]{2,1,0:T(8,128)(2,1)S(1)} %get-tuple-element.97.refs_3_), channel_id=1, source_target_pairs={{0,4},{1,5},{2,6},{3,7},{8,12},{9,13},{10,14},{11,15},{16,20},{17,... | collective-permute-start | bytes 1105928 | tf_op jit(solution)/shard_map/ppermute | solution.py:564
  91.1 1.4 %collective-permute-start.17 = (f32[264,128]{1,0:T(8,128)S(1)}, f32[264,128]{1,0:T(8,128)S(1)}, u32[]{:S(2)}, u32[]{:S(2)}) collective-permute-start(f32[264,128]{1,0:T(8,128)S(1)} %add.9.refs_9_), channel_id=1, source_target_pairs={{0,8},{8,0},{16,24},{24,16},{1,9},{9,1},{17,25},{25,17},{2,10},{10... | collective-permute-start | bytes 405512 | tf_op jit(solution)/shard_map/ppermute | solution.py:581
  92.6 9.7 %collective-permute-start.18 = (f32[264,128]{1,0:T(8,128)S(1)}, f32[264,128]{1,0:T(8,128)S(1)}, u32[]{:S(2)}, u32[]{:S(2)}) collective-permute-start(f32[264,128]{1,0:T(8,128)S(1)} %add.10.refs_8_), channel_id=1, source_target_pairs={{0,16},{8,24},{16,0},{24,8},{1,17},{9,25},{17,1},{25,9},{2,18},{10... | collective-permute-start | bytes 405512 | tf_op jit(solution)/shard_map/ppermute | solution.py:581
  96.0 1.6 %copy-start.1 = (bf16[1024,1024]{1,0:T(8,128)(2,1)S(1)}, bf16[1024,1024]{1,0:T(8,128)(2,1)}, u32[]{:S(2)}) copy-start(bf16[1024,1024]{1,0:T(8,128)(2,1)} %refs_6_.7) | copy-start | bytes 6291460
  96.0 1.6 %copy-start.14 = (f32[16]{0:T(128)S(1)}, f32[16]{0:T(128)}, u32[]{:S(2)}) copy-start(f32[16]{0:T(128)} %refs_1_.25) | copy-start | bytes 196

commit v7 on v6

--- a/solution.py
+++ b/solution.py
@@ -352,7 +352,7 @@
     )(*prefetch, *args)
 
 
-VMEM_BYTES = 36 * 1024 * 1024
+VMEM_BYTES = 24 * 1024 * 1024
 
 
 def held(array):
@@ -603,12 +603,11 @@
     ("query", 2, 1, False),
     ("query", 3, 1, False),
     ("add", 0, 0, False),
-    ("attend", 0, 2, False),
+    ("attend", 0, 3, False),
     ("add", 0, 0, False),
-    ("attend", 2, 1, False),
+    ("attend", 3, 1, False),
     ("add", 0, 0, False),
     ("sum", 0, 0, False),
-    ("attend", 3, 1, False),
 )
 
 

time: 110 us -> 109 us (level)
  Pallas kernels: 41.5 us -> 40.3 us
    pallas_call x18 -> x17, Pallas kernels: 41.5 us -> 40.3 us  [call(): pl.pallas_call(kernel, grid_spec=pltpu.PrefetchScalarGridSpec(num_scalar_...]
    ppermute x3, waiting for transfers between devices: 1.35 us -> 2.45 us  [fused_body(): crossing = lax.ppermute(summed, *rounds.pop(0))]
  transfers between devices with their start and end apart: 19 -> 19, of which waited for: 7 -> 9; matrix products, arithmetic and copies ran while one was open for 0% -> 0% of each run, Pallas kernels for 32% -> 30%
where the time goes in v7:
time: 109 us
  Pallas kernels  40.3 us (37%)
  waiting for transfers between devices  33.7 us (31%)
  starting transfers between devices  32.4 us (30%)
  between operations  1.64 us (2%)
    pallas_call x17, Pallas kernels, call(): pl.pallas_call(kernel, grid_spec=pltpu.PrefetchScalarGridSpec(num_scalar_...  40.3 us
    ppermute x12, waiting for transfers between devices, swap_blocks(): lax.ppermute(part, 'lon', [(i, (i + shift) % count) for i in range(count)])  31.2 us
    ppermute x12, starting transfers between devices, swap_blocks(): lax.ppermute(part, 'lon', [(i, (i + shift) % count) for i in range(count)])  18.5 us
    ppermute x4, starting transfers between devices, fused_body(): earlier = [lax.ppermute(part, 'frame', [(0, 1)]) for part in keyval]  10.8 us
    ppermute x3, starting transfers between devices, fused_body(): crossing = lax.ppermute(summed, *rounds.pop(0))  3.14 us
    ppermute x3, waiting for transfers between devices, fused_body(): crossing = lax.ppermute(summed, *rounds.pop(0))  2.45 us
  transfers between devices with their start and end apart: 19, of which 9 were waited for; matrix products, arithmetic and copies ran while one was open for 0% of the time, Pallas kernels for 30%

profile of v7, /device:TPU:8, one launch (start us, length us, event | category | flops | bytes accessed | tf_op | source)
XLA Modules:
  0.0 108.8 jit_solution(17281496257560230908)
XLA Ops:
  0.6 0.0 copy-start.10
  0.6 0.6 copy-done.10
  1.3 3.6 %shard_map.193 = (bf16[2,208,256]{2,1,0:T(8,128)(2,1)S(1)}, bf16[2,208,256]{2,1,0:T(8,128)(2,1)S(1)}, bf16[2,208,256]{2,1,0:T(8,128)(2,1)S(1)}, bf16[2,208,256]{2,1,0:T(8,128)(2,1)S(1)}, f32[8,128]{1,0:T(8,128)S(1)}) custom-call(s32[1,4]{1,0:T(1,128)S(1)} %copy-done.10, bf16[1,1,4,360,1024]{4,3,2,1,0:T(8,128)(2,1)} %refs_1_.19, bf16[720,1024]{1,0:T(8,128)(2,1)} %refs_2_.9, ...), custom_call_target="tpu_custom_call" | custom-call | flops 1024 | bytes 1024 | tf_op jit(solution)/shard_map/pallas_call | solution.py:339
  4.9 1.6 %collective-permute-start = (bf16[2,208,256]{2,1,0:T(8,128)(2,1)S(1)}, bf16[2,208,256]{2,1,0:T(8,128)(2,1)S(1)}, u32[]{:S(2)}, u32[]{:S(2)}) collective-permute-start(bf16[2,208,256]{2,1,0:T(8,128)(2,1)S(1)} %get-tuple-element.56), channel_id=1, source_target_pairs={{0,1},{1,2},{2,3},{3,0},{4,5},{5,6},{6,7},{7,4},{8,9},{9,10},{10,1... | collective-permute-start | bytes 638984 | tf_op jit(solution)/shard_map/ppermute | solution.py:366
  6.6 1.1 collective-permute-start.4
  7.6 1.9 %collective-permute-start.5 = (bf16[2,208,256]{2,1,0:T(8,128)(2,1)S(1)}, bf16[2,208,256]{2,1,0:T(8,128)(2,1)S(1)}, u32[]{:S(2)}, u32[]{:S(2)}) collective-permute-start(bf16[2,208,256]{2,1,0:T(8,128)(2,1)S(1)} %get-tuple-element.67), channel_id=1, source_target_pairs={{0,3},{1,0},{2,1},{3,2},{4,7},{5,4},{6,5},{7,6},{8,11},{9,8},{10,9... | collective-permute-start | bytes 638984 | tf_op jit(solution)/shard_map/ppermute | solution.py:366
  9.6 11.4 %collective-permute-done.refs_5_.refs_1_ = bf16[2,208,256]{2,1,0:T(8,128)(2,1)S(1)} collective-permute-done((bf16[2,208,256]{2,1,0:T(8,128)(2,1)S(1)}, bf16[2,208,256]{2,1,0:T(8,128)(2,1)S(1)}, u32[]{:S(2)}, u32[]{:S(2)}) %collective-permute-start) | collective-permute-done | bytes 213024 | tf_op jit(solution)/shard_map/ppermute | solution.py:366
  21.0 3.6 %shard_map.194 = (bf16[2,208,256]{2,1,0:T(8,128)(2,1)S(1)}, bf16[2,208,256]{2,1,0:T(8,128)(2,1)S(1)}, bf16[2,208,256]{2,1,0:T(8,128)(2,1)S(1)}, bf16[2,208,256]{2,1,0:T(8,128)(2,1)S(1)}, f32[8,128]{1,0:T(8,128)S(1)}) custom-call(s32[1,4]{1,0:T(1,128)S(1)} %copy-done.10, bf16[1,1,4,360,1024]{4,3,2,1,0:T(8,128)(2,1)} %refs_1_.19, bf16[720,1024]{1,0:T(8,128)(2,1)} %refs_2_.9, ...), custom_call_target="tpu_custom_call" | custom-call | flops 1024 | bytes 1024 | tf_op jit(solution)/shard_map/pallas_call | solution.py:339
  24.6 3.0 %collective-permute-start.1 = (bf16[2,208,256]{2,1,0:T(8,128)(2,1)S(1)}, bf16[2,208,256]{2,1,0:T(8,128)(2,1)S(1)}, u32[]{:S(2)}, u32[]{:S(2)}) collective-permute-start(bf16[2,208,256]{2,1,0:T(8,128)(2,1)S(1)} %get-tuple-element.59), channel_id=1, source_target_pairs={{0,1},{1,2},{2,3},{3,0},{4,5},{5,6},{6,7},{7,4},{8,9},{9,10},{10,1... | collective-permute-start | bytes 638984 | tf_op jit(solution)/shard_map/ppermute | solution.py:366
  27.6 0.0 collective-permute-start.2
  27.6 1.5 %collective-permute-start.3 = (bf16[2,208,256]{2,1,0:T(8,128)(2,1)S(1)}, bf16[2,208,256]{2,1,0:T(8,128)(2,1)S(1)}, u32[]{:S(2)}, u32[]{:S(2)}) collective-permute-start(bf16[2,208,256]{2,1,0:T(8,128)(2,1)S(1)} %get-tuple-element.61), channel_id=1, source_target_pairs={{0,3},{1,0},{2,1},{3,2},{4,7},{5,4},{6,5},{7,6},{8,11},{9,8},{10,9... | collective-permute-start | bytes 638984 | tf_op jit(solution)/shard_map/ppermute | solution.py:366
  29.1 0.2 shard_map.195
  29.3 3.3 %collective-permute-done.4.refs_2_ = bf16[2,208,256]{2,1,0:T(8,128)(2,1)S(1)} collective-permute-done((bf16[2,208,256]{2,1,0:T(8,128)(2,1)S(1)}, bf16[2,208,256]{2,1,0:T(8,128)(2,1)S(1)}, u32[]{:S(2)}, u32[]{:S(2)}) %collective-permute-start.4) | collective-permute-done | bytes 213024 | tf_op jit(solution)/shard_map/ppermute | solution.py:366
  32.7 3.2 %collective-permute-done.5.refs_3_ = bf16[2,208,256]{2,1,0:T(8,128)(2,1)S(1)} collective-permute-done((bf16[2,208,256]{2,1,0:T(8,128)(2,1)S(1)}, bf16[2,208,256]{2,1,0:T(8,128)(2,1)S(1)}, u32[]{:S(2)}, u32[]{:S(2)}) %collective-permute-start.5) | collective-permute-done | bytes 213024 | tf_op jit(solution)/shard_map/ppermute | solution.py:366
  35.8 0.0 copy-start.5
  35.8 3.4 %shard_map.196 = (bf16[2,736,256]{2,1,0:T(8,128)(2,1)S(1)}, bf16[2,736,256]{2,1,0:T(8,128)(2,1)S(1)}, f32[8,128]{1,0:T(8,128)S(1)}) custom-call(bf16[2,208,256]{2,1,0:T(8,128)(2,1)S(1)} %get-tuple-element.65.refs_0_, bf16[2,208,256]{2,1,0:T(8,128)(2,1)S(1)} %collective-permute-done.refs_5_.refs_1_, bf16[2,208,256]{2,1,0:T(8,128)(2,1)S(1)} %collective-permute-done.4.refs_2_, ...), custom_call_target="tpu_custom_call" | custom-call | flops 1024 | bytes 1024 | tf_op jit(solution)/shard_map/pallas_call | solution.py:339
  39.3 1.0 shard_map.197
  40.3 2.7 %collective-permute-start.6 = (bf16[2,208,256]{2,1,0:T(8,128)(2,1)S(1)}, bf16[2,208,256]{2,1,0:T(8,128)(2,1)S(1)}, u32[]{:S(2)}, u32[]{:S(2)}) collective-permute-start(bf16[2,208,256]{2,1,0:T(8,128)(2,1)S(1)} %get-tuple-element.73), channel_id=1, source_target_pairs={{0,2},{1,3},{2,0},{3,1},{4,6},{5,7},{6,4},{7,5},{8,10},{9,11},{10,... | collective-permute-start | bytes 638984 | tf_op jit(solution)/shard_map/ppermute | solution.py:366
  43.0 0.0 collective-permute-start.10
  43.0 0.0 collective-permute-done.1.refs_1_
  43.0 2.0 %collective-permute-start.11 = (bf16[2,208,256]{2,1,0:T(8,128)(2,1)S(1)}, bf16[2,208,256]{2,1,0:T(8,128)(2,1)S(1)}, u32[]{:S(2)}, u32[]{:S(2)}) collective-permute-start(bf16[2,208,256]{2,1,0:T(8,128)(2,1)S(1)} %get-tuple-element.84), channel_id=1, source_target_pairs={{0,3},{1,0},{2,1},{3,2},{4,7},{5,4},{6,5},{7,6},{8,11},{9,8},{10,9... | collective-permute-start | bytes 638984 | tf_op jit(solution)/shard_map/ppermute | solution.py:366
  45.1 3.8 %collective-permute-done.2.refs_2_ = bf16[2,208,256]{2,1,0:T(8,128)(2,1)S(1)} collective-permute-done((bf16[2,208,256]{2,1,0:T(8,128)(2,1)S(1)}, bf16[2,208,256]{2,1,0:T(8,128)(2,1)S(1)}, u32[]{:S(2)}, u32[]{:S(2)}) %collective-permute-start.2) | collective-permute-done | bytes 213024 | tf_op jit(solution)/shard_map/ppermute | solution.py:366
  48.8 5.3 %collective-permute-done.3.refs_3_ = bf16[2,208,256]{2,1,0:T(8,128)(2,1)S(1)} collective-permute-done((bf16[2,208,256]{2,1,0:T(8,128)(2,1)S(1)}, bf16[2,208,256]{2,1,0:T(8,128)(2,1)S(1)}, u32[]{:S(2)}, u32[]{:S(2)}) %collective-permute-start.3) | collective-permute-done | bytes 213024 | tf_op jit(solution)/shard_map/ppermute | solution.py:366
  54.1 3.4 %shard_map.198 = (bf16[2,736,256]{2,1,0:T(8,128)(2,1)S(1)}, bf16[2,736,256]{2,1,0:T(8,128)(2,1)S(1)}, f32[8,128]{1,0:T(8,128)S(1)}) custom-call(bf16[2,208,256]{2,1,0:T(8,128)(2,1)S(1)} %get-tuple-element.58.refs_0_, bf16[2,208,256]{2,1,0:T(8,128)(2,1)S(1)} %collective-permute-done.1.refs_1_, bf16[2,208,256]{2,1,0:T(8,128)(2,1)S(1)} %collective-permute-done.2.refs_2_, ...), custom_call_target="tpu_custom_call" | custom-call | flops 1024 | bytes 1024 | tf_op jit(solution)/shard_map/pallas_call | solution.py:339
  57.5 0.0 copy-start
  57.5 1.3 %shard_map.199 = (f32[264,128]{1,0:T(8,128)S(1)}, f32[8,128]{1,0:T(8,128)S(1)}) custom-call(bf16[2,736,256]{2,1,0:T(8,128)(2,1)S(1)} %get-tuple-element.74.refs_0_, bf16[2,736,256]{2,1,0:T(8,128)(2,1)S(1)} %get-tuple-element.75.refs_1_, bf16[4,2,368,256]{3,2,1,0:T(8,128)(2,1)S(1)} %bitcast.2, f32[8,128]{1,0:T(8,128)S(1)} %get-tuple-element.76.refs_3_), custom_call_target="tpu_custom_call" | custom-call | flops 1024 | bytes 1024 | tf_op jit(solution)/shard_map/pallas_call | solution.py:339
  58.8 0.0 copy-start.2
  58.8 0.0 copy-start.6
  58.8 0.0 copy-start.11
  58.8 0.0 collective-permute-done.6.refs_2_.refs_5_
  58.8 1.0 shard_map.200
  59.9 0.1 collective-permute-start.7
  59.9 3.6 %collective-permute-start.8 = (bf16[2,208,256]{2,1,0:T(8,128)(2,1)S(1)}, bf16[2,208,256]{2,1,0:T(8,128)(2,1)S(1)}, u32[]{:S(2)}, u32[]{:S(2)}) collective-permute-start(bf16[2,208,256]{2,1,0:T(8,128)(2,1)S(1)} %get-tuple-element.80), channel_id=1, source_target_pairs={{0,2},{1,3},{2,0},{3,1},{4,6},{5,7},{6,4},{7,5},{8,10},{9,11},{10,... | collective-permute-start | bytes 638984 | tf_op jit(solution)/shard_map/ppermute | solution.py:366
  63.5 0.9 collective-permute-start.9
  64.4 0.0 collective-permute-done.10.refs_4_
  64.4 1.5 %collective-permute-start.16 = (f32[264,128]{1,0:T(8,128)S(1)}, f32[264,128]{1,0:T(8,128)S(1)}, u32[]{:S(2)}, u32[]{:S(2)}) collective-permute-start(f32[264,128]{1,0:T(8,128)S(1)} %get-tuple-element.101), channel_id=1, source_target_pairs={{0,4},{4,0},{1,5},{5,1},{2,6},{6,2},{3,7},{7,3},{8,12},{12,8},{9,1... | collective-permute-start | bytes 405512 | tf_op jit(solution)/shard_map/ppermute | solution.py:577
  65.9 0.0 collective-permute-done.11.refs_6_
  66.0 0.0 copy-start.1
  66.0 3.2 %shard_map.201 = (bf16[2,360,1024]{2,1,0:T(8,128)(2,1)S(1)}, bf16[2,360,256]{2,1,0:T(8,128)(2,1)S(1)}, bf16[2,360,256]{2,1,0:T(8,128)(2,1)S(1)}, f32[8,128]{1,0:T(8,128)S(1)}) custom-call(s32[1,4]{1,0:T(1,128)S(1)} %copy-done.11, bf16[1,1,4,360,1024]{4,3,2,1,0:T(8,128)(2,1)S(1)} %copy-done, bf16[720,1024]{1,0:T(8,128)(2,1)} %refs_2_.9, ...), custom_call_target="tpu_custom_call" | custom-call | flops 1024 | bytes 1024 | tf_op jit(solution)/shard_map/pallas_call | solution.py:339
  69.2 2.5 %collective-permute-start.13 = (bf16[2,360,256]{2,1,0:T(8,128)(2,1)S(1)}, bf16[2,360,256]{2,1,0:T(8,128)(2,1)S(1)}, u32[]{:S(2)}, u32[]{:S(2)}) collective-permute-start(bf16[2,360,256]{2,1,0:T(8,128)(2,1)S(1)} %get-tuple-element.97.refs_3_), channel_id=1, source_target_pairs={{0,4},{1,5},{2,6},{3,7},{8,12},{9,13},{10,14},{11,15},{16,20},{17,... | collective-permute-start | bytes 1105928 | tf_op jit(solution)/shard_map/ppermute | solution.py:564
  71.7 2.3 %shard_map.202 = (bf16[2,360,1024]{2,1,0:T(8,128)(2,1)S(1)}, f32[8,128]{1,0:T(8,128)S(1)}) custom-call(bf16[2,360,1024]{2,1,0:T(8,128)(2,1)S(1)} %get-tuple-element.86.refs_0_.refs_7_, bf16[1024,1024]{1,0:T(8,128)(2,1)S(1)} %copy-done.1, f32[8,128]{1,0:T(8,128)S(1)} %get-tuple-element.87.refs_2_), custom_call_target="tpu_custom_call" | custom-call | flops 1024 | bytes 1024 | tf_op jit(solution)/shard_map/pallas_call | solution.py:339
  74.0 2.2 %collective-permute-done.7.refs_4_ = bf16[2,208,256]{2,1,0:T(8,128)(2,1)S(1)} collective-permute-done((bf16[2,208,256]{2,1,0:T(8,128)(2,1)S(1)}, bf16[2,208,256]{2,1,0:T(8,128)(2,1)S(1)}, u32[]{:S(2)}, u32[]{:S(2)}) %collective-permute-start.7) | collective-permute-done | bytes 213024 | tf_op jit(solution)/shard_map/ppermute | solution.py:366
  76.2 3.4 %collective-permute-start.14 = (bf16[2,360,256]{2,1,0:T(8,128)(2,1)S(1)}, bf16[2,360,256]{2,1,0:T(8,128)(2,1)S(1)}, u32[]{:S(2)}, u32[]{:S(2)}) collective-permute-start(bf16[2,360,256]{2,1,0:T(8,128)(2,1)S(1)} %get-tuple-element.98.refs_4_), channel_id=1, source_target_pairs={{0,4},{1,5},{2,6},{3,7},{8,12},{9,13},{10,14},{11,15},{16,20},{17,... | collective-permute-start | bytes 1105928 | tf_op jit(solution)/shard_map/ppermute | solution.py:564
  79.6 0.0 collective-permute-done.8.refs_5_
  79.6 2.2 %collective-permute-done.9.refs_6_ = bf16[2,208,256]{2,1,0:T(8,128)(2,1)S(1)} collective-permute-done((bf16[2,208,256]{2,1,0:T(8,128)(2,1)S(1)}, bf16[2,208,256]{2,1,0:T(8,128)(2,1)S(1)}, u32[]{:S(2)}, u32[]{:S(2)}) %collective-permute-start.9) | collective-permute-done | bytes 213024 | tf_op jit(solution)/shard_map/ppermute | solution.py:366
  81.8 2.2 %shard_map.203 = (bf16[1,360,1024]{2,1,0:T(8,128)(2,1)S(1)}, bf16[1,360,512]{2,1,0:T(8,128)(2,1)S(1)}, f32[8,128]{1,0:T(8,128)S(1)}) custom-call(s32[1,4]{1,0:T(1,128)S(1)} %copy-done.11, bf16[1,1,4,360,1024]{4,3,2,1,0:T(8,128)(2,1)S(1)} %copy-done, bf16[720,1024]{1,0:T(8,128)(2,1)} %refs_2_.9, bf16[2,208,256]{2,1,0:T(8,128)(2,1)S(1)} %get-tuple-element.78.refs_3_, ...), custom_call_target="tpu_custom_call" | custom-call | flops 1024 | bytes 1024 | tf_op jit(solution)/shard_map/pallas_call | solution.py:339
  84.0 3.4 %collective-permute-start.15 = (bf16[1,360,512]{2,1,0:T(8,128)(2,1)S(1)}, bf16[1,360,512]{2,1,0:T(8,128)(2,1)S(1)}, u32[]{:S(2)}, u32[]{:S(2)}) collective-permute-start(bf16[1,360,512]{2,1,0:T(8,128)(2,1)S(1)} %get-tuple-element.100.refs_9_), channel_id=1, source_target_pairs={{0,4},{1,5},{2,6},{3,7},{8,12},{9,13},{10,14},{11,15},{16,20},{17,... | collective-permute-start | bytes 1105928 | tf_op jit(solution)/shard_map/ppermute | solution.py:564
  87.4 2.2 %shard_map.204 = (bf16[1,360,1024]{2,1,0:T(8,128)(2,1)S(1)}, bf16[1,360,512]{2,1,0:T(8,128)(2,1)S(1)}, f32[8,128]{1,0:T(8,128)S(1)}) custom-call(s32[1,4]{1,0:T(1,128)S(1)} %copy-done.11, bf16[1,1,4,360,1024]{4,3,2,1,0:T(8,128)(2,1)S(1)} %copy-done, bf16[720,1024]{1,0:T(8,128)(2,1)} %refs_2_.9, bf16[2,208,256]{2,1,0:T(8,128)(2,1)S(1)} %get-tuple-element.78.refs_3_, ...), custom_call_target="tpu_custom_call" | custom-call | flops 1024 | bytes 1024 | tf_op jit(solution)/shard_map/pallas_call | solution.py:339
  89.6 1.5 %collective-permute-start.12 = (bf16[1,360,512]{2,1,0:T(8,128)(2,1)S(1)}, bf16[1,360,512]{2,1,0:T(8,128)(2,1)S(1)}, u32[]{:S(2)}, u32[]{:S(2)}) collective-permute-start(bf16[1,360,512]{2,1,0:T(8,128)(2,1)S(1)} %get-tuple-element.95.refs_3_), channel_id=1, source_target_pairs={{0,4},{1,5},{2,6},{3,7},{8,12},{9,13},{10,14},{11,15},{16,20},{17,... | collective-permute-start | bytes 1105928 | tf_op jit(solution)/shard_map/ppermute | solution.py:564
  91.1 0.0 collective-permute-done.16
  91.2 0.1 collective-permute-start.17
  91.2 1.3 %collective-permute-done.17 = f32[264,128]{1,0:T(8,128)S(1)} collective-permute-done((f32[264,128]{1,0:T(8,128)S(1)}, f32[264,128]{1,0:T(8,128)S(1)}, u32[]{:S(2)}, u32[]{:S(2)}) %collective-permute-start.17) | collective-permute-done | bytes 135200 | tf_op jit(solution)/shard_map/ppermute | solution.py:581
  92.6 1.6 %collective-permute-start.18 = (f32[264,128]{1,0:T(8,128)S(1)}, f32[264,128]{1,0:T(8,128)S(1)}, u32[]{:S(2)}, u32[]{:S(2)}) collective-permute-start(f32[264,128]{1,0:T(8,128)S(1)} %add.10.refs_8_), channel_id=1, source_target_pairs={{0,16},{8,24},{16,0},{24,8},{1,17},{9,25},{17,1},{25,9},{2,18},{10... | collective-permute-start | bytes 405512 | tf_op jit(solution)/shard_map/ppermute | solution.py:581
  94.8 1.2 %shard_map.205 = (bf16[1,360,1024]{2,1,0:T(8,128)(2,1)S(1)}, f32[8,128]{1,0:T(8,128)S(1)}) custom-call(bf16[1,360,1024]{2,1,0:T(8,128)(2,1)S(1)} %get-tuple-element.91.refs_0_.refs_11_, bf16[1024,1024]{1,0:T(8,128)(2,1)S(1)} %copy-done.1, f32[8,128]{1,0:T(8,128)S(1)} %get-tuple-element.92.refs_2_), custom_call_target="tpu_custom_call" | custom-call | flops 1024 | bytes 1024 | tf_op jit(solution)/shard_map/pallas_call | solution.py:339
  96.0 0.0 copy-start.3
  96.0 0.0 copy-start.14
  96.0 1.2 %shard_map.206 = (bf16[1,360,1024]{2,1,0:T(8,128)(2,1)S(1)}, f32[8,128]{1,0:T(8,128)S(1)}) custom-call(bf16[1,360,1024]{2,1,0:T(8,128)(2,1)S(1)} %get-tuple-element.90.refs_0_.refs_5_, bf16[1024,1024]{1,0:T(8,128)(2,1)S(1)} %copy-done.1, f32[8,128]{1,0:T(8,128)S(1)} %get-tuple-element.93.refs_2_), custom_call_target="tpu_custom_call" | custom-call | flops 1024 | bytes 1024 | tf_op jit(solution)/shard_map/pallas_call | solution.py:339
  97.2 1.1 %collective-permute-done.18 = f32[264,128]{1,0:T(8,128)S(1)} collective-permute-done((f32[264,128]{1,0:T(8,128)S(1)}, f32[264,128]{1,0:T(8,128)S(1)}, u32[]{:S(2)}, u32[]{:S(2)}) %collective-permute-start.18) | collective-permute-done | bytes 135200 | tf_op jit(solution)/shard_map/ppermute | solution.py:581
  98.3 0.0 collective-permute-done.13.refs_5_
  98.4 0.0 collective-permute-done.15.refs_10_
  98.4 6.5 %shard_map.207 = (bf16[1,1,4,360,1024]{4,3,2,1,0:T(8,128)(2,1)}, f32[8,128]{1,0:T(8,128)S(1)}) custom-call(s32[1]{0:T(128)S(6)} %copy.23.refs_0_, f32[16]{0:T(128)S(1)} %copy-done.14, bf16[2,360,1024]{2,1,0:T(8,128)(2,1)S(1)} %get-tuple-element.96.refs_2_, bf16[2,360,256]{2,1,0:T(8,128)(2,1)S(1)} %get-tuple-element.97.refs_3_, ...), custom_call_target="tpu_custom_call" | custom-call | flops 1024 | bytes 1024 | tf_op jit(solution)/shard_map/pallas_call | solution.py:339
  104.9 0.0 collective-permute-done.12.refs_4_
  104.9 3.1 %shard_map.208 = (bf16[1,1,4,360,1024]{4,3,2,1,0:T(8,128)(2,1)}, f32[8,128]{1,0:T(8,128)S(1)}) custom-call(s32[1]{0:T(128)S(6)} %copy.23.refs_0_, f32[16]{0:T(128)S(1)} %copy-done.14, bf16[1,360,1024]{2,1,0:T(8,128)(2,1)S(1)} %get-tuple-element.94.refs_2_, bf16[1,360,512]{2,1,0:T(8,128)(2,1)S(1)} %get-tuple-element.95.refs_3_, ...), custom_call_target="tpu_custom_call", output_to_operand_aliasing={{0}: (7, {})} | custom-call | flops 1024 | bytes 1024 | tf_op jit(solution)/shard_map/pallas_call | solution.py:339
  108.0 0.8 shard_map.209
  (24 shorter events, 0.1 us)
Async XLA Ops:
  0.6 0.7 copy-start.10
  4.9 16.0 %collective-permute-start = (bf16[2,208,256]{2,1,0:T(8,128)(2,1)S(1)}, bf16[2,208,256]{2,1,0:T(8,128)(2,1)S(1)}, u32[]{:S(2)}, u32[]{:S(2)}) collective-permute-start(bf16[2,208,256]{2,1,0:T(8,128)(2,1)S(1)} %get-tuple-element.56), channel_id=1, source_target_pairs={{0,1},{1,2},{2,3},{3,0},{4,5},{5,6},{6,7},{7,4},{8,9},{9,10},{10,1... | collective-permute-start | bytes 638984 | tf_op jit(solution)/shard_map/ppermute | solution.py:366
  6.6 26.1 %collective-permute-start.4 = (bf16[2,208,256]{2,1,0:T(8,128)(2,1)S(1)}, bf16[2,208,256]{2,1,0:T(8,128)(2,1)S(1)}, u32[]{:S(2)}, u32[]{:S(2)}) collective-permute-start(bf16[2,208,256]{2,1,0:T(8,128)(2,1)S(1)} %get-tuple-element.66), channel_id=1, source_target_pairs={{0,2},{1,3},{2,0},{3,1},{4,6},{5,7},{6,4},{7,5},{8,10},{9,11},{10,... | collective-permute-start | bytes 638984 | tf_op jit(solution)/shard_map/ppermute | solution.py:366
  7.6 28.2 %collective-permute-start.5 = (bf16[2,208,256]{2,1,0:T(8,128)(2,1)S(1)}, bf16[2,208,256]{2,1,0:T(8,128)(2,1)S(1)}, u32[]{:S(2)}, u32[]{:S(2)}) collective-permute-start(bf16[2,208,256]{2,1,0:T(8,128)(2,1)S(1)} %get-tuple-element.67), channel_id=1, source_target_pairs={{0,3},{1,0},{2,1},{3,2},{4,7},{5,4},{6,5},{7,6},{8,11},{9,8},{10,9... | collective-permute-start | bytes 638984 | tf_op jit(solution)/shard_map/ppermute | solution.py:366
  21.0 8.2 %copy-start.8 = (bf16[2,4,64,64]{3,2,1,0:T(8,128)(2,1)S(1)}, bf16[2,4,64,64]{3,2,1,0:T(8,128)(2,1)}, u32[]{:S(2)}) copy-start(bf16[2,4,64,64]{3,2,1,0:T(8,128)(2,1)} %refs_0_.10) | copy-start | bytes 196612
  21.0 8.2 %copy-start.9 = (bf16[2,4,64,64]{3,2,1,0:T(8,128)(2,1)S(1)}, bf16[2,4,64,64]{3,2,1,0:T(8,128)(2,1)}, u32[]{:S(2)}) copy-start(bf16[2,4,64,64]{3,2,1,0:T(8,128)(2,1)} %refs_1_.15) | copy-start | bytes 196612
  21.0 14.9 %copy-start.4 = (bf16[736,832]{1,0:T(8,128)(2,1)S(1)}, bf16[736,832]{1,0:T(8,128)(2,1)}, u32[]{:S(2)}) copy-start(bf16[736,832]{1,0:T(8,128)(2,1)} %constant.9.clone.refs_4_) | copy-start | bytes 3674116
  21.0 14.9 %copy-start.12 = (f32[2,256]{1,0:T(2,128)S(1)}, f32[2,256]{1,0:T(2,128)}, u32[]{:S(2)}) copy-start(f32[2,256]{1,0:T(2,128)} %refs_6_.4) | copy-start | bytes 6148
  21.0 14.9 %copy-start.13 = (f32[2,256]{1,0:T(2,128)S(1)}, f32[2,256]{1,0:T(2,128)}, u32[]{:S(2)}) copy-start(f32[2,256]{1,0:T(2,128)} %refs_8_.6) | copy-start | bytes 6148
  24.6 18.4 %collective-permute-start.1 = (bf16[2,208,256]{2,1,0:T(8,128)(2,1)S(1)}, bf16[2,208,256]{2,1,0:T(8,128)(2,1)S(1)}, u32[]{:S(2)}, u32[]{:S(2)}) collective-permute-start(bf16[2,208,256]{2,1,0:T(8,128)(2,1)S(1)} %get-tuple-element.59), channel_id=1, source_target_pairs={{0,1},{1,2},{2,3},{3,0},{4,5},{5,6},{6,7},{7,4},{8,9},{9,10},{10,1... | collective-permute-start | bytes 638984 | tf_op jit(solution)/shard_map/ppermute | solution.py:366
  27.6 21.2 %collective-permute-start.2 = (bf16[2,208,256]{2,1,0:T(8,128)(2,1)S(1)}, bf16[2,208,256]{2,1,0:T(8,128)(2,1)S(1)}, u32[]{:S(2)}, u32[]{:S(2)}) collective-permute-start(bf16[2,208,256]{2,1,0:T(8,128)(2,1)S(1)} %get-tuple-element.60), channel_id=1, source_target_pairs={{0,2},{1,3},{2,0},{3,1},{4,6},{5,7},{6,4},{7,5},{8,10},{9,11},{10,... | collective-permute-start | bytes 638984 | tf_op jit(solution)/shard_map/ppermute | solution.py:366
  27.6 26.5 %collective-permute-start.3 = (bf16[2,208,256]{2,1,0:T(8,128)(2,1)S(1)}, bf16[2,208,256]{2,1,0:T(8,128)(2,1)S(1)}, u32[]{:S(2)}, u32[]{:S(2)}) collective-permute-start(bf16[2,208,256]{2,1,0:T(8,128)(2,1)S(1)} %get-tuple-element.61), channel_id=1, source_target_pairs={{0,3},{1,0},{2,1},{3,2},{4,7},{5,4},{6,5},{7,6},{8,11},{9,8},{10,9... | collective-permute-start | bytes 638984 | tf_op jit(solution)/shard_map/ppermute | solution.py:366
  35.8 3.4 %copy-start.5 = (bf16[4,208,736]{2,1,0:T(8,128)(2,1)S(1)}, bf16[4,208,736]{2,1,0:T(8,128)(2,1)}, u32[]{:S(2)}) copy-start(bf16[4,208,736]{2,1,0:T(8,128)(2,1)} %constant.10.clone.refs_1_) | copy-start | bytes 3674116
  40.3 18.5 %collective-permute-start.6 = (bf16[2,208,256]{2,1,0:T(8,128)(2,1)S(1)}, bf16[2,208,256]{2,1,0:T(8,128)(2,1)S(1)}, u32[]{:S(2)}, u32[]{:S(2)}) collective-permute-start(bf16[2,208,256]{2,1,0:T(8,128)(2,1)S(1)} %get-tuple-element.73), channel_id=1, source_target_pairs={{0,2},{1,3},{2,0},{3,1},{4,6},{5,7},{6,4},{7,5},{8,10},{9,11},{10,... | collective-permute-start | bytes 638984 | tf_op jit(solution)/shard_map/ppermute | solution.py:366
  43.0 21.4 %collective-permute-start.10 = (bf16[2,208,256]{2,1,0:T(8,128)(2,1)S(1)}, bf16[2,208,256]{2,1,0:T(8,128)(2,1)S(1)}, u32[]{:S(2)}, u32[]{:S(2)}) collective-permute-start(bf16[2,208,256]{2,1,0:T(8,128)(2,1)S(1)} %get-tuple-element.83), channel_id=1, source_target_pairs={{0,1},{1,2},{2,3},{3,0},{4,5},{5,6},{6,7},{7,4},{8,9},{9,10},{10,1... | collective-permute-start | bytes 638984 | tf_op jit(solution)/shard_map/ppermute | solution.py:366
  43.0 22.9 %collective-permute-start.11 = (bf16[2,208,256]{2,1,0:T(8,128)(2,1)S(1)}, bf16[2,208,256]{2,1,0:T(8,128)(2,1)S(1)}, u32[]{:S(2)}, u32[]{:S(2)}) collective-permute-start(bf16[2,208,256]{2,1,0:T(8,128)(2,1)S(1)} %get-tuple-element.84), channel_id=1, source_target_pairs={{0,3},{1,0},{2,1},{3,2},{4,7},{5,4},{6,5},{7,6},{8,11},{9,8},{10,9... | collective-permute-start | bytes 638984 | tf_op jit(solution)/shard_map/ppermute | solution.py:366
  54.1 3.4 %copy-start.7 = (bf16[1,1,4,2,368,256]{5,4,3,2,1,0:T(8,128)(2,1)S(1)}, bf16[1,1,4,2,368,256]{5,4,3,2,1,0:T(8,128)(2,1)}, u32[]{:S(2)}) copy-start(bf16[1,1,4,2,368,256]{5,4,3,2,1,0:T(8,128)(2,1)} %param.31) | copy-start | bytes 4521988
  57.5 8.5 %copy-start = (bf16[1,1,4,360,1024]{4,3,2,1,0:T(8,128)(2,1)S(1)}, bf16[1,1,4,360,1024]{4,3,2,1,0:T(8,128)(2,1)}, u32[]{:S(2)}) copy-start(bf16[1,1,4,360,1024]{4,3,2,1,0:T(8,128)(2,1)} %refs_1_.19) | copy-start | bytes 8847364
  58.8 7.2 %copy-start.2 = (bf16[1024,512]{1,0:T(8,128)(2,1)S(1)}, bf16[1024,512]{1,0:T(8,128)(2,1)}, u32[]{:S(2)}) copy-start(bf16[1024,512]{1,0:T(8,128)(2,1)} %refs_8_.9) | copy-start | bytes 3145732
  58.8 7.2 %copy-start.6 = (bf16[360,208]{1,0:T(8,128)(2,1)S(1)}, bf16[360,208]{1,0:T(8,128)(2,1)}, u32[]{:S(2)}) copy-start(bf16[360,208]{1,0:T(8,128)(2,1)} %constant.11.clone.refs_7_) | copy-start | bytes 449284
  58.8 7.2 %copy-start.11 = (s32[1,4]{1,0:T(1,128)S(1)}, s32[1,4]{1,0:T(1,128)}, u32[]{:S(2)}) copy-start(s32[1,4]{1,0:T(1,128)} %refs_0_.13) | copy-start | bytes 52
  59.9 16.3 %collective-permute-start.7 = (bf16[2,208,256]{2,1,0:T(8,128)(2,1)S(1)}, bf16[2,208,256]{2,1,0:T(8,128)(2,1)S(1)}, u32[]{:S(2)}, u32[]{:S(2)}) collective-permute-start(bf16[2,208,256]{2,1,0:T(8,128)(2,1)S(1)} %get-tuple-element.79), channel_id=1, source_target_pairs={{0,1},{1,2},{2,3},{3,0},{4,5},{5,6},{6,7},{7,4},{8,9},{9,10},{10,1... | collective-permute-start | bytes 638984 | tf_op jit(solution)/shard_map/ppermute | solution.py:366
  59.9 19.7 %collective-permute-start.8 = (bf16[2,208,256]{2,1,0:T(8,128)(2,1)S(1)}, bf16[2,208,256]{2,1,0:T(8,128)(2,1)S(1)}, u32[]{:S(2)}, u32[]{:S(2)}) collective-permute-start(bf16[2,208,256]{2,1,0:T(8,128)(2,1)S(1)} %get-tuple-element.80), channel_id=1, source_target_pairs={{0,2},{1,3},{2,0},{3,1},{4,6},{5,7},{6,4},{7,5},{8,10},{9,11},{10,... | collective-permute-start | bytes 638984 | tf_op jit(solution)/shard_map/ppermute | solution.py:366
  63.5 18.2 %collective-permute-start.9 = (bf16[2,208,256]{2,1,0:T(8,128)(2,1)S(1)}, bf16[2,208,256]{2,1,0:T(8,128)(2,1)S(1)}, u32[]{:S(2)}, u32[]{:S(2)}) collective-permute-start(bf16[2,208,256]{2,1,0:T(8,128)(2,1)S(1)} %get-tuple-element.81), channel_id=1, source_target_pairs={{0,3},{1,0},{2,1},{3,2},{4,7},{5,4},{6,5},{7,6},{8,11},{9,8},{10,9... | collective-permute-start | bytes 638984 | tf_op jit(solution)/shard_map/ppermute | solution.py:366
  64.4 26.7 %collective-permute-start.16 = (f32[264,128]{1,0:T(8,128)S(1)}, f32[264,128]{1,0:T(8,128)S(1)}, u32[]{:S(2)}, u32[]{:S(2)}) collective-permute-start(f32[264,128]{1,0:T(8,128)S(1)} %get-tuple-element.101), channel_id=1, source_target_pairs={{0,4},{4,0},{1,5},{5,1},{2,6},{6,2},{3,7},{7,3},{8,12},{12,8},{9,1... | collective-permute-start | bytes 405512 | tf_op jit(solution)/shard_map/ppermute | solution.py:577
  66.0 5.7 %copy-start.1 = (bf16[1024,1024]{1,0:T(8,128)(2,1)S(1)}, bf16[1024,1024]{1,0:T(8,128)(2,1)}, u32[]{:S(2)}) copy-start(bf16[1024,1024]{1,0:T(8,128)(2,1)} %refs_1_.21) | copy-start | bytes 6291460
  69.2 29.1 %collective-permute-start.13 = (bf16[2,360,256]{2,1,0:T(8,128)(2,1)S(1)}, bf16[2,360,256]{2,1,0:T(8,128)(2,1)S(1)}, u32[]{:S(2)}, u32[]{:S(2)}) collective-permute-start(bf16[2,360,256]{2,1,0:T(8,128)(2,1)S(1)} %get-tuple-element.97.refs_3_), channel_id=1, source_target_pairs={{0,4},{1,5},{2,6},{3,7},{8,12},{9,13},{10,14},{11,15},{16,20},{17,... | collective-permute-start | bytes 1105928 | tf_op jit(solution)/shard_map/ppermute | solution.py:564
  76.2 22.1 %collective-permute-start.14 = (bf16[2,360,256]{2,1,0:T(8,128)(2,1)S(1)}, bf16[2,360,256]{2,1,0:T(8,128)(2,1)S(1)}, u32[]{:S(2)}, u32[]{:S(2)}) collective-permute-start(bf16[2,360,256]{2,1,0:T(8,128)(2,1)S(1)} %get-tuple-element.98.refs_4_), channel_id=1, source_target_pairs={{0,4},{1,5},{2,6},{3,7},{8,12},{9,13},{10,14},{11,15},{16,20},{17,... | collective-permute-start | bytes 1105928 | tf_op jit(solution)/shard_map/ppermute | solution.py:564
  84.0 14.4 %collective-permute-start.15 = (bf16[1,360,512]{2,1,0:T(8,128)(2,1)S(1)}, bf16[1,360,512]{2,1,0:T(8,128)(2,1)S(1)}, u32[]{:S(2)}, u32[]{:S(2)}) collective-permute-start(bf16[1,360,512]{2,1,0:T(8,128)(2,1)S(1)} %get-tuple-element.100.refs_9_), channel_id=1, source_target_pairs={{0,4},{1,5},{2,6},{3,7},{8,12},{9,13},{10,14},{11,15},{16,20},{17,... | collective-permute-start | bytes 1105928 | tf_op jit(solution)/shard_map/ppermute | solution.py:564
  89.6 15.3 %collective-permute-start.12 = (bf16[1,360,512]{2,1,0:T(8,128)(2,1)S(1)}, bf16[1,360,512]{2,1,0:T(8,128)(2,1)S(1)}, u32[]{:S(2)}, u32[]{:S(2)}) collective-permute-start(bf16[1,360,512]{2,1,0:T(8,128)(2,1)S(1)} %get-tuple-element.95.refs_3_), channel_id=1, source_target_pairs={{0,4},{1,5},{2,6},{3,7},{8,12},{9,13},{10,14},{11,15},{16,20},{17,... | collective-permute-start | bytes 1105928 | tf_op jit(solution)/shard_map/ppermute | solution.py:564
  91.2 1.4 %collective-permute-start.17 = (f32[264,128]{1,0:T(8,128)S(1)}, f32[264,128]{1,0:T(8,128)S(1)}, u32[]{:S(2)}, u32[]{:S(2)}) collective-permute-start(f32[264,128]{1,0:T(8,128)S(1)} %add.9.refs_13_), channel_id=1, source_target_pairs={{0,8},{8,0},{16,24},{24,16},{1,9},{9,1},{17,25},{25,17},{2,10},{10... | collective-permute-start | bytes 405512 | tf_op jit(solution)/shard_map/ppermute | solution.py:581
  92.6 5.7 %collective-permute-start.18 = (f32[264,128]{1,0:T(8,128)S(1)}, f32[264,128]{1,0:T(8,128)S(1)}, u32[]{:S(2)}, u32[]{:S(2)}) collective-permute-start(f32[264,128]{1,0:T(8,128)S(1)} %add.10.refs_8_), channel_id=1, source_target_pairs={{0,16},{8,24},{16,0},{24,8},{1,17},{9,25},{17,1},{25,9},{2,18},{10... | collective-permute-start | bytes 405512 | tf_op jit(solution)/shard_map/ppermute | solution.py:581
  96.0 2.4 %copy-start.3 = (bf16[1024,1024]{1,0:T(8,128)(2,1)S(1)}, bf16[1024,1024]{1,0:T(8,128)(2,1)}, u32[]{:S(2)}) copy-start(bf16[1024,1024]{1,0:T(8,128)(2,1)} %refs_6_.5) | copy-start | bytes 6291460
  96.0 2.3 %copy-start.14 = (f32[16]{0:T(128)S(1)}, f32[16]{0:T(128)}, u32[]{:S(2)}) copy-start(f32[16]{0:T(128)} %refs_1_.23) | copy-start | bytes 196

commit v8 on v7

--- a/solution.py
+++ b/solution.py
@@ -601,13 +601,13 @@
     ("expand", 2, 1, False),
     ("expand", 3, 1, False),
     ("query", 2, 1, False),
+    ("add", 0, 0, False),
     ("query", 3, 1, False),
-    ("add", 0, 0, False),
     ("attend", 0, 3, False),
     ("add", 0, 0, False),
-    ("attend", 3, 1, False),
     ("add", 0, 0, False),
     ("sum", 0, 0, False),
+    ("attend", 3, 1, False),
 )
 
 

time: 109 us -> 109 us (level)
  transfers between devices with their start and end apart: 19 -> 19, of which waited for: 9 -> 9; matrix products, arithmetic and copies ran while one was open for 0% -> 0% of each run, Pallas kernels for 30% -> 31%
where the time goes in v8:
time: 109 us
  Pallas kernels  40.3 us (37%)
  waiting for transfers between devices  33.7 us (31%)
  starting transfers between devices  32.4 us (30%)
  between operations  1.64 us (2%)
    pallas_call x17, Pallas kernels, call(): pl.pallas_call(kernel, grid_spec=pltpu.PrefetchScalarGridSpec(num_scalar_...  40.3 us
    ppermute x12, waiting for transfers between devices, swap_blocks(): lax.ppermute(part, 'lon', [(i, (i + shift) % count) for i in range(count)])  31.2 us
    ppermute x12, starting transfers between devices, swap_blocks(): lax.ppermute(part, 'lon', [(i, (i + shift) % count) for i in range(count)])  18.5 us
    ppermute x4, starting transfers between devices, fused_body(): earlier = [lax.ppermute(part, 'frame', [(0, 1)]) for part in keyval]  10.8 us
    ppermute x3, starting transfers between devices, fused_body(): crossing = lax.ppermute(summed, *rounds.pop(0))  3.14 us
    ppermute x3, waiting for transfers between devices, fused_body(): crossing = lax.ppermute(summed, *rounds.pop(0))  2.45 us
  transfers between devices with their start and end apart: 19, of which 9 were waited for; matrix products, arithmetic and copies ran while one was open for 0% of the time, Pallas kernels for 31%

profile of v8, /device:TPU:8, one launch (start us, length us, event | category | flops | bytes accessed | tf_op | source)
XLA Modules:
  0.0 108.8 jit_solution(8080835727458907022)
XLA Ops:
  0.6 0.0 copy-start.10
  0.6 0.6 copy-done.10
  1.3 3.6 %shard_map.193 = (bf16[2,208,256]{2,1,0:T(8,128)(2,1)S(1)}, bf16[2,208,256]{2,1,0:T(8,128)(2,1)S(1)}, bf16[2,208,256]{2,1,0:T(8,128)(2,1)S(1)}, bf16[2,208,256]{2,1,0:T(8,128)(2,1)S(1)}, f32[8,128]{1,0:T(8,128)S(1)}) custom-call(s32[1,4]{1,0:T(1,128)S(1)} %copy-done.10, bf16[1,1,4,360,1024]{4,3,2,1,0:T(8,128)(2,1)} %refs_1_.19, bf16[720,1024]{1,0:T(8,128)(2,1)} %refs_2_.9, ...), custom_call_target="tpu_custom_call" | custom-call | flops 1024 | bytes 1024 | tf_op jit(solution)/shard_map/pallas_call | solution.py:339
  4.9 1.6 %collective-permute-start = (bf16[2,208,256]{2,1,0:T(8,128)(2,1)S(1)}, bf16[2,208,256]{2,1,0:T(8,128)(2,1)S(1)}, u32[]{:S(2)}, u32[]{:S(2)}) collective-permute-start(bf16[2,208,256]{2,1,0:T(8,128)(2,1)S(1)} %get-tuple-element.56), channel_id=1, source_target_pairs={{0,1},{1,2},{2,3},{3,0},{4,5},{5,6},{6,7},{7,4},{8,9},{9,10},{10,1... | collective-permute-start | bytes 638984 | tf_op jit(solution)/shard_map/ppermute | solution.py:366
  6.6 1.1 collective-permute-start.4
  7.6 1.9 %collective-permute-start.5 = (bf16[2,208,256]{2,1,0:T(8,128)(2,1)S(1)}, bf16[2,208,256]{2,1,0:T(8,128)(2,1)S(1)}, u32[]{:S(2)}, u32[]{:S(2)}) collective-permute-start(bf16[2,208,256]{2,1,0:T(8,128)(2,1)S(1)} %get-tuple-element.67), channel_id=1, source_target_pairs={{0,3},{1,0},{2,1},{3,2},{4,7},{5,4},{6,5},{7,6},{8,11},{9,8},{10,9... | collective-permute-start | bytes 638984 | tf_op jit(solution)/shard_map/ppermute | solution.py:366
  9.6 11.4 %collective-permute-done.refs_5_.refs_1_ = bf16[2,208,256]{2,1,0:T(8,128)(2,1)S(1)} collective-permute-done((bf16[2,208,256]{2,1,0:T(8,128)(2,1)S(1)}, bf16[2,208,256]{2,1,0:T(8,128)(2,1)S(1)}, u32[]{:S(2)}, u32[]{:S(2)}) %collective-permute-start) | collective-permute-done | bytes 213024 | tf_op jit(solution)/shard_map/ppermute | solution.py:366
  21.0 3.6 %shard_map.194 = (bf16[2,208,256]{2,1,0:T(8,128)(2,1)S(1)}, bf16[2,208,256]{2,1,0:T(8,128)(2,1)S(1)}, bf16[2,208,256]{2,1,0:T(8,128)(2,1)S(1)}, bf16[2,208,256]{2,1,0:T(8,128)(2,1)S(1)}, f32[8,128]{1,0:T(8,128)S(1)}) custom-call(s32[1,4]{1,0:T(1,128)S(1)} %copy-done.10, bf16[1,1,4,360,1024]{4,3,2,1,0:T(8,128)(2,1)} %refs_1_.19, bf16[720,1024]{1,0:T(8,128)(2,1)} %refs_2_.9, ...), custom_call_target="tpu_custom_call" | custom-call | flops 1024 | bytes 1024 | tf_op jit(solution)/shard_map/pallas_call | solution.py:339
  24.6 3.0 %collective-permute-start.1 = (bf16[2,208,256]{2,1,0:T(8,128)(2,1)S(1)}, bf16[2,208,256]{2,1,0:T(8,128)(2,1)S(1)}, u32[]{:S(2)}, u32[]{:S(2)}) collective-permute-start(bf16[2,208,256]{2,1,0:T(8,128)(2,1)S(1)} %get-tuple-element.59), channel_id=1, source_target_pairs={{0,1},{1,2},{2,3},{3,0},{4,5},{5,6},{6,7},{7,4},{8,9},{9,10},{10,1... | collective-permute-start | bytes 638984 | tf_op jit(solution)/shard_map/ppermute | solution.py:366
  27.6 0.0 collective-permute-start.2
  27.6 1.5 %collective-permute-start.3 = (bf16[2,208,256]{2,1,0:T(8,128)(2,1)S(1)}, bf16[2,208,256]{2,1,0:T(8,128)(2,1)S(1)}, u32[]{:S(2)}, u32[]{:S(2)}) collective-permute-start(bf16[2,208,256]{2,1,0:T(8,128)(2,1)S(1)} %get-tuple-element.61), channel_id=1, source_target_pairs={{0,3},{1,0},{2,1},{3,2},{4,7},{5,4},{6,5},{7,6},{8,11},{9,8},{10,9... | collective-permute-start | bytes 638984 | tf_op jit(solution)/shard_map/ppermute | solution.py:366
  29.1 0.2 shard_map.195
  29.3 3.3 %collective-permute-done.4.refs_2_ = bf16[2,208,256]{2,1,0:T(8,128)(2,1)S(1)} collective-permute-done((bf16[2,208,256]{2,1,0:T(8,128)(2,1)S(1)}, bf16[2,208,256]{2,1,0:T(8,128)(2,1)S(1)}, u32[]{:S(2)}, u32[]{:S(2)}) %collective-permute-start.4) | collective-permute-done | bytes 213024 | tf_op jit(solution)/shard_map/ppermute | solution.py:366
  32.7 3.2 %collective-permute-done.5.refs_3_ = bf16[2,208,256]{2,1,0:T(8,128)(2,1)S(1)} collective-permute-done((bf16[2,208,256]{2,1,0:T(8,128)(2,1)S(1)}, bf16[2,208,256]{2,1,0:T(8,128)(2,1)S(1)}, u32[]{:S(2)}, u32[]{:S(2)}) %collective-permute-start.5) | collective-permute-done | bytes 213024 | tf_op jit(solution)/shard_map/ppermute | solution.py:366
  35.8 0.0 copy-start.5
  35.8 3.4 %shard_map.196 = (bf16[2,736,256]{2,1,0:T(8,128)(2,1)S(1)}, bf16[2,736,256]{2,1,0:T(8,128)(2,1)S(1)}, f32[8,128]{1,0:T(8,128)S(1)}) custom-call(bf16[2,208,256]{2,1,0:T(8,128)(2,1)S(1)} %get-tuple-element.65.refs_0_, bf16[2,208,256]{2,1,0:T(8,128)(2,1)S(1)} %collective-permute-done.refs_5_.refs_1_, bf16[2,208,256]{2,1,0:T(8,128)(2,1)S(1)} %collective-permute-done.4.refs_2_, ...), custom_call_target="tpu_custom_call" | custom-call | flops 1024 | bytes 1024 | tf_op jit(solution)/shard_map/pallas_call | solution.py:339
  39.3 1.0 shard_map.197
  40.3 2.7 %collective-permute-start.6 = (bf16[2,208,256]{2,1,0:T(8,128)(2,1)S(1)}, bf16[2,208,256]{2,1,0:T(8,128)(2,1)S(1)}, u32[]{:S(2)}, u32[]{:S(2)}) collective-permute-start(bf16[2,208,256]{2,1,0:T(8,128)(2,1)S(1)} %get-tuple-element.73), channel_id=1, source_target_pairs={{0,2},{1,3},{2,0},{3,1},{4,6},{5,7},{6,4},{7,5},{8,10},{9,11},{10,... | collective-permute-start | bytes 638984 | tf_op jit(solution)/shard_map/ppermute | solution.py:366
  43.0 0.0 collective-permute-start.10
  43.0 0.0 collective-permute-done.1.refs_1_
  43.0 2.0 %collective-permute-start.11 = (bf16[2,208,256]{2,1,0:T(8,128)(2,1)S(1)}, bf16[2,208,256]{2,1,0:T(8,128)(2,1)S(1)}, u32[]{:S(2)}, u32[]{:S(2)}) collective-permute-start(bf16[2,208,256]{2,1,0:T(8,128)(2,1)S(1)} %get-tuple-element.84), channel_id=1, source_target_pairs={{0,3},{1,0},{2,1},{3,2},{4,7},{5,4},{6,5},{7,6},{8,11},{9,8},{10,9... | collective-permute-start | bytes 638984 | tf_op jit(solution)/shard_map/ppermute | solution.py:366
  45.1 3.8 %collective-permute-done.2.refs_2_ = bf16[2,208,256]{2,1,0:T(8,128)(2,1)S(1)} collective-permute-done((bf16[2,208,256]{2,1,0:T(8,128)(2,1)S(1)}, bf16[2,208,256]{2,1,0:T(8,128)(2,1)S(1)}, u32[]{:S(2)}, u32[]{:S(2)}) %collective-permute-start.2) | collective-permute-done | bytes 213024 | tf_op jit(solution)/shard_map/ppermute | solution.py:366
  48.8 5.3 %collective-permute-done.3.refs_3_ = bf16[2,208,256]{2,1,0:T(8,128)(2,1)S(1)} collective-permute-done((bf16[2,208,256]{2,1,0:T(8,128)(2,1)S(1)}, bf16[2,208,256]{2,1,0:T(8,128)(2,1)S(1)}, u32[]{:S(2)}, u32[]{:S(2)}) %collective-permute-start.3) | collective-permute-done | bytes 213024 | tf_op jit(solution)/shard_map/ppermute | solution.py:366
  54.1 3.4 %shard_map.198 = (bf16[2,736,256]{2,1,0:T(8,128)(2,1)S(1)}, bf16[2,736,256]{2,1,0:T(8,128)(2,1)S(1)}, f32[8,128]{1,0:T(8,128)S(1)}) custom-call(bf16[2,208,256]{2,1,0:T(8,128)(2,1)S(1)} %get-tuple-element.58.refs_0_, bf16[2,208,256]{2,1,0:T(8,128)(2,1)S(1)} %collective-permute-done.1.refs_1_, bf16[2,208,256]{2,1,0:T(8,128)(2,1)S(1)} %collective-permute-done.2.refs_2_, ...), custom_call_target="tpu_custom_call" | custom-call | flops 1024 | bytes 1024 | tf_op jit(solution)/shard_map/pallas_call | solution.py:339
  57.5 0.0 copy-start
  57.5 1.3 %shard_map.199 = (f32[264,128]{1,0:T(8,128)S(1)}, f32[8,128]{1,0:T(8,128)S(1)}) custom-call(bf16[2,736,256]{2,1,0:T(8,128)(2,1)S(1)} %get-tuple-element.74.refs_0_, bf16[2,736,256]{2,1,0:T(8,128)(2,1)S(1)} %get-tuple-element.75.refs_1_, bf16[4,2,368,256]{3,2,1,0:T(8,128)(2,1)S(1)} %bitcast.2, f32[8,128]{1,0:T(8,128)S(1)} %get-tuple-element.76.refs_3_), custom_call_target="tpu_custom_call" | custom-call | flops 1024 | bytes 1024 | tf_op jit(solution)/shard_map/pallas_call | solution.py:339
  58.8 0.0 copy-start.2
  58.8 0.0 copy-start.6
  58.8 0.0 copy-start.11
  58.8 0.0 collective-permute-done.6.refs_2_.refs_5_
  58.8 1.0 shard_map.200
  59.9 0.1 collective-permute-start.7
  59.9 3.6 %collective-permute-start.8 = (bf16[2,208,256]{2,1,0:T(8,128)(2,1)S(1)}, bf16[2,208,256]{2,1,0:T(8,128)(2,1)S(1)}, u32[]{:S(2)}, u32[]{:S(2)}) collective-permute-start(bf16[2,208,256]{2,1,0:T(8,128)(2,1)S(1)} %get-tuple-element.80), channel_id=1, source_target_pairs={{0,2},{1,3},{2,0},{3,1},{4,6},{5,7},{6,4},{7,5},{8,10},{9,11},{10,... | collective-permute-start | bytes 638984 | tf_op jit(solution)/shard_map/ppermute | solution.py:366
  63.5 0.9 collective-permute-start.9
  64.4 0.0 collective-permute-done.10.refs_4_
  64.4 1.5 %collective-permute-start.12 = (f32[264,128]{1,0:T(8,128)S(1)}, f32[264,128]{1,0:T(8,128)S(1)}, u32[]{:S(2)}, u32[]{:S(2)}) collective-permute-start(f32[264,128]{1,0:T(8,128)S(1)} %get-tuple-element.91), channel_id=1, source_target_pairs={{0,4},{4,0},{1,5},{5,1},{2,6},{6,2},{3,7},{7,3},{8,12},{12,8},{9,1... | collective-permute-start | bytes 405512 | tf_op jit(solution)/shard_map/ppermute | solution.py:577
  65.9 0.0 collective-permute-done.11.refs_6_
  66.0 0.0 copy-start.1
  66.0 3.2 %shard_map.201 = (bf16[2,360,1024]{2,1,0:T(8,128)(2,1)S(1)}, bf16[2,360,256]{2,1,0:T(8,128)(2,1)S(1)}, bf16[2,360,256]{2,1,0:T(8,128)(2,1)S(1)}, f32[8,128]{1,0:T(8,128)S(1)}) custom-call(s32[1,4]{1,0:T(1,128)S(1)} %copy-done.11, bf16[1,1,4,360,1024]{4,3,2,1,0:T(8,128)(2,1)S(1)} %copy-done, bf16[720,1024]{1,0:T(8,128)(2,1)} %refs_2_.9, ...), custom_call_target="tpu_custom_call" | custom-call | flops 1024 | bytes 1024 | tf_op jit(solution)/shard_map/pallas_call | solution.py:339
  69.2 2.5 %collective-permute-start.14 = (bf16[2,360,256]{2,1,0:T(8,128)(2,1)S(1)}, bf16[2,360,256]{2,1,0:T(8,128)(2,1)S(1)}, u32[]{:S(2)}, u32[]{:S(2)}) collective-permute-start(bf16[2,360,256]{2,1,0:T(8,128)(2,1)S(1)} %get-tuple-element.98.refs_3_), channel_id=1, source_target_pairs={{0,4},{1,5},{2,6},{3,7},{8,12},{9,13},{10,14},{11,15},{16,20},{17,... | collective-permute-start | bytes 1105928 | tf_op jit(solution)/shard_map/ppermute | solution.py:564
  71.7 2.3 %shard_map.202 = (bf16[2,360,1024]{2,1,0:T(8,128)(2,1)S(1)}, f32[8,128]{1,0:T(8,128)S(1)}) custom-call(bf16[2,360,1024]{2,1,0:T(8,128)(2,1)S(1)} %get-tuple-element.86.refs_0_.refs_7_, bf16[1024,1024]{1,0:T(8,128)(2,1)S(1)} %copy-done.1, f32[8,128]{1,0:T(8,128)S(1)} %get-tuple-element.87.refs_2_), custom_call_target="tpu_custom_call" | custom-call | flops 1024 | bytes 1024 | tf_op jit(solution)/shard_map/pallas_call | solution.py:339
  74.0 2.2 %collective-permute-done.7.refs_4_ = bf16[2,208,256]{2,1,0:T(8,128)(2,1)S(1)} collective-permute-done((bf16[2,208,256]{2,1,0:T(8,128)(2,1)S(1)}, bf16[2,208,256]{2,1,0:T(8,128)(2,1)S(1)}, u32[]{:S(2)}, u32[]{:S(2)}) %collective-permute-start.7) | collective-permute-done | bytes 213024 | tf_op jit(solution)/shard_map/ppermute | solution.py:366
  76.2 3.4 %collective-permute-start.15 = (bf16[2,360,256]{2,1,0:T(8,128)(2,1)S(1)}, bf16[2,360,256]{2,1,0:T(8,128)(2,1)S(1)}, u32[]{:S(2)}, u32[]{:S(2)}) collective-permute-start(bf16[2,360,256]{2,1,0:T(8,128)(2,1)S(1)} %get-tuple-element.99.refs_4_), channel_id=1, source_target_pairs={{0,4},{1,5},{2,6},{3,7},{8,12},{9,13},{10,14},{11,15},{16,20},{17,... | collective-permute-start | bytes 1105928 | tf_op jit(solution)/shard_map/ppermute | solution.py:564
  79.6 0.0 collective-permute-done.8.refs_5_
  79.6 2.2 %collective-permute-done.9.refs_6_ = bf16[2,208,256]{2,1,0:T(8,128)(2,1)S(1)} collective-permute-done((bf16[2,208,256]{2,1,0:T(8,128)(2,1)S(1)}, bf16[2,208,256]{2,1,0:T(8,128)(2,1)S(1)}, u32[]{:S(2)}, u32[]{:S(2)}) %collective-permute-start.9) | collective-permute-done | bytes 213024 | tf_op jit(solution)/shard_map/ppermute | solution.py:366
  81.8 2.2 %shard_map.203 = (bf16[1,360,1024]{2,1,0:T(8,128)(2,1)S(1)}, bf16[1,360,512]{2,1,0:T(8,128)(2,1)S(1)}, f32[8,128]{1,0:T(8,128)S(1)}) custom-call(s32[1,4]{1,0:T(1,128)S(1)} %copy-done.11, bf16[1,1,4,360,1024]{4,3,2,1,0:T(8,128)(2,1)S(1)} %copy-done, bf16[720,1024]{1,0:T(8,128)(2,1)} %refs_2_.9, bf16[2,208,256]{2,1,0:T(8,128)(2,1)S(1)} %get-tuple-element.78.refs_3_, ...), custom_call_target="tpu_custom_call" | custom-call | flops 1024 | bytes 1024 | tf_op jit(solution)/shard_map/pallas_call | solution.py:339
  84.0 3.4 %collective-permute-start.16 = (bf16[1,360,512]{2,1,0:T(8,128)(2,1)S(1)}, bf16[1,360,512]{2,1,0:T(8,128)(2,1)S(1)}, u32[]{:S(2)}, u32[]{:S(2)}) collective-permute-start(bf16[1,360,512]{2,1,0:T(8,128)(2,1)S(1)} %get-tuple-element.101.refs_9_), channel_id=1, source_target_pairs={{0,4},{1,5},{2,6},{3,7},{8,12},{9,13},{10,14},{11,15},{16,20},{17,... | collective-permute-start | bytes 1105928 | tf_op jit(solution)/shard_map/ppermute | solution.py:564
  87.4 2.2 %shard_map.204 = (bf16[1,360,1024]{2,1,0:T(8,128)(2,1)S(1)}, bf16[1,360,512]{2,1,0:T(8,128)(2,1)S(1)}, f32[8,128]{1,0:T(8,128)S(1)}) custom-call(s32[1,4]{1,0:T(1,128)S(1)} %copy-done.11, bf16[1,1,4,360,1024]{4,3,2,1,0:T(8,128)(2,1)S(1)} %copy-done, bf16[720,1024]{1,0:T(8,128)(2,1)} %refs_2_.9, bf16[2,208,256]{2,1,0:T(8,128)(2,1)S(1)} %get-tuple-element.78.refs_3_, ...), custom_call_target="tpu_custom_call" | custom-call | flops 1024 | bytes 1024 | tf_op jit(solution)/shard_map/pallas_call | solution.py:339
  89.6 1.5 %collective-permute-start.13 = (bf16[1,360,512]{2,1,0:T(8,128)(2,1)S(1)}, bf16[1,360,512]{2,1,0:T(8,128)(2,1)S(1)}, u32[]{:S(2)}, u32[]{:S(2)}) collective-permute-start(bf16[1,360,512]{2,1,0:T(8,128)(2,1)S(1)} %get-tuple-element.96.refs_3_), channel_id=1, source_target_pairs={{0,4},{1,5},{2,6},{3,7},{8,12},{9,13},{10,14},{11,15},{16,20},{17,... | collective-permute-start | bytes 1105928 | tf_op jit(solution)/shard_map/ppermute | solution.py:564
  91.1 0.0 collective-permute-done.12
  91.2 0.1 collective-permute-start.17
  91.2 1.3 %collective-permute-done.17 = f32[264,128]{1,0:T(8,128)S(1)} collective-permute-done((f32[264,128]{1,0:T(8,128)S(1)}, f32[264,128]{1,0:T(8,128)S(1)}, u32[]{:S(2)}, u32[]{:S(2)}) %collective-permute-start.17) | collective-permute-done | bytes 135200 | tf_op jit(solution)/shard_map/ppermute | solution.py:581
  92.6 1.6 %collective-permute-start.18 = (f32[264,128]{1,0:T(8,128)S(1)}, f32[264,128]{1,0:T(8,128)S(1)}, u32[]{:S(2)}, u32[]{:S(2)}) collective-permute-start(f32[264,128]{1,0:T(8,128)S(1)} %add.10.refs_1_), channel_id=1, source_target_pairs={{0,16},{8,24},{16,0},{24,8},{1,17},{9,25},{17,1},{25,9},{2,18},{10... | collective-permute-start | bytes 405512 | tf_op jit(solution)/shard_map/ppermute | solution.py:581
  94.8 1.2 %shard_map.205 = (bf16[1,360,1024]{2,1,0:T(8,128)(2,1)S(1)}, f32[8,128]{1,0:T(8,128)S(1)}) custom-call(bf16[1,360,1024]{2,1,0:T(8,128)(2,1)S(1)} %get-tuple-element.92.refs_0_.refs_11_, bf16[1024,1024]{1,0:T(8,128)(2,1)S(1)} %copy-done.1, f32[8,128]{1,0:T(8,128)S(1)} %get-tuple-element.93.refs_2_), custom_call_target="tpu_custom_call" | custom-call | flops 1024 | bytes 1024 | tf_op jit(solution)/shard_map/pallas_call | solution.py:339
  96.0 0.0 copy-start.3
  96.0 0.0 copy-start.14
  96.0 1.2 %shard_map.206 = (bf16[1,360,1024]{2,1,0:T(8,128)(2,1)S(1)}, f32[8,128]{1,0:T(8,128)S(1)}) custom-call(bf16[1,360,1024]{2,1,0:T(8,128)(2,1)S(1)} %get-tuple-element.90.refs_0_.refs_5_, bf16[1024,1024]{1,0:T(8,128)(2,1)S(1)} %copy-done.1, f32[264,128]{1,0:T(8,128)S(1)} %add.9.refs_2_, f32[8,128]{1,0:T(8,128)S(1)} %get-tuple-element.94.refs_3_), custom_call_target="tpu_custom_call" | custom-call | flops 1024 | bytes 1024 | tf_op jit(solution)/shard_map/pallas_call | solution.py:339
  97.2 1.1 %collective-permute-done.18 = f32[264,128]{1,0:T(8,128)S(1)} collective-permute-done((f32[264,128]{1,0:T(8,128)S(1)}, f32[264,128]{1,0:T(8,128)S(1)}, u32[]{:S(2)}, u32[]{:S(2)}) %collective-permute-start.18) | collective-permute-done | bytes 135200 | tf_op jit(solution)/shard_map/ppermute | solution.py:581
  98.3 0.0 collective-permute-done.14.refs_5_
  98.3 0.0 collective-permute-done.15.refs_6_
  98.4 6.5 %shard_map.207 = (bf16[1,1,4,360,1024]{4,3,2,1,0:T(8,128)(2,1)}, f32[8,128]{1,0:T(8,128)S(1)}) custom-call(s32[1]{0:T(128)S(6)} %copy.23.refs_0_, f32[16]{0:T(128)S(1)} %copy-done.14, bf16[2,360,1024]{2,1,0:T(8,128)(2,1)S(1)} %get-tuple-element.97.refs_2_, bf16[2,360,256]{2,1,0:T(8,128)(2,1)S(1)} %get-tuple-element.98.refs_3_, ...), custom_call_target="tpu_custom_call" | custom-call | flops 1024 | bytes 1024 | tf_op jit(solution)/shard_map/pallas_call | solution.py:339
  104.9 0.8 shard_map.208
  105.7 0.0 collective-permute-done.13.refs_4_
  105.7 3.1 %shard_map.209 = (bf16[1,1,4,360,1024]{4,3,2,1,0:T(8,128)(2,1)}, f32[8,128]{1,0:T(8,128)}) custom-call(s32[1]{0:T(128)S(6)} %copy.23.refs_0_, f32[16]{0:T(128)S(1)} %copy-done.14, bf16[1,360,1024]{2,1,0:T(8,128)(2,1)S(1)} %get-tuple-element.95.refs_2_, bf16[1,360,512]{2,1,0:T(8,128)(2,1)S(1)} %get-tuple-element.96.refs_3_, ...), custom_call_target="tpu_custom_call", output_to_operand_aliasing={{0}: (7, {})} | custom-call | flops 1024 | bytes 1024 | tf_op jit(solution)/shard_map/pallas_call | solution.py:339
  (24 shorter events, 0.1 us)
Async XLA Ops:
  0.6 0.7 copy-start.10
  4.9 16.0 %collective-permute-start = (bf16[2,208,256]{2,1,0:T(8,128)(2,1)S(1)}, bf16[2,208,256]{2,1,0:T(8,128)(2,1)S(1)}, u32[]{:S(2)}, u32[]{:S(2)}) collective-permute-start(bf16[2,208,256]{2,1,0:T(8,128)(2,1)S(1)} %get-tuple-element.56), channel_id=1, source_target_pairs={{0,1},{1,2},{2,3},{3,0},{4,5},{5,6},{6,7},{7,4},{8,9},{9,10},{10,1... | collective-permute-start | bytes 638984 | tf_op jit(solution)/shard_map/ppermute | solution.py:366
  6.6 26.1 %collective-permute-start.4 = (bf16[2,208,256]{2,1,0:T(8,128)(2,1)S(1)}, bf16[2,208,256]{2,1,0:T(8,128)(2,1)S(1)}, u32[]{:S(2)}, u32[]{:S(2)}) collective-permute-start(bf16[2,208,256]{2,1,0:T(8,128)(2,1)S(1)} %get-tuple-element.66), channel_id=1, source_target_pairs={{0,2},{1,3},{2,0},{3,1},{4,6},{5,7},{6,4},{7,5},{8,10},{9,11},{10,... | collective-permute-start | bytes 638984 | tf_op jit(solution)/shard_map/ppermute | solution.py:366
  7.6 28.2 %collective-permute-start.5 = (bf16[2,208,256]{2,1,0:T(8,128)(2,1)S(1)}, bf16[2,208,256]{2,1,0:T(8,128)(2,1)S(1)}, u32[]{:S(2)}, u32[]{:S(2)}) collective-permute-start(bf16[2,208,256]{2,1,0:T(8,128)(2,1)S(1)} %get-tuple-element.67), channel_id=1, source_target_pairs={{0,3},{1,0},{2,1},{3,2},{4,7},{5,4},{6,5},{7,6},{8,11},{9,8},{10,9... | collective-permute-start | bytes 638984 | tf_op jit(solution)/shard_map/ppermute | solution.py:366
  21.0 8.2 %copy-start.8 = (bf16[2,4,64,64]{3,2,1,0:T(8,128)(2,1)S(1)}, bf16[2,4,64,64]{3,2,1,0:T(8,128)(2,1)}, u32[]{:S(2)}) copy-start(bf16[2,4,64,64]{3,2,1,0:T(8,128)(2,1)} %refs_0_.10) | copy-start | bytes 196612
  21.0 8.2 %copy-start.9 = (bf16[2,4,64,64]{3,2,1,0:T(8,128)(2,1)S(1)}, bf16[2,4,64,64]{3,2,1,0:T(8,128)(2,1)}, u32[]{:S(2)}) copy-start(bf16[2,4,64,64]{3,2,1,0:T(8,128)(2,1)} %refs_1_.15) | copy-start | bytes 196612
  21.0 14.9 %copy-start.4 = (bf16[736,832]{1,0:T(8,128)(2,1)S(1)}, bf16[736,832]{1,0:T(8,128)(2,1)}, u32[]{:S(2)}) copy-start(bf16[736,832]{1,0:T(8,128)(2,1)} %constant.9.clone.refs_4_) | copy-start | bytes 3674116
  21.0 14.9 %copy-start.12 = (f32[2,256]{1,0:T(2,128)S(1)}, f32[2,256]{1,0:T(2,128)}, u32[]{:S(2)}) copy-start(f32[2,256]{1,0:T(2,128)} %refs_6_.4) | copy-start | bytes 6148
  21.0 14.9 %copy-start.13 = (f32[2,256]{1,0:T(2,128)S(1)}, f32[2,256]{1,0:T(2,128)}, u32[]{:S(2)}) copy-start(f32[2,256]{1,0:T(2,128)} %refs_8_.6) | copy-start | bytes 6148
  24.6 18.4 %collective-permute-start.1 = (bf16[2,208,256]{2,1,0:T(8,128)(2,1)S(1)}, bf16[2,208,256]{2,1,0:T(8,128)(2,1)S(1)}, u32[]{:S(2)}, u32[]{:S(2)}) collective-permute-start(bf16[2,208,256]{2,1,0:T(8,128)(2,1)S(1)} %get-tuple-element.59), channel_id=1, source_target_pairs={{0,1},{1,2},{2,3},{3,0},{4,5},{5,6},{6,7},{7,4},{8,9},{9,10},{10,1... | collective-permute-start | bytes 638984 | tf_op jit(solution)/shard_map/ppermute | solution.py:366
  27.6 21.2 %collective-permute-start.2 = (bf16[2,208,256]{2,1,0:T(8,128)(2,1)S(1)}, bf16[2,208,256]{2,1,0:T(8,128)(2,1)S(1)}, u32[]{:S(2)}, u32[]{:S(2)}) collective-permute-start(bf16[2,208,256]{2,1,0:T(8,128)(2,1)S(1)} %get-tuple-element.60), channel_id=1, source_target_pairs={{0,2},{1,3},{2,0},{3,1},{4,6},{5,7},{6,4},{7,5},{8,10},{9,11},{10,... | collective-permute-start | bytes 638984 | tf_op jit(solution)/shard_map/ppermute | solution.py:366
  27.6 26.5 %collective-permute-start.3 = (bf16[2,208,256]{2,1,0:T(8,128)(2,1)S(1)}, bf16[2,208,256]{2,1,0:T(8,128)(2,1)S(1)}, u32[]{:S(2)}, u32[]{:S(2)}) collective-permute-start(bf16[2,208,256]{2,1,0:T(8,128)(2,1)S(1)} %get-tuple-element.61), channel_id=1, source_target_pairs={{0,3},{1,0},{2,1},{3,2},{4,7},{5,4},{6,5},{7,6},{8,11},{9,8},{10,9... | collective-permute-start | bytes 638984 | tf_op jit(solution)/shard_map/ppermute | solution.py:366
  35.8 3.4 %copy-start.5 = (bf16[4,208,736]{2,1,0:T(8,128)(2,1)S(1)}, bf16[4,208,736]{2,1,0:T(8,128)(2,1)}, u32[]{:S(2)}) copy-start(bf16[4,208,736]{2,1,0:T(8,128)(2,1)} %constant.10.clone.refs_1_) | copy-start | bytes 3674116
  40.3 18.5 %collective-permute-start.6 = (bf16[2,208,256]{2,1,0:T(8,128)(2,1)S(1)}, bf16[2,208,256]{2,1,0:T(8,128)(2,1)S(1)}, u32[]{:S(2)}, u32[]{:S(2)}) collective-permute-start(bf16[2,208,256]{2,1,0:T(8,128)(2,1)S(1)} %get-tuple-element.73), channel_id=1, source_target_pairs={{0,2},{1,3},{2,0},{3,1},{4,6},{5,7},{6,4},{7,5},{8,10},{9,11},{10,... | collective-permute-start | bytes 638984 | tf_op jit(solution)/shard_map/ppermute | solution.py:366
  43.0 21.4 %collective-permute-start.10 = (bf16[2,208,256]{2,1,0:T(8,128)(2,1)S(1)}, bf16[2,208,256]{2,1,0:T(8,128)(2,1)S(1)}, u32[]{:S(2)}, u32[]{:S(2)}) collective-permute-start(bf16[2,208,256]{2,1,0:T(8,128)(2,1)S(1)} %get-tuple-element.83), channel_id=1, source_target_pairs={{0,1},{1,2},{2,3},{3,0},{4,5},{5,6},{6,7},{7,4},{8,9},{9,10},{10,1... | collective-permute-start | bytes 638984 | tf_op jit(solution)/shard_map/ppermute | solution.py:366
  43.0 22.9 %collective-permute-start.11 = (bf16[2,208,256]{2,1,0:T(8,128)(2,1)S(1)}, bf16[2,208,256]{2,1,0:T(8,128)(2,1)S(1)}, u32[]{:S(2)}, u32[]{:S(2)}) collective-permute-start(bf16[2,208,256]{2,1,0:T(8,128)(2,1)S(1)} %get-tuple-element.84), channel_id=1, source_target_pairs={{0,3},{1,0},{2,1},{3,2},{4,7},{5,4},{6,5},{7,6},{8,11},{9,8},{10,9... | collective-permute-start | bytes 638984 | tf_op jit(solution)/shard_map/ppermute | solution.py:366
  54.1 3.4 %copy-start.7 = (bf16[1,1,4,2,368,256]{5,4,3,2,1,0:T(8,128)(2,1)S(1)}, bf16[1,1,4,2,368,256]{5,4,3,2,1,0:T(8,128)(2,1)}, u32[]{:S(2)}) copy-start(bf16[1,1,4,2,368,256]{5,4,3,2,1,0:T(8,128)(2,1)} %param.31) | copy-start | bytes 4521988
  57.5 8.5 %copy-start = (bf16[1,1,4,360,1024]{4,3,2,1,0:T(8,128)(2,1)S(1)}, bf16[1,1,4,360,1024]{4,3,2,1,0:T(8,128)(2,1)}, u32[]{:S(2)}) copy-start(bf16[1,1,4,360,1024]{4,3,2,1,0:T(8,128)(2,1)} %refs_1_.19) | copy-start | bytes 8847364
  58.8 7.2 %copy-start.2 = (bf16[1024,512]{1,0:T(8,128)(2,1)S(1)}, bf16[1024,512]{1,0:T(8,128)(2,1)}, u32[]{:S(2)}) copy-start(bf16[1024,512]{1,0:T(8,128)(2,1)} %refs_8_.9) | copy-start | bytes 3145732
  58.8 7.2 %copy-start.6 = (bf16[360,208]{1,0:T(8,128)(2,1)S(1)}, bf16[360,208]{1,0:T(8,128)(2,1)}, u32[]{:S(2)}) copy-start(bf16[360,208]{1,0:T(8,128)(2,1)} %constant.11.clone.refs_7_) | copy-start | bytes 449284
  58.8 7.2 %copy-start.11 = (s32[1,4]{1,0:T(1,128)S(1)}, s32[1,4]{1,0:T(1,128)}, u32[]{:S(2)}) copy-start(s32[1,4]{1,0:T(1,128)} %refs_0_.13) | copy-start | bytes 52
  59.9 16.3 %collective-permute-start.7 = (bf16[2,208,256]{2,1,0:T(8,128)(2,1)S(1)}, bf16[2,208,256]{2,1,0:T(8,128)(2,1)S(1)}, u32[]{:S(2)}, u32[]{:S(2)}) collective-permute-start(bf16[2,208,256]{2,1,0:T(8,128)(2,1)S(1)} %get-tuple-element.79), channel_id=1, source_target_pairs={{0,1},{1,2},{2,3},{3,0},{4,5},{5,6},{6,7},{7,4},{8,9},{9,10},{10,1... | collective-permute-start | bytes 638984 | tf_op jit(solution)/shard_map/ppermute | solution.py:366
  59.9 19.7 %collective-permute-start.8 = (bf16[2,208,256]{2,1,0:T(8,128)(2,1)S(1)}, bf16[2,208,256]{2,1,0:T(8,128)(2,1)S(1)}, u32[]{:S(2)}, u32[]{:S(2)}) collective-permute-start(bf16[2,208,256]{2,1,0:T(8,128)(2,1)S(1)} %get-tuple-element.80), channel_id=1, source_target_pairs={{0,2},{1,3},{2,0},{3,1},{4,6},{5,7},{6,4},{7,5},{8,10},{9,11},{10,... | collective-permute-start | bytes 638984 | tf_op jit(solution)/shard_map/ppermute | solution.py:366
  63.5 18.2 %collective-permute-start.9 = (bf16[2,208,256]{2,1,0:T(8,128)(2,1)S(1)}, bf16[2,208,256]{2,1,0:T(8,128)(2,1)S(1)}, u32[]{:S(2)}, u32[]{:S(2)}) collective-permute-start(bf16[2,208,256]{2,1,0:T(8,128)(2,1)S(1)} %get-tuple-element.81), channel_id=1, source_target_pairs={{0,3},{1,0},{2,1},{3,2},{4,7},{5,4},{6,5},{7,6},{8,11},{9,8},{10,9... | collective-permute-start | bytes 638984 | tf_op jit(solution)/shard_map/ppermute | solution.py:366
  64.4 26.7 %collective-permute-start.12 = (f32[264,128]{1,0:T(8,128)S(1)}, f32[264,128]{1,0:T(8,128)S(1)}, u32[]{:S(2)}, u32[]{:S(2)}) collective-permute-start(f32[264,128]{1,0:T(8,128)S(1)} %get-tuple-element.91), channel_id=1, source_target_pairs={{0,4},{4,0},{1,5},{5,1},{2,6},{6,2},{3,7},{7,3},{8,12},{12,8},{9,1... | collective-permute-start | bytes 405512 | tf_op jit(solution)/shard_map/ppermute | solution.py:577
  66.0 5.7 %copy-start.1 = (bf16[1024,1024]{1,0:T(8,128)(2,1)S(1)}, bf16[1024,1024]{1,0:T(8,128)(2,1)}, u32[]{:S(2)}) copy-start(bf16[1024,1024]{1,0:T(8,128)(2,1)} %refs_1_.21) | copy-start | bytes 6291460
  69.2 29.1 %collective-permute-start.14 = (bf16[2,360,256]{2,1,0:T(8,128)(2,1)S(1)}, bf16[2,360,256]{2,1,0:T(8,128)(2,1)S(1)}, u32[]{:S(2)}, u32[]{:S(2)}) collective-permute-start(bf16[2,360,256]{2,1,0:T(8,128)(2,1)S(1)} %get-tuple-element.98.refs_3_), channel_id=1, source_target_pairs={{0,4},{1,5},{2,6},{3,7},{8,12},{9,13},{10,14},{11,15},{16,20},{17,... | collective-permute-start | bytes 1105928 | tf_op jit(solution)/shard_map/ppermute | solution.py:564
  76.2 22.1 %collective-permute-start.15 = (bf16[2,360,256]{2,1,0:T(8,128)(2,1)S(1)}, bf16[2,360,256]{2,1,0:T(8,128)(2,1)S(1)}, u32[]{:S(2)}, u32[]{:S(2)}) collective-permute-start(bf16[2,360,256]{2,1,0:T(8,128)(2,1)S(1)} %get-tuple-element.99.refs_4_), channel_id=1, source_target_pairs={{0,4},{1,5},{2,6},{3,7},{8,12},{9,13},{10,14},{11,15},{16,20},{17,... | collective-permute-start | bytes 1105928 | tf_op jit(solution)/shard_map/ppermute | solution.py:564
  84.0 14.4 %collective-permute-start.16 = (bf16[1,360,512]{2,1,0:T(8,128)(2,1)S(1)}, bf16[1,360,512]{2,1,0:T(8,128)(2,1)S(1)}, u32[]{:S(2)}, u32[]{:S(2)}) collective-permute-start(bf16[1,360,512]{2,1,0:T(8,128)(2,1)S(1)} %get-tuple-element.101.refs_9_), channel_id=1, source_target_pairs={{0,4},{1,5},{2,6},{3,7},{8,12},{9,13},{10,14},{11,15},{16,20},{17,... | collective-permute-start | bytes 1105928 | tf_op jit(solution)/shard_map/ppermute | solution.py:564
  89.6 16.1 %collective-permute-start.13 = (bf16[1,360,512]{2,1,0:T(8,128)(2,1)S(1)}, bf16[1,360,512]{2,1,0:T(8,128)(2,1)S(1)}, u32[]{:S(2)}, u32[]{:S(2)}) collective-permute-start(bf16[1,360,512]{2,1,0:T(8,128)(2,1)S(1)} %get-tuple-element.96.refs_3_), channel_id=1, source_target_pairs={{0,4},{1,5},{2,6},{3,7},{8,12},{9,13},{10,14},{11,15},{16,20},{17,... | collective-permute-start | bytes 1105928 | tf_op jit(solution)/shard_map/ppermute | solution.py:564
  91.2 1.4 %collective-permute-start.17 = (f32[264,128]{1,0:T(8,128)S(1)}, f32[264,128]{1,0:T(8,128)S(1)}, u32[]{:S(2)}, u32[]{:S(2)}) collective-permute-start(f32[264,128]{1,0:T(8,128)S(1)} %add.9.refs_2_), channel_id=1, source_target_pairs={{0,8},{8,0},{16,24},{24,16},{1,9},{9,1},{17,25},{25,17},{2,10},{10... | collective-permute-start | bytes 405512 | tf_op jit(solution)/shard_map/ppermute | solution.py:581
  92.6 5.7 %collective-permute-start.18 = (f32[264,128]{1,0:T(8,128)S(1)}, f32[264,128]{1,0:T(8,128)S(1)}, u32[]{:S(2)}, u32[]{:S(2)}) collective-permute-start(f32[264,128]{1,0:T(8,128)S(1)} %add.10.refs_1_), channel_id=1, source_target_pairs={{0,16},{8,24},{16,0},{24,8},{1,17},{9,25},{17,1},{25,9},{2,18},{10... | collective-permute-start | bytes 405512 | tf_op jit(solution)/shard_map/ppermute | solution.py:581
  96.0 2.4 %copy-start.3 = (bf16[1024,1024]{1,0:T(8,128)(2,1)S(1)}, bf16[1024,1024]{1,0:T(8,128)(2,1)}, u32[]{:S(2)}) copy-start(bf16[1024,1024]{1,0:T(8,128)(2,1)} %refs_6_.5) | copy-start | bytes 6291460
  96.0 2.3 %copy-start.14 = (f32[16]{0:T(128)S(1)}, f32[16]{0:T(128)}, u32[]{:S(2)}) copy-start(f32[16]{0:T(128)} %refs_1_.23) | copy-start | bytes 196
